TPU v7x, 32 devices: a whole 2x2x4 slice. The times are simulated.
32 devices in a mesh: ctx: 16 (over z, y, x), tp: 2 (over core).
Axes of the slice: x: 2, y: 2, z: 4, core: 2. Of those that a mesh axis runs over, the one named last changes fastest.
Arguments:
- tokens: bfloat16 [2048, 4096], P('ctx'), may hold values from -6 to 6
- weights: bfloat16 [2, 2048, 3, 4096], P('tp', 'ctx'), may hold values from -0.09375 to 0.09375
- residues: float32 [2, 2048, 16], P('tp', 'ctx'), may hold values from -1.5 to 1.5
- decay_rates: float32 [2, 2048, 16], P('tp', 'ctx'), may hold values from 0.00024414062 to 0.03
- cotangent: bfloat16 [4096, 2048], P('tp', 'ctx'), may hold values from -6 to 6
Outputs:
- hyena_out: bfloat16 [4096, 2048], P('tp', 'ctx')
- grad_input: bfloat16 [2048, 4096], P('ctx', 'tp')
- grad_residue: float32 [2, 2048, 16], P('tp', 'ctx')
All inputs are finite; a program needn't handle non-finite values.
Results may differ from a plain program's by a relative error of at most 0.018.
Values may be sent and summed in bfloat16 or wider, within the bound.
No kernel may reach another device: no remote copies, remote signals or barrier semaphores. Data moves between devices by JAX's collectives and lax.ppermute only.
A program may use at most 128 MiB of HBM per device.

v0:
```python
import functools
import math

import jax
import jax.numpy as jnp
from jax import lax
from jax.experimental import pallas as pl
from jax.experimental.pallas import tpu as pltpu
from jax.sharding import PartitionSpec as P


def precise(form, left, right):
    return jnp.einsum(
        form, left, right, precision=lax.Precision.HIGHEST, preferred_element_type=jnp.float32
    )


def tripled(form, left, right):
    return jnp.einsum(
        form, left, right, precision=lax.Precision.HIGH, preferred_element_type=jnp.float32
    )


def angle_table(row_count, col_count, period):
    product = (
        jnp.arange(row_count, dtype=jnp.int32)[:, None]
        * jnp.arange(col_count, dtype=jnp.int32)[None, :]
        % period
    )
    angles = product.astype(jnp.float32) * (2.0 * math.pi / period)
    return (jnp.cos(angles), jnp.sin(angles))


def make_tables(length):
    padded = 2 * length
    outer = math.gcd(padded, 1 << (padded.bit_length() - 1) // 2)
    inner = padded // outer
    cos_outer, sin_outer = angle_table(outer, outer, outer)
    cos_inner, sin_inner = angle_table(inner, inner, inner)
    twist_cos, twist_sin = angle_table(outer, inner, padded)
    return (outer, inner, cos_outer, sin_outer, cos_inner, sin_inner, twist_cos, twist_sin)


def spectrum(signal, tables, product):
    outer, inner, cos_outer, sin_outer, cos_inner, sin_inner, twist_cos, twist_sin = tables
    half_rows = outer // 2
    blocks = signal.reshape(signal.shape[0], half_rows, inner)
    first_re = product("kp,bpq->bkq", cos_outer[:, :half_rows], blocks)
    first_im = -product("kp,bpq->bkq", sin_outer[:, :half_rows], blocks)
    turned_re = first_re * twist_cos + first_im * twist_sin
    turned_im = first_im * twist_cos - first_re * twist_sin
    spec_re = product("bkq,qj->bkj", turned_re, cos_inner) + product(
        "bkq,qj->bkj", turned_im, sin_inner
    )
    spec_im = product("bkq,qj->bkj", turned_im, cos_inner) - product(
        "bkq,qj->bkj", turned_re, sin_inner
    )
    return (spec_re, spec_im)


def signal_of(spec_re, spec_im, tables):
    outer, inner, cos_outer, sin_outer, cos_inner, sin_inner, twist_cos, twist_sin = tables
    half_rows = outer // 2
    back_re = tripled("bkj,jq->bkq", spec_re, cos_inner) - tripled(
        "bkj,jq->bkq", spec_im, sin_inner
    )
    back_im = tripled("bkj,jq->bkq", spec_im, cos_inner) + tripled(
        "bkj,jq->bkq", spec_re, sin_inner
    )
    turned_re = back_re * twist_cos - back_im * twist_sin
    turned_im = back_im * twist_cos + back_re * twist_sin
    values = tripled("pk,bkq->bpq", cos_outer[:half_rows, :], turned_re) - tripled(
        "pk,bkq->bpq", sin_outer[:half_rows, :], turned_im
    )
    return values.reshape(values.shape[0], half_rows * inner) * (1.0 / (outer * inner))


def spec_product(left_re, left_im, right_re, right_im):
    return (left_re * right_re - left_im * right_im, left_re * right_im + left_im * right_re)


def conj_product(left_re, left_im, right_re, right_im):
    return (left_re * right_re + left_im * right_im, left_re * right_im - left_im * right_re)


def filter_basis(residue_loc, rate_loc, length):
    position = jnp.arange(length, dtype=jnp.float32)
    basis_all = jnp.sqrt(2.0 * rate_loc)[:, :, None] * jnp.exp(
        -rate_loc[:, :, None] * position[None, None, :]
    )
    return (basis_all, precise("cm,cmt->ct", residue_loc, basis_all))


def forward_cols(gated_cols, taps_re, taps_im, tables):
    gated_re, gated_im = spectrum(gated_cols.astype(jnp.float32), tables, tripled)
    conv_re, conv_im = spec_product(gated_re, gated_im, taps_re, taps_im)
    conv_cols = signal_of(conv_re, conv_im, tables).astype(jnp.bfloat16)
    return (conv_cols, gated_re, gated_im)


def backward_cols(slope_cols, gated_re, gated_im, taps_re, taps_im, basis_all, tables, length):
    slope_re, slope_im = spectrum(slope_cols.astype(jnp.float32), tables, tripled)
    grad_re, grad_im = conj_product(taps_re, taps_im, slope_re, slope_im)
    back_cols = signal_of(grad_re, grad_im, tables).astype(jnp.bfloat16)
    lag_re, lag_im = conj_product(gated_re, gated_im, slope_re, slope_im)
    taps_grad = signal_of(lag_re, lag_im, tables)
    grad_residue = precise("ct,cmt->cm", taps_grad, basis_all) * (1.0 / math.sqrt(length))
    return (back_cols, grad_residue)


def gather_weights(tokens, weights, residues, decay_rates, cotangent):
    gathered = lax.all_gather(weights, "ctx", axis=1, tiled=True)
    projected = jnp.einsum("xcpd,td->xcpt", gathered, tokens, preferred_element_type=jnp.float32)
    features = projected[0].astype(jnp.bfloat16)
    query_f = features[:, 0].astype(jnp.float32)
    key_part = features[:, 1].astype(jnp.float32)
    value_part = features[:, 2].astype(jnp.float32)
    gated_in = (key_part * value_part).astype(jnp.bfloat16)
    slope_in = (cotangent.astype(jnp.float32) * query_f).astype(jnp.bfloat16)
    length = tokens.shape[0] * lax.axis_size("ctx")
    tables = make_tables(length)
    basis_all, taps_full = filter_basis(residues[0], decay_rates[0], length)
    taps_re, taps_im = spectrum(taps_full, tables, precise)
    gated_cols = lax.all_to_all(gated_in, "ctx", split_axis=0, concat_axis=1, tiled=True)
    conv_cols, gated_re, gated_im = forward_cols(gated_cols, taps_re, taps_im, tables)
    conv_rows = lax.all_to_all(conv_cols, "ctx", split_axis=1, concat_axis=0, tiled=True)
    slope_cols = lax.all_to_all(slope_in, "ctx", split_axis=0, concat_axis=1, tiled=True)
    back_cols, grad_residue = backward_cols(
        slope_cols, gated_re, gated_im, taps_re, taps_im, basis_all, tables, length
    )
    back_rows = lax.all_to_all(back_cols, "ctx", split_axis=1, concat_axis=0, tiled=True)
    conv_f = conv_rows.astype(jnp.float32)
    back_f = back_rows.astype(jnp.float32)
    hyena_out = (query_f * conv_f).astype(jnp.bfloat16)
    grad_query = (cotangent.astype(jnp.float32) * conv_f).astype(jnp.bfloat16)
    grad_key = (back_f * value_part).astype(jnp.bfloat16)
    grad_value = (back_f * key_part).astype(jnp.bfloat16)
    grad_proj = jnp.stack([grad_query, grad_key, grad_value], axis=1)
    partial_value = jnp.einsum(
        "cpt,cpd->td", grad_proj, gathered[0], preferred_element_type=jnp.float32
    )
    grad_input = lax.psum_scatter(
        partial_value.astype(jnp.bfloat16), "tp", scatter_dimension=1, tiled=True
    )
    return (hyena_out, grad_input, grad_residue[None])


GROUP = 4
PLANE = 4
VMEM = 56 * 2**20


def rounded(value):
    return value.astype(jnp.bfloat16).astype(jnp.float32)


def earlier_sum(finals, rate, span, back):
    count = finals.shape[0]
    row = lax.broadcasted_iota(jnp.int32, finals.shape, 0)

    def shifted(value, by):
        if back:
            moved = pltpu.roll(value, count - by, 0)
            return jnp.where(row < count - by, moved, 0.0)
        moved = pltpu.roll(value, by, 0)
        return jnp.where(row >= by, moved, 0.0)

    total = shifted(finals, 1)
    by = 1
    while by < count:
        total = total + jnp.exp(rate * (-1.0 * span * by)) * shifted(total, by)
        by *= 2
    return total


def scan_kernel(
    groups,
    runs,
    order,
    me_ref,
    residue_ref,
    rate_ref,
    *refs,
):
    inputs = 1 + max(run[0] for run in runs)
    arrays, refs = refs[: 2 * inputs + 1], refs[2 * inputs + 1 :]
    hyena_ref, grad_ref = refs[:2]
    proj_refs, refs = refs[2 : 2 + len(order)], refs[2 + len(order) :]
    gated_s, slope_s, conv_s, back_s, feats_s, arrived = refs[:6]
    held = refs[6:]
    cot_ref, own, other = held[0], held[1 : 1 + inputs], held[1 + inputs :]
    copies = [
        pltpu.make_async_copy(array, here, arrived.at[k])
        for k, (array, here) in enumerate(zip(arrays, held))
    ]
    for copy in copies:
        copy.start()
    length, width = cot_ref.shape
    chunks = PLANE * groups
    span = length // chunks
    modes = rate_ref.shape[0]
    me = me_ref[0]

    def place(group, member):
        return lax.rem(me // PLANE + group, groups) * PLANE + (member ^ lax.rem(me, PLANE))

    def aligned(start, size):
        return pl.ds(pl.multiple_of(start, size), size)

    copies[0].wait()
    waited = set()
    for source, offset, group, base, members, count, first in sorted(runs):
        if source not in waited:
            waited.add(source)
            copies[1 + source].wait()
            copies[1 + inputs + source].wait()

        def before(step, _, source=source, offset=offset, group=group, base=base, count=count, first=first):
            member = base + step
            index = place(group, member)
            rows = pl.ds(pl.multiple_of(offset + step * count, 16), count)
            feats = own[source][rows, :] + other[source][rows, :].astype(jnp.float32)
            feats = rounded(feats)
            slot = (group * PLANE + member) * span + first
            feats_s[pl.ds(pl.multiple_of(slot, 16), count), :] = feats
            cot = cot_ref[pl.ds(pl.multiple_of(index * span + first, 16), count), :]
            query, key = feats[:, :width], feats[:, width : 2 * width]
            into = pl.ds(first * chunks + index, count, stride=chunks)
            gated_s[into, :] = rounded(key * feats[:, 2 * width :])
            slope_s[into, :] = rounded(cot.astype(jnp.float32) * query)
            return 0

        lax.fori_loop(0, members, before, 0)

    def at(step):
        return aligned(step * chunks, chunks)

    zero = jnp.zeros((chunks, width), jnp.float32)
    scale = 1.0 / math.sqrt(length)
    for first in range(0, modes, GROUP):
        count = min(GROUP, modes - first)
        rates = [
            jnp.broadcast_to(rate_ref[m : m + 1, :], (chunks, width))
            for m in range(first, first + count)
        ]
        decays = [jnp.exp(-rate) for rate in rates]
        norms = [jnp.sqrt(2.0 * rate) for rate in rates]
        gains = [
            residue_ref[first + n : first + n + 1, :] * norms[n] for n in range(count)
        ]

        def sums(step, state):
            ahead, behind = state
            gated = gated_s[at(step), :]
            slope = slope_s[at(span - 1 - step), :]
            return (
                tuple(decays[n] * ahead[n] + gated for n in range(count)),
                tuple(decays[n] * behind[n] + slope for n in range(count)),
            )

        ahead, behind = lax.fori_loop(0, span, sums, ((zero,) * count, (zero,) * count), unroll=8)
        ahead = tuple(earlier_sum(ahead[n], rates[n], span, False) for n in range(count))
        behind = tuple(earlier_sum(behind[n], rates[n], span, True) for n in range(count))

        def outs(step, state):
            ahead, behind, grads = state
            other = span - 1 - step
            gated = gated_s[at(step), :]
            slope = slope_s[at(step), :]
            slope_back = slope_s[at(other), :]
            ahead = tuple(decays[n] * ahead[n] + gated for n in range(count))
            behind = tuple(decays[n] * behind[n] + slope_back for n in range(count))
            grads = tuple(grads[n] + slope * ahead[n] for n in range(count))
            conv = sum(gains[n] * ahead[n] for n in range(count))
            back = sum(gains[n] * behind[n] for n in range(count))
            if first:
                conv = conv + conv_s[at(step), :]
                back = back + back_s[at(other), :]
            conv_s[at(step), :] = conv
            back_s[at(other), :] = back
            return ahead, behind, grads

        _, _, grads = lax.fori_loop(0, span, outs, (ahead, behind, (zero,) * count), unroll=4)
        for n in range(count):
            total = jnp.sum(grads[n] * norms[n], axis=0, keepdims=True) * scale
            grad_ref[first + n : first + n + 1, :] = total

    for proj_ref, pieces in zip(proj_refs, order):
        start = 0
        for group, base, members in pieces:

            def after(step, _, proj_ref=proj_ref, start=start, group=group, base=base):
                member = base + step
                index = place(group, member)
                feats = feats_s[aligned((group * PLANE + member) * span, span), :]
                query, key = feats[:, :width], feats[:, width : 2 * width]
                cot = cot_ref[aligned(index * span, span), :].astype(jnp.float32)
                conv = rounded(conv_s[pl.ds(index, span, stride=chunks), :])
                back = rounded(back_s[pl.ds(index, span, stride=chunks), :])
                hyena_ref[aligned(index * span, span), :] = narrowed(query * conv)
                rows = aligned(start + step * span, span)
                proj_ref[rows, :width] = narrowed(cot * conv)
                proj_ref[rows, width : 2 * width] = narrowed(back * feats[:, 2 * width :])
                proj_ref[rows, 2 * width :] = narrowed(back * key)
                return 0

            lax.fori_loop(0, members, after, 0)
            start += members * span


def scan_all(me, cot_cols, residue_rows, rate_rows, runs, order, own, other):
    length, width = cot_cols.shape
    span = length // (PLANE * PLANE)
    vmem = pl.BlockSpec(memory_space=pltpu.VMEM)
    arrays = (cot_cols, *own, *other)
    outs = pl.pallas_call(
        functools.partial(scan_kernel, PLANE, runs, order),
        out_shape=(
            jax.ShapeDtypeStruct((length, width), jnp.bfloat16),
            jax.ShapeDtypeStruct(rate_rows.shape, jnp.float32),
        )
        + tuple(
            jax.ShapeDtypeStruct((span * sum(piece[2] for piece in pieces), 3 * width), jnp.bfloat16)
            for pieces in order
        ),
        in_specs=[pl.BlockSpec(memory_space=pltpu.SMEM), vmem, vmem]
        + [pl.BlockSpec(memory_space=pl.ANY)] * len(arrays),
        out_specs=(vmem,) * (2 + len(order)),
        scratch_shapes=[pltpu.VMEM((length, width), jnp.float32)] * 4
        + [pltpu.VMEM((length, 3 * width), jnp.float32), pltpu.SemaphoreType.DMA((len(arrays),))]
        + [pltpu.VMEM(array.shape, array.dtype) for array in arrays],
        compiler_params=pltpu.CompilerParams(vmem_limit_bytes=40 * 2**20),
        name="modal_scan",
    )(me, residue_rows, rate_rows, *arrays)
    return outs[0], outs[1], outs[2:]


def swapped(value):
    return lax.ppermute(value, "tp", [(0, 1), (1, 0)])


def over_x(value):
    return lax.ppermute(value, "ctx", [(i, i ^ 1) for i in range(lax.axis_size("ctx"))])


def over_y(value):
    return lax.ppermute(value, "ctx", [(i, i ^ 2) for i in range(lax.axis_size("ctx"))])


def up(value):
    count = lax.axis_size("ctx")
    return lax.ppermute(value, "ctx", [(i, (i + PLANE) % count) for i in range(count)])


def down(value):
    count = lax.axis_size("ctx")
    return lax.ppermute(value, "ctx", [((i + PLANE) % count, i) for i in range(count)])


def stack(*parts):
    return jnp.concatenate(parts, axis=0)


def beside(*parts):
    return jnp.concatenate(parts, axis=1)


def narrowed(value):
    return value.astype(jnp.bfloat16)


def widened(value):
    return value.astype(jnp.float32)


def halves_kernel(plan, core_ref, *refs):
    arrays, outs, arrived = refs[: -1 - len(plan)], refs[-1 - len(plan) : -1], refs[-1]
    copies = []
    for k, (out, (index, count, mine)) in enumerate(zip(outs, plan)):
        half = out.shape[1]
        side = core_ref[0] if mine else 1 - core_ref[0]
        columns = pl.ds(pl.multiple_of(side * half, half), half)
        part = arrays[index].at[pl.ds(0, count), columns]
        copies.append(pltpu.make_async_copy(part, out, arrived.at[k]))
    for copy in copies:
        copy.start()
    for copy in copies:
        copy.wait()


def halves(arrays, *plan):
    core = lax.axis_index("tp").astype(jnp.int32).reshape(1)
    shapes = [(count, arrays[index].shape[1] // 2) for index, count, _ in plan]
    moved = sum(4 * rows * columns for rows, columns in shapes)
    return pl.pallas_call(
        functools.partial(halves_kernel, plan),
        out_shape=tuple(jax.ShapeDtypeStruct(shape, jnp.bfloat16) for shape in shapes),
        in_specs=[pl.BlockSpec(memory_space=pltpu.SMEM)]
        + [pl.BlockSpec(memory_space=pl.ANY)] * len(arrays),
        out_specs=(pl.BlockSpec(memory_space=pltpu.VMEM),) * len(plan),
        scratch_shapes=[pltpu.SemaphoreType.DMA((len(plan),))],
        compiler_params=pltpu.CompilerParams(vmem_limit_bytes=VMEM),
        cost_estimate=pl.CostEstimate(flops=0, bytes_accessed=moved, transcendentals=0),
        name="halves",
    )(core, *arrays)


def assemble_kernel(inputs, plans, *refs):
    arrays, refs = refs[:inputs], refs[inputs:]
    outs, refs = refs[: len(plans)], refs[len(plans) :]
    arrived, held = refs[0], refs[1:]
    started, k, slot = [], 0, 0
    pending = []
    for out, plan in zip(outs, plans):
        for row, col, height, width, sources in plan:
            here = out.at[pl.ds(row, height), pl.ds(col, width)]
            single = len(sources) == 1
            mine = []
            for index, from_row, from_col in sources:
                part = arrays[index].at[pl.ds(from_row, height), pl.ds(from_col, width)]
                into = here if single else held[slot]
                copy = pltpu.make_async_copy(part, into, arrived.at[k])
                copy.start()
                mine.append((copy, into))
                k += 1
                slot += 0 if single else 1
            if single:
                started.append(mine[0][0])
            else:
                pending.append((here, mine))
    for here, mine in pending:
        for copy, _ in mine:
            copy.wait()
        here[...] = narrowed(sum(widened(into[...]) for _, into in mine))
    for copy in started:
        copy.wait()


def assemble(arrays, *plans):
    sources = [(piece, source) for plan in plans for piece in plan for source in piece[4]]
    sums = [piece for piece, _ in sources if len(piece[4]) > 1]
    shapes = [
        (max(p[0] + p[2] for p in plan), max(p[1] + p[3] for p in plan)) for plan in plans
    ]
    moved = sum(2 * rows * cols for rows, cols in shapes)
    return pl.pallas_call(
        functools.partial(assemble_kernel, len(arrays), plans),
        out_shape=tuple(jax.ShapeDtypeStruct(shape, jnp.bfloat16) for shape in shapes),
        in_specs=[pl.BlockSpec(memory_space=pl.ANY)] * len(arrays),
        out_specs=(pl.BlockSpec(memory_space=pltpu.VMEM),) * len(plans),
        scratch_shapes=[pltpu.SemaphoreType.DMA((len(sources),))]
        + [pltpu.VMEM((piece[2], piece[3]), jnp.bfloat16) for piece in sums],
        compiler_params=pltpu.CompilerParams(vmem_limit_bytes=24 * 2**20),
        cost_estimate=pl.CostEstimate(flops=moved, bytes_accessed=4 * moved, transcendentals=0),
        name="assemble",
    )(*arrays)


def rows_of(*parts):
    plan, start = [], 0
    for index, first, count in parts:
        plan.append((start, count, [(index, first, 0)]))
        start += count
    return plan


def full_width(columns, plan):
    return [(row, 0, count, columns, sources) for row, count, sources in plan]


def columns_of(height, *parts):
    plan, start = [], 0
    for width, sources in parts:
        plan.append((0, start, height, width, sources))
        start += width
    return plan


def all_ways(for_x, for_y, for_above, for_below):
    return lax.optimization_barrier((over_x(for_x), over_y(for_y), up(for_above), down(for_below)))


def project(parts, kept, taken):
    rows = stack(*parts)
    own, given = (
        jnp.einsum("td,rd->tr", rows, matrix, preferred_element_type=jnp.float32)
        for matrix in (kept, taken)
    )
    return own, swapped(narrowed(given))


def columns_held(rows):
    return lax.all_to_all(rows.T, "ctx", split_axis=1, concat_axis=0, tiled=True)


def gather_groups(tokens, wide, matrices, later):
    span = tokens.shape[0]
    n, m = span * 3 // 4, span // 4
    nh, mh = n // 2, m // 2
    columns = tokens.shape[1]

    def put(arrays, *plans):
        return assemble(arrays, *[full_width(columns, rows_of(*plan)) for plan in plans])

    own_x, own_y, wide_3, wide_1 = all_ways(tokens, tokens, wide, wide)
    own_x, matrices = lax.optimization_barrier((own_x, matrices))
    first = (tokens, own_x, own_y, wide_3, wide_1)
    members = ((0, n, m), (1, n, m), (2, n, m))
    sent = put(
        first,
        ((2, 0, nh), (2, n, mh), (3, 0, n), (4, 0, n)),
        ((1, nh, nh), (1, n + mh, mh), (3, 0, n), (4, 0, n)),
        ((3, 0, nh), *members),
        ((4, nh, nh), *members),
    )
    sent, first = lax.optimization_barrier((sent, first))
    second = all_ways(*sent)
    start = nh + mh
    wide_2 = ((2, 0, nh), (3, 0, nh))
    across = ((0, nh, mh), (1, nh, mh))
    third = all_ways(
        *put(
            second,
            ((1, start, nh), (1, start + n, nh), *wide_2),
            ((0, start + nh, nh), (0, start + n + nh, nh), *wide_2),
            (*across, (2, nh, nh)),
            (*across, (3, 2 * nh, nh)),
        )
    )
    fourth = all_ways(
        *put(third, ((1, n, nh),), ((0, n + nh, nh),), ((2, 0, mh),), ((3, mh, mh),))
    )
    runs = [
        (0, 0, 0, 0, 3, span, 0),
        (0, 3 * span, 3, 0, 1, n, 0),
        (0, 3 * span + n, 1, 0, 1, n, 0),
    ]
    offset = 0
    for side in range(2):
        runs += [
            (1, offset, 0, 3, 1, nh, side * nh),
            (1, offset + nh, 0, 3, 1, mh, n + side * mh),
            (1, offset + start, 3, 1 + side, 1, n, 0),
            (1, offset + start + n, 1, 1 + side, 1, n, 0),
        ]
        offset += start + 2 * n
    for side in range(2):
        runs += [
            (1, offset, 2, 0, 1, nh, side * nh),
            (1, offset + nh, 3 - 2 * side, 0, 3, m, n),
        ]
        offset += nh + 3 * m
    offset = 0
    for side in range(2):
        runs += [
            (2, offset, 3, 3, 1, nh, side * nh),
            (2, offset + nh, 1, 3, 1, nh, side * nh),
            (2, offset + n, 2, 1 + side, 1, n, 0),
        ]
        offset += 2 * n
    runs += [
        (2, offset, 3, 3, 1, m, n),
        (2, offset + m, 2, 0, 1, m, n),
        (2, offset + 2 * m, 2, 1, 1, mh, n),
        (2, offset + 2 * m + mh, 1, 3, 1, m, n),
        (2, offset + 3 * m + mh, 2, 1, 1, mh, n + mh),
        (2, offset + 3 * m + 2 * mh, 2, 2, 1, m, n),
        (3, 0, 2, 3, 1, nh, 0),
        (3, nh, 2, 3, 1, nh, nh),
        (3, n, 2, 3, 1, mh, n),
        (3, n + mh, 2, 3, 1, mh, n + mh),
    ]
    parts = [project(part, *matrices) for part in (first, second, third, fourth)]
    later, first = lax.optimization_barrier((later, parts[0][1]))
    parts[0] = (parts[0][0], first)
    later = columns_held(later)
    return parts, tuple(runs), matrices, later


ORDER = (((2, 0, 4), (1, 3, 1), (3, 3, 1)), ((1, 0, 3), (3, 0, 3), (0, 3, 1), (0, 0, 3)))


def scatter_sum(early, later, matrix, hyena):
    span = early.shape[0] // 6
    columns = matrix.shape[1]
    wide, narrow = columns * 3 // 8, columns // 8
    places = {}
    for array, pieces in enumerate((ORDER[0], ORDER[1][:3], ORDER[1][3:])):
        row = 0
        for group, base, members in pieces:
            for member in range(base, base + members):
                places[group, member] = (array, row)
                row += span

    def product(part, other):
        both = beside(part, other)
        return narrowed(jnp.dot(both, matrix, preferred_element_type=jnp.float32))

    def term(group, member, side, *more):
        array, row = places[group, member]
        return (wide, [(array, row, side * wide), *more])

    def low(group, member, side, *more):
        array, row = places[group, member]
        return (narrow, [(array, row, 2 * wide + side * narrow), *more])

    def put(arrays, *plans):
        return assemble(arrays, *[columns_of(span, *plan) for plan in plans])

    early = product(early, swapped(early))
    other = swapped(later)
    first = all_ways(
        *put([early], [term(2, 3, 0)], [term(2, 3, 1)], [low(2, 3, 0)], [low(2, 3, 1)])
    )
    later, first = lax.optimization_barrier((later, first))
    x, y, below, above = range(1, 5)
    second = all_ways(
        *put(
            [early, *first],
            [term(2, 1, 0), term(2, 1, 1, (y, 0, 0)), term(1, 3, 0), term(3, 3, 0)],
            [term(2, 2, 0, (x, 0, 0)), term(2, 2, 1), term(1, 3, 1), term(3, 3, 1)],
            [low(1, 3, 0, (below, 0, 0)), low(1, 3, 1), *[low(2, k, 0) for k in range(3)]],
            [low(3, 3, 0), low(3, 3, 1, (above, 0, 0)), *[low(2, k, 1) for k in range(3)]],
        )
    )
    own = product(later[7 * span :], other[7 * span :])
    later = product(later[: 7 * span], other[: 7 * span])
    later, hyena, second = lax.optimization_barrier((later, hyena, second))
    hyena_out = lax.all_to_all(hyena, "ctx", split_axis=0, concat_axis=1, tiled=True).T
    x, y, below, above = range(2, 6)

    def low_3(side):
        return low(0, 3, side, (below, 0, side * narrow), (above, 0, side * narrow))

    def sum_2(side):
        return term(2, 0, side, (x, 0, side * wide), (y, 0, side * wide))

    for_above, for_below = [], []
    for k in range(3):
        start = (2 + k) * narrow
        for_above += [low(1, k, 0, (below, 0, start)), low(1, k, 1)]
        for_below += [low(3, k, 0), low(3, k, 1, (above, 0, start))]
    third = all_ways(
        *put(
            [early, later, *second],
            [
                term(1, 1, 0),
                term(1, 1, 1, (y, 0, 2 * wide)),
                term(3, 1, 0),
                term(3, 1, 1, (y, 0, 3 * wide)),
                term(0, 3, 0),
                low_3(0),
            ],
            [
                term(1, 2, 0, (x, 0, 2 * wide)),
                term(1, 2, 1),
                term(3, 2, 0, (x, 0, 3 * wide)),
                term(3, 2, 1),
                term(0, 3, 1),
                low_3(1),
            ],
            [sum_2(0), *for_above],
            [sum_2(1), *for_below],
        )
    )

    x, y, below, above = range(3, 7)

    def low_own(k, side, *more):
        start = wide + (2 * k + side) * narrow
        return low(0, k, side, (below, 0, start), (above, 0, start), *more)

    def own_sum(group, side, *more):
        start = (group - 1 + side) * wide
        return term(group, 0, side, (x, 0, start), (y, 0, start), *more)

    *sent, base = put(
            [early, later, own, *third],
            [
                term(0, 1, 0),
                term(0, 1, 1, (y, 0, 4 * wide)),
                low_own(1, 0),
                low_own(1, 1, (y, 0, 5 * wide)),
            ],
            [
                term(0, 2, 0, (x, 0, 4 * wide)),
                term(0, 2, 1),
                low_own(2, 0, (x, 0, 5 * wide)),
                low_own(2, 1),
            ],
            [own_sum(1, 0, (below, 0, 0)), own_sum(1, 1)],
            [own_sum(3, 0), own_sum(3, 1, (above, 0, 0))],
            [term(0, 0, 0), term(0, 0, 1), low_own(0, 0), low_own(0, 1)],
        )
    (grad_input,) = put(
        [base, *all_ways(*sent)],
        [
            (2 * wide, [(way, 0, 0) for way in range(5)]),
            (2 * narrow, [(way, 0, 2 * wide) for way in range(3)]),
        ],
    )
    return grad_input, hyena_out


def gather_tokens(tokens, weights, residues, decay_rates, cotangent):
    me = lax.axis_index("ctx").astype(jnp.int32).reshape(1)
    channels, span = weights.shape[1], tokens.shape[0]
    rows = weights[0].swapaxes(0, 1).reshape(3 * channels, weights.shape[3])
    *tokens_half, kept, given = halves(
        (tokens, rows),
        (0, span, True),
        (0, span * 3 // 4, True),
        (1, 3 * channels, True),
        (1, 3 * channels, False),
    )
    taken = swapped(given)
    parts, runs, (kept, taken), cot_cols = gather_groups(*tokens_half, (kept, taken), cotangent)
    own, other = zip(*parts)
    hyena, grads, (early, later) = scan_all(
        me, cot_cols, residues[0].T, decay_rates[0].T, runs, ORDER, own, other
    )
    grad_input, hyena_out = scatter_sum(early, later, stack(kept, taken), hyena)
    return (hyena_out, grad_input, grads.T[None])


def shards(tokens, weights, residues, decay_rates, cotangent):
    ctx, tp = lax.axis_size("ctx"), lax.axis_size("tp")
    if ctx == 4 * PLANE and tp == 2 and weights.size * tp > 2 * tokens.size:
        return gather_tokens(tokens, weights, residues, decay_rates, cotangent)
    return gather_weights(tokens, weights, residues, decay_rates, cotangent)


def solution(mesh):
    return jax.shard_map(
        shards,
        mesh=mesh,
        in_specs=(
            P("ctx", None),
            P("tp", "ctx", None, None),
            P("tp", "ctx", None),
            P("tp", "ctx", None),
            P("tp", "ctx"),
        ),
        out_specs=(P("tp", "ctx"), P("ctx", "tp"), P("tp", "ctx", None)),
        check_vma=False,
    )
```

profile of v0, /device:TPU:0, one launch (start us, length us, event | category | flops | bytes accessed | tf_op | source)
XLA Modules:
  0.0 215.8 jit_solution(8068834867384011032)
XLA Ops:
  0.6 4.2 %halves.1 = (bf16[128,2048]{1,0:T(8,128)(2,1)}, bf16[96,2048]{1,0:T(8,128)(2,1)}, bf16[384,2048]{1,0:T(8,128)(2,1)}, bf16[384,2048]{1,0:T(8,128)(2,1)}) custom-call(s32[1]{0:T(128)} %bitcast.5.core_ref, bf16[128,4096]{1,0:T(8,128)(2,1)} %refs_0_.1, bf16[384,4096]{1,0:T(8,128)(2,1)} %bitcast.49), custom_call_target="tpu_custom_call" | custom-call | bytes 8126464 | tf_op jit(solution)/shard_map/halves/pallas_call | solution.py:395
  5.4 2.6 %collective-permute-start = (bf16[128,2048]{1,0:T(8,128)(2,1)}, bf16[128,2048]{1,0:T(8,128)(2,1)S(1)}, u32[]{:S(2)}, u32[]{:S(2)}) collective-permute-start(bf16[128,2048]{1,0:T(8,128)(2,1)} %get-tuple-element.110.refs_0_), channel_id=1, source_target_pairs={{0,2},{2,0},{4,6},{6,4},{8,10},{10,8},{12,14},{14,12},{16,18},{18,... | collective-permute-start | bytes 1572872 | tf_op jit(solution)/shard_map/ppermute | solution.py:343
  7.9 1.5 collective-permute-start.1
  9.5 1.6 collective-permute-start.2
  11.0 2.2 %collective-permute-start.3 = (bf16[96,2048]{1,0:T(8,128)(2,1)}, bf16[96,2048]{1,0:T(8,128)(2,1)S(1)}, u32[]{:S(2)}, u32[]{:S(2)}) collective-permute-start(bf16[96,2048]{1,0:T(8,128)(2,1)} %get-tuple-element.98), channel_id=1, source_target_pairs={{8,0},{10,2},{12,4},{14,6},{16,8},{18,10},{20,12},{22,14},{24,16},... | collective-permute-start | bytes 1179656 | tf_op jit(solution)/shard_map/ppermute | solution.py:357
  13.3 10.2 %collective-permute-done.2.refs_3_ = bf16[96,2048]{1,0:T(8,128)(2,1)S(1)} collective-permute-done((bf16[96,2048]{1,0:T(8,128)(2,1)}, bf16[96,2048]{1,0:T(8,128)(2,1)S(1)}, u32[]{:S(2)}, u32[]{:S(2)}) %collective-permute-start.2) | collective-permute-done | bytes 393248 | tf_op jit(solution)/shard_map/ppermute | solution.py:352
  23.5 6.8 %collective-permute-done.3.refs_4_ = bf16[96,2048]{1,0:T(8,128)(2,1)S(1)} collective-permute-done((bf16[96,2048]{1,0:T(8,128)(2,1)}, bf16[96,2048]{1,0:T(8,128)(2,1)S(1)}, u32[]{:S(2)}, u32[]{:S(2)}) %collective-permute-start.3) | collective-permute-done | bytes 393248 | tf_op jit(solution)/shard_map/ppermute | solution.py:357
  30.3 1.4 copy-done.2
  31.8 4.8 %assemble.8 = (bf16[256,2048]{1,0:T(8,128)(2,1)}, bf16[256,2048]{1,0:T(8,128)(2,1)}, bf16[144,2048]{1,0:T(8,128)(2,1)}, bf16[144,2048]{1,0:T(8,128)(2,1)}) custom-call(bf16[128,2048]{1,0:T(8,128)(2,1)S(1)} %copy-done.2, bf16[128,2048]{1,0:T(8,128)(2,1)S(1)} %collective-permute-done.refs_1_, bf16[128,2048]{1,0:T(8,128)(2,1)S(1)} %collective-permute-done.1.refs_2_, ...), custom_call_target="tpu_custom_call" | custom-call | flops 3276800 | bytes 13107200 | tf_op jit(solution)/shard_map/assemble/pallas_call | solution.py:446
  38.8 2.7 %collective-permute-start.9 = (bf16[144,2048]{1,0:T(8,128)(2,1)}, bf16[144,2048]{1,0:T(8,128)(2,1)S(1)}, u32[]{:S(2)}, u32[]{:S(2)}) collective-permute-start(bf16[144,2048]{1,0:T(8,128)(2,1)} %get-tuple-element.121), channel_id=1, source_target_pairs={{8,0},{10,2},{12,4},{14,6},{16,8},{18,10},{20,12},{22,14},{24,16},... | collective-permute-start | bytes 1769480 | tf_op jit(solution)/shard_map/ppermute | solution.py:357
  41.7 2.2 %convolution_convert_fusion.4 = bf16[576,384]{1,0:T(8,128)(2,1)} fusion(bf16[576,2048]{1,0:T(8,128)(2,1)S(1)} %constant_dynamic-update-slice_fusion, bf16[384,2048]{1,0:T(8,128)(2,1)S(1)} %collective-permute-done.4), kind=kOutput, calls=%fused_computation.7 | convolution fusion | flops 906190848 | bytes 4374528 | tf_op jit(solution)/shard_map/td,rd->tr/dot_general | solution.py:486
  43.9 4.5 %fusion.12.refs_1_ = f32[576,384]{1,0:T(8,128)} fusion(bf16[576,2048]{1,0:T(8,128)(2,1)} %copy-done.17, bf16[384,2048]{1,0:T(8,128)(2,1)} %get-tuple-element.117), kind=kOutput, calls=%fused_computation.38 | convolution fusion | flops 905969664 | bytes 4816896 | tf_op jit(solution)/shard_map/td,rd->tr/dot_general | solution.py:486
  48.4 2.0 copy.8
  50.5 4.2 %all-to-all-start = ((bf16[128,16,128]{2,0,1:T(8,128)(2,1)}), bf16[128,16,128]{2,0,1:T(8,128)(2,1)}, u32[]{:S(2)}, u32[]{:S(2)}) async-start(bf16[128,16,128]{2,0,1:T(8,128)(2,1)} %copy.8), calls=%async_computation | async-start | bytes 1048576 | tf_op jit(solution)/shard_map/all_to_all | solution.py:493
  55.9 12.1 %collective-permute-done.9.refs_3_ = bf16[144,2048]{1,0:T(8,128)(2,1)S(1)} collective-permute-done((bf16[144,2048]{1,0:T(8,128)(2,1)}, bf16[144,2048]{1,0:T(8,128)(2,1)S(1)}, u32[]{:S(2)}, u32[]{:S(2)}) %collective-permute-start.9) | collective-permute-done | bytes 589856 | tf_op jit(solution)/shard_map/ppermute | solution.py:357
  68.1 3.0 %assemble.9 = (bf16[192,2048]{1,0:T(8,128)(2,1)S(1)}, bf16[192,2048]{1,0:T(8,128)(2,1)S(1)}, bf16[80,2048]{1,0:T(8,128)(2,1)S(1)}, bf16[80,2048]{1,0:T(8,128)(2,1)S(1)}) custom-call(bf16[256,2048]{1,0:T(8,128)(2,1)S(1)} %collective-permute-done.6.refs_0_, bf16[256,2048]{1,0:T(8,128)(2,1)S(1)} %collective-permute-done.7.refs_1_, ...), custom_call_target="tpu_custom_call" | custom-call | flops 2228224 | bytes 8912896 | tf_op jit(solution)/shard_map/assemble/pallas_call | solution.py:446
  71.2 1.6 collective-permute-start.10
  74.4 3.4 %collective-permute-start.13 = (bf16[80,2048]{1,0:T(8,128)(2,1)S(1)}, bf16[80,2048]{1,0:T(8,128)(2,1)S(1)}, u32[]{:S(2)}, u32[]{:S(2)}) collective-permute-start(bf16[80,2048]{1,0:T(8,128)(2,1)S(1)} %get-tuple-element.129), channel_id=1, source_target_pairs={{8,0},{10,2},{12,4},{14,6},{16,8},{18,10},{20,12},{22,14},{24,16},... | collective-permute-start | bytes 983048 | tf_op jit(solution)/shard_map/ppermute | solution.py:357
  77.9 2.7 %convolution_convert_fusion.3 = bf16[800,384]{1,0:T(8,128)(2,1)} fusion(bf16[800,2048]{1,0:T(8,128)(2,1)S(1)} %constant_dynamic-update-slice_fusion.5, bf16[384,2048]{1,0:T(8,128)(2,1)S(1)} %copy-done.11), kind=kOutput, calls=%fused_computation.6 | convolution fusion | flops 1258598400 | bytes 5464064 | tf_op jit(solution)/shard_map/td,rd->tr/dot_general | solution.py:486
  80.6 1.9 fusion.13.refs_2_
  82.5 3.9 %collective-permute-done.12.refs_2_ = bf16[80,2048]{1,0:T(8,128)(2,1)S(1)} collective-permute-done((bf16[80,2048]{1,0:T(8,128)(2,1)S(1)}, bf16[80,2048]{1,0:T(8,128)(2,1)S(1)}, u32[]{:S(2)}, u32[]{:S(2)}) %collective-permute-start.12) | collective-permute-done | bytes 327712 | tf_op jit(solution)/shard_map/ppermute | solution.py:352
  86.3 3.0 %collective-permute-done.13.refs_3_ = bf16[80,2048]{1,0:T(8,128)(2,1)S(1)} collective-permute-done((bf16[80,2048]{1,0:T(8,128)(2,1)S(1)}, bf16[80,2048]{1,0:T(8,128)(2,1)S(1)}, u32[]{:S(2)}, u32[]{:S(2)}) %collective-permute-start.13) | collective-permute-done | bytes 327712 | tf_op jit(solution)/shard_map/ppermute | solution.py:357
  89.3 2.6 %collective-permute-done.10.refs_0_ = bf16[192,2048]{1,0:T(8,128)(2,1)S(1)} collective-permute-done((bf16[192,2048]{1,0:T(8,128)(2,1)S(1)}, bf16[192,2048]{1,0:T(8,128)(2,1)S(1)}, u32[]{:S(2)}, u32[]{:S(2)}) %collective-permute-start.10) | collective-permute-done | bytes 786464 | tf_op jit(solution)/shard_map/ppermute | solution.py:343
  95.5 2.8 %collective-permute-start.17 = (bf16[16,2048]{1,0:T(8,128)(2,1)S(1)}, bf16[16,2048]{1,0:T(8,128)(2,1)S(1)}, u32[]{:S(2)}, u32[]{:S(2)}) collective-permute-start(bf16[16,2048]{1,0:T(8,128)(2,1)S(1)} %get-tuple-element.137), channel_id=1, source_target_pairs={{8,0},{10,2},{12,4},{14,6},{16,8},{18,10},{20,12},{22,14},{24,16},... | collective-permute-start | bytes 196616 | tf_op jit(solution)/shard_map/ppermute | solution.py:357
  98.4 2.1 convolution_convert_fusion.5
  100.5 1.3 fusion.14.refs_3_
  104.2 14.2 %modal_scan.1 = (bf16[2048,128]{1,0:T(8,128)(2,1)S(1)}, f32[16,128]{1,0:T(8,128)}, bf16[768,384]{1,0:T(8,128)(2,1)S(1)}, bf16[1280,384]{1,0:T(8,128)(2,1)S(1)}) custom-call(s32[1]{0:T(128)} %bitcast.me_ref, f32[16,128]{1,0:T(8,128)S(1)} %bitcast.47, f32[16,128]{1,0:T(8,128)S(1)} %bitcast.48, bf16[2048,128]{1,0:T(8,128)(2,1)} %bitcast.12.refs_0_, ...), custom_call_target="tpu_custom_call" | custom-call | tf_op jit(solution)/shard_map/modal_scan/pallas_call | solution.py:316
  120.5 2.8 %convolution_convert_fusion.1.refs_0_ = bf16[768,2048]{1,0:T(8,128)(2,1)S(1)} fusion(bf16[768,2048]{1,0:T(8,128)(2,1)S(1)} %constant_dynamic-update-slice_fusion.17, bf16[768,384]{1,0:T(8,128)(2,1)S(1)} %collective-permute-done.21, bf16[768,384]{1,0:T(8,128)(2,1)S(1)} %get-tuple-element.144), kind=kOutput, calls=%fused_computation.1 | convolution fusion | flops 2419851264 | bytes 7471104 | tf_op jit(solution)/shard_map/dot_general | solution.py:597
  125.9 3.8 %collective-permute-start.25 = (bf16[128,256]{1,0:T(8,128)(2,1)S(1)}, bf16[128,256]{1,0:T(8,128)(2,1)S(1)}, u32[]{:S(2)}, u32[]{:S(2)}) collective-permute-start(bf16[128,256]{1,0:T(8,128)(2,1)S(1)} %get-tuple-element.148), channel_id=1, source_target_pairs={{8,0},{10,2},{12,4},{14,6},{16,8},{18,10},{20,12},{22,14},{24,16},... | collective-permute-start | bytes 196616 | tf_op jit(solution)/shard_map/ppermute | solution.py:357
  129.7 2.5 %collective-permute-done.24.refs_3_ = bf16[128,256]{1,0:T(8,128)(2,1)S(1)} collective-permute-done((bf16[128,256]{1,0:T(8,128)(2,1)S(1)}, bf16[128,256]{1,0:T(8,128)(2,1)S(1)}, u32[]{:S(2)}, u32[]{:S(2)}) %collective-permute-start.24) | collective-permute-done | bytes 65568 | tf_op jit(solution)/shard_map/ppermute | solution.py:352
  132.2 1.4 assemble.12
  135.4 3.8 %collective-permute-start.30 = (bf16[128,1280]{1,0:T(8,128)(2,1)S(1)}, bf16[128,1280]{1,0:T(8,128)(2,1)S(1)}, u32[]{:S(2)}, u32[]{:S(2)}) collective-permute-start(bf16[128,1280]{1,0:T(8,128)(2,1)S(1)} %get-tuple-element.162), channel_id=1, source_target_pairs={{8,0},{10,2},{12,4},{14,6},{16,8},{18,10},{20,12},{22,14},{24,16},... | collective-permute-start | bytes 983048 | tf_op jit(solution)/shard_map/ppermute | solution.py:357
  140.3 3.2 %convolution_convert_fusion.refs_1_ = bf16[896,2048]{1,0:T(8,128)(2,1)S(1)} fusion(bf16[768,2048]{1,0:T(8,128)(2,1)S(1)} %constant_dynamic-update-slice_fusion.17, bf16[896,384]{1,0:T(8,128)(2,1)S(1)} %slice.16, bf16[896,384]{1,0:T(8,128)(2,1)S(1)} %slice.12), kind=kOutput, calls=%fused_computation | convolution fusion | flops 2823159808 | bytes 8192000 | tf_op jit(solution)/shard_map/dot_general | solution.py:597
  143.6 4.2 %collective-permute-done.29.refs_4_ = bf16[128,1280]{1,0:T(8,128)(2,1)S(1)} collective-permute-done((bf16[128,1280]{1,0:T(8,128)(2,1)S(1)}, bf16[128,1280]{1,0:T(8,128)(2,1)S(1)}, u32[]{:S(2)}, u32[]{:S(2)}) %collective-permute-start.29) | collective-permute-done | bytes 327712 | tf_op jit(solution)/shard_map/ppermute | solution.py:352
  147.8 2.6 %collective-permute-done.30.refs_5_ = bf16[128,1280]{1,0:T(8,128)(2,1)S(1)} collective-permute-done((bf16[128,1280]{1,0:T(8,128)(2,1)S(1)}, bf16[128,1280]{1,0:T(8,128)(2,1)S(1)}, u32[]{:S(2)}, u32[]{:S(2)}) %collective-permute-start.30) | collective-permute-done | bytes 327712 | tf_op jit(solution)/shard_map/ppermute | solution.py:357
  152.3 3.5 %assemble.13 = (bf16[128,4096]{1,0:T(8,128)(2,1)}, bf16[128,4096]{1,0:T(8,128)(2,1)}, bf16[128,2304]{1,0:T(8,128)(2,1)}, bf16[128,2304]{1,0:T(8,128)(2,1)}) custom-call(bf16[768,2048]{1,0:T(8,128)(2,1)S(1)} %convolution_convert_fusion.1.refs_0_, bf16[896,2048]{1,0:T(8,128)(2,1)S(1)} %convolution_convert_fusion.refs_1_, ...), custom_call_target="tpu_custom_call" | custom-call | flops 3276800 | bytes 13107200 | tf_op jit(solution)/shard_map/assemble/pallas_call | solution.py:446
  158.3 3.7 %collective-permute-start.34 = (bf16[128,2304]{1,0:T(8,128)(2,1)}, bf16[128,2304]{1,0:T(8,128)(2,1)}, u32[]{:S(2)}, u32[]{:S(2)}) collective-permute-start(bf16[128,2304]{1,0:T(8,128)(2,1)} %get-tuple-element.176), channel_id=1, source_target_pairs={{8,0},{10,2},{12,4},{14,6},{16,8},{18,10},{20,12},{22,14},{24,16},... | collective-permute-start | bytes 1769480 | tf_op jit(solution)/shard_map/ppermute | solution.py:357
  162.0 4.5 %all-to-all-start.1 = ((bf16[16,128,128]{2,1,0:T(8,128)(2,1)}), bf16[16,128,128]{2,1,0:T(8,128)(2,1)}, u32[]{:S(2)}, u32[]{:S(2)}) async-start(bf16[16,128,128]{2,1,0:T(8,128)(2,1)} %bitcast.46), calls=%async_computation.1 | async-start | bytes 1048576 | tf_op jit(solution)/shard_map/all_to_all | solution.py:629
  167.5 3.5 %convolution_convert_fusion.2.refs_2_ = bf16[384,2048]{1,0:T(8,128)(2,1)S(1)} fusion(bf16[768,2048]{1,0:T(8,128)(2,1)} %copy-done.16, bf16[384,384]{1,0:T(8,128)(2,1)S(1)} %slice-done, bf16[384,384]{1,0:T(8,128)(2,1)S(1)} %slice.14), kind=kOutput, calls=%fused_computation.2 | convolution fusion | flops 1209925632 | bytes 5308416 | tf_op jit(solution)/shard_map/dot_general | solution.py:597
  170.9 5.6 %collective-permute-done.33.refs_5_ = bf16[128,2304]{1,0:T(8,128)(2,1)} collective-permute-done((bf16[128,2304]{1,0:T(8,128)(2,1)}, bf16[128,2304]{1,0:T(8,128)(2,1)}, u32[]{:S(2)}, u32[]{:S(2)}) %collective-permute-start.33) | collective-permute-done | bytes 589856 | tf_op jit(solution)/shard_map/ppermute | solution.py:352
  176.5 10.0 %collective-permute-done.34.refs_6_ = bf16[128,2304]{1,0:T(8,128)(2,1)} collective-permute-done((bf16[128,2304]{1,0:T(8,128)(2,1)}, bf16[128,2304]{1,0:T(8,128)(2,1)}, u32[]{:S(2)}, u32[]{:S(2)}) %collective-permute-start.34) | collective-permute-done | bytes 589856 | tf_op jit(solution)/shard_map/ppermute | solution.py:357
  186.6 3.7 %assemble.14 = (bf16[128,2048]{1,0:T(8,128)(2,1)}, bf16[128,2048]{1,0:T(8,128)(2,1)}, bf16[128,1536]{1,0:T(8,128)(2,1)}, bf16[128,1536]{1,0:T(8,128)(2,1)S(1)}, bf16[128,2048]{1,0:T(8,128)(2,1)S(1)}) custom-call(bf16[768,2048]{1,0:T(8,128)(2,1)S(1)} %convolution_convert_fusion.1.refs_0_, bf16[896,2048]{1,0:T(8,128)(2,1)S(1)} %copy-done.1, ...), custom_call_target="tpu_custom_call" | custom-call | flops 2359296 | bytes 9437184 | tf_op jit(solution)/shard_map/assemble/pallas_call | solution.py:446
  192.4 1.9 collective-permute-start.37
  194.3 1.9 collective-permute-start.38
  196.2 2.0 copy.9
  198.3 8.2 %collective-permute-done.37.refs_3_ = bf16[128,1536]{1,0:T(8,128)(2,1)S(1)} collective-permute-done((bf16[128,1536]{1,0:T(8,128)(2,1)}, bf16[128,1536]{1,0:T(8,128)(2,1)S(1)}, u32[]{:S(2)}, u32[]{:S(2)}) %collective-permute-start.37) | collective-permute-done | bytes 393248 | tf_op jit(solution)/shard_map/ppermute | solution.py:352
  206.5 6.4 %collective-permute-done.38.refs_4_ = bf16[128,1536]{1,0:T(8,128)(2,1)S(1)} collective-permute-done((bf16[128,1536]{1,0:T(8,128)(2,1)S(1)}, bf16[128,1536]{1,0:T(8,128)(2,1)S(1)}, u32[]{:S(2)}, u32[]{:S(2)}) %collective-permute-start.38) | collective-permute-done | bytes 393248 | tf_op jit(solution)/shard_map/ppermute | solution.py:357
  213.9 1.7 assemble.15
  (117 shorter events, 28.1 us)
Async XLA Ops:
  4.9 25.5 %collective-permute-start.4 = (bf16[384,2048]{1,0:T(8,128)(2,1)}, bf16[384,2048]{1,0:T(8,128)(2,1)S(1)}, u32[]{:S(2)}, u32[]{:S(2)}) collective-permute-start(bf16[384,2048]{1,0:T(8,128)(2,1)} %get-tuple-element.101), channel_id=1, source_target_pairs={{0,1},{1,0},{2,3},{3,2},{4,5},{5,4},{6,7},{7,6},{8,9},{9,8},{10,11... | collective-permute-start | bytes 4718600 | tf_op jit(solution)/shard_map/ppermute | solution.py:339
  5.4 24.9 %collective-permute-start = (bf16[128,2048]{1,0:T(8,128)(2,1)}, bf16[128,2048]{1,0:T(8,128)(2,1)S(1)}, u32[]{:S(2)}, u32[]{:S(2)}) collective-permute-start(bf16[128,2048]{1,0:T(8,128)(2,1)} %get-tuple-element.110.refs_0_), channel_id=1, source_target_pairs={{0,2},{2,0},{4,6},{6,4},{8,10},{10,8},{12,14},{14,12},{16,18},{18,... | collective-permute-start | bytes 1572872 | tf_op jit(solution)/shard_map/ppermute | solution.py:343
  7.9 22.4 %collective-permute-start.1 = (bf16[128,2048]{1,0:T(8,128)(2,1)}, bf16[128,2048]{1,0:T(8,128)(2,1)S(1)}, u32[]{:S(2)}, u32[]{:S(2)}) collective-permute-start(bf16[128,2048]{1,0:T(8,128)(2,1)} %get-tuple-element.110.refs_0_), channel_id=1, source_target_pairs={{0,4},{2,6},{4,0},{6,2},{8,12},{10,14},{12,8},{14,10},{16,20},{18,... | collective-permute-start | bytes 1572872 | tf_op jit(solution)/shard_map/ppermute | solution.py:347
  9.5 14.0 %collective-permute-start.2 = (bf16[96,2048]{1,0:T(8,128)(2,1)}, bf16[96,2048]{1,0:T(8,128)(2,1)S(1)}, u32[]{:S(2)}, u32[]{:S(2)}) collective-permute-start(bf16[96,2048]{1,0:T(8,128)(2,1)} %get-tuple-element.98), channel_id=1, source_target_pairs={{0,8},{2,10},{4,12},{6,14},{8,16},{10,18},{12,20},{14,22},{16,24},... | collective-permute-start | bytes 1179656 | tf_op jit(solution)/shard_map/ppermute | solution.py:352
  11.0 19.3 %collective-permute-start.3 = (bf16[96,2048]{1,0:T(8,128)(2,1)}, bf16[96,2048]{1,0:T(8,128)(2,1)S(1)}, u32[]{:S(2)}, u32[]{:S(2)}) collective-permute-start(bf16[96,2048]{1,0:T(8,128)(2,1)} %get-tuple-element.98), channel_id=1, source_target_pairs={{8,0},{10,2},{12,4},{14,6},{16,8},{18,10},{20,12},{22,14},{24,16},... | collective-permute-start | bytes 1179656 | tf_op jit(solution)/shard_map/ppermute | solution.py:357
  30.3 11.4 %copy-start.10 = (bf16[384,2048]{1,0:T(8,128)(2,1)}, bf16[384,2048]{1,0:T(8,128)(2,1)S(1)}, u32[]{:S(2)}) copy-start(bf16[384,2048]{1,0:T(8,128)(2,1)S(1)} %collective-permute-done.4) | copy-start | bytes 4718596
  36.6 31.5 %collective-permute-start.6 = (bf16[256,2048]{1,0:T(8,128)(2,1)}, bf16[256,2048]{1,0:T(8,128)(2,1)S(1)}, u32[]{:S(2)}, u32[]{:S(2)}) collective-permute-start(bf16[256,2048]{1,0:T(8,128)(2,1)} %get-tuple-element.118), channel_id=1, source_target_pairs={{0,2},{2,0},{4,6},{6,4},{8,10},{10,8},{12,14},{14,12},{16,18},{18,... | collective-permute-start | bytes 3145736 | tf_op jit(solution)/shard_map/ppermute | solution.py:343
  37.2 30.9 %collective-permute-start.7 = (bf16[256,2048]{1,0:T(8,128)(2,1)}, bf16[256,2048]{1,0:T(8,128)(2,1)S(1)}, u32[]{:S(2)}, u32[]{:S(2)}) collective-permute-start(bf16[256,2048]{1,0:T(8,128)(2,1)} %get-tuple-element.119), channel_id=1, source_target_pairs={{0,4},{2,6},{4,0},{6,2},{8,12},{10,14},{12,8},{14,10},{16,20},{18,... | collective-permute-start | bytes 3145736 | tf_op jit(solution)/shard_map/ppermute | solution.py:347
  37.7 18.3 %collective-permute-start.8 = (bf16[144,2048]{1,0:T(8,128)(2,1)}, bf16[144,2048]{1,0:T(8,128)(2,1)S(1)}, u32[]{:S(2)}, u32[]{:S(2)}) collective-permute-start(bf16[144,2048]{1,0:T(8,128)(2,1)} %get-tuple-element.120), channel_id=1, source_target_pairs={{0,8},{2,10},{4,12},{6,14},{8,16},{10,18},{12,20},{14,22},{16,24},... | collective-permute-start | bytes 1769480 | tf_op jit(solution)/shard_map/ppermute | solution.py:352
  38.8 29.3 %collective-permute-start.9 = (bf16[144,2048]{1,0:T(8,128)(2,1)}, bf16[144,2048]{1,0:T(8,128)(2,1)S(1)}, u32[]{:S(2)}, u32[]{:S(2)}) collective-permute-start(bf16[144,2048]{1,0:T(8,128)(2,1)} %get-tuple-element.121), channel_id=1, source_target_pairs={{8,0},{10,2},{12,4},{14,6},{16,8},{18,10},{20,12},{22,14},{24,16},... | collective-permute-start | bytes 1769480 | tf_op jit(solution)/shard_map/ppermute | solution.py:357
  43.9 4.5 %collective-permute-start.5 = (bf16[576,384]{1,0:T(8,128)(2,1)}, bf16[576,384]{1,0:T(8,128)(2,1)}, u32[]{:S(2)}, u32[]{:S(2)}) collective-permute-start(bf16[576,384]{1,0:T(8,128)(2,1)} %convolution_convert_fusion.4), channel_id=1, source_target_pairs={{0,1},{1,0},{2,3},{3,2},{4,5},{5,4},{6,7},{7,6},{8,9},{9,8},{10,11... | collective-permute-start | bytes 1327112 | tf_op jit(solution)/shard_map/ppermute | solution.py:339
  50.5 53.4 %all-to-all-start = ((bf16[128,16,128]{2,0,1:T(8,128)(2,1)}), bf16[128,16,128]{2,0,1:T(8,128)(2,1)}, u32[]{:S(2)}, u32[]{:S(2)}) async-start(bf16[128,16,128]{2,0,1:T(8,128)(2,1)} %copy.8), calls=%async_computation | async-start | bytes 1048576 | tf_op jit(solution)/shard_map/all_to_all | solution.py:493
  71.2 20.7 %collective-permute-start.10 = (bf16[192,2048]{1,0:T(8,128)(2,1)S(1)}, bf16[192,2048]{1,0:T(8,128)(2,1)S(1)}, u32[]{:S(2)}, u32[]{:S(2)}) collective-permute-start(bf16[192,2048]{1,0:T(8,128)(2,1)S(1)} %get-tuple-element.126), channel_id=1, source_target_pairs={{0,2},{2,0},{4,6},{6,4},{8,10},{10,8},{12,14},{14,12},{16,18},{18,... | collective-permute-start | bytes 2359304 | tf_op jit(solution)/shard_map/ppermute | solution.py:343
  72.7 19.2 %collective-permute-start.11 = (bf16[192,2048]{1,0:T(8,128)(2,1)S(1)}, bf16[192,2048]{1,0:T(8,128)(2,1)S(1)}, u32[]{:S(2)}, u32[]{:S(2)}) collective-permute-start(bf16[192,2048]{1,0:T(8,128)(2,1)S(1)} %get-tuple-element.127), channel_id=1, source_target_pairs={{0,4},{2,6},{4,0},{6,2},{8,12},{10,14},{12,8},{14,10},{16,20},{18,... | collective-permute-start | bytes 2359304 | tf_op jit(solution)/shard_map/ppermute | solution.py:347
  73.9 12.4 %collective-permute-start.12 = (bf16[80,2048]{1,0:T(8,128)(2,1)S(1)}, bf16[80,2048]{1,0:T(8,128)(2,1)S(1)}, u32[]{:S(2)}, u32[]{:S(2)}) collective-permute-start(bf16[80,2048]{1,0:T(8,128)(2,1)S(1)} %get-tuple-element.128), channel_id=1, source_target_pairs={{0,8},{2,10},{4,12},{6,14},{8,16},{10,18},{12,20},{14,22},{16,24},... | collective-permute-start | bytes 983048 | tf_op jit(solution)/shard_map/ppermute | solution.py:352
  74.4 14.9 %collective-permute-start.13 = (bf16[80,2048]{1,0:T(8,128)(2,1)S(1)}, bf16[80,2048]{1,0:T(8,128)(2,1)S(1)}, u32[]{:S(2)}, u32[]{:S(2)}) collective-permute-start(bf16[80,2048]{1,0:T(8,128)(2,1)S(1)} %get-tuple-element.129), channel_id=1, source_target_pairs={{8,0},{10,2},{12,4},{14,6},{16,8},{18,10},{20,12},{22,14},{24,16},... | collective-permute-start | bytes 983048 | tf_op jit(solution)/shard_map/ppermute | solution.py:357
  80.6 23.3 %collective-permute-start.18 = (bf16[800,384]{1,0:T(8,128)(2,1)}, bf16[800,384]{1,0:T(8,128)(2,1)}, u32[]{:S(2)}, u32[]{:S(2)}) collective-permute-start(bf16[800,384]{1,0:T(8,128)(2,1)} %convolution_convert_fusion.3), channel_id=1, source_target_pairs={{0,1},{1,0},{2,3},{3,2},{4,5},{5,4},{6,7},{7,6},{8,9},{9,8},{10,11... | collective-permute-start | bytes 1843208 | tf_op jit(solution)/shard_map/ppermute | solution.py:339
  92.7 9.3 %collective-permute-start.14 = (bf16[48,2048]{1,0:T(8,128)(2,1)S(1)}, bf16[48,2048]{1,0:T(8,128)(2,1)S(1)}, u32[]{:S(2)}, u32[]{:S(2)}) collective-permute-start(bf16[48,2048]{1,0:T(8,128)(2,1)S(1)} %get-tuple-element.134), channel_id=1, source_target_pairs={{0,2},{2,0},{4,6},{6,4},{8,10},{10,8},{12,14},{14,12},{16,18},{18,... | collective-permute-start | bytes 589832 | tf_op jit(solution)/shard_map/ppermute | solution.py:343
  93.7 8.3 %collective-permute-start.15 = (bf16[48,2048]{1,0:T(8,128)(2,1)S(1)}, bf16[48,2048]{1,0:T(8,128)(2,1)S(1)}, u32[]{:S(2)}, u32[]{:S(2)}) collective-permute-start(bf16[48,2048]{1,0:T(8,128)(2,1)S(1)} %get-tuple-element.135), channel_id=1, source_target_pairs={{0,4},{2,6},{4,0},{6,2},{8,12},{10,14},{12,8},{14,10},{16,20},{18,... | collective-permute-start | bytes 589832 | tf_op jit(solution)/shard_map/ppermute | solution.py:347
  94.5 7.4 %collective-permute-start.16 = (bf16[16,2048]{1,0:T(8,128)(2,1)S(1)}, bf16[16,2048]{1,0:T(8,128)(2,1)S(1)}, u32[]{:S(2)}, u32[]{:S(2)}) collective-permute-start(bf16[16,2048]{1,0:T(8,128)(2,1)S(1)} %get-tuple-element.136), channel_id=1, source_target_pairs={{0,8},{2,10},{4,12},{6,14},{8,16},{10,18},{12,20},{14,22},{16,24},... | collective-permute-start | bytes 196616 | tf_op jit(solution)/shard_map/ppermute | solution.py:352
  95.5 6.5 %collective-permute-start.17 = (bf16[16,2048]{1,0:T(8,128)(2,1)S(1)}, bf16[16,2048]{1,0:T(8,128)(2,1)S(1)}, u32[]{:S(2)}, u32[]{:S(2)}) collective-permute-start(bf16[16,2048]{1,0:T(8,128)(2,1)S(1)} %get-tuple-element.137), channel_id=1, source_target_pairs={{8,0},{10,2},{12,4},{14,6},{16,8},{18,10},{20,12},{22,14},{24,16},... | collective-permute-start | bytes 196616 | tf_op jit(solution)/shard_map/ppermute | solution.py:357
  101.9 2.3 %collective-permute-start.19 = (bf16[544,384]{1,0:T(8,128)(2,1)}, bf16[544,384]{1,0:T(8,128)(2,1)}, u32[]{:S(2)}, u32[]{:S(2)}) collective-permute-start(bf16[544,384]{1,0:T(8,128)(2,1)} %convolution_convert_fusion.5), channel_id=1, source_target_pairs={{0,1},{1,0},{2,3},{3,2},{4,5},{5,4},{6,7},{7,6},{8,9},{9,8},{10,11... | collective-permute-start | bytes 1253384 | tf_op jit(solution)/shard_map/ppermute | solution.py:339
  102.7 1.5 collective-permute-start.20
  104.2 14.7 %copy-start.14 = (bf16[384,2048]{1,0:T(8,128)(2,1)S(1)}, bf16[384,2048]{1,0:T(8,128)(2,1)}, u32[]{:S(2)}) copy-start(bf16[384,2048]{1,0:T(8,128)(2,1)} %get-tuple-element.117) | copy-start | bytes 4718596
  118.4 20.8 %copy-start.3 = (bf16[1280,384]{1,0:T(8,128)(2,1)}, bf16[1280,384]{1,0:T(8,128)(2,1)S(1)}, u32[]{:S(2)}) copy-start(bf16[1280,384]{1,0:T(8,128)(2,1)S(1)} %get-tuple-element.153) | copy-start | bytes 2949124
  118.4 2.1 collective-permute-start.21
  119.0 20.2 %collective-permute-start.26 = (bf16[1280,384]{1,0:T(8,128)(2,1)S(1)}, bf16[1280,384]{1,0:T(8,128)(2,1)S(1)}, u32[]{:S(2)}, u32[]{:S(2)}) collective-permute-start(bf16[1280,384]{1,0:T(8,128)(2,1)S(1)} %get-tuple-element.153), channel_id=1, source_target_pairs={{0,1},{1,0},{2,3},{3,2},{4,5},{5,4},{6,7},{7,6},{8,9},{9,8},{10,11... | collective-permute-start | bytes 2949128 | tf_op jit(solution)/shard_map/ppermute | solution.py:339
  120.5 19.8 %copy-start.16 = (bf16[768,2048]{1,0:T(8,128)(2,1)}, bf16[768,2048]{1,0:T(8,128)(2,1)S(1)}, u32[]{:S(2)}) copy-start(bf16[768,2048]{1,0:T(8,128)(2,1)S(1)} %constant_dynamic-update-slice_fusion.17) | copy-start | bytes 9437188
  123.5 8.7 %collective-permute-start.22 = (bf16[128,768]{1,0:T(8,128)(2,1)S(1)}, bf16[128,768]{1,0:T(8,128)(2,1)S(1)}, u32[]{:S(2)}, u32[]{:S(2)}) collective-permute-start(bf16[128,768]{1,0:T(8,128)(2,1)S(1)} %get-tuple-element.145), channel_id=1, source_target_pairs={{0,2},{2,0},{4,6},{6,4},{8,10},{10,8},{12,14},{14,12},{16,18},{18,... | collective-permute-start | bytes 589832 | tf_op jit(solution)/shard_map/ppermute | solution.py:343
  124.8 7.4 %collective-permute-start.23 = (bf16[128,768]{1,0:T(8,128)(2,1)S(1)}, bf16[128,768]{1,0:T(8,128)(2,1)S(1)}, u32[]{:S(2)}, u32[]{:S(2)}) collective-permute-start(bf16[128,768]{1,0:T(8,128)(2,1)S(1)} %get-tuple-element.146), channel_id=1, source_target_pairs={{0,4},{2,6},{4,0},{6,2},{8,12},{10,14},{12,8},{14,10},{16,20},{18,... | collective-permute-start | bytes 589832 | tf_op jit(solution)/shard_map/ppermute | solution.py:347
  125.9 6.3 %collective-permute-start.24 = (bf16[128,256]{1,0:T(8,128)(2,1)S(1)}, bf16[128,256]{1,0:T(8,128)(2,1)S(1)}, u32[]{:S(2)}, u32[]{:S(2)}) collective-permute-start(bf16[128,256]{1,0:T(8,128)(2,1)S(1)} %get-tuple-element.147), channel_id=1, source_target_pairs={{0,8},{2,10},{4,12},{6,14},{8,16},{10,18},{12,20},{14,22},{16,24},... | collective-permute-start | bytes 196616 | tf_op jit(solution)/shard_map/ppermute | solution.py:352
  125.9 6.3 %collective-permute-start.25 = (bf16[128,256]{1,0:T(8,128)(2,1)S(1)}, bf16[128,256]{1,0:T(8,128)(2,1)S(1)}, u32[]{:S(2)}, u32[]{:S(2)}) collective-permute-start(bf16[128,256]{1,0:T(8,128)(2,1)S(1)} %get-tuple-element.148), channel_id=1, source_target_pairs={{8,0},{10,2},{12,4},{14,6},{16,8},{18,10},{20,12},{22,14},{24,16},... | collective-permute-start | bytes 196616 | tf_op jit(solution)/shard_map/ppermute | solution.py:357
  133.6 18.2 %collective-permute-start.27 = (bf16[128,3072]{1,0:T(8,128)(2,1)S(1)}, bf16[128,3072]{1,0:T(8,128)(2,1)S(1)}, u32[]{:S(2)}, u32[]{:S(2)}) collective-permute-start(bf16[128,3072]{1,0:T(8,128)(2,1)S(1)} %get-tuple-element.159), channel_id=1, source_target_pairs={{0,2},{2,0},{4,6},{6,4},{8,10},{10,8},{12,14},{14,12},{16,18},{18,... | collective-permute-start | bytes 2359304 | tf_op jit(solution)/shard_map/ppermute | solution.py:343
  134.5 17.8 %collective-permute-start.28 = (bf16[128,3072]{1,0:T(8,128)(2,1)S(1)}, bf16[128,3072]{1,0:T(8,128)(2,1)S(1)}, u32[]{:S(2)}, u32[]{:S(2)}) collective-permute-start(bf16[128,3072]{1,0:T(8,128)(2,1)S(1)} %get-tuple-element.160), channel_id=1, source_target_pairs={{0,4},{2,6},{4,0},{6,2},{8,12},{10,14},{12,8},{14,10},{16,20},{18,... | collective-permute-start | bytes 2359304 | tf_op jit(solution)/shard_map/ppermute | solution.py:347
  135.3 12.5 %collective-permute-start.29 = (bf16[128,1280]{1,0:T(8,128)(2,1)S(1)}, bf16[128,1280]{1,0:T(8,128)(2,1)S(1)}, u32[]{:S(2)}, u32[]{:S(2)}) collective-permute-start(bf16[128,1280]{1,0:T(8,128)(2,1)S(1)} %get-tuple-element.161), channel_id=1, source_target_pairs={{0,8},{2,10},{4,12},{6,14},{8,16},{10,18},{12,20},{14,22},{16,24},... | collective-permute-start | bytes 983048 | tf_op jit(solution)/shard_map/ppermute | solution.py:352
  135.4 15.0 %collective-permute-start.30 = (bf16[128,1280]{1,0:T(8,128)(2,1)S(1)}, bf16[128,1280]{1,0:T(8,128)(2,1)S(1)}, u32[]{:S(2)}, u32[]{:S(2)}) collective-permute-start(bf16[128,1280]{1,0:T(8,128)(2,1)S(1)} %get-tuple-element.162), channel_id=1, source_target_pairs={{8,0},{10,2},{12,4},{14,6},{16,8},{18,10},{20,12},{22,14},{24,16},... | collective-permute-start | bytes 983048 | tf_op jit(solution)/shard_map/ppermute | solution.py:357
  143.5 12.2 %copy-start = (bf16[896,2048]{1,0:T(8,128)(2,1)}, bf16[896,2048]{1,0:T(8,128)(2,1)S(1)}, u32[]{:S(2)}) copy-start(bf16[896,2048]{1,0:T(8,128)(2,1)S(1)} %convolution_convert_fusion.refs_1_) | copy-start | bytes 11010052
  152.3 15.2 %slice-start = ((bf16[1280,384]{1,0:T(8,128)(2,1)}), bf16[384,384]{1,0:T(8,128)(2,1)S(1)}, s32[]{:S(2)}) async-start(bf16[1280,384]{1,0:T(8,128)(2,1)} %copy-done.15), calls=%async_computation.2 | async-start | bytes 589824 | tf_op jit(solution)/shard_map/slice | solution.py:626
  155.8 30.8 %collective-permute-start.31 = (bf16[128,4096]{1,0:T(8,128)(2,1)}, bf16[128,4096]{1,0:T(8,128)(2,1)}, u32[]{:S(2)}, u32[]{:S(2)}) collective-permute-start(bf16[128,4096]{1,0:T(8,128)(2,1)} %get-tuple-element.173), channel_id=1, source_target_pairs={{0,2},{2,0},{4,6},{6,4},{8,10},{10,8},{12,14},{14,12},{16,18},{18,... | collective-permute-start | bytes 3145736 | tf_op jit(solution)/shard_map/ppermute | solution.py:343
  157.0 29.6 %collective-permute-start.32 = (bf16[128,4096]{1,0:T(8,128)(2,1)}, bf16[128,4096]{1,0:T(8,128)(2,1)}, u32[]{:S(2)}, u32[]{:S(2)}) collective-permute-start(bf16[128,4096]{1,0:T(8,128)(2,1)} %get-tuple-element.174), channel_id=1, source_target_pairs={{0,4},{2,6},{4,0},{6,2},{8,12},{10,14},{12,8},{14,10},{16,20},{18,... | collective-permute-start | bytes 3145736 | tf_op jit(solution)/shard_map/ppermute | solution.py:347
  158.2 18.4 %collective-permute-start.33 = (bf16[128,2304]{1,0:T(8,128)(2,1)}, bf16[128,2304]{1,0:T(8,128)(2,1)}, u32[]{:S(2)}, u32[]{:S(2)}) collective-permute-start(bf16[128,2304]{1,0:T(8,128)(2,1)} %get-tuple-element.175), channel_id=1, source_target_pairs={{0,8},{2,10},{4,12},{6,14},{8,16},{10,18},{12,20},{14,22},{16,24},... | collective-permute-start | bytes 1769480 | tf_op jit(solution)/shard_map/ppermute | solution.py:352
  158.3 28.3 %collective-permute-start.34 = (bf16[128,2304]{1,0:T(8,128)(2,1)}, bf16[128,2304]{1,0:T(8,128)(2,1)}, u32[]{:S(2)}, u32[]{:S(2)}) collective-permute-start(bf16[128,2304]{1,0:T(8,128)(2,1)} %get-tuple-element.176), channel_id=1, source_target_pairs={{8,0},{10,2},{12,4},{14,6},{16,8},{18,10},{20,12},{22,14},{24,16},... | collective-permute-start | bytes 1769480 | tf_op jit(solution)/shard_map/ppermute | solution.py:357
  162.0 34.2 %all-to-all-start.1 = ((bf16[16,128,128]{2,1,0:T(8,128)(2,1)}), bf16[16,128,128]{2,1,0:T(8,128)(2,1)}, u32[]{:S(2)}, u32[]{:S(2)}) async-start(bf16[16,128,128]{2,1,0:T(8,128)(2,1)} %bitcast.46), calls=%async_computation.1 | async-start | bytes 1048576 | tf_op jit(solution)/shard_map/all_to_all | solution.py:629
  167.5 19.1 %copy-start.1 = (bf16[896,2048]{1,0:T(8,128)(2,1)S(1)}, bf16[896,2048]{1,0:T(8,128)(2,1)}, u32[]{:S(2)}) copy-start(bf16[896,2048]{1,0:T(8,128)(2,1)} %copy-done) | copy-start | bytes 11010052
  191.1 21.7 %collective-permute-start.35 = (bf16[128,2048]{1,0:T(8,128)(2,1)}, bf16[128,2048]{1,0:T(8,128)(2,1)S(1)}, u32[]{:S(2)}, u32[]{:S(2)}) collective-permute-start(bf16[128,2048]{1,0:T(8,128)(2,1)} %get-tuple-element.182), channel_id=1, source_target_pairs={{0,2},{2,0},{4,6},{6,4},{8,10},{10,8},{12,14},{14,12},{16,18},{18,... | collective-permute-start | bytes 1572872 | tf_op jit(solution)/shard_map/ppermute | solution.py:343
  192.0 20.8 %collective-permute-start.36 = (bf16[128,2048]{1,0:T(8,128)(2,1)}, bf16[128,2048]{1,0:T(8,128)(2,1)S(1)}, u32[]{:S(2)}, u32[]{:S(2)}) collective-permute-start(bf16[128,2048]{1,0:T(8,128)(2,1)} %get-tuple-element.183), channel_id=1, source_target_pairs={{0,4},{2,6},{4,0},{6,2},{8,12},{10,14},{12,8},{14,10},{16,20},{18,... | collective-permute-start | bytes 1572872 | tf_op jit(solution)/shard_map/ppermute | solution.py:347
  192.4 14.1 %collective-permute-start.37 = (bf16[128,1536]{1,0:T(8,128)(2,1)}, bf16[128,1536]{1,0:T(8,128)(2,1)S(1)}, u32[]{:S(2)}, u32[]{:S(2)}) collective-permute-start(bf16[128,1536]{1,0:T(8,128)(2,1)} %get-tuple-element.184), channel_id=1, source_target_pairs={{0,8},{2,10},{4,12},{6,14},{8,16},{10,18},{12,20},{14,22},{16,24},... | collective-permute-start | bytes 1179656 | tf_op jit(solution)/shard_map/ppermute | solution.py:352
  194.3 18.5 %collective-permute-start.38 = (bf16[128,1536]{1,0:T(8,128)(2,1)S(1)}, bf16[128,1536]{1,0:T(8,128)(2,1)S(1)}, u32[]{:S(2)}, u32[]{:S(2)}) collective-permute-start(bf16[128,1536]{1,0:T(8,128)(2,1)S(1)} %get-tuple-element.185), channel_id=1, source_target_pairs={{8,0},{10,2},{12,4},{14,6},{16,8},{18,10},{20,12},{22,14},{24,16},... | collective-permute-start | bytes 1179656 | tf_op jit(solution)/shard_map/ppermute | solution.py:357
  (12 other events, 26.4 us)
where the time goes:
time: 216 us
  waiting for transfers between devices  81.6 us (38%)
  starting transfers between devices  58.7 us (27%)
  Pallas kernels  37.2 us (17%)
  matrix products  25.4 us (12%)
  local copies, waits for them, and re-layouts  11.5 us (5%)
    ppermute x8, waiting for transfers between devices, down(): lax.ppermute(value, 'ctx', [((i + PLANE) % count, i) for i in range(count)])  40.9 us
    ppermute x8, waiting for transfers between devices, up(): lax.ppermute(value, 'ctx', [(i, (i + PLANE) % count) for i in range(count)])  35.8 us
    ppermute x8, starting transfers between devices, down(): lax.ppermute(value, 'ctx', [((i + PLANE) % count, i) for i in range(count)])  24.3 us
    pallas_call x8, Pallas kernels, assemble(): pl.pallas_call(functools.partial(assemble_kernel, len(arrays), plans), ou...  18.9 us
    dot_general x8, matrix products, project(): jnp.einsum('td,rd->tr', rows, matrix, preferred_element_type=jnp.float32)  15.9 us
    pallas_call x1, Pallas kernels, scan_all(): pl.pallas_call(functools.partial(scan_kernel, PLANE, runs, order), out_sh...  14.2 us
    ppermute x8, starting transfers between devices, over_x(): lax.ppermute(value, 'ctx', [(i, i ^ 1) for i in range(lax.axis_size('ctx'...  10.1 us
    dot_general x3, matrix products, product(): return narrowed(jnp.dot(both, matrix, preferred_element_type=jnp.float32))  9.52 us
  transfers between devices with their start and end apart: 41, of which 17 were waited for; matrix products, arithmetic and copies ran while one was open for 15% of the time, Pallas kernels for 4%

commit v1 on v0

--- a/solution.py
+++ b/solution.py
@@ -406,51 +406,30 @@
 
 
 def assemble_kernel(inputs, plans, *refs):
-    arrays, refs = refs[:inputs], refs[inputs:]
-    outs, refs = refs[: len(plans)], refs[len(plans) :]
-    arrived, held = refs[0], refs[1:]
-    started, k, slot = [], 0, 0
-    pending = []
+    arrays, outs = refs[:inputs], refs[inputs:]
     for out, plan in zip(outs, plans):
         for row, col, height, width, sources in plan:
-            here = out.at[pl.ds(row, height), pl.ds(col, width)]
-            single = len(sources) == 1
-            mine = []
-            for index, from_row, from_col in sources:
-                part = arrays[index].at[pl.ds(from_row, height), pl.ds(from_col, width)]
-                into = here if single else held[slot]
-                copy = pltpu.make_async_copy(part, into, arrived.at[k])
-                copy.start()
-                mine.append((copy, into))
-                k += 1
-                slot += 0 if single else 1
-            if single:
-                started.append(mine[0][0])
-            else:
-                pending.append((here, mine))
-    for here, mine in pending:
-        for copy, _ in mine:
-            copy.wait()
-        here[...] = narrowed(sum(widened(into[...]) for _, into in mine))
-    for copy in started:
-        copy.wait()
+            parts = [
+                arrays[index][from_row : from_row + height, from_col : from_col + width]
+                for index, from_row, from_col in sources
+            ]
+            if len(parts) > 1:
+                parts = [narrowed(sum(widened(part) for part in parts))]
+            out[row : row + height, col : col + width] = parts[0]
 
 
 def assemble(arrays, *plans):
-    sources = [(piece, source) for plan in plans for piece in plan for source in piece[4]]
-    sums = [piece for piece, _ in sources if len(piece[4]) > 1]
     shapes = [
         (max(p[0] + p[2] for p in plan), max(p[1] + p[3] for p in plan)) for plan in plans
     ]
     moved = sum(2 * rows * cols for rows, cols in shapes)
+    vmem = pl.BlockSpec(memory_space=pltpu.VMEM)
     return pl.pallas_call(
         functools.partial(assemble_kernel, len(arrays), plans),
         out_shape=tuple(jax.ShapeDtypeStruct(shape, jnp.bfloat16) for shape in shapes),
-        in_specs=[pl.BlockSpec(memory_space=pl.ANY)] * len(arrays),
-        out_specs=(pl.BlockSpec(memory_space=pltpu.VMEM),) * len(plans),
-        scratch_shapes=[pltpu.SemaphoreType.DMA((len(sources),))]
-        + [pltpu.VMEM((piece[2], piece[3]), jnp.bfloat16) for piece in sums],
-        compiler_params=pltpu.CompilerParams(vmem_limit_bytes=24 * 2**20),
+        in_specs=[vmem] * len(arrays),
+        out_specs=(vmem,) * len(plans),
+        compiler_params=pltpu.CompilerParams(vmem_limit_bytes=32 * 2**20),
         cost_estimate=pl.CostEstimate(flops=moved, bytes_accessed=4 * moved, transcendentals=0),
         name="assemble",
     )(*arrays)
@@ -477,7 +456,9 @@
 
 
 def all_ways(for_x, for_y, for_above, for_below):
-    return lax.optimization_barrier((over_x(for_x), over_y(for_y), up(for_above), down(for_below)))
+    from_below, from_above = up(for_above), down(for_below)
+    got_x, got_y = over_x(for_x), over_y(for_y)
+    return lax.optimization_barrier((got_x, got_y, from_below, from_above))
 
 
 def project(parts, kept, taken):
@@ -503,7 +484,6 @@
         return assemble(arrays, *[full_width(columns, rows_of(*plan)) for plan in plans])
 
     own_x, own_y, wide_3, wide_1 = all_ways(tokens, tokens, wide, wide)
-    own_x, matrices = lax.optimization_barrier((own_x, matrices))
     first = (tokens, own_x, own_y, wide_3, wide_1)
     members = ((0, n, m), (1, n, m), (2, n, m))
     sent = put(
@@ -706,13 +686,8 @@
     me = lax.axis_index("ctx").astype(jnp.int32).reshape(1)
     channels, span = weights.shape[1], tokens.shape[0]
     rows = weights[0].swapaxes(0, 1).reshape(3 * channels, weights.shape[3])
-    *tokens_half, kept, given = halves(
-        (tokens, rows),
-        (0, span, True),
-        (0, span * 3 // 4, True),
-        (1, 3 * channels, True),
-        (1, 3 * channels, False),
-    )
+    tokens_half = halves((tokens,), (0, span, True), (0, span * 3 // 4, True))
+    kept, given = halves((rows,), (0, 3 * channels, True), (0, 3 * channels, False))
     taken = swapped(given)
     parts, runs, (kept, taken), cot_cols = gather_groups(*tokens_half, (kept, taken), cotangent)
     own, other = zip(*parts)

time: 216 us -> 214 us (level)
  Pallas kernels: 37.2 us -> 27.4 us
  matrix products: 25.4 us -> 29.3 us
  local copies, waits for them, and re-layouts: 11.5 us -> 15.4 us
  waiting for transfers between devices: 81.6 us -> 79.2 us
  starting transfers between devices: 58.7 us -> 61 us
    pallas_call x8, Pallas kernels: 18.9 us -> 7.73 us  [assemble(): pl.pallas_call(functools.partial(assemble_kernel, len(arrays), plans), ou...]
    ppermute x8, waiting for transfers between devices: 35.8 us -> 41.6 us  [up(): lax.ppermute(value, 'ctx', [(i, (i + PLANE) % count) for i in range(count)])]
    ppermute x8, starting transfers between devices: 6.32 us -> 11.5 us  [up(): lax.ppermute(value, 'ctx', [(i, (i + PLANE) % count) for i in range(count)])]
    ppermute x8, starting transfers between devices: 24.3 us -> 19.1 us  [down(): lax.ppermute(value, 'ctx', [((i + PLANE) % count, i) for i in range(count)])]
    ppermute x8, waiting for transfers between devices: 40.9 us -> 36.9 us  [down(): lax.ppermute(value, 'ctx', [((i + PLANE) % count, i) for i in range(count)])]
    dot_general x8, matrix products: 15.9 us -> 19.8 us  [project(): jnp.einsum('td,rd->tr', rows, matrix, preferred_element_type=jnp.float32)]
    ppermute x8, waiting for transfers between devices: 3.92 us -> 0.39 us  [over_x(): lax.ppermute(value, 'ctx', [(i, i ^ 1) for i in range(lax.axis_size('ctx'...]
    unnamed x50 -> x62, local copies, waits for them, and re-layouts: 6.08 us -> 9.53 us
  transfers between devices with their start and end apart: 41 -> 41, of which waited for: 17 -> 15; matrix products, arithmetic and copies ran while one was open for 15% -> 17% of each run, Pallas kernels for 4% -> 4%
where the time goes in v1:
time: 214 us
  waiting for transfers between devices  79.2 us (37%)
  starting transfers between devices  61 us (29%)
  matrix products  29.3 us (14%)
  Pallas kernels  27.4 us (13%)
  local copies, waits for them, and re-layouts  15.4 us (7%)
    ppermute x8, waiting for transfers between devices, up(): lax.ppermute(value, 'ctx', [(i, (i + PLANE) % count) for i in range(count)])  41.6 us
    ppermute x8, waiting for transfers between devices, down(): lax.ppermute(value, 'ctx', [((i + PLANE) % count, i) for i in range(count)])  36.9 us
    dot_general x8, matrix products, project(): jnp.einsum('td,rd->tr', rows, matrix, preferred_element_type=jnp.float32)  19.8 us
    ppermute x8, starting transfers between devices, down(): lax.ppermute(value, 'ctx', [((i + PLANE) % count, i) for i in range(count)])  19.1 us
    pallas_call x1, Pallas kernels, scan_all(): pl.pallas_call(functools.partial(scan_kernel, PLANE, runs, order), out_sh...  14 us
    ppermute x8, starting transfers between devices, up(): lax.ppermute(value, 'ctx', [(i, (i + PLANE) % count) for i in range(count)])  11.5 us
    ppermute x8, starting transfers between devices, over_x(): lax.ppermute(value, 'ctx', [(i, i ^ 1) for i in range(lax.axis_size('ctx'...  11.1 us
    dot_general x3, matrix products, product(): return narrowed(jnp.dot(both, matrix, preferred_element_type=jnp.float32))  9.53 us
  transfers between devices with their start and end apart: 41, of which 15 were waited for; matrix products, arithmetic and copies ran while one was open for 17% of the time, Pallas kernels for 4%

profile of v1, /device:TPU:0, one launch (start us, length us, event | category | flops | bytes accessed | tf_op | source)
XLA Modules:
  0.0 213.5 jit_solution(6423369137378387002)
XLA Ops:
  0.6 2.1 halves.2
  2.7 3.0 %collective-permute-start = (bf16[128,2048]{1,0:T(8,128)(2,1)}, bf16[128,2048]{1,0:T(8,128)(2,1)S(1)}, u32[]{:S(2)}, u32[]{:S(2)}) collective-permute-start(bf16[128,2048]{1,0:T(8,128)(2,1)} %get-tuple-element.104.refs_0_), channel_id=1, source_target_pairs={{0,2},{2,0},{4,6},{6,4},{8,10},{10,8},{12,14},{14,12},{16,18},{18,... | collective-permute-start | bytes 1572872 | tf_op jit(solution)/shard_map/ppermute | solution.py:343
  5.7 1.5 collective-permute-start.1
  7.3 1.6 collective-permute-start.2
  8.8 2.2 %collective-permute-start.3 = (bf16[96,2048]{1,0:T(8,128)(2,1)}, bf16[96,2048]{1,0:T(8,128)(2,1)S(1)}, u32[]{:S(2)}, u32[]{:S(2)}) collective-permute-start(bf16[96,2048]{1,0:T(8,128)(2,1)} %get-tuple-element.95), channel_id=1, source_target_pairs={{8,0},{10,2},{12,4},{14,6},{16,8},{18,10},{20,12},{22,14},{24,16},... | collective-permute-start | bytes 1179656 | tf_op jit(solution)/shard_map/ppermute | solution.py:357
  11.1 3.6 %halves.3 = (bf16[384,2048]{1,0:T(8,128)(2,1)}, bf16[384,2048]{1,0:T(8,128)(2,1)}) custom-call(s32[1]{0:T(128)} %bitcast.5.core_ref, bf16[384,4096]{1,0:T(8,128)(2,1)} %bitcast.50), custom_call_target="tpu_custom_call" | custom-call | bytes 6291456 | tf_op jit(solution)/shard_map/halves/pallas_call | solution.py:395
  14.7 6.6 %collective-permute-done.2.refs_3_ = bf16[96,2048]{1,0:T(8,128)(2,1)S(1)} collective-permute-done((bf16[96,2048]{1,0:T(8,128)(2,1)}, bf16[96,2048]{1,0:T(8,128)(2,1)S(1)}, u32[]{:S(2)}, u32[]{:S(2)}) %collective-permute-start.2) | collective-permute-done | bytes 393248 | tf_op jit(solution)/shard_map/ppermute | solution.py:352
  21.4 6.1 %collective-permute-done.3.refs_4_ = bf16[96,2048]{1,0:T(8,128)(2,1)S(1)} collective-permute-done((bf16[96,2048]{1,0:T(8,128)(2,1)}, bf16[96,2048]{1,0:T(8,128)(2,1)S(1)}, u32[]{:S(2)}, u32[]{:S(2)}) %collective-permute-start.3) | collective-permute-done | bytes 393248 | tf_op jit(solution)/shard_map/ppermute | solution.py:357
  30.0 2.7 %collective-permute-start.9 = (bf16[144,2048]{1,0:T(8,128)(2,1)S(1)}, bf16[144,2048]{1,0:T(8,128)(2,1)S(1)}, u32[]{:S(2)}, u32[]{:S(2)}) collective-permute-start(bf16[144,2048]{1,0:T(8,128)(2,1)S(1)} %get-tuple-element.115), channel_id=1, source_target_pairs={{8,0},{10,2},{12,4},{14,6},{16,8},{18,10},{20,12},{22,14},{24,16},... | collective-permute-start | bytes 1769480 | tf_op jit(solution)/shard_map/ppermute | solution.py:357
  32.9 2.3 %fusion.12.refs_1_ = f32[576,384]{1,0:T(8,128)} fusion(bf16[576,2048]{1,0:T(8,128)(2,1)S(1)} %constant_dynamic-update-slice_fusion, bf16[384,2048]{1,0:T(8,128)(2,1)S(1)} %copy-done.18), kind=kOutput, calls=%fused_computation.38 | convolution fusion | flops 905969664 | bytes 4816896 | tf_op jit(solution)/shard_map/td,rd->tr/dot_general | solution.py:467
  35.2 11.7 %collective-permute-done.8.refs_2_ = bf16[144,2048]{1,0:T(8,128)(2,1)S(1)} collective-permute-done((bf16[144,2048]{1,0:T(8,128)(2,1)S(1)}, bf16[144,2048]{1,0:T(8,128)(2,1)S(1)}, u32[]{:S(2)}, u32[]{:S(2)}) %collective-permute-start.8) | collective-permute-done | bytes 589856 | tf_op jit(solution)/shard_map/ppermute | solution.py:352
  46.9 10.1 %collective-permute-done.9.refs_3_ = bf16[144,2048]{1,0:T(8,128)(2,1)S(1)} collective-permute-done((bf16[144,2048]{1,0:T(8,128)(2,1)S(1)}, bf16[144,2048]{1,0:T(8,128)(2,1)S(1)}, u32[]{:S(2)}, u32[]{:S(2)}) %collective-permute-start.9) | collective-permute-done | bytes 589856 | tf_op jit(solution)/shard_map/ppermute | solution.py:357
  58.3 1.5 collective-permute-start.10
  59.8 1.5 collective-permute-start.11
  61.6 3.5 %collective-permute-start.13 = (bf16[80,2048]{1,0:T(8,128)(2,1)}, bf16[80,2048]{1,0:T(8,128)(2,1)S(1)}, u32[]{:S(2)}, u32[]{:S(2)}) collective-permute-start(bf16[80,2048]{1,0:T(8,128)(2,1)} %get-tuple-element.123), channel_id=1, source_target_pairs={{8,0},{10,2},{12,4},{14,6},{16,8},{18,10},{20,12},{22,14},{24,16},... | collective-permute-start | bytes 983048 | tf_op jit(solution)/shard_map/ppermute | solution.py:357
  65.4 3.0 %fusion.13.refs_2_ = f32[800,384]{1,0:T(8,128)} fusion(bf16[800,2048]{1,0:T(8,128)(2,1)S(1)} %constant_dynamic-update-slice_fusion.5, bf16[384,2048]{1,0:T(8,128)(2,1)S(1)} %copy-done.18), kind=kOutput, calls=%fused_computation.39 | convolution fusion | flops 1258291200 | bytes 6078464 | tf_op jit(solution)/shard_map/td,rd->tr/dot_general | solution.py:467
  68.3 2.8 %convolution_convert_fusion.4 = bf16[576,384]{1,0:T(8,128)(2,1)S(1)} fusion(bf16[576,2048]{1,0:T(8,128)(2,1)S(1)} %constant_dynamic-update-slice_fusion, bf16[384,2048]{1,0:T(8,128)(2,1)} %collective-permute-done.4), kind=kOutput, calls=%fused_computation.7 | convolution fusion | flops 906190848 | bytes 4374528 | tf_op jit(solution)/shard_map/td,rd->tr/dot_general | solution.py:467
  71.2 4.2 %convolution_convert_fusion.3 = bf16[800,384]{1,0:T(8,128)(2,1)} fusion(bf16[800,2048]{1,0:T(8,128)(2,1)S(1)} %constant_dynamic-update-slice_fusion.5, bf16[384,2048]{1,0:T(8,128)(2,1)} %collective-permute-done.4), kind=kOutput, calls=%fused_computation.6 | convolution fusion | flops 1258598400 | bytes 5464064 | tf_op jit(solution)/shard_map/td,rd->tr/dot_general | solution.py:467
  77.6 3.6 %all-to-all-start = ((bf16[128,16,128]{2,0,1:T(8,128)(2,1)}), bf16[128,16,128]{2,0,1:T(8,128)(2,1)S(1)}, u32[]{:S(2)}, u32[]{:S(2)}) async-start(bf16[128,16,128]{2,0,1:T(8,128)(2,1)} %copy.8), calls=%async_computation | async-start | bytes 1048576 | tf_op jit(solution)/shard_map/all_to_all | solution.py:474
  81.4 1.9 collective-permute-start.14
  86.2 2.3 %collective-permute-start.17 = (bf16[16,2048]{1,0:T(8,128)(2,1)S(1)}, bf16[16,2048]{1,0:T(8,128)(2,1)S(1)}, u32[]{:S(2)}, u32[]{:S(2)}) collective-permute-start(bf16[16,2048]{1,0:T(8,128)(2,1)S(1)} %get-tuple-element.131), channel_id=1, source_target_pairs={{8,0},{10,2},{12,4},{14,6},{16,8},{18,10},{20,12},{22,14},{24,16},... | collective-permute-start | bytes 196616 | tf_op jit(solution)/shard_map/ppermute | solution.py:357
  90.0 2.7 %convolution_convert_fusion.5 = bf16[544,384]{1,0:T(8,128)(2,1)S(1)} fusion(bf16[544,2048]{1,0:T(8,128)(2,1)S(1)} %constant_dynamic-update-slice_fusion.9, bf16[384,2048]{1,0:T(8,128)(2,1)} %collective-permute-done.4), kind=kOutput, calls=%fused_computation.8 | convolution fusion | flops 855846912 | bytes 4218880 | tf_op jit(solution)/shard_map/td,rd->tr/dot_general | solution.py:467
  92.8 3.6 %collective-permute-done.16 = bf16[16,2048]{1,0:T(8,128)(2,1)S(1)} collective-permute-done((bf16[16,2048]{1,0:T(8,128)(2,1)S(1)}, bf16[16,2048]{1,0:T(8,128)(2,1)S(1)}, u32[]{:S(2)}, u32[]{:S(2)}) %collective-permute-start.16) | collective-permute-done | bytes 65568 | tf_op jit(solution)/shard_map/ppermute | solution.py:352
  96.5 2.1 %convolution_convert_fusion.6 = bf16[128,384]{1,0:T(8,128)(2,1)S(1)} fusion(bf16[128,2048]{1,0:T(8,128)(2,1)S(1)} %constant_dynamic-update-slice_fusion.13, bf16[384,2048]{1,0:T(8,128)(2,1)} %collective-permute-done.4), kind=kOutput, calls=%fused_computation.12 | convolution fusion | flops 201375744 | bytes 2195456 | tf_op jit(solution)/shard_map/td,rd->tr/dot_general | solution.py:467
  105.8 14.0 %modal_scan.1 = (bf16[2048,128]{1,0:T(8,128)(2,1)S(1)}, f32[16,128]{1,0:T(8,128)}, bf16[768,384]{1,0:T(8,128)(2,1)S(1)}, bf16[1280,384]{1,0:T(8,128)(2,1)S(1)}) custom-call(s32[1]{0:T(128)} %bitcast.me_ref, f32[16,128]{1,0:T(8,128)S(1)} %bitcast.48, f32[16,128]{1,0:T(8,128)S(1)} %bitcast.49, bf16[2048,128]{1,0:T(8,128)(2,1)S(1)} %bitcast.46, ...), custom_call_target="tpu_custom_call" | custom-call | tf_op jit(solution)/shard_map/modal_scan/pallas_call | solution.py:316
  120.6 1.6 constant_dynamic-update-slice_fusion.17
  122.3 2.8 %convolution_convert_fusion.1.refs_0_ = bf16[768,2048]{1,0:T(8,128)(2,1)S(1)} fusion(bf16[768,2048]{1,0:T(8,128)(2,1)S(1)} %constant_dynamic-update-slice_fusion.17, bf16[768,384]{1,0:T(8,128)(2,1)S(1)} %collective-permute-done.21, bf16[768,384]{1,0:T(8,128)(2,1)S(1)} %get-tuple-element.138), kind=kOutput, calls=%fused_computation.1 | convolution fusion | flops 2419851264 | bytes 7471104 | tf_op jit(solution)/shard_map/dot_general | solution.py:577
  125.1 1.5 collective-permute-start.22
  128.2 2.6 %collective-permute-start.24 = (bf16[128,256]{1,0:T(8,128)(2,1)S(1)}, bf16[128,256]{1,0:T(8,128)(2,1)S(1)}, u32[]{:S(2)}, u32[]{:S(2)}) collective-permute-start(bf16[128,256]{1,0:T(8,128)(2,1)S(1)} %get-tuple-element.141), channel_id=1, source_target_pairs={{0,8},{2,10},{4,12},{6,14},{8,16},{10,18},{12,20},{14,22},{16,24},... | collective-permute-start | bytes 196616 | tf_op jit(solution)/shard_map/ppermute | solution.py:352
  132.0 2.4 %collective-permute-done.24.refs_3_ = bf16[128,256]{1,0:T(8,128)(2,1)S(1)} collective-permute-done((bf16[128,256]{1,0:T(8,128)(2,1)S(1)}, bf16[128,256]{1,0:T(8,128)(2,1)S(1)}, u32[]{:S(2)}, u32[]{:S(2)}) %collective-permute-start.24) | collective-permute-done | bytes 65568 | tf_op jit(solution)/shard_map/ppermute | solution.py:352
  136.5 2.1 collective-permute-start.29
  138.6 1.7 collective-permute-start.30
  141.4 3.2 %convolution_convert_fusion.refs_1_ = bf16[896,2048]{1,0:T(8,128)(2,1)S(1)} fusion(bf16[768,2048]{1,0:T(8,128)(2,1)S(1)} %constant_dynamic-update-slice_fusion.17, bf16[896,384]{1,0:T(8,128)(2,1)S(1)} %slice.16, bf16[896,384]{1,0:T(8,128)(2,1)S(1)} %slice.12), kind=kOutput, calls=%fused_computation | convolution fusion | flops 2823159808 | bytes 8192000 | tf_op jit(solution)/shard_map/dot_general | solution.py:577
  144.7 4.3 %collective-permute-done.29.refs_4_ = bf16[128,1280]{1,0:T(8,128)(2,1)S(1)} collective-permute-done((bf16[128,1280]{1,0:T(8,128)(2,1)S(1)}, bf16[128,1280]{1,0:T(8,128)(2,1)S(1)}, u32[]{:S(2)}, u32[]{:S(2)}) %collective-permute-start.29) | collective-permute-done | bytes 327712 | tf_op jit(solution)/shard_map/ppermute | solution.py:352
  149.0 4.7 %collective-permute-done.30.refs_5_ = bf16[128,1280]{1,0:T(8,128)(2,1)S(1)} collective-permute-done((bf16[128,1280]{1,0:T(8,128)(2,1)S(1)}, bf16[128,1280]{1,0:T(8,128)(2,1)S(1)}, u32[]{:S(2)}, u32[]{:S(2)}) %collective-permute-start.30) | collective-permute-done | bytes 327712 | tf_op jit(solution)/shard_map/ppermute | solution.py:357
  154.3 1.8 assemble.13
  158.2 2.3 %collective-permute-start.33 = (bf16[128,2304]{1,0:T(8,128)(2,1)}, bf16[128,2304]{1,0:T(8,128)(2,1)}, u32[]{:S(2)}, u32[]{:S(2)}) collective-permute-start(bf16[128,2304]{1,0:T(8,128)(2,1)} %get-tuple-element.169), channel_id=1, source_target_pairs={{0,8},{2,10},{4,12},{6,14},{8,16},{10,18},{12,20},{14,22},{16,24},... | collective-permute-start | bytes 1769480 | tf_op jit(solution)/shard_map/ppermute | solution.py:352
  160.5 1.5 collective-permute-start.34
  162.0 4.5 %all-to-all-start.1 = ((bf16[16,128,128]{2,1,0:T(8,128)(2,1)}), bf16[16,128,128]{2,1,0:T(8,128)(2,1)}, u32[]{:S(2)}, u32[]{:S(2)}) async-start(bf16[16,128,128]{2,1,0:T(8,128)(2,1)} %bitcast.47), calls=%async_computation.1 | async-start | bytes 1048576 | tf_op jit(solution)/shard_map/all_to_all | solution.py:609
  167.5 3.5 %convolution_convert_fusion.2.refs_2_ = bf16[384,2048]{1,0:T(8,128)(2,1)S(1)} fusion(bf16[768,2048]{1,0:T(8,128)(2,1)} %copy-done.22, bf16[384,384]{1,0:T(8,128)(2,1)S(1)} %slice-done, bf16[384,384]{1,0:T(8,128)(2,1)S(1)} %slice.14), kind=kOutput, calls=%fused_computation.2 | convolution fusion | flops 1209925632 | bytes 5308416 | tf_op jit(solution)/shard_map/dot_general | solution.py:577
  171.0 5.6 %collective-permute-done.33.refs_5_ = bf16[128,2304]{1,0:T(8,128)(2,1)} collective-permute-done((bf16[128,2304]{1,0:T(8,128)(2,1)}, bf16[128,2304]{1,0:T(8,128)(2,1)}, u32[]{:S(2)}, u32[]{:S(2)}) %collective-permute-start.33) | collective-permute-done | bytes 589856 | tf_op jit(solution)/shard_map/ppermute | solution.py:352
  176.6 11.8 %collective-permute-done.34.refs_6_ = bf16[128,2304]{1,0:T(8,128)(2,1)} collective-permute-done((bf16[128,2304]{1,0:T(8,128)(2,1)}, bf16[128,2304]{1,0:T(8,128)(2,1)}, u32[]{:S(2)}, u32[]{:S(2)}) %collective-permute-start.34) | collective-permute-done | bytes 589856 | tf_op jit(solution)/shard_map/ppermute | solution.py:357
  188.4 3.1 %assemble.14 = (bf16[128,2048]{1,0:T(8,128)(2,1)}, bf16[128,2048]{1,0:T(8,128)(2,1)}, bf16[128,1536]{1,0:T(8,128)(2,1)}, bf16[128,1536]{1,0:T(8,128)(2,1)S(1)}, bf16[128,2048]{1,0:T(8,128)(2,1)S(1)}) custom-call(bf16[768,2048]{1,0:T(8,128)(2,1)S(1)} %convolution_convert_fusion.1.refs_0_, bf16[896,2048]{1,0:T(8,128)(2,1)S(1)} %copy-done.1, ...), custom_call_target="tpu_custom_call" | custom-call | flops 2359296 | bytes 9437184 | tf_op jit(solution)/shard_map/assemble/pallas_call | solution.py:427
  192.9 1.8 collective-permute-start.36
  194.7 3.8 %collective-permute-start.38 = (bf16[128,1536]{1,0:T(8,128)(2,1)S(1)}, bf16[128,1536]{1,0:T(8,128)(2,1)S(1)}, u32[]{:S(2)}, u32[]{:S(2)}) collective-permute-start(bf16[128,1536]{1,0:T(8,128)(2,1)S(1)} %get-tuple-element.179), channel_id=1, source_target_pairs={{8,0},{10,2},{12,4},{14,6},{16,8},{18,10},{20,12},{22,14},{24,16},... | collective-permute-start | bytes 1179656 | tf_op jit(solution)/shard_map/ppermute | solution.py:357
  198.6 2.0 copy.9
  200.6 7.4 %collective-permute-done.37.refs_3_ = bf16[128,1536]{1,0:T(8,128)(2,1)S(1)} collective-permute-done((bf16[128,1536]{1,0:T(8,128)(2,1)}, bf16[128,1536]{1,0:T(8,128)(2,1)S(1)}, u32[]{:S(2)}, u32[]{:S(2)}) %collective-permute-start.37) | collective-permute-done | bytes 393248 | tf_op jit(solution)/shard_map/ppermute | solution.py:352
  208.0 3.4 %collective-permute-done.38.refs_4_ = bf16[128,1536]{1,0:T(8,128)(2,1)S(1)} collective-permute-done((bf16[128,1536]{1,0:T(8,128)(2,1)S(1)}, bf16[128,1536]{1,0:T(8,128)(2,1)S(1)}, u32[]{:S(2)}, u32[]{:S(2)}) %collective-permute-start.38) | collective-permute-done | bytes 393248 | tf_op jit(solution)/shard_map/ppermute | solution.py:357
  (130 shorter events, 32.4 us)
Async XLA Ops:
  2.7 24.8 %copy-start.2 = (bf16[128,2048]{1,0:T(8,128)(2,1)S(1)}, bf16[128,2048]{1,0:T(8,128)(2,1)}, u32[]{:S(2)}) copy-start(bf16[128,2048]{1,0:T(8,128)(2,1)} %get-tuple-element.104.refs_0_) | copy-start | bytes 1572868
  2.7 24.8 %collective-permute-start = (bf16[128,2048]{1,0:T(8,128)(2,1)}, bf16[128,2048]{1,0:T(8,128)(2,1)S(1)}, u32[]{:S(2)}, u32[]{:S(2)}) collective-permute-start(bf16[128,2048]{1,0:T(8,128)(2,1)} %get-tuple-element.104.refs_0_), channel_id=1, source_target_pairs={{0,2},{2,0},{4,6},{6,4},{8,10},{10,8},{12,14},{14,12},{16,18},{18,... | collective-permute-start | bytes 1572872 | tf_op jit(solution)/shard_map/ppermute | solution.py:343
  5.7 21.8 %collective-permute-start.1 = (bf16[128,2048]{1,0:T(8,128)(2,1)}, bf16[128,2048]{1,0:T(8,128)(2,1)S(1)}, u32[]{:S(2)}, u32[]{:S(2)}) collective-permute-start(bf16[128,2048]{1,0:T(8,128)(2,1)} %get-tuple-element.104.refs_0_), channel_id=1, source_target_pairs={{0,4},{2,6},{4,0},{6,2},{8,12},{10,14},{12,8},{14,10},{16,20},{18,... | collective-permute-start | bytes 1572872 | tf_op jit(solution)/shard_map/ppermute | solution.py:347
  7.3 14.1 %collective-permute-start.2 = (bf16[96,2048]{1,0:T(8,128)(2,1)}, bf16[96,2048]{1,0:T(8,128)(2,1)S(1)}, u32[]{:S(2)}, u32[]{:S(2)}) collective-permute-start(bf16[96,2048]{1,0:T(8,128)(2,1)} %get-tuple-element.95), channel_id=1, source_target_pairs={{0,8},{2,10},{4,12},{6,14},{8,16},{10,18},{12,20},{14,22},{16,24},... | collective-permute-start | bytes 1179656 | tf_op jit(solution)/shard_map/ppermute | solution.py:352
  8.8 18.7 %collective-permute-start.3 = (bf16[96,2048]{1,0:T(8,128)(2,1)}, bf16[96,2048]{1,0:T(8,128)(2,1)S(1)}, u32[]{:S(2)}, u32[]{:S(2)}) collective-permute-start(bf16[96,2048]{1,0:T(8,128)(2,1)} %get-tuple-element.95), channel_id=1, source_target_pairs={{8,0},{10,2},{12,4},{14,6},{16,8},{18,10},{20,12},{22,14},{24,16},... | collective-permute-start | bytes 1179656 | tf_op jit(solution)/shard_map/ppermute | solution.py:357
  14.7 53.7 %collective-permute-start.4 = (bf16[384,2048]{1,0:T(8,128)(2,1)}, bf16[384,2048]{1,0:T(8,128)(2,1)}, u32[]{:S(2)}, u32[]{:S(2)}) collective-permute-start(bf16[384,2048]{1,0:T(8,128)(2,1)} %get-tuple-element.109), channel_id=1, source_target_pairs={{0,1},{1,0},{2,3},{3,2},{4,5},{5,4},{6,7},{7,6},{8,9},{9,8},{10,11... | collective-permute-start | bytes 4718600 | tf_op jit(solution)/shard_map/ppermute | solution.py:339
  27.7 29.3 %collective-permute-start.6 = (bf16[256,2048]{1,0:T(8,128)(2,1)S(1)}, bf16[256,2048]{1,0:T(8,128)(2,1)S(1)}, u32[]{:S(2)}, u32[]{:S(2)}) collective-permute-start(bf16[256,2048]{1,0:T(8,128)(2,1)S(1)} %get-tuple-element.112), channel_id=1, source_target_pairs={{0,2},{2,0},{4,6},{6,4},{8,10},{10,8},{12,14},{14,12},{16,18},{18,... | collective-permute-start | bytes 3145736 | tf_op jit(solution)/shard_map/ppermute | solution.py:343
  28.3 28.7 %collective-permute-start.7 = (bf16[256,2048]{1,0:T(8,128)(2,1)S(1)}, bf16[256,2048]{1,0:T(8,128)(2,1)S(1)}, u32[]{:S(2)}, u32[]{:S(2)}) collective-permute-start(bf16[256,2048]{1,0:T(8,128)(2,1)S(1)} %get-tuple-element.113), channel_id=1, source_target_pairs={{0,4},{2,6},{4,0},{6,2},{8,12},{10,14},{12,8},{14,10},{16,20},{18,... | collective-permute-start | bytes 3145736 | tf_op jit(solution)/shard_map/ppermute | solution.py:347
  28.9 18.1 %collective-permute-start.8 = (bf16[144,2048]{1,0:T(8,128)(2,1)S(1)}, bf16[144,2048]{1,0:T(8,128)(2,1)S(1)}, u32[]{:S(2)}, u32[]{:S(2)}) collective-permute-start(bf16[144,2048]{1,0:T(8,128)(2,1)S(1)} %get-tuple-element.114), channel_id=1, source_target_pairs={{0,8},{2,10},{4,12},{6,14},{8,16},{10,18},{12,20},{14,22},{16,24},... | collective-permute-start | bytes 1769480 | tf_op jit(solution)/shard_map/ppermute | solution.py:352
  30.0 27.1 %collective-permute-start.9 = (bf16[144,2048]{1,0:T(8,128)(2,1)S(1)}, bf16[144,2048]{1,0:T(8,128)(2,1)S(1)}, u32[]{:S(2)}, u32[]{:S(2)}) collective-permute-start(bf16[144,2048]{1,0:T(8,128)(2,1)S(1)} %get-tuple-element.115), channel_id=1, source_target_pairs={{8,0},{10,2},{12,4},{14,6},{16,8},{18,10},{20,12},{22,14},{24,16},... | collective-permute-start | bytes 1769480 | tf_op jit(solution)/shard_map/ppermute | solution.py:357
  58.3 23.0 %collective-permute-start.10 = (bf16[192,2048]{1,0:T(8,128)(2,1)}, bf16[192,2048]{1,0:T(8,128)(2,1)S(1)}, u32[]{:S(2)}, u32[]{:S(2)}) collective-permute-start(bf16[192,2048]{1,0:T(8,128)(2,1)} %get-tuple-element.120), channel_id=1, source_target_pairs={{0,2},{2,0},{4,6},{6,4},{8,10},{10,8},{12,14},{14,12},{16,18},{18,... | collective-permute-start | bytes 2359304 | tf_op jit(solution)/shard_map/ppermute | solution.py:343
  59.8 21.5 %collective-permute-start.11 = (bf16[192,2048]{1,0:T(8,128)(2,1)S(1)}, bf16[192,2048]{1,0:T(8,128)(2,1)S(1)}, u32[]{:S(2)}, u32[]{:S(2)}) collective-permute-start(bf16[192,2048]{1,0:T(8,128)(2,1)S(1)} %get-tuple-element.121), channel_id=1, source_target_pairs={{0,4},{2,6},{4,0},{6,2},{8,12},{10,14},{12,8},{14,10},{16,20},{18,... | collective-permute-start | bytes 2359304 | tf_op jit(solution)/shard_map/ppermute | solution.py:347
  61.3 19.9 %collective-permute-start.12 = (bf16[80,2048]{1,0:T(8,128)(2,1)}, bf16[80,2048]{1,0:T(8,128)(2,1)S(1)}, u32[]{:S(2)}, u32[]{:S(2)}) collective-permute-start(bf16[80,2048]{1,0:T(8,128)(2,1)} %get-tuple-element.122), channel_id=1, source_target_pairs={{0,8},{2,10},{4,12},{6,14},{8,16},{10,18},{12,20},{14,22},{16,24},... | collective-permute-start | bytes 983048 | tf_op jit(solution)/shard_map/ppermute | solution.py:352
  61.6 19.7 %collective-permute-start.13 = (bf16[80,2048]{1,0:T(8,128)(2,1)}, bf16[80,2048]{1,0:T(8,128)(2,1)S(1)}, u32[]{:S(2)}, u32[]{:S(2)}) collective-permute-start(bf16[80,2048]{1,0:T(8,128)(2,1)} %get-tuple-element.123), channel_id=1, source_target_pairs={{8,0},{10,2},{12,4},{14,6},{16,8},{18,10},{20,12},{22,14},{24,16},... | collective-permute-start | bytes 983048 | tf_op jit(solution)/shard_map/ppermute | solution.py:357
  71.2 4.3 %collective-permute-start.5 = (bf16[576,384]{1,0:T(8,128)(2,1)S(1)}, bf16[576,384]{1,0:T(8,128)(2,1)S(1)}, u32[]{:S(2)}, u32[]{:S(2)}) collective-permute-start(bf16[576,384]{1,0:T(8,128)(2,1)S(1)} %convolution_convert_fusion.4), channel_id=1, source_target_pairs={{0,1},{1,0},{2,3},{3,2},{4,5},{5,4},{6,7},{7,6},{8,9},{9,8},{10,11... | collective-permute-start | bytes 1327112 | tf_op jit(solution)/shard_map/ppermute | solution.py:339
  76.2 24.3 %collective-permute-start.18 = (bf16[800,384]{1,0:T(8,128)(2,1)}, bf16[800,384]{1,0:T(8,128)(2,1)}, u32[]{:S(2)}, u32[]{:S(2)}) collective-permute-start(bf16[800,384]{1,0:T(8,128)(2,1)} %convolution_convert_fusion.3), channel_id=1, source_target_pairs={{0,1},{1,0},{2,3},{3,2},{4,5},{5,4},{6,7},{7,6},{8,9},{9,8},{10,11... | collective-permute-start | bytes 1843208 | tf_op jit(solution)/shard_map/ppermute | solution.py:339
  77.6 24.2 %all-to-all-start = ((bf16[128,16,128]{2,0,1:T(8,128)(2,1)}), bf16[128,16,128]{2,0,1:T(8,128)(2,1)S(1)}, u32[]{:S(2)}, u32[]{:S(2)}) async-start(bf16[128,16,128]{2,0,1:T(8,128)(2,1)} %copy.8), calls=%async_computation | async-start | bytes 1048576 | tf_op jit(solution)/shard_map/all_to_all | solution.py:474
  81.4 14.9 %collective-permute-start.14 = (bf16[48,2048]{1,0:T(8,128)(2,1)S(1)}, bf16[48,2048]{1,0:T(8,128)(2,1)S(1)}, u32[]{:S(2)}, u32[]{:S(2)}) collective-permute-start(bf16[48,2048]{1,0:T(8,128)(2,1)S(1)} %get-tuple-element.128), channel_id=1, source_target_pairs={{0,2},{2,0},{4,6},{6,4},{8,10},{10,8},{12,14},{14,12},{16,18},{18,... | collective-permute-start | bytes 589832 | tf_op jit(solution)/shard_map/ppermute | solution.py:343
  83.3 13.1 %collective-permute-start.15 = (bf16[48,2048]{1,0:T(8,128)(2,1)S(1)}, bf16[48,2048]{1,0:T(8,128)(2,1)S(1)}, u32[]{:S(2)}, u32[]{:S(2)}) collective-permute-start(bf16[48,2048]{1,0:T(8,128)(2,1)S(1)} %get-tuple-element.129), channel_id=1, source_target_pairs={{0,4},{2,6},{4,0},{6,2},{8,12},{10,14},{12,8},{14,10},{16,20},{18,... | collective-permute-start | bytes 589832 | tf_op jit(solution)/shard_map/ppermute | solution.py:347
  84.7 11.6 %collective-permute-start.16 = (bf16[16,2048]{1,0:T(8,128)(2,1)S(1)}, bf16[16,2048]{1,0:T(8,128)(2,1)S(1)}, u32[]{:S(2)}, u32[]{:S(2)}) collective-permute-start(bf16[16,2048]{1,0:T(8,128)(2,1)S(1)} %get-tuple-element.130), channel_id=1, source_target_pairs={{0,8},{2,10},{4,12},{6,14},{8,16},{10,18},{12,20},{14,22},{16,24},... | collective-permute-start | bytes 196616 | tf_op jit(solution)/shard_map/ppermute | solution.py:352
  86.2 10.1 %collective-permute-start.17 = (bf16[16,2048]{1,0:T(8,128)(2,1)S(1)}, bf16[16,2048]{1,0:T(8,128)(2,1)S(1)}, u32[]{:S(2)}, u32[]{:S(2)}) collective-permute-start(bf16[16,2048]{1,0:T(8,128)(2,1)S(1)} %get-tuple-element.131), channel_id=1, source_target_pairs={{8,0},{10,2},{12,4},{14,6},{16,8},{18,10},{20,12},{22,14},{24,16},... | collective-permute-start | bytes 196616 | tf_op jit(solution)/shard_map/ppermute | solution.py:357
  96.3 4.8 %collective-permute-start.19 = (bf16[544,384]{1,0:T(8,128)(2,1)S(1)}, bf16[544,384]{1,0:T(8,128)(2,1)S(1)}, u32[]{:S(2)}, u32[]{:S(2)}) collective-permute-start(bf16[544,384]{1,0:T(8,128)(2,1)S(1)} %convolution_convert_fusion.5), channel_id=1, source_target_pairs={{0,1},{1,0},{2,3},{3,2},{4,5},{5,4},{6,7},{7,6},{8,9},{9,8},{10,11... | collective-permute-start | bytes 1253384 | tf_op jit(solution)/shard_map/ppermute | solution.py:339
  98.6 1.9 collective-permute-start.20
  105.8 14.1 %copy-start.20 = (bf16[384,2048]{1,0:T(8,128)(2,1)S(1)}, bf16[384,2048]{1,0:T(8,128)(2,1)}, u32[]{:S(2)}) copy-start(bf16[384,2048]{1,0:T(8,128)(2,1)} %get-tuple-element.111) | copy-start | bytes 4718596
  119.8 20.5 %copy-start.4 = (bf16[1280,384]{1,0:T(8,128)(2,1)}, bf16[1280,384]{1,0:T(8,128)(2,1)S(1)}, u32[]{:S(2)}) copy-start(bf16[1280,384]{1,0:T(8,128)(2,1)S(1)} %get-tuple-element.147) | copy-start | bytes 2949124
  119.8 2.4 %collective-permute-start.21 = (bf16[768,384]{1,0:T(8,128)(2,1)S(1)}, bf16[768,384]{1,0:T(8,128)(2,1)S(1)}, u32[]{:S(2)}, u32[]{:S(2)}) collective-permute-start(bf16[768,384]{1,0:T(8,128)(2,1)S(1)} %get-tuple-element.138), channel_id=1, source_target_pairs={{0,1},{1,0},{2,3},{3,2},{4,5},{5,4},{6,7},{7,6},{8,9},{9,8},{10,11... | collective-permute-start | bytes 1769480 | tf_op jit(solution)/shard_map/ppermute | solution.py:339
  120.1 20.3 %collective-permute-start.26 = (bf16[1280,384]{1,0:T(8,128)(2,1)S(1)}, bf16[1280,384]{1,0:T(8,128)(2,1)S(1)}, u32[]{:S(2)}, u32[]{:S(2)}) collective-permute-start(bf16[1280,384]{1,0:T(8,128)(2,1)S(1)} %get-tuple-element.147), channel_id=1, source_target_pairs={{0,1},{1,0},{2,3},{3,2},{4,5},{5,4},{6,7},{7,6},{8,9},{9,8},{10,11... | collective-permute-start | bytes 2949128 | tf_op jit(solution)/shard_map/ppermute | solution.py:339
  122.2 19.2 %copy-start.22 = (bf16[768,2048]{1,0:T(8,128)(2,1)}, bf16[768,2048]{1,0:T(8,128)(2,1)S(1)}, u32[]{:S(2)}) copy-start(bf16[768,2048]{1,0:T(8,128)(2,1)S(1)} %constant_dynamic-update-slice_fusion.17) | copy-start | bytes 9437188
  125.1 10.0 %collective-permute-start.22 = (bf16[128,768]{1,0:T(8,128)(2,1)S(1)}, bf16[128,768]{1,0:T(8,128)(2,1)S(1)}, u32[]{:S(2)}, u32[]{:S(2)}) collective-permute-start(bf16[128,768]{1,0:T(8,128)(2,1)S(1)} %get-tuple-element.139), channel_id=1, source_target_pairs={{0,2},{2,0},{4,6},{6,4},{8,10},{10,8},{12,14},{14,12},{16,18},{18,... | collective-permute-start | bytes 589832 | tf_op jit(solution)/shard_map/ppermute | solution.py:343
  126.7 8.4 %collective-permute-start.23 = (bf16[128,768]{1,0:T(8,128)(2,1)S(1)}, bf16[128,768]{1,0:T(8,128)(2,1)S(1)}, u32[]{:S(2)}, u32[]{:S(2)}) collective-permute-start(bf16[128,768]{1,0:T(8,128)(2,1)S(1)} %get-tuple-element.140), channel_id=1, source_target_pairs={{0,4},{2,6},{4,0},{6,2},{8,12},{10,14},{12,8},{14,10},{16,20},{18,... | collective-permute-start | bytes 589832 | tf_op jit(solution)/shard_map/ppermute | solution.py:347
  128.2 6.2 %collective-permute-start.24 = (bf16[128,256]{1,0:T(8,128)(2,1)S(1)}, bf16[128,256]{1,0:T(8,128)(2,1)S(1)}, u32[]{:S(2)}, u32[]{:S(2)}) collective-permute-start(bf16[128,256]{1,0:T(8,128)(2,1)S(1)} %get-tuple-element.141), channel_id=1, source_target_pairs={{0,8},{2,10},{4,12},{6,14},{8,16},{10,18},{12,20},{14,22},{16,24},... | collective-permute-start | bytes 196616 | tf_op jit(solution)/shard_map/ppermute | solution.py:352
  130.8 4.3 %collective-permute-start.25 = (bf16[128,256]{1,0:T(8,128)(2,1)S(1)}, bf16[128,256]{1,0:T(8,128)(2,1)S(1)}, u32[]{:S(2)}, u32[]{:S(2)}) collective-permute-start(bf16[128,256]{1,0:T(8,128)(2,1)S(1)} %get-tuple-element.142), channel_id=1, source_target_pairs={{8,0},{10,2},{12,4},{14,6},{16,8},{18,10},{20,12},{22,14},{24,16},... | collective-permute-start | bytes 196616 | tf_op jit(solution)/shard_map/ppermute | solution.py:357
  135.3 18.7 %collective-permute-start.27 = (bf16[128,3072]{1,0:T(8,128)(2,1)S(1)}, bf16[128,3072]{1,0:T(8,128)(2,1)S(1)}, u32[]{:S(2)}, u32[]{:S(2)}) collective-permute-start(bf16[128,3072]{1,0:T(8,128)(2,1)S(1)} %get-tuple-element.153), channel_id=1, source_target_pairs={{0,2},{2,0},{4,6},{6,4},{8,10},{10,8},{12,14},{14,12},{16,18},{18,... | collective-permute-start | bytes 2359304 | tf_op jit(solution)/shard_map/ppermute | solution.py:343
  135.9 18.4 %collective-permute-start.28 = (bf16[128,3072]{1,0:T(8,128)(2,1)S(1)}, bf16[128,3072]{1,0:T(8,128)(2,1)S(1)}, u32[]{:S(2)}, u32[]{:S(2)}) collective-permute-start(bf16[128,3072]{1,0:T(8,128)(2,1)S(1)} %get-tuple-element.154), channel_id=1, source_target_pairs={{0,4},{2,6},{4,0},{6,2},{8,12},{10,14},{12,8},{14,10},{16,20},{18,... | collective-permute-start | bytes 2359304 | tf_op jit(solution)/shard_map/ppermute | solution.py:347
  136.5 12.5 %collective-permute-start.29 = (bf16[128,1280]{1,0:T(8,128)(2,1)S(1)}, bf16[128,1280]{1,0:T(8,128)(2,1)S(1)}, u32[]{:S(2)}, u32[]{:S(2)}) collective-permute-start(bf16[128,1280]{1,0:T(8,128)(2,1)S(1)} %get-tuple-element.155), channel_id=1, source_target_pairs={{0,8},{2,10},{4,12},{6,14},{8,16},{10,18},{12,20},{14,22},{16,24},... | collective-permute-start | bytes 983048 | tf_op jit(solution)/shard_map/ppermute | solution.py:352
  138.6 15.1 %collective-permute-start.30 = (bf16[128,1280]{1,0:T(8,128)(2,1)S(1)}, bf16[128,1280]{1,0:T(8,128)(2,1)S(1)}, u32[]{:S(2)}, u32[]{:S(2)}) collective-permute-start(bf16[128,1280]{1,0:T(8,128)(2,1)S(1)} %get-tuple-element.156), channel_id=1, source_target_pairs={{8,0},{10,2},{12,4},{14,6},{16,8},{18,10},{20,12},{22,14},{24,16},... | collective-permute-start | bytes 983048 | tf_op jit(solution)/shard_map/ppermute | solution.py:357
  144.7 11.5 %copy-start = (bf16[896,2048]{1,0:T(8,128)(2,1)}, bf16[896,2048]{1,0:T(8,128)(2,1)S(1)}, u32[]{:S(2)}) copy-start(bf16[896,2048]{1,0:T(8,128)(2,1)S(1)} %convolution_convert_fusion.refs_1_) | copy-start | bytes 11010052
  154.3 13.2 %slice-start = ((bf16[1280,384]{1,0:T(8,128)(2,1)}), bf16[384,384]{1,0:T(8,128)(2,1)S(1)}, s32[]{:S(2)}) async-start(bf16[1280,384]{1,0:T(8,128)(2,1)} %copy-done.21), calls=%async_computation.2 | async-start | bytes 589824 | tf_op jit(solution)/shard_map/slice | solution.py:606
  156.2 32.2 %collective-permute-start.31 = (bf16[128,4096]{1,0:T(8,128)(2,1)}, bf16[128,4096]{1,0:T(8,128)(2,1)}, u32[]{:S(2)}, u32[]{:S(2)}) collective-permute-start(bf16[128,4096]{1,0:T(8,128)(2,1)} %get-tuple-element.167), channel_id=1, source_target_pairs={{0,2},{2,0},{4,6},{6,4},{8,10},{10,8},{12,14},{14,12},{16,18},{18,... | collective-permute-start | bytes 3145736 | tf_op jit(solution)/shard_map/ppermute | solution.py:343
  157.6 30.8 %collective-permute-start.32 = (bf16[128,4096]{1,0:T(8,128)(2,1)}, bf16[128,4096]{1,0:T(8,128)(2,1)}, u32[]{:S(2)}, u32[]{:S(2)}) collective-permute-start(bf16[128,4096]{1,0:T(8,128)(2,1)} %get-tuple-element.168), channel_id=1, source_target_pairs={{0,4},{2,6},{4,0},{6,2},{8,12},{10,14},{12,8},{14,10},{16,20},{18,... | collective-permute-start | bytes 3145736 | tf_op jit(solution)/shard_map/ppermute | solution.py:347
  158.2 18.4 %collective-permute-start.33 = (bf16[128,2304]{1,0:T(8,128)(2,1)}, bf16[128,2304]{1,0:T(8,128)(2,1)}, u32[]{:S(2)}, u32[]{:S(2)}) collective-permute-start(bf16[128,2304]{1,0:T(8,128)(2,1)} %get-tuple-element.169), channel_id=1, source_target_pairs={{0,8},{2,10},{4,12},{6,14},{8,16},{10,18},{12,20},{14,22},{16,24},... | collective-permute-start | bytes 1769480 | tf_op jit(solution)/shard_map/ppermute | solution.py:352
  160.5 27.9 %collective-permute-start.34 = (bf16[128,2304]{1,0:T(8,128)(2,1)}, bf16[128,2304]{1,0:T(8,128)(2,1)}, u32[]{:S(2)}, u32[]{:S(2)}) collective-permute-start(bf16[128,2304]{1,0:T(8,128)(2,1)} %get-tuple-element.170), channel_id=1, source_target_pairs={{8,0},{10,2},{12,4},{14,6},{16,8},{18,10},{20,12},{22,14},{24,16},... | collective-permute-start | bytes 1769480 | tf_op jit(solution)/shard_map/ppermute | solution.py:357
  162.0 36.5 %all-to-all-start.1 = ((bf16[16,128,128]{2,1,0:T(8,128)(2,1)}), bf16[16,128,128]{2,1,0:T(8,128)(2,1)}, u32[]{:S(2)}, u32[]{:S(2)}) async-start(bf16[16,128,128]{2,1,0:T(8,128)(2,1)} %bitcast.47), calls=%async_computation.1 | async-start | bytes 1048576 | tf_op jit(solution)/shard_map/all_to_all | solution.py:609
  167.5 20.9 %copy-start.1 = (bf16[896,2048]{1,0:T(8,128)(2,1)S(1)}, bf16[896,2048]{1,0:T(8,128)(2,1)}, u32[]{:S(2)}) copy-start(bf16[896,2048]{1,0:T(8,128)(2,1)} %copy-done) | copy-start | bytes 11010052
  192.3 19.1 %collective-permute-start.35 = (bf16[128,2048]{1,0:T(8,128)(2,1)}, bf16[128,2048]{1,0:T(8,128)(2,1)S(1)}, u32[]{:S(2)}, u32[]{:S(2)}) collective-permute-start(bf16[128,2048]{1,0:T(8,128)(2,1)} %get-tuple-element.176), channel_id=1, source_target_pairs={{0,2},{2,0},{4,6},{6,4},{8,10},{10,8},{12,14},{14,12},{16,18},{18,... | collective-permute-start | bytes 1572872 | tf_op jit(solution)/shard_map/ppermute | solution.py:343
  192.9 18.5 %collective-permute-start.36 = (bf16[128,2048]{1,0:T(8,128)(2,1)}, bf16[128,2048]{1,0:T(8,128)(2,1)S(1)}, u32[]{:S(2)}, u32[]{:S(2)}) collective-permute-start(bf16[128,2048]{1,0:T(8,128)(2,1)} %get-tuple-element.177), channel_id=1, source_target_pairs={{0,4},{2,6},{4,0},{6,2},{8,12},{10,14},{12,8},{14,10},{16,20},{18,... | collective-permute-start | bytes 1572872 | tf_op jit(solution)/shard_map/ppermute | solution.py:347
  194.7 13.3 %collective-permute-start.37 = (bf16[128,1536]{1,0:T(8,128)(2,1)}, bf16[128,1536]{1,0:T(8,128)(2,1)S(1)}, u32[]{:S(2)}, u32[]{:S(2)}) collective-permute-start(bf16[128,1536]{1,0:T(8,128)(2,1)} %get-tuple-element.178), channel_id=1, source_target_pairs={{0,8},{2,10},{4,12},{6,14},{8,16},{10,18},{12,20},{14,22},{16,24},... | collective-permute-start | bytes 1179656 | tf_op jit(solution)/shard_map/ppermute | solution.py:352
  194.7 16.6 %collective-permute-start.38 = (bf16[128,1536]{1,0:T(8,128)(2,1)S(1)}, bf16[128,1536]{1,0:T(8,128)(2,1)S(1)}, u32[]{:S(2)}, u32[]{:S(2)}) collective-permute-start(bf16[128,1536]{1,0:T(8,128)(2,1)S(1)} %get-tuple-element.179), channel_id=1, source_target_pairs={{8,0},{10,2},{12,4},{14,6},{16,8},{18,10},{20,12},{22,14},{24,16},... | collective-permute-start | bytes 1179656 | tf_op jit(solution)/shard_map/ppermute | solution.py:357
  (18 other events, 51.2 us)

commit v2 on v1

--- a/solution.py
+++ b/solution.py
@@ -1,5 +1,6 @@
 import functools
 import math
+import operator
 
 import jax
 import jax.numpy as jnp
@@ -154,6 +155,10 @@
     return value.astype(jnp.bfloat16).astype(jnp.float32)
 
 
+def added_up(parts):
+    return functools.reduce(operator.add, parts)
+
+
 def earlier_sum(finals, rate, span, back):
     count = finals.shape[0]
     row = lax.broadcasted_iota(jnp.int32, finals.shape, 0)
@@ -186,15 +191,8 @@
     arrays, refs = refs[: 2 * inputs + 1], refs[2 * inputs + 1 :]
     hyena_ref, grad_ref = refs[:2]
     proj_refs, refs = refs[2 : 2 + len(order)], refs[2 + len(order) :]
-    gated_s, slope_s, conv_s, back_s, feats_s, arrived = refs[:6]
-    held = refs[6:]
-    cot_ref, own, other = held[0], held[1 : 1 + inputs], held[1 + inputs :]
-    copies = [
-        pltpu.make_async_copy(array, here, arrived.at[k])
-        for k, (array, here) in enumerate(zip(arrays, held))
-    ]
-    for copy in copies:
-        copy.start()
+    gated_s, slope_s, conv_s, back_s, feats_s = refs
+    cot_ref, own, other = arrays[0], arrays[1 : 1 + inputs], arrays[1 + inputs :]
     length, width = cot_ref.shape
     chunks = PLANE * groups
     span = length // chunks
@@ -207,13 +205,7 @@
     def aligned(start, size):
         return pl.ds(pl.multiple_of(start, size), size)
 
-    copies[0].wait()
-    waited = set()
-    for source, offset, group, base, members, count, first in sorted(runs):
-        if source not in waited:
-            waited.add(source)
-            copies[1 + source].wait()
-            copies[1 + inputs + source].wait()
+    for source, offset, group, base, members, count, first in runs:
 
         def before(step, _, source=source, offset=offset, group=group, base=base, count=count, first=first):
             member = base + step
@@ -258,7 +250,7 @@
                 tuple(decays[n] * behind[n] + slope for n in range(count)),
             )
 
-        ahead, behind = lax.fori_loop(0, span, sums, ((zero,) * count, (zero,) * count), unroll=8)
+        ahead, behind = lax.fori_loop(0, span, sums, ((zero,) * count, (zero,) * count), unroll=16)
         ahead = tuple(earlier_sum(ahead[n], rates[n], span, False) for n in range(count))
         behind = tuple(earlier_sum(behind[n], rates[n], span, True) for n in range(count))
 
@@ -271,8 +263,8 @@
             ahead = tuple(decays[n] * ahead[n] + gated for n in range(count))
             behind = tuple(decays[n] * behind[n] + slope_back for n in range(count))
             grads = tuple(grads[n] + slope * ahead[n] for n in range(count))
-            conv = sum(gains[n] * ahead[n] for n in range(count))
-            back = sum(gains[n] * behind[n] for n in range(count))
+            conv = added_up(gains[n] * ahead[n] for n in range(count))
+            back = added_up(gains[n] * behind[n] for n in range(count))
             if first:
                 conv = conv + conv_s[at(step), :]
                 back = back + back_s[at(other), :]
@@ -280,7 +272,7 @@
             back_s[at(other), :] = back
             return ahead, behind, grads
 
-        _, _, grads = lax.fori_loop(0, span, outs, (ahead, behind, (zero,) * count), unroll=4)
+        _, _, grads = lax.fori_loop(0, span, outs, (ahead, behind, (zero,) * count), unroll=8)
         for n in range(count):
             total = jnp.sum(grads[n] * norms[n], axis=0, keepdims=True) * scale
             grad_ref[first + n : first + n + 1, :] = total
@@ -323,12 +315,10 @@
             jax.ShapeDtypeStruct((span * sum(piece[2] for piece in pieces), 3 * width), jnp.bfloat16)
             for pieces in order
         ),
-        in_specs=[pl.BlockSpec(memory_space=pltpu.SMEM), vmem, vmem]
-        + [pl.BlockSpec(memory_space=pl.ANY)] * len(arrays),
+        in_specs=[pl.BlockSpec(memory_space=pltpu.SMEM)] + [vmem] * (2 + len(arrays)),
         out_specs=(vmem,) * (2 + len(order)),
         scratch_shapes=[pltpu.VMEM((length, width), jnp.float32)] * 4
-        + [pltpu.VMEM((length, 3 * width), jnp.float32), pltpu.SemaphoreType.DMA((len(arrays),))]
-        + [pltpu.VMEM(array.shape, array.dtype) for array in arrays],
+        + [pltpu.VMEM((length, 3 * width), jnp.float32)],
         compiler_params=pltpu.CompilerParams(vmem_limit_bytes=40 * 2**20),
         name="modal_scan",
     )(me, residue_rows, rate_rows, *arrays)
@@ -414,7 +404,7 @@
                 for index, from_row, from_col in sources
             ]
             if len(parts) > 1:
-                parts = [narrowed(sum(widened(part) for part in parts))]
+                parts = [narrowed(added_up(widened(part) for part in parts))]
             out[row : row + height, col : col + width] = parts[0]
 
 
@@ -551,8 +541,8 @@
         (3, n + mh, 2, 3, 1, mh, n + mh),
     ]
     parts = [project(part, *matrices) for part in (first, second, third, fourth)]
-    later, first = lax.optimization_barrier((later, parts[0][1]))
-    parts[0] = (parts[0][0], first)
+    later, first = lax.optimization_barrier((later, parts[0][0]))
+    parts[0] = (first, parts[0][1])
     later = columns_held(later)
     return parts, tuple(runs), matrices, later
 
@@ -592,7 +582,7 @@
     first = all_ways(
         *put([early], [term(2, 3, 0)], [term(2, 3, 1)], [low(2, 3, 0)], [low(2, 3, 1)])
     )
-    later, first = lax.optimization_barrier((later, first))
+    later, hyena, first = lax.optimization_barrier((later, hyena, first))
     x, y, below, above = range(1, 5)
     second = all_ways(
         *put(
@@ -605,7 +595,7 @@
     )
     own = product(later[7 * span :], other[7 * span :])
     later = product(later[: 7 * span], other[: 7 * span])
-    later, hyena, second = lax.optimization_barrier((later, hyena, second))
+    later, second = lax.optimization_barrier((later, second))
     hyena_out = lax.all_to_all(hyena, "ctx", split_axis=0, concat_axis=1, tiled=True).T
     x, y, below, above = range(2, 6)
 

time: 214 us -> 206 us (0.963)
  waiting for transfers between devices: 79.2 us -> 74.4 us
    ppermute x8, waiting for transfers between devices: 41.6 us -> 30.4 us  [up(): lax.ppermute(value, 'ctx', [(i, (i + PLANE) % count) for i in range(count)])]
    ppermute x8, starting transfers between devices: 11.5 us -> 8.09 us  [up(): lax.ppermute(value, 'ctx', [(i, (i + PLANE) % count) for i in range(count)])]
    ppermute x8, starting transfers between devices: 19.1 us -> 22.5 us  [down(): lax.ppermute(value, 'ctx', [((i + PLANE) % count, i) for i in range(count)])]
    ppermute x8, waiting for transfers between devices: 0.39 us -> 3.1 us  [over_x(): lax.ppermute(value, 'ctx', [(i, i ^ 1) for i in range(lax.axis_size('ctx'...]
    unnamed x62, local copies, waits for them, and re-layouts: 9.53 us -> 6.93 us
    ppermute x8, waiting for transfers between devices: 36.9 us -> 39.4 us  [down(): lax.ppermute(value, 'ctx', [((i + PLANE) % count, i) for i in range(count)])]
  transfers between devices with their start and end apart: 41 -> 41, of which waited for: 15 -> 16; matrix products, arithmetic and copies ran while one was open for 17% -> 19% of each run, Pallas kernels for 4% -> 4%
where the time goes in v2:
time: 206 us; the launch traced here: 205 us
  waiting for transfers between devices  74.4 us (36%)
  starting transfers between devices  58.9 us (29%)
  matrix products  29.2 us (14%)
  Pallas kernels  27.5 us (13%)
  local copies, waits for them, and re-layouts  13.8 us (7%)
    ppermute x8, waiting for transfers between devices, down(): lax.ppermute(value, 'ctx', [((i + PLANE) % count, i) for i in range(count)])  39.4 us
    ppermute x8, waiting for transfers between devices, up(): lax.ppermute(value, 'ctx', [(i, (i + PLANE) % count) for i in range(count)])  30.4 us
    ppermute x8, starting transfers between devices, down(): lax.ppermute(value, 'ctx', [((i + PLANE) % count, i) for i in range(count)])  22.5 us
    dot_general x8, matrix products, project(): jnp.einsum('td,rd->tr', rows, matrix, preferred_element_type=jnp.float32)  19.5 us
    pallas_call x1, Pallas kernels, scan_all(): pl.pallas_call(functools.partial(scan_kernel, PLANE, runs, order), out_sh...  13.3 us
    ppermute x8, starting transfers between devices, over_x(): lax.ppermute(value, 'ctx', [(i, i ^ 1) for i in range(lax.axis_size('ctx'...  10.4 us
    dot_general x3, matrix products, product(): return narrowed(jnp.dot(both, matrix, preferred_element_type=jnp.float32))  9.67 us
    pallas_call x8, Pallas kernels, assemble(): pl.pallas_call(functools.partial(assemble_kernel, len(arrays), plans), ou...  8.5 us
  transfers between devices with their start and end apart: 41, of which 16 were waited for; matrix products, arithmetic and copies ran while one was open for 19% of the time, Pallas kernels for 4%

profile of v2, /device:TPU:0, one launch (start us, length us, event | category | flops | bytes accessed | tf_op | source)
XLA Modules:
  0.0 204.9 jit_solution(6182584096886287879)
XLA Ops:
  0.6 2.1 %halves.2 = (bf16[128,2048]{1,0:T(8,128)(2,1)}, bf16[96,2048]{1,0:T(8,128)(2,1)}) custom-call(s32[1]{0:T(128)} %bitcast.5.core_ref, bf16[128,4096]{1,0:T(8,128)(2,1)} %refs_0_.1), custom_call_target="tpu_custom_call" | custom-call | bytes 1835008 | tf_op jit(solution)/shard_map/halves/pallas_call | solution.py:385
  2.7 3.0 %collective-permute-start = (bf16[128,2048]{1,0:T(8,128)(2,1)}, bf16[128,2048]{1,0:T(8,128)(2,1)S(1)}, u32[]{:S(2)}, u32[]{:S(2)}) collective-permute-start(bf16[128,2048]{1,0:T(8,128)(2,1)} %get-tuple-element.104.refs_0_), channel_id=1, source_target_pairs={{0,2},{2,0},{4,6},{6,4},{8,10},{10,8},{12,14},{14,12},{16,18},{18,... | collective-permute-start | bytes 1572872 | tf_op jit(solution)/shard_map/ppermute | solution.py:333
  5.7 1.5 collective-permute-start.1
  7.3 1.6 collective-permute-start.2
  8.8 2.2 %collective-permute-start.3 = (bf16[96,2048]{1,0:T(8,128)(2,1)}, bf16[96,2048]{1,0:T(8,128)(2,1)S(1)}, u32[]{:S(2)}, u32[]{:S(2)}) collective-permute-start(bf16[96,2048]{1,0:T(8,128)(2,1)} %get-tuple-element.95), channel_id=1, source_target_pairs={{8,0},{10,2},{12,4},{14,6},{16,8},{18,10},{20,12},{22,14},{24,16},... | collective-permute-start | bytes 1179656 | tf_op jit(solution)/shard_map/ppermute | solution.py:347
  11.1 3.5 %halves.3 = (bf16[384,2048]{1,0:T(8,128)(2,1)}, bf16[384,2048]{1,0:T(8,128)(2,1)}) custom-call(s32[1]{0:T(128)} %bitcast.5.core_ref, bf16[384,4096]{1,0:T(8,128)(2,1)} %bitcast.49), custom_call_target="tpu_custom_call" | custom-call | bytes 6291456 | tf_op jit(solution)/shard_map/halves/pallas_call | solution.py:385
  14.7 6.7 %collective-permute-done.2.refs_3_ = bf16[96,2048]{1,0:T(8,128)(2,1)S(1)} collective-permute-done((bf16[96,2048]{1,0:T(8,128)(2,1)}, bf16[96,2048]{1,0:T(8,128)(2,1)S(1)}, u32[]{:S(2)}, u32[]{:S(2)}) %collective-permute-start.2) | collective-permute-done | bytes 393248 | tf_op jit(solution)/shard_map/ppermute | solution.py:342
  21.4 6.1 %collective-permute-done.3.refs_4_ = bf16[96,2048]{1,0:T(8,128)(2,1)S(1)} collective-permute-done((bf16[96,2048]{1,0:T(8,128)(2,1)}, bf16[96,2048]{1,0:T(8,128)(2,1)S(1)}, u32[]{:S(2)}, u32[]{:S(2)}) %collective-permute-start.3) | collective-permute-done | bytes 393248 | tf_op jit(solution)/shard_map/ppermute | solution.py:347
  27.5 2.1 %assemble.8 = (bf16[256,2048]{1,0:T(8,128)(2,1)}, bf16[256,2048]{1,0:T(8,128)(2,1)}, bf16[144,2048]{1,0:T(8,128)(2,1)}, bf16[144,2048]{1,0:T(8,128)(2,1)}) custom-call(bf16[128,2048]{1,0:T(8,128)(2,1)S(1)} %copy-done.2, bf16[128,2048]{1,0:T(8,128)(2,1)S(1)} %collective-permute-done.refs_1_, bf16[128,2048]{1,0:T(8,128)(2,1)S(1)} %collective-permute-done.1.refs_2_, ...), custom_call_target="tpu_custom_call" | custom-call | flops 3276800 | bytes 13107200 | tf_op jit(solution)/shard_map/assemble/pallas_call | solution.py:417
  31.9 2.7 %collective-permute-start.7 = (bf16[144,2048]{1,0:T(8,128)(2,1)}, bf16[144,2048]{1,0:T(8,128)(2,1)S(1)}, u32[]{:S(2)}, u32[]{:S(2)}) collective-permute-start(bf16[144,2048]{1,0:T(8,128)(2,1)} %get-tuple-element.115), channel_id=1, source_target_pairs={{8,0},{10,2},{12,4},{14,6},{16,8},{18,10},{20,12},{22,14},{24,16},... | collective-permute-start | bytes 1769480 | tf_op jit(solution)/shard_map/ppermute | solution.py:347
  36.9 2.3 %fusion.12.refs_1_ = f32[576,384]{1,0:T(8,128)} fusion(bf16[576,2048]{1,0:T(8,128)(2,1)S(1)} %constant_dynamic-update-slice_fusion, bf16[384,2048]{1,0:T(8,128)(2,1)S(1)} %copy-done.17), kind=kOutput, calls=%fused_computation.38 | convolution fusion | flops 905969664 | bytes 4816896 | tf_op jit(solution)/shard_map/td,rd->tr/dot_general | solution.py:457
  39.3 2.0 copy.8
  41.3 4.3 %all-to-all-start = ((bf16[128,16,128]{2,0,1:T(8,128)(2,1)}), bf16[128,16,128]{2,0,1:T(8,128)(2,1)}, u32[]{:S(2)}, u32[]{:S(2)}) async-start(bf16[128,16,128]{2,0,1:T(8,128)(2,1)} %copy.8), calls=%async_computation | async-start | bytes 1048576 | tf_op jit(solution)/shard_map/all_to_all | solution.py:464
  45.6 3.5 %collective-permute-done.6.refs_2_ = bf16[144,2048]{1,0:T(8,128)(2,1)S(1)} collective-permute-done((bf16[144,2048]{1,0:T(8,128)(2,1)}, bf16[144,2048]{1,0:T(8,128)(2,1)S(1)}, u32[]{:S(2)}, u32[]{:S(2)}) %collective-permute-start.6) | collective-permute-done | bytes 589856 | tf_op jit(solution)/shard_map/ppermute | solution.py:342
  49.0 12.1 %collective-permute-done.7.refs_3_ = bf16[144,2048]{1,0:T(8,128)(2,1)S(1)} collective-permute-done((bf16[144,2048]{1,0:T(8,128)(2,1)}, bf16[144,2048]{1,0:T(8,128)(2,1)S(1)}, u32[]{:S(2)}, u32[]{:S(2)}) %collective-permute-start.7) | collective-permute-done | bytes 589856 | tf_op jit(solution)/shard_map/ppermute | solution.py:347
  61.3 1.6 collective-permute-start.8
  64.5 3.4 %collective-permute-start.11 = (bf16[80,2048]{1,0:T(8,128)(2,1)S(1)}, bf16[80,2048]{1,0:T(8,128)(2,1)S(1)}, u32[]{:S(2)}, u32[]{:S(2)}) collective-permute-start(bf16[80,2048]{1,0:T(8,128)(2,1)S(1)} %get-tuple-element.123), channel_id=1, source_target_pairs={{8,0},{10,2},{12,4},{14,6},{16,8},{18,10},{20,12},{22,14},{24,16},... | collective-permute-start | bytes 983048 | tf_op jit(solution)/shard_map/ppermute | solution.py:347
  69.3 1.9 fusion.13.refs_2_
  71.2 4.3 %convolution_convert_fusion.3 = bf16[800,384]{1,0:T(8,128)(2,1)} fusion(bf16[800,2048]{1,0:T(8,128)(2,1)S(1)} %constant_dynamic-update-slice_fusion.5, bf16[384,2048]{1,0:T(8,128)(2,1)} %collective-permute-done.16), kind=kOutput, calls=%fused_computation.6 | convolution fusion | flops 1258598400 | bytes 5464064 | tf_op jit(solution)/shard_map/td,rd->tr/dot_general | solution.py:457
  75.5 3.6 %convolution_convert_fusion.4 = bf16[576,384]{1,0:T(8,128)(2,1)} fusion(bf16[576,2048]{1,0:T(8,128)(2,1)S(1)} %copy-done.23, bf16[384,2048]{1,0:T(8,128)(2,1)} %collective-permute-done.16), kind=kOutput, calls=%fused_computation.7 | convolution fusion | flops 906190848 | bytes 4374528 | tf_op jit(solution)/shard_map/td,rd->tr/dot_general | solution.py:457
  79.0 2.6 %collective-permute-done.11.refs_3_ = bf16[80,2048]{1,0:T(8,128)(2,1)S(1)} collective-permute-done((bf16[80,2048]{1,0:T(8,128)(2,1)S(1)}, bf16[80,2048]{1,0:T(8,128)(2,1)S(1)}, u32[]{:S(2)}, u32[]{:S(2)}) %collective-permute-start.11) | collective-permute-done | bytes 327712 | tf_op jit(solution)/shard_map/ppermute | solution.py:347
  81.6 1.8 collective-permute-done.8.refs_0_
  85.7 2.3 %collective-permute-start.14 = (bf16[16,2048]{1,0:T(8,128)(2,1)S(1)}, bf16[16,2048]{1,0:T(8,128)(2,1)S(1)}, u32[]{:S(2)}, u32[]{:S(2)}) collective-permute-start(bf16[16,2048]{1,0:T(8,128)(2,1)S(1)} %get-tuple-element.130), channel_id=1, source_target_pairs={{0,8},{2,10},{4,12},{6,14},{8,16},{10,18},{12,20},{14,22},{16,24},... | collective-permute-start | bytes 196616 | tf_op jit(solution)/shard_map/ppermute | solution.py:342
  87.9 1.6 collective-permute-start.15
  89.6 1.3 fusion.14.refs_3_
  91.0 3.5 %convolution_convert_fusion.5 = bf16[544,384]{1,0:T(8,128)(2,1)} fusion(bf16[544,2048]{1,0:T(8,128)(2,1)S(1)} %constant_dynamic-update-slice_fusion.9, bf16[384,2048]{1,0:T(8,128)(2,1)} %collective-permute-done.16), kind=kOutput, calls=%fused_computation.8 | convolution fusion | flops 855846912 | bytes 4218880 | tf_op jit(solution)/shard_map/td,rd->tr/dot_general | solution.py:457
  95.1 2.1 %convolution_convert_fusion.6 = bf16[128,384]{1,0:T(8,128)(2,1)S(1)} fusion(bf16[128,2048]{1,0:T(8,128)(2,1)S(1)} %constant_dynamic-update-slice_fusion.13, bf16[384,2048]{1,0:T(8,128)(2,1)} %collective-permute-done.16), kind=kOutput, calls=%fused_computation.12 | convolution fusion | flops 201375744 | bytes 2195456 | tf_op jit(solution)/shard_map/td,rd->tr/dot_general | solution.py:457
  98.6 13.3 %modal_scan.1 = (bf16[2048,128]{1,0:T(8,128)(2,1)S(1)}, f32[16,128]{1,0:T(8,128)}, bf16[768,384]{1,0:T(8,128)(2,1)S(1)}, bf16[1280,384]{1,0:T(8,128)(2,1)S(1)}) custom-call(s32[1]{0:T(128)} %bitcast.me_ref, f32[16,128]{1,0:T(8,128)S(1)} %bitcast.47, f32[16,128]{1,0:T(8,128)S(1)} %bitcast.48, bf16[2048,128]{1,0:T(8,128)(2,1)} %bitcast.12.refs_0_, ...), custom_call_target="tpu_custom_call" | custom-call | tf_op jit(solution)/shard_map/modal_scan/pallas_call | solution.py:308
  112.7 1.5 constant_dynamic-update-slice_fusion.17
  114.2 2.9 %convolution_convert_fusion.1.refs_0_ = bf16[768,2048]{1,0:T(8,128)(2,1)S(1)} fusion(bf16[768,2048]{1,0:T(8,128)(2,1)S(1)} %constant_dynamic-update-slice_fusion.17, bf16[768,384]{1,0:T(8,128)(2,1)S(1)} %collective-permute-done.21, bf16[768,384]{1,0:T(8,128)(2,1)S(1)} %get-tuple-element.139), kind=kOutput, calls=%fused_computation.1 | convolution fusion | flops 2419851264 | bytes 7471104 | tf_op jit(solution)/shard_map/dot_general | solution.py:567
  119.3 3.8 %collective-permute-start.25 = (bf16[128,256]{1,0:T(8,128)(2,1)S(1)}, bf16[128,256]{1,0:T(8,128)(2,1)S(1)}, u32[]{:S(2)}, u32[]{:S(2)}) collective-permute-start(bf16[128,256]{1,0:T(8,128)(2,1)S(1)} %get-tuple-element.143), channel_id=1, source_target_pairs={{8,0},{10,2},{12,4},{14,6},{16,8},{18,10},{20,12},{22,14},{24,16},... | collective-permute-start | bytes 196616 | tf_op jit(solution)/shard_map/ppermute | solution.py:347
  123.1 2.3 %collective-permute-done.24.refs_3_ = bf16[128,256]{1,0:T(8,128)(2,1)S(1)} collective-permute-done((bf16[128,256]{1,0:T(8,128)(2,1)S(1)}, bf16[128,256]{1,0:T(8,128)(2,1)S(1)}, u32[]{:S(2)}, u32[]{:S(2)}) %collective-permute-start.24) | collective-permute-done | bytes 65568 | tf_op jit(solution)/shard_map/ppermute | solution.py:342
  127.7 3.8 %collective-permute-start.30 = (bf16[128,1280]{1,0:T(8,128)(2,1)S(1)}, bf16[128,1280]{1,0:T(8,128)(2,1)S(1)}, u32[]{:S(2)}, u32[]{:S(2)}) collective-permute-start(bf16[128,1280]{1,0:T(8,128)(2,1)S(1)} %get-tuple-element.157), channel_id=1, source_target_pairs={{8,0},{10,2},{12,4},{14,6},{16,8},{18,10},{20,12},{22,14},{24,16},... | collective-permute-start | bytes 983048 | tf_op jit(solution)/shard_map/ppermute | solution.py:347
  132.6 3.3 %convolution_convert_fusion.refs_1_ = bf16[896,2048]{1,0:T(8,128)(2,1)S(1)} fusion(bf16[768,2048]{1,0:T(8,128)(2,1)S(1)} %constant_dynamic-update-slice_fusion.17, bf16[896,384]{1,0:T(8,128)(2,1)S(1)} %slice.16, bf16[896,384]{1,0:T(8,128)(2,1)S(1)} %slice.12), kind=kOutput, calls=%fused_computation | convolution fusion | flops 2823159808 | bytes 8192000 | tf_op jit(solution)/shard_map/dot_general | solution.py:567
  136.0 4.2 %collective-permute-done.29.refs_4_ = bf16[128,1280]{1,0:T(8,128)(2,1)S(1)} collective-permute-done((bf16[128,1280]{1,0:T(8,128)(2,1)S(1)}, bf16[128,1280]{1,0:T(8,128)(2,1)S(1)}, u32[]{:S(2)}, u32[]{:S(2)}) %collective-permute-start.29) | collective-permute-done | bytes 327712 | tf_op jit(solution)/shard_map/ppermute | solution.py:342
  140.2 2.3 %collective-permute-done.30.refs_5_ = bf16[128,1280]{1,0:T(8,128)(2,1)S(1)} collective-permute-done((bf16[128,1280]{1,0:T(8,128)(2,1)S(1)}, bf16[128,1280]{1,0:T(8,128)(2,1)S(1)}, u32[]{:S(2)}, u32[]{:S(2)}) %collective-permute-start.30) | collective-permute-done | bytes 327712 | tf_op jit(solution)/shard_map/ppermute | solution.py:347
  144.5 1.8 assemble.13
  148.5 3.6 %collective-permute-start.34 = (bf16[128,2304]{1,0:T(8,128)(2,1)}, bf16[128,2304]{1,0:T(8,128)(2,1)}, u32[]{:S(2)}, u32[]{:S(2)}) collective-permute-start(bf16[128,2304]{1,0:T(8,128)(2,1)} %get-tuple-element.170), channel_id=1, source_target_pairs={{8,0},{10,2},{12,4},{14,6},{16,8},{18,10},{20,12},{22,14},{24,16},... | collective-permute-start | bytes 1769480 | tf_op jit(solution)/shard_map/ppermute | solution.py:347
  152.1 4.5 %all-to-all-start.1 = ((bf16[16,128,128]{2,1,0:T(8,128)(2,1)}), bf16[16,128,128]{2,1,0:T(8,128)(2,1)}, u32[]{:S(2)}, u32[]{:S(2)}) async-start(bf16[16,128,128]{2,1,0:T(8,128)(2,1)} %bitcast.46), calls=%async_computation.1 | async-start | bytes 1048576 | tf_op jit(solution)/shard_map/all_to_all | solution.py:599
  157.6 3.5 %convolution_convert_fusion.2.refs_2_ = bf16[384,2048]{1,0:T(8,128)(2,1)S(1)} fusion(bf16[768,2048]{1,0:T(8,128)(2,1)} %copy-done.21, bf16[384,384]{1,0:T(8,128)(2,1)S(1)} %slice-done, bf16[384,384]{1,0:T(8,128)(2,1)S(1)} %slice.14), kind=kOutput, calls=%fused_computation.2 | convolution fusion | flops 1209925632 | bytes 5308416 | tf_op jit(solution)/shard_map/dot_general | solution.py:567
  161.1 5.6 %collective-permute-done.33.refs_5_ = bf16[128,2304]{1,0:T(8,128)(2,1)} collective-permute-done((bf16[128,2304]{1,0:T(8,128)(2,1)}, bf16[128,2304]{1,0:T(8,128)(2,1)}, u32[]{:S(2)}, u32[]{:S(2)}) %collective-permute-start.33) | collective-permute-done | bytes 589856 | tf_op jit(solution)/shard_map/ppermute | solution.py:342
  166.7 10.0 %collective-permute-done.34.refs_6_ = bf16[128,2304]{1,0:T(8,128)(2,1)} collective-permute-done((bf16[128,2304]{1,0:T(8,128)(2,1)}, bf16[128,2304]{1,0:T(8,128)(2,1)}, u32[]{:S(2)}, u32[]{:S(2)}) %collective-permute-start.34) | collective-permute-done | bytes 589856 | tf_op jit(solution)/shard_map/ppermute | solution.py:347
  176.7 3.1 %assemble.14 = (bf16[128,2048]{1,0:T(8,128)(2,1)}, bf16[128,2048]{1,0:T(8,128)(2,1)}, bf16[128,1536]{1,0:T(8,128)(2,1)}, bf16[128,1536]{1,0:T(8,128)(2,1)S(1)}, bf16[128,2048]{1,0:T(8,128)(2,1)S(1)}) custom-call(bf16[768,2048]{1,0:T(8,128)(2,1)S(1)} %convolution_convert_fusion.1.refs_0_, bf16[896,2048]{1,0:T(8,128)(2,1)S(1)} %copy-done.1, ...), custom_call_target="tpu_custom_call" | custom-call | flops 2359296 | bytes 9437184 | tf_op jit(solution)/shard_map/assemble/pallas_call | solution.py:417
  182.3 2.4 %collective-permute-start.37 = (bf16[128,1536]{1,0:T(8,128)(2,1)}, bf16[128,1536]{1,0:T(8,128)(2,1)S(1)}, u32[]{:S(2)}, u32[]{:S(2)}) collective-permute-start(bf16[128,1536]{1,0:T(8,128)(2,1)} %get-tuple-element.178), channel_id=1, source_target_pairs={{0,8},{2,10},{4,12},{6,14},{8,16},{10,18},{12,20},{14,22},{16,24},... | collective-permute-start | bytes 1179656 | tf_op jit(solution)/shard_map/ppermute | solution.py:342
  184.7 1.4 collective-permute-start.38
  186.1 2.0 copy.9
  188.2 8.2 %collective-permute-done.37.refs_3_ = bf16[128,1536]{1,0:T(8,128)(2,1)S(1)} collective-permute-done((bf16[128,1536]{1,0:T(8,128)(2,1)}, bf16[128,1536]{1,0:T(8,128)(2,1)S(1)}, u32[]{:S(2)}, u32[]{:S(2)}) %collective-permute-start.37) | collective-permute-done | bytes 393248 | tf_op jit(solution)/shard_map/ppermute | solution.py:342
  196.4 6.4 %collective-permute-done.38.refs_4_ = bf16[128,1536]{1,0:T(8,128)(2,1)S(1)} collective-permute-done((bf16[128,1536]{1,0:T(8,128)(2,1)S(1)}, bf16[128,1536]{1,0:T(8,128)(2,1)S(1)}, u32[]{:S(2)}, u32[]{:S(2)}) %collective-permute-start.38) | collective-permute-done | bytes 393248 | tf_op jit(solution)/shard_map/ppermute | solution.py:347
  (130 shorter events, 28.3 us)
Async XLA Ops:
  2.7 24.8 %copy-start.2 = (bf16[128,2048]{1,0:T(8,128)(2,1)S(1)}, bf16[128,2048]{1,0:T(8,128)(2,1)}, u32[]{:S(2)}) copy-start(bf16[128,2048]{1,0:T(8,128)(2,1)} %get-tuple-element.104.refs_0_) | copy-start | bytes 1572868
  2.7 24.8 %collective-permute-start = (bf16[128,2048]{1,0:T(8,128)(2,1)}, bf16[128,2048]{1,0:T(8,128)(2,1)S(1)}, u32[]{:S(2)}, u32[]{:S(2)}) collective-permute-start(bf16[128,2048]{1,0:T(8,128)(2,1)} %get-tuple-element.104.refs_0_), channel_id=1, source_target_pairs={{0,2},{2,0},{4,6},{6,4},{8,10},{10,8},{12,14},{14,12},{16,18},{18,... | collective-permute-start | bytes 1572872 | tf_op jit(solution)/shard_map/ppermute | solution.py:333
  5.7 21.8 %collective-permute-start.1 = (bf16[128,2048]{1,0:T(8,128)(2,1)}, bf16[128,2048]{1,0:T(8,128)(2,1)S(1)}, u32[]{:S(2)}, u32[]{:S(2)}) collective-permute-start(bf16[128,2048]{1,0:T(8,128)(2,1)} %get-tuple-element.104.refs_0_), channel_id=1, source_target_pairs={{0,4},{2,6},{4,0},{6,2},{8,12},{10,14},{12,8},{14,10},{16,20},{18,... | collective-permute-start | bytes 1572872 | tf_op jit(solution)/shard_map/ppermute | solution.py:337
  7.3 14.1 %collective-permute-start.2 = (bf16[96,2048]{1,0:T(8,128)(2,1)}, bf16[96,2048]{1,0:T(8,128)(2,1)S(1)}, u32[]{:S(2)}, u32[]{:S(2)}) collective-permute-start(bf16[96,2048]{1,0:T(8,128)(2,1)} %get-tuple-element.95), channel_id=1, source_target_pairs={{0,8},{2,10},{4,12},{6,14},{8,16},{10,18},{12,20},{14,22},{16,24},... | collective-permute-start | bytes 1179656 | tf_op jit(solution)/shard_map/ppermute | solution.py:342
  8.8 18.7 %collective-permute-start.3 = (bf16[96,2048]{1,0:T(8,128)(2,1)}, bf16[96,2048]{1,0:T(8,128)(2,1)S(1)}, u32[]{:S(2)}, u32[]{:S(2)}) collective-permute-start(bf16[96,2048]{1,0:T(8,128)(2,1)} %get-tuple-element.95), channel_id=1, source_target_pairs={{8,0},{10,2},{12,4},{14,6},{16,8},{18,10},{20,12},{22,14},{24,16},... | collective-permute-start | bytes 1179656 | tf_op jit(solution)/shard_map/ppermute | solution.py:347
  14.6 56.5 %collective-permute-start.16 = (bf16[384,2048]{1,0:T(8,128)(2,1)}, bf16[384,2048]{1,0:T(8,128)(2,1)}, u32[]{:S(2)}, u32[]{:S(2)}) collective-permute-start(bf16[384,2048]{1,0:T(8,128)(2,1)} %get-tuple-element.136), channel_id=1, source_target_pairs={{0,1},{1,0},{2,3},{3,2},{4,5},{5,4},{6,7},{7,6},{8,9},{9,8},{10,11... | collective-permute-start | bytes 4718600 | tf_op jit(solution)/shard_map/ppermute | solution.py:329
  29.7 31.4 %collective-permute-start.4 = (bf16[256,2048]{1,0:T(8,128)(2,1)}, bf16[256,2048]{1,0:T(8,128)(2,1)S(1)}, u32[]{:S(2)}, u32[]{:S(2)}) collective-permute-start(bf16[256,2048]{1,0:T(8,128)(2,1)} %get-tuple-element.112), channel_id=1, source_target_pairs={{0,2},{2,0},{4,6},{6,4},{8,10},{10,8},{12,14},{14,12},{16,18},{18,... | collective-permute-start | bytes 3145736 | tf_op jit(solution)/shard_map/ppermute | solution.py:333
  30.3 30.8 %collective-permute-start.5 = (bf16[256,2048]{1,0:T(8,128)(2,1)}, bf16[256,2048]{1,0:T(8,128)(2,1)S(1)}, u32[]{:S(2)}, u32[]{:S(2)}) collective-permute-start(bf16[256,2048]{1,0:T(8,128)(2,1)} %get-tuple-element.113), channel_id=1, source_target_pairs={{0,4},{2,6},{4,0},{6,2},{8,12},{10,14},{12,8},{14,10},{16,20},{18,... | collective-permute-start | bytes 3145736 | tf_op jit(solution)/shard_map/ppermute | solution.py:337
  30.8 18.3 %collective-permute-start.6 = (bf16[144,2048]{1,0:T(8,128)(2,1)}, bf16[144,2048]{1,0:T(8,128)(2,1)S(1)}, u32[]{:S(2)}, u32[]{:S(2)}) collective-permute-start(bf16[144,2048]{1,0:T(8,128)(2,1)} %get-tuple-element.114), channel_id=1, source_target_pairs={{0,8},{2,10},{4,12},{6,14},{8,16},{10,18},{12,20},{14,22},{16,24},... | collective-permute-start | bytes 1769480 | tf_op jit(solution)/shard_map/ppermute | solution.py:342
  31.9 29.2 %collective-permute-start.7 = (bf16[144,2048]{1,0:T(8,128)(2,1)}, bf16[144,2048]{1,0:T(8,128)(2,1)S(1)}, u32[]{:S(2)}, u32[]{:S(2)}) collective-permute-start(bf16[144,2048]{1,0:T(8,128)(2,1)} %get-tuple-element.115), channel_id=1, source_target_pairs={{8,0},{10,2},{12,4},{14,6},{16,8},{18,10},{20,12},{22,14},{24,16},... | collective-permute-start | bytes 1769480 | tf_op jit(solution)/shard_map/ppermute | solution.py:347
  41.3 56.6 %all-to-all-start = ((bf16[128,16,128]{2,0,1:T(8,128)(2,1)}), bf16[128,16,128]{2,0,1:T(8,128)(2,1)}, u32[]{:S(2)}, u32[]{:S(2)}) async-start(bf16[128,16,128]{2,0,1:T(8,128)(2,1)} %copy.8), calls=%async_computation | async-start | bytes 1048576 | tf_op jit(solution)/shard_map/all_to_all | solution.py:464
  61.3 22.2 %collective-permute-start.8 = (bf16[192,2048]{1,0:T(8,128)(2,1)S(1)}, bf16[192,2048]{1,0:T(8,128)(2,1)S(1)}, u32[]{:S(2)}, u32[]{:S(2)}) collective-permute-start(bf16[192,2048]{1,0:T(8,128)(2,1)S(1)} %get-tuple-element.120), channel_id=1, source_target_pairs={{0,2},{2,0},{4,6},{6,4},{8,10},{10,8},{12,14},{14,12},{16,18},{18,... | collective-permute-start | bytes 2359304 | tf_op jit(solution)/shard_map/ppermute | solution.py:333
  62.8 20.7 %collective-permute-start.9 = (bf16[192,2048]{1,0:T(8,128)(2,1)S(1)}, bf16[192,2048]{1,0:T(8,128)(2,1)S(1)}, u32[]{:S(2)}, u32[]{:S(2)}) collective-permute-start(bf16[192,2048]{1,0:T(8,128)(2,1)S(1)} %get-tuple-element.121), channel_id=1, source_target_pairs={{0,4},{2,6},{4,0},{6,2},{8,12},{10,14},{12,8},{14,10},{16,20},{18,... | collective-permute-start | bytes 2359304 | tf_op jit(solution)/shard_map/ppermute | solution.py:337
  64.0 15.1 %collective-permute-start.10 = (bf16[80,2048]{1,0:T(8,128)(2,1)S(1)}, bf16[80,2048]{1,0:T(8,128)(2,1)S(1)}, u32[]{:S(2)}, u32[]{:S(2)}) collective-permute-start(bf16[80,2048]{1,0:T(8,128)(2,1)S(1)} %get-tuple-element.122), channel_id=1, source_target_pairs={{0,8},{2,10},{4,12},{6,14},{8,16},{10,18},{12,20},{14,22},{16,24},... | collective-permute-start | bytes 983048 | tf_op jit(solution)/shard_map/ppermute | solution.py:342
  64.5 17.2 %collective-permute-start.11 = (bf16[80,2048]{1,0:T(8,128)(2,1)S(1)}, bf16[80,2048]{1,0:T(8,128)(2,1)S(1)}, u32[]{:S(2)}, u32[]{:S(2)}) collective-permute-start(bf16[80,2048]{1,0:T(8,128)(2,1)S(1)} %get-tuple-element.123), channel_id=1, source_target_pairs={{8,0},{10,2},{12,4},{14,6},{16,8},{18,10},{20,12},{22,14},{24,16},... | collective-permute-start | bytes 983048 | tf_op jit(solution)/shard_map/ppermute | solution.py:347
  75.5 22.5 %collective-permute-start.18 = (bf16[800,384]{1,0:T(8,128)(2,1)}, bf16[800,384]{1,0:T(8,128)(2,1)}, u32[]{:S(2)}, u32[]{:S(2)}) collective-permute-start(bf16[800,384]{1,0:T(8,128)(2,1)} %convolution_convert_fusion.3), channel_id=1, source_target_pairs={{0,1},{1,0},{2,3},{3,2},{4,5},{5,4},{6,7},{7,6},{8,9},{9,8},{10,11... | collective-permute-start | bytes 1843208 | tf_op jit(solution)/shard_map/ppermute | solution.py:329
  83.6 11.4 %collective-permute-start.12 = (bf16[48,2048]{1,0:T(8,128)(2,1)S(1)}, bf16[48,2048]{1,0:T(8,128)(2,1)S(1)}, u32[]{:S(2)}, u32[]{:S(2)}) collective-permute-start(bf16[48,2048]{1,0:T(8,128)(2,1)S(1)} %get-tuple-element.128), channel_id=1, source_target_pairs={{0,2},{2,0},{4,6},{6,4},{8,10},{10,8},{12,14},{14,12},{16,18},{18,... | collective-permute-start | bytes 589832 | tf_op jit(solution)/shard_map/ppermute | solution.py:333
  84.7 10.3 %collective-permute-start.13 = (bf16[48,2048]{1,0:T(8,128)(2,1)S(1)}, bf16[48,2048]{1,0:T(8,128)(2,1)S(1)}, u32[]{:S(2)}, u32[]{:S(2)}) collective-permute-start(bf16[48,2048]{1,0:T(8,128)(2,1)S(1)} %get-tuple-element.129), channel_id=1, source_target_pairs={{0,4},{2,6},{4,0},{6,2},{8,12},{10,14},{12,8},{14,10},{16,20},{18,... | collective-permute-start | bytes 589832 | tf_op jit(solution)/shard_map/ppermute | solution.py:337
  85.7 8.8 %collective-permute-start.14 = (bf16[16,2048]{1,0:T(8,128)(2,1)S(1)}, bf16[16,2048]{1,0:T(8,128)(2,1)S(1)}, u32[]{:S(2)}, u32[]{:S(2)}) collective-permute-start(bf16[16,2048]{1,0:T(8,128)(2,1)S(1)} %get-tuple-element.130), channel_id=1, source_target_pairs={{0,8},{2,10},{4,12},{6,14},{8,16},{10,18},{12,20},{14,22},{16,24},... | collective-permute-start | bytes 196616 | tf_op jit(solution)/shard_map/ppermute | solution.py:342
  87.9 6.6 %collective-permute-start.15 = (bf16[16,2048]{1,0:T(8,128)(2,1)S(1)}, bf16[16,2048]{1,0:T(8,128)(2,1)S(1)}, u32[]{:S(2)}, u32[]{:S(2)}) collective-permute-start(bf16[16,2048]{1,0:T(8,128)(2,1)S(1)} %get-tuple-element.131), channel_id=1, source_target_pairs={{8,0},{10,2},{12,4},{14,6},{16,8},{18,10},{20,12},{22,14},{24,16},... | collective-permute-start | bytes 196616 | tf_op jit(solution)/shard_map/ppermute | solution.py:347
  94.5 3.5 %collective-permute-start.17 = (bf16[576,384]{1,0:T(8,128)(2,1)}, bf16[576,384]{1,0:T(8,128)(2,1)}, u32[]{:S(2)}, u32[]{:S(2)}) collective-permute-start(bf16[576,384]{1,0:T(8,128)(2,1)} %convolution_convert_fusion.4), channel_id=1, source_target_pairs={{0,1},{1,0},{2,3},{3,2},{4,5},{5,4},{6,7},{7,6},{8,9},{9,8},{10,11... | collective-permute-start | bytes 1327112 | tf_op jit(solution)/shard_map/ppermute | solution.py:329
  94.5 4.1 %collective-permute-start.19 = (bf16[544,384]{1,0:T(8,128)(2,1)}, bf16[544,384]{1,0:T(8,128)(2,1)}, u32[]{:S(2)}, u32[]{:S(2)}) collective-permute-start(bf16[544,384]{1,0:T(8,128)(2,1)} %convolution_convert_fusion.5), channel_id=1, source_target_pairs={{0,1},{1,0},{2,3},{3,2},{4,5},{5,4},{6,7},{7,6},{8,9},{9,8},{10,11... | collective-permute-start | bytes 1253384 | tf_op jit(solution)/shard_map/ppermute | solution.py:329
  97.2 1.4 collective-permute-start.20
  98.6 13.5 %copy-start.19 = (bf16[384,2048]{1,0:T(8,128)(2,1)S(1)}, bf16[384,2048]{1,0:T(8,128)(2,1)}, u32[]{:S(2)}) copy-start(bf16[384,2048]{1,0:T(8,128)(2,1)} %get-tuple-element.109) | copy-start | bytes 4718596
  111.9 19.6 %copy-start.10 = (bf16[1280,384]{1,0:T(8,128)(2,1)}, bf16[1280,384]{1,0:T(8,128)(2,1)S(1)}, u32[]{:S(2)}) copy-start(bf16[1280,384]{1,0:T(8,128)(2,1)S(1)} %get-tuple-element.149) | copy-start | bytes 2949124
  111.9 2.3 %collective-permute-start.21 = (bf16[768,384]{1,0:T(8,128)(2,1)S(1)}, bf16[768,384]{1,0:T(8,128)(2,1)S(1)}, u32[]{:S(2)}, u32[]{:S(2)}) collective-permute-start(bf16[768,384]{1,0:T(8,128)(2,1)S(1)} %get-tuple-element.139), channel_id=1, source_target_pairs={{0,1},{1,0},{2,3},{3,2},{4,5},{5,4},{6,7},{7,6},{8,9},{9,8},{10,11... | collective-permute-start | bytes 1769480 | tf_op jit(solution)/shard_map/ppermute | solution.py:329
  112.3 19.3 %collective-permute-start.26 = (bf16[1280,384]{1,0:T(8,128)(2,1)S(1)}, bf16[1280,384]{1,0:T(8,128)(2,1)S(1)}, u32[]{:S(2)}, u32[]{:S(2)}) collective-permute-start(bf16[1280,384]{1,0:T(8,128)(2,1)S(1)} %get-tuple-element.149), channel_id=1, source_target_pairs={{0,1},{1,0},{2,3},{3,2},{4,5},{5,4},{6,7},{7,6},{8,9},{9,8},{10,11... | collective-permute-start | bytes 2949128 | tf_op jit(solution)/shard_map/ppermute | solution.py:329
  114.2 18.4 %copy-start.21 = (bf16[768,2048]{1,0:T(8,128)(2,1)}, bf16[768,2048]{1,0:T(8,128)(2,1)S(1)}, u32[]{:S(2)}) copy-start(bf16[768,2048]{1,0:T(8,128)(2,1)S(1)} %constant_dynamic-update-slice_fusion.17) | copy-start | bytes 9437188
  117.2 8.2 %collective-permute-start.22 = (bf16[128,768]{1,0:T(8,128)(2,1)S(1)}, bf16[128,768]{1,0:T(8,128)(2,1)S(1)}, u32[]{:S(2)}, u32[]{:S(2)}) collective-permute-start(bf16[128,768]{1,0:T(8,128)(2,1)S(1)} %get-tuple-element.140), channel_id=1, source_target_pairs={{0,2},{2,0},{4,6},{6,4},{8,10},{10,8},{12,14},{14,12},{16,18},{18,... | collective-permute-start | bytes 589832 | tf_op jit(solution)/shard_map/ppermute | solution.py:333
  118.3 7.2 %collective-permute-start.23 = (bf16[128,768]{1,0:T(8,128)(2,1)S(1)}, bf16[128,768]{1,0:T(8,128)(2,1)S(1)}, u32[]{:S(2)}, u32[]{:S(2)}) collective-permute-start(bf16[128,768]{1,0:T(8,128)(2,1)S(1)} %get-tuple-element.141), channel_id=1, source_target_pairs={{0,4},{2,6},{4,0},{6,2},{8,12},{10,14},{12,8},{14,10},{16,20},{18,... | collective-permute-start | bytes 589832 | tf_op jit(solution)/shard_map/ppermute | solution.py:337
  119.3 6.1 %collective-permute-start.24 = (bf16[128,256]{1,0:T(8,128)(2,1)S(1)}, bf16[128,256]{1,0:T(8,128)(2,1)S(1)}, u32[]{:S(2)}, u32[]{:S(2)}) collective-permute-start(bf16[128,256]{1,0:T(8,128)(2,1)S(1)} %get-tuple-element.142), channel_id=1, source_target_pairs={{0,8},{2,10},{4,12},{6,14},{8,16},{10,18},{12,20},{14,22},{16,24},... | collective-permute-start | bytes 196616 | tf_op jit(solution)/shard_map/ppermute | solution.py:342
  119.3 6.1 %collective-permute-start.25 = (bf16[128,256]{1,0:T(8,128)(2,1)S(1)}, bf16[128,256]{1,0:T(8,128)(2,1)S(1)}, u32[]{:S(2)}, u32[]{:S(2)}) collective-permute-start(bf16[128,256]{1,0:T(8,128)(2,1)S(1)} %get-tuple-element.143), channel_id=1, source_target_pairs={{8,0},{10,2},{12,4},{14,6},{16,8},{18,10},{20,12},{22,14},{24,16},... | collective-permute-start | bytes 196616 | tf_op jit(solution)/shard_map/ppermute | solution.py:347
  125.6 18.0 %collective-permute-start.27 = (bf16[128,3072]{1,0:T(8,128)(2,1)S(1)}, bf16[128,3072]{1,0:T(8,128)(2,1)S(1)}, u32[]{:S(2)}, u32[]{:S(2)}) collective-permute-start(bf16[128,3072]{1,0:T(8,128)(2,1)S(1)} %get-tuple-element.154), channel_id=1, source_target_pairs={{0,2},{2,0},{4,6},{6,4},{8,10},{10,8},{12,14},{14,12},{16,18},{18,... | collective-permute-start | bytes 2359304 | tf_op jit(solution)/shard_map/ppermute | solution.py:333
  126.8 17.7 %collective-permute-start.28 = (bf16[128,3072]{1,0:T(8,128)(2,1)S(1)}, bf16[128,3072]{1,0:T(8,128)(2,1)S(1)}, u32[]{:S(2)}, u32[]{:S(2)}) collective-permute-start(bf16[128,3072]{1,0:T(8,128)(2,1)S(1)} %get-tuple-element.155), channel_id=1, source_target_pairs={{0,4},{2,6},{4,0},{6,2},{8,12},{10,14},{12,8},{14,10},{16,20},{18,... | collective-permute-start | bytes 2359304 | tf_op jit(solution)/shard_map/ppermute | solution.py:337
  127.7 12.5 %collective-permute-start.29 = (bf16[128,1280]{1,0:T(8,128)(2,1)S(1)}, bf16[128,1280]{1,0:T(8,128)(2,1)S(1)}, u32[]{:S(2)}, u32[]{:S(2)}) collective-permute-start(bf16[128,1280]{1,0:T(8,128)(2,1)S(1)} %get-tuple-element.156), channel_id=1, source_target_pairs={{0,8},{2,10},{4,12},{6,14},{8,16},{10,18},{12,20},{14,22},{16,24},... | collective-permute-start | bytes 983048 | tf_op jit(solution)/shard_map/ppermute | solution.py:342
  127.7 14.7 %collective-permute-start.30 = (bf16[128,1280]{1,0:T(8,128)(2,1)S(1)}, bf16[128,1280]{1,0:T(8,128)(2,1)S(1)}, u32[]{:S(2)}, u32[]{:S(2)}) collective-permute-start(bf16[128,1280]{1,0:T(8,128)(2,1)S(1)} %get-tuple-element.157), channel_id=1, source_target_pairs={{8,0},{10,2},{12,4},{14,6},{16,8},{18,10},{20,12},{22,14},{24,16},... | collective-permute-start | bytes 983048 | tf_op jit(solution)/shard_map/ppermute | solution.py:347
  135.9 10.4 %copy-start = (bf16[896,2048]{1,0:T(8,128)(2,1)}, bf16[896,2048]{1,0:T(8,128)(2,1)S(1)}, u32[]{:S(2)}) copy-start(bf16[896,2048]{1,0:T(8,128)(2,1)S(1)} %convolution_convert_fusion.refs_1_) | copy-start | bytes 11010052
  135.9 21.7 %slice-start = ((bf16[1280,384]{1,0:T(8,128)(2,1)}), bf16[384,384]{1,0:T(8,128)(2,1)S(1)}, s32[]{:S(2)}) async-start(bf16[1280,384]{1,0:T(8,128)(2,1)} %copy-done.20), calls=%async_computation.2 | async-start | bytes 589824 | tf_op jit(solution)/shard_map/slice | solution.py:596
  146.3 30.3 %collective-permute-start.31 = (bf16[128,4096]{1,0:T(8,128)(2,1)}, bf16[128,4096]{1,0:T(8,128)(2,1)}, u32[]{:S(2)}, u32[]{:S(2)}) collective-permute-start(bf16[128,4096]{1,0:T(8,128)(2,1)} %get-tuple-element.167), channel_id=1, source_target_pairs={{0,2},{2,0},{4,6},{6,4},{8,10},{10,8},{12,14},{14,12},{16,18},{18,... | collective-permute-start | bytes 3145736 | tf_op jit(solution)/shard_map/ppermute | solution.py:333
  147.2 29.4 %collective-permute-start.32 = (bf16[128,4096]{1,0:T(8,128)(2,1)}, bf16[128,4096]{1,0:T(8,128)(2,1)}, u32[]{:S(2)}, u32[]{:S(2)}) collective-permute-start(bf16[128,4096]{1,0:T(8,128)(2,1)} %get-tuple-element.168), channel_id=1, source_target_pairs={{0,4},{2,6},{4,0},{6,2},{8,12},{10,14},{12,8},{14,10},{16,20},{18,... | collective-permute-start | bytes 3145736 | tf_op jit(solution)/shard_map/ppermute | solution.py:337
  148.3 18.4 %collective-permute-start.33 = (bf16[128,2304]{1,0:T(8,128)(2,1)}, bf16[128,2304]{1,0:T(8,128)(2,1)}, u32[]{:S(2)}, u32[]{:S(2)}) collective-permute-start(bf16[128,2304]{1,0:T(8,128)(2,1)} %get-tuple-element.169), channel_id=1, source_target_pairs={{0,8},{2,10},{4,12},{6,14},{8,16},{10,18},{12,20},{14,22},{16,24},... | collective-permute-start | bytes 1769480 | tf_op jit(solution)/shard_map/ppermute | solution.py:342
  148.5 28.1 %collective-permute-start.34 = (bf16[128,2304]{1,0:T(8,128)(2,1)}, bf16[128,2304]{1,0:T(8,128)(2,1)}, u32[]{:S(2)}, u32[]{:S(2)}) collective-permute-start(bf16[128,2304]{1,0:T(8,128)(2,1)} %get-tuple-element.170), channel_id=1, source_target_pairs={{8,0},{10,2},{12,4},{14,6},{16,8},{18,10},{20,12},{22,14},{24,16},... | collective-permute-start | bytes 1769480 | tf_op jit(solution)/shard_map/ppermute | solution.py:347
  152.1 34.0 %all-to-all-start.1 = ((bf16[16,128,128]{2,1,0:T(8,128)(2,1)}), bf16[16,128,128]{2,1,0:T(8,128)(2,1)}, u32[]{:S(2)}, u32[]{:S(2)}) async-start(bf16[16,128,128]{2,1,0:T(8,128)(2,1)} %bitcast.46), calls=%async_computation.1 | async-start | bytes 1048576 | tf_op jit(solution)/shard_map/all_to_all | solution.py:599
  157.6 19.1 %copy-start.1 = (bf16[896,2048]{1,0:T(8,128)(2,1)S(1)}, bf16[896,2048]{1,0:T(8,128)(2,1)}, u32[]{:S(2)}) copy-start(bf16[896,2048]{1,0:T(8,128)(2,1)} %copy-done) | copy-start | bytes 11010052
  180.6 22.2 %collective-permute-start.35 = (bf16[128,2048]{1,0:T(8,128)(2,1)}, bf16[128,2048]{1,0:T(8,128)(2,1)S(1)}, u32[]{:S(2)}, u32[]{:S(2)}) collective-permute-start(bf16[128,2048]{1,0:T(8,128)(2,1)} %get-tuple-element.176), channel_id=1, source_target_pairs={{0,2},{2,0},{4,6},{6,4},{8,10},{10,8},{12,14},{14,12},{16,18},{18,... | collective-permute-start | bytes 1572872 | tf_op jit(solution)/shard_map/ppermute | solution.py:333
  181.7 21.1 %collective-permute-start.36 = (bf16[128,2048]{1,0:T(8,128)(2,1)}, bf16[128,2048]{1,0:T(8,128)(2,1)S(1)}, u32[]{:S(2)}, u32[]{:S(2)}) collective-permute-start(bf16[128,2048]{1,0:T(8,128)(2,1)} %get-tuple-element.177), channel_id=1, source_target_pairs={{0,4},{2,6},{4,0},{6,2},{8,12},{10,14},{12,8},{14,10},{16,20},{18,... | collective-permute-start | bytes 1572872 | tf_op jit(solution)/shard_map/ppermute | solution.py:337
  182.3 14.1 %collective-permute-start.37 = (bf16[128,1536]{1,0:T(8,128)(2,1)}, bf16[128,1536]{1,0:T(8,128)(2,1)S(1)}, u32[]{:S(2)}, u32[]{:S(2)}) collective-permute-start(bf16[128,1536]{1,0:T(8,128)(2,1)} %get-tuple-element.178), channel_id=1, source_target_pairs={{0,8},{2,10},{4,12},{6,14},{8,16},{10,18},{12,20},{14,22},{16,24},... | collective-permute-start | bytes 1179656 | tf_op jit(solution)/shard_map/ppermute | solution.py:342
  184.7 18.0 %collective-permute-start.38 = (bf16[128,1536]{1,0:T(8,128)(2,1)S(1)}, bf16[128,1536]{1,0:T(8,128)(2,1)S(1)}, u32[]{:S(2)}, u32[]{:S(2)}) collective-permute-start(bf16[128,1536]{1,0:T(8,128)(2,1)S(1)} %get-tuple-element.179), channel_id=1, source_target_pairs={{8,0},{10,2},{12,4},{14,6},{16,8},{18,10},{20,12},{22,14},{24,16},... | collective-permute-start | bytes 1179656 | tf_op jit(solution)/shard_map/ppermute | solution.py:347
  (18 other events, 65.2 us)

commit v3 on v2

--- a/solution.py
+++ b/solution.py
@@ -409,6 +409,12 @@
 
 
 def assemble(arrays, *plans):
+    used = sorted({source[0] for plan in plans for piece in plan for source in piece[4]})
+    arrays = [arrays[index] for index in used]
+    plans = [
+        [(*piece[:4], [(used.index(source[0]), *source[1:]) for source in piece[4]]) for piece in plan]
+        for plan in plans
+    ]
     shapes = [
         (max(p[0] + p[2] for p in plan), max(p[1] + p[3] for p in plan)) for plan in plans
     ]
@@ -547,15 +553,19 @@
     return parts, tuple(runs), matrices, later
 
 
-ORDER = (((2, 0, 4), (1, 3, 1), (3, 3, 1)), ((1, 0, 3), (3, 0, 3), (0, 3, 1), (0, 0, 3)))
-
-
-def scatter_sum(early, later, matrix, hyena):
-    span = early.shape[0] // 6
+ORDER = (
+    ((2, 3, 1),),
+    ((2, 0, 3), (1, 3, 1), (3, 3, 1)),
+    ((1, 0, 3), (3, 0, 3), (0, 3, 1), (0, 0, 3)),
+)
+
+
+def scatter_sum(first, early, later, matrix, hyena):
+    span = first.shape[0]
     columns = matrix.shape[1]
     wide, narrow = columns * 3 // 8, columns // 8
     places = {}
-    for array, pieces in enumerate((ORDER[0], ORDER[1][:3], ORDER[1][3:])):
+    for array, pieces in enumerate((*ORDER[:2], ORDER[2][:3], ORDER[2][3:])):
         row = 0
         for group, base, members in pieces:
             for member in range(base, base + members):
@@ -577,16 +587,18 @@
     def put(arrays, *plans):
         return assemble(arrays, *[columns_of(span, *plan) for plan in plans])
 
-    early = product(early, swapped(early))
+    first = product(first, swapped(first))
+    other_early = swapped(early)
+    sent = put([first], [term(2, 3, 0)], [term(2, 3, 1)], [low(2, 3, 0)], [low(2, 3, 1)])
+    early, sent = lax.optimization_barrier((early, sent))
+    first = all_ways(*sent)
+    early = product(early, other_early)
+    later, hyena, first = lax.optimization_barrier((later, hyena, first))
     other = swapped(later)
-    first = all_ways(
-        *put([early], [term(2, 3, 0)], [term(2, 3, 1)], [low(2, 3, 0)], [low(2, 3, 1)])
-    )
-    later, hyena, first = lax.optimization_barrier((later, hyena, first))
-    x, y, below, above = range(1, 5)
+    x, y, below, above = range(2, 6)
     second = all_ways(
         *put(
-            [early, *first],
+            [early, early, *first],
             [term(2, 1, 0), term(2, 1, 1, (y, 0, 0)), term(1, 3, 0), term(3, 3, 0)],
             [term(2, 2, 0, (x, 0, 0)), term(2, 2, 1), term(1, 3, 1), term(3, 3, 1)],
             [low(1, 3, 0, (below, 0, 0)), low(1, 3, 1), *[low(2, k, 0) for k in range(3)]],
@@ -597,7 +609,7 @@
     later = product(later[: 7 * span], other[: 7 * span])
     later, second = lax.optimization_barrier((later, second))
     hyena_out = lax.all_to_all(hyena, "ctx", split_axis=0, concat_axis=1, tiled=True).T
-    x, y, below, above = range(2, 6)
+    x, y, below, above = range(3, 7)
 
     def low_3(side):
         return low(0, 3, side, (below, 0, side * narrow), (above, 0, side * narrow))
@@ -612,7 +624,7 @@
         for_below += [low(3, k, 0), low(3, k, 1, (above, 0, start))]
     third = all_ways(
         *put(
-            [early, later, *second],
+            [early, early, later, *second],
             [
                 term(1, 1, 0),
                 term(1, 1, 1, (y, 0, 2 * wide)),
@@ -634,7 +646,7 @@
         )
     )
 
-    x, y, below, above = range(3, 7)
+    x, y, below, above = range(4, 8)
 
     def low_own(k, side, *more):
         start = wide + (2 * k + side) * narrow
@@ -644,8 +656,8 @@
         start = (group - 1 + side) * wide
         return term(group, 0, side, (x, 0, start), (y, 0, start), *more)
 
-    *sent, base = put(
-            [early, later, own, *third],
+    sent = put(
+        [early, early, later, own, *third],
             [
                 term(0, 1, 0),
                 term(0, 1, 1, (y, 0, 4 * wide)),
@@ -660,8 +672,11 @@
             ],
             [own_sum(1, 0, (below, 0, 0)), own_sum(1, 1)],
             [own_sum(3, 0), own_sum(3, 1, (above, 0, 0))],
-            [term(0, 0, 0), term(0, 0, 1), low_own(0, 0), low_own(0, 1)],
-        )
+    )
+    (base,) = put(
+        [early, early, later, own, *third],
+        [term(0, 0, 0), term(0, 0, 1), low_own(0, 0), low_own(0, 1)],
+    )
     (grad_input,) = put(
         [base, *all_ways(*sent)],
         [
@@ -681,10 +696,10 @@
     taken = swapped(given)
     parts, runs, (kept, taken), cot_cols = gather_groups(*tokens_half, (kept, taken), cotangent)
     own, other = zip(*parts)
-    hyena, grads, (early, later) = scan_all(
+    hyena, grads, proj = scan_all(
         me, cot_cols, residues[0].T, decay_rates[0].T, runs, ORDER, own, other
     )
-    grad_input, hyena_out = scatter_sum(early, later, stack(kept, taken), hyena)
+    grad_input, hyena_out = scatter_sum(*proj, stack(kept, taken), hyena)
     return (hyena_out, grad_input, grads.T[None])
 
 

time: 206 us -> 216 us (1.049)
  waiting for transfers between devices: 74.4 us -> 78.6 us
  local copies, waits for them, and re-layouts: 13.8 us -> 16.4 us
    all_to_all x1, waiting for transfers between devices: 0.01 us -> 6.59 us  [scatter_sum(): lax.all_to_all(hyena, 'ctx', split_axis=0, concat_axis=1, tiled=True)]
    ppermute x8, waiting for transfers between devices: 30.4 us -> 26.4 us  [up(): lax.ppermute(value, 'ctx', [(i, (i + PLANE) % count) for i in range(count)])]
    unnamed x62, local copies, waits for them, and re-layouts: 6.93 us -> 9.59 us
    ppermute x8, waiting for transfers between devices: 39.4 us -> 41.6 us  [down(): lax.ppermute(value, 'ctx', [((i + PLANE) % count, i) for i in range(count)])]
    pallas_call x8 -> x9, Pallas kernels: 8.5 us -> 9.61 us  [assemble(): pl.pallas_call(functools.partial(assemble_kernel, len(arrays), plans), ou...]
    dot_general x3 -> x4, matrix products: 9.67 us -> 9.62 us  [product(): return narrowed(jnp.dot(both, matrix, preferred_element_type=jnp.float32))]
  transfers between devices with their start and end apart: 41 -> 42, of which waited for: 16 -> 16; matrix products, arithmetic and copies ran while one was open for 19% -> 18% of each run, Pallas kernels for 4% -> 4%
where the time goes in v3:
time: 216 us; the launch traced here: 215 us
  waiting for transfers between devices  78.6 us (36%)
  starting transfers between devices  59.8 us (28%)
  matrix products  30.1 us (14%)
  Pallas kernels  28.7 us (13%)
  local copies, waits for them, and re-layouts  16.4 us (8%)
    ppermute x8, waiting for transfers between devices, down(): lax.ppermute(value, 'ctx', [((i + PLANE) % count, i) for i in range(count)])  41.6 us
    ppermute x8, waiting for transfers between devices, up(): lax.ppermute(value, 'ctx', [(i, (i + PLANE) % count) for i in range(count)])  26.4 us
    ppermute x8, starting transfers between devices, down(): lax.ppermute(value, 'ctx', [((i + PLANE) % count, i) for i in range(count)])  24.3 us
    dot_general x8, matrix products, project(): jnp.einsum('td,rd->tr', rows, matrix, preferred_element_type=jnp.float32)  20.5 us
    pallas_call x1, Pallas kernels, scan_all(): pl.pallas_call(functools.partial(scan_kernel, PLANE, runs, order), out_sh...  13.4 us
    ppermute x8, starting transfers between devices, over_x(): lax.ppermute(value, 'ctx', [(i, i ^ 1) for i in range(lax.axis_size('ctx'...  10.5 us
    dot_general x4, matrix products, product(): return narrowed(jnp.dot(both, matrix, preferred_element_type=jnp.float32))  9.62 us
    pallas_call x9, Pallas kernels, assemble(): pl.pallas_call(functools.partial(assemble_kernel, len(arrays), plans), ou...  9.61 us
  transfers between devices with their start and end apart: 42, of which 16 were waited for; matrix products, arithmetic and copies ran while one was open for 18% of the time, Pallas kernels for 4%

profile of v3, /device:TPU:0, one launch (start us, length us, event | category | flops | bytes accessed | tf_op | source)
XLA Modules:
  0.0 214.9 jit_solution(5192628142155648521)
XLA Ops:
  0.6 2.1 halves.2
  2.7 3.0 %collective-permute-start = (bf16[128,2048]{1,0:T(8,128)(2,1)}, bf16[128,2048]{1,0:T(8,128)(2,1)S(1)}, u32[]{:S(2)}, u32[]{:S(2)}) collective-permute-start(bf16[128,2048]{1,0:T(8,128)(2,1)} %get-tuple-element.109.refs_0_), channel_id=1, source_target_pairs={{0,2},{2,0},{4,6},{6,4},{8,10},{10,8},{12,14},{14,12},{16,18},{18,... | collective-permute-start | bytes 1572872 | tf_op jit(solution)/shard_map/ppermute | solution.py:333
  7.3 1.6 collective-permute-start.2
  8.8 2.2 %collective-permute-start.3 = (bf16[96,2048]{1,0:T(8,128)(2,1)}, bf16[96,2048]{1,0:T(8,128)(2,1)S(1)}, u32[]{:S(2)}, u32[]{:S(2)}) collective-permute-start(bf16[96,2048]{1,0:T(8,128)(2,1)} %get-tuple-element.100), channel_id=1, source_target_pairs={{8,0},{10,2},{12,4},{14,6},{16,8},{18,10},{20,12},{22,14},{24,16},... | collective-permute-start | bytes 1179656 | tf_op jit(solution)/shard_map/ppermute | solution.py:347
  11.1 3.7 %halves.3 = (bf16[384,2048]{1,0:T(8,128)(2,1)}, bf16[384,2048]{1,0:T(8,128)(2,1)}) custom-call(s32[1]{0:T(128)} %bitcast.5.core_ref, bf16[384,4096]{1,0:T(8,128)(2,1)} %bitcast.49), custom_call_target="tpu_custom_call" | custom-call | bytes 6291456 | tf_op jit(solution)/shard_map/halves/pallas_call | solution.py:385
  14.8 2.8 %constant_dynamic-update-slice_fusion.18 = bf16[768,2048]{1,0:T(8,128)(2,1)} fusion(bf16[384,2048]{1,0:T(8,128)(2,1)} %get-tuple-element.114), kind=kLoop, calls=%fused_computation.38 | loop fusion | bytes 3145728
  17.7 3.7 %collective-permute-done.2.refs_3_ = bf16[96,2048]{1,0:T(8,128)(2,1)S(1)} collective-permute-done((bf16[96,2048]{1,0:T(8,128)(2,1)}, bf16[96,2048]{1,0:T(8,128)(2,1)S(1)}, u32[]{:S(2)}, u32[]{:S(2)}) %collective-permute-start.2) | collective-permute-done | bytes 393248 | tf_op jit(solution)/shard_map/ppermute | solution.py:342
  21.4 6.1 %collective-permute-done.3.refs_4_ = bf16[96,2048]{1,0:T(8,128)(2,1)S(1)} collective-permute-done((bf16[96,2048]{1,0:T(8,128)(2,1)}, bf16[96,2048]{1,0:T(8,128)(2,1)S(1)}, u32[]{:S(2)}, u32[]{:S(2)}) %collective-permute-start.3) | collective-permute-done | bytes 393248 | tf_op jit(solution)/shard_map/ppermute | solution.py:347
  27.5 2.1 assemble.9
  31.9 2.7 %collective-permute-start.7 = (bf16[144,2048]{1,0:T(8,128)(2,1)}, bf16[144,2048]{1,0:T(8,128)(2,1)S(1)}, u32[]{:S(2)}, u32[]{:S(2)}) collective-permute-start(bf16[144,2048]{1,0:T(8,128)(2,1)} %get-tuple-element.120), channel_id=1, source_target_pairs={{8,0},{10,2},{12,4},{14,6},{16,8},{18,10},{20,12},{22,14},{24,16},... | collective-permute-start | bytes 1769480 | tf_op jit(solution)/shard_map/ppermute | solution.py:347
  35.9 2.3 %fusion.16.refs_1_ = f32[576,384]{1,0:T(8,128)} fusion(bf16[576,2048]{1,0:T(8,128)(2,1)S(1)} %constant_dynamic-update-slice_fusion, bf16[384,2048]{1,0:T(8,128)(2,1)S(1)} %copy-done.19), kind=kOutput, calls=%fused_computation.43 | convolution fusion | flops 905969664 | bytes 4816896 | tf_op jit(solution)/shard_map/td,rd->tr/dot_general | solution.py:463
  38.3 2.0 copy.8
  40.3 4.2 %all-to-all-start = ((bf16[128,16,128]{2,0,1:T(8,128)(2,1)}), bf16[128,16,128]{2,0,1:T(8,128)(2,1)}, u32[]{:S(2)}, u32[]{:S(2)}) async-start(bf16[128,16,128]{2,0,1:T(8,128)(2,1)} %copy.8), calls=%async_computation | async-start | bytes 1048576 | tf_op jit(solution)/shard_map/all_to_all | solution.py:470
  44.5 4.5 %collective-permute-done.6.refs_2_ = bf16[144,2048]{1,0:T(8,128)(2,1)S(1)} collective-permute-done((bf16[144,2048]{1,0:T(8,128)(2,1)}, bf16[144,2048]{1,0:T(8,128)(2,1)S(1)}, u32[]{:S(2)}, u32[]{:S(2)}) %collective-permute-start.6) | collective-permute-done | bytes 589856 | tf_op jit(solution)/shard_map/ppermute | solution.py:342
  49.1 12.1 %collective-permute-done.7.refs_3_ = bf16[144,2048]{1,0:T(8,128)(2,1)S(1)} collective-permute-done((bf16[144,2048]{1,0:T(8,128)(2,1)}, bf16[144,2048]{1,0:T(8,128)(2,1)S(1)}, u32[]{:S(2)}, u32[]{:S(2)}) %collective-permute-start.7) | collective-permute-done | bytes 589856 | tf_op jit(solution)/shard_map/ppermute | solution.py:347
  61.3 1.6 collective-permute-start.8
  64.5 3.4 %collective-permute-start.11 = (bf16[80,2048]{1,0:T(8,128)(2,1)S(1)}, bf16[80,2048]{1,0:T(8,128)(2,1)S(1)}, u32[]{:S(2)}, u32[]{:S(2)}) collective-permute-start(bf16[80,2048]{1,0:T(8,128)(2,1)S(1)} %get-tuple-element.128), channel_id=1, source_target_pairs={{8,0},{10,2},{12,4},{14,6},{16,8},{18,10},{20,12},{22,14},{24,16},... | collective-permute-start | bytes 983048 | tf_op jit(solution)/shard_map/ppermute | solution.py:347
  69.3 1.9 fusion.17.refs_2_
  71.2 4.3 %convolution_convert_fusion.4 = bf16[800,384]{1,0:T(8,128)(2,1)} fusion(bf16[800,2048]{1,0:T(8,128)(2,1)S(1)} %constant_dynamic-update-slice_fusion.5, bf16[384,2048]{1,0:T(8,128)(2,1)} %collective-permute-done.16), kind=kOutput, calls=%fused_computation.7 | convolution fusion | flops 1258598400 | bytes 5464064 | tf_op jit(solution)/shard_map/td,rd->tr/dot_general | solution.py:463
  75.5 3.6 %convolution_convert_fusion.5 = bf16[576,384]{1,0:T(8,128)(2,1)} fusion(bf16[576,2048]{1,0:T(8,128)(2,1)S(1)} %copy-done.23, bf16[384,2048]{1,0:T(8,128)(2,1)} %collective-permute-done.16), kind=kOutput, calls=%fused_computation.8 | convolution fusion | flops 906190848 | bytes 4374528 | tf_op jit(solution)/shard_map/td,rd->tr/dot_general | solution.py:463
  79.1 2.5 %collective-permute-done.11.refs_3_ = bf16[80,2048]{1,0:T(8,128)(2,1)S(1)} collective-permute-done((bf16[80,2048]{1,0:T(8,128)(2,1)S(1)}, bf16[80,2048]{1,0:T(8,128)(2,1)S(1)}, u32[]{:S(2)}, u32[]{:S(2)}) %collective-permute-start.11) | collective-permute-done | bytes 327712 | tf_op jit(solution)/shard_map/ppermute | solution.py:347
  81.7 1.8 collective-permute-done.8.refs_0_
  85.7 2.3 %collective-permute-start.14 = (bf16[16,2048]{1,0:T(8,128)(2,1)S(1)}, bf16[16,2048]{1,0:T(8,128)(2,1)S(1)}, u32[]{:S(2)}, u32[]{:S(2)}) collective-permute-start(bf16[16,2048]{1,0:T(8,128)(2,1)S(1)} %get-tuple-element.135), channel_id=1, source_target_pairs={{0,8},{2,10},{4,12},{6,14},{8,16},{10,18},{12,20},{14,22},{16,24},... | collective-permute-start | bytes 196616 | tf_op jit(solution)/shard_map/ppermute | solution.py:342
  88.0 1.6 collective-permute-start.15
  89.7 2.2 %fusion.18.refs_3_ = f32[544,384]{1,0:T(8,128)} fusion(bf16[544,2048]{1,0:T(8,128)(2,1)S(1)} %constant_dynamic-update-slice_fusion.9, bf16[384,2048]{1,0:T(8,128)(2,1)S(1)} %copy-done.20), kind=kOutput, calls=%fused_computation.45 | convolution fusion | flops 855638016 | bytes 4636672 | tf_op jit(solution)/shard_map/td,rd->tr/dot_general | solution.py:463
  91.9 3.5 %convolution_convert_fusion.6 = bf16[544,384]{1,0:T(8,128)(2,1)} fusion(bf16[544,2048]{1,0:T(8,128)(2,1)S(1)} %constant_dynamic-update-slice_fusion.9, bf16[384,2048]{1,0:T(8,128)(2,1)} %collective-permute-done.16), kind=kOutput, calls=%fused_computation.9 | convolution fusion | flops 855846912 | bytes 4218880 | tf_op jit(solution)/shard_map/td,rd->tr/dot_general | solution.py:463
  96.0 2.1 convolution_convert_fusion.7
  102.0 13.4 %modal_scan.1 = (bf16[2048,128]{1,0:T(8,128)(2,1)}, f32[16,128]{1,0:T(8,128)}, bf16[128,384]{1,0:T(8,128)(2,1)S(1)}, bf16[640,384]{1,0:T(8,128)(2,1)S(1)}, bf16[1280,384]{1,0:T(8,128)(2,1)S(1)}) custom-call(s32[1]{0:T(128)} %bitcast.me_ref, f32[16,128]{1,0:T(8,128)S(1)} %bitcast.47, f32[16,128]{1,0:T(8,128)S(1)} %bitcast.48, ...), custom_call_target="tpu_custom_call" | custom-call | tf_op jit(solution)/shard_map/modal_scan/pallas_call | solution.py:308
  120.2 3.8 %collective-permute-start.25 = (bf16[128,256]{1,0:T(8,128)(2,1)S(1)}, bf16[128,256]{1,0:T(8,128)(2,1)S(1)}, u32[]{:S(2)}, u32[]{:S(2)}) collective-permute-start(bf16[128,256]{1,0:T(8,128)(2,1)S(1)} %get-tuple-element.153), channel_id=1, source_target_pairs={{8,0},{10,2},{12,4},{14,6},{16,8},{18,10},{20,12},{22,14},{24,16},... | collective-permute-start | bytes 196616 | tf_op jit(solution)/shard_map/ppermute | solution.py:347
  124.1 2.5 %collective-permute-done.24.refs_3_ = bf16[128,256]{1,0:T(8,128)(2,1)S(1)} collective-permute-done((bf16[128,256]{1,0:T(8,128)(2,1)S(1)}, bf16[128,256]{1,0:T(8,128)(2,1)S(1)}, u32[]{:S(2)}, u32[]{:S(2)}) %collective-permute-start.24) | collective-permute-done | bytes 65568 | tf_op jit(solution)/shard_map/ppermute | solution.py:342
  126.7 2.3 %convolution_convert_fusion.1.refs_0_ = bf16[640,2048]{1,0:T(8,128)(2,1)S(1)} fusion(bf16[768,2048]{1,0:T(8,128)(2,1)S(1)} %constant_dynamic-update-slice_fusion.17, bf16[640,384]{1,0:T(8,128)(2,1)S(1)} %collective-permute-done.27, bf16[640,384]{1,0:T(8,128)(2,1)S(1)} %get-tuple-element.160), kind=kOutput, calls=%fused_computation.1 | convolution fusion | flops 2016542720 | bytes 6750208 | tf_op jit(solution)/shard_map/dot_general | solution.py:577
  131.3 3.8 %collective-permute-start.31 = (bf16[128,1280]{1,0:T(8,128)(2,1)S(1)}, bf16[128,1280]{1,0:T(8,128)(2,1)S(1)}, u32[]{:S(2)}, u32[]{:S(2)}) collective-permute-start(bf16[128,1280]{1,0:T(8,128)(2,1)S(1)} %get-tuple-element.168), channel_id=1, source_target_pairs={{8,0},{10,2},{12,4},{14,6},{16,8},{18,10},{20,12},{22,14},{24,16},... | collective-permute-start | bytes 983048 | tf_op jit(solution)/shard_map/ppermute | solution.py:347
  135.2 8.5 %collective-permute-done.30.refs_4_ = bf16[128,1280]{1,0:T(8,128)(2,1)S(1)} collective-permute-done((bf16[128,1280]{1,0:T(8,128)(2,1)S(1)}, bf16[128,1280]{1,0:T(8,128)(2,1)S(1)}, u32[]{:S(2)}, u32[]{:S(2)}) %collective-permute-start.30) | collective-permute-done | bytes 327712 | tf_op jit(solution)/shard_map/ppermute | solution.py:342
  143.7 4.1 %collective-permute-done.31.refs_5_ = bf16[128,1280]{1,0:T(8,128)(2,1)S(1)} collective-permute-done((bf16[128,1280]{1,0:T(8,128)(2,1)S(1)}, bf16[128,1280]{1,0:T(8,128)(2,1)S(1)}, u32[]{:S(2)}, u32[]{:S(2)}) %collective-permute-start.31) | collective-permute-done | bytes 327712 | tf_op jit(solution)/shard_map/ppermute | solution.py:347
  150.1 3.3 %convolution_convert_fusion.refs_1_.refs_0_ = bf16[896,2048]{1,0:T(8,128)(2,1)S(1)} fusion(bf16[768,2048]{1,0:T(8,128)(2,1)S(1)} %constant_dynamic-update-slice_fusion.17, bf16[896,384]{1,0:T(8,128)(2,1)S(1)} %slice.17, bf16[896,384]{1,0:T(8,128)(2,1)S(1)} %slice.14), kind=kOutput, calls=%fused_computation | convolution fusion | flops 2823159808 | bytes 8192000 | tf_op jit(solution)/shard_map/dot_general | solution.py:577
  153.4 1.8 assemble.14
  158.3 3.5 %collective-permute-start.35 = (bf16[128,2304]{1,0:T(8,128)(2,1)S(1)}, bf16[128,2304]{1,0:T(8,128)(2,1)S(1)}, u32[]{:S(2)}, u32[]{:S(2)}) collective-permute-start(bf16[128,2304]{1,0:T(8,128)(2,1)S(1)} %get-tuple-element.181), channel_id=1, source_target_pairs={{8,0},{10,2},{12,4},{14,6},{16,8},{18,10},{20,12},{22,14},{24,16},... | collective-permute-start | bytes 1769480 | tf_op jit(solution)/shard_map/ppermute | solution.py:347
  161.8 4.5 %all-to-all-start.1 = ((bf16[16,128,128]{2,1,0:T(8,128)(2,1)}), bf16[16,128,128]{2,1,0:T(8,128)(2,1)}, u32[]{:S(2)}, u32[]{:S(2)}) async-start(bf16[16,128,128]{2,1,0:T(8,128)(2,1)} %bitcast.13), calls=%async_computation.1 | async-start | bytes 1048576 | tf_op jit(solution)/shard_map/all_to_all | solution.py:611
  167.3 3.5 %convolution_convert_fusion.2.refs_0_.refs_1_ = bf16[384,2048]{1,0:T(8,128)(2,1)S(1)} fusion(bf16[768,2048]{1,0:T(8,128)(2,1)} %copy-done.18, bf16[384,384]{1,0:T(8,128)(2,1)S(1)} %slice.16, bf16[384,384]{1,0:T(8,128)(2,1)S(1)} %slice.12), kind=kOutput, calls=%fused_computation.2 | convolution fusion | flops 1209925632 | bytes 5308416 | tf_op jit(solution)/shard_map/dot_general | solution.py:577
  170.8 5.5 %collective-permute-done.34.refs_1_.refs_4_ = bf16[128,2304]{1,0:T(8,128)(2,1)S(1)} collective-permute-done((bf16[128,2304]{1,0:T(8,128)(2,1)}, bf16[128,2304]{1,0:T(8,128)(2,1)S(1)}, u32[]{:S(2)}, u32[]{:S(2)}) %collective-permute-start.34) | collective-permute-done | bytes 589856 | tf_op jit(solution)/shard_map/ppermute | solution.py:342
  176.2 11.2 %collective-permute-done.35.refs_2_.refs_5_ = bf16[128,2304]{1,0:T(8,128)(2,1)S(1)} collective-permute-done((bf16[128,2304]{1,0:T(8,128)(2,1)S(1)}, bf16[128,2304]{1,0:T(8,128)(2,1)S(1)}, u32[]{:S(2)}, u32[]{:S(2)}) %collective-permute-start.35) | collective-permute-done | bytes 589856 | tf_op jit(solution)/shard_map/ppermute | solution.py:347
  187.5 2.9 %assemble.16 = (bf16[128,2048]{1,0:T(8,128)(2,1)}, bf16[128,2048]{1,0:T(8,128)(2,1)}, bf16[128,1536]{1,0:T(8,128)(2,1)}, bf16[128,1536]{1,0:T(8,128)(2,1)}) custom-call(bf16[896,2048]{1,0:T(8,128)(2,1)S(1)} %copy-done.1, bf16[384,2048]{1,0:T(8,128)(2,1)S(1)} %convolution_convert_fusion.2.refs_0_.refs_1_, bf16[128,4096]{1,0:T(8,128)(2,1)} %collective-permute-done.32.refs_2_, ...), custom_call_target="tpu_custom_call" | custom-call | flops 1835008 | bytes 7340032 | tf_op jit(solution)/shard_map/assemble/pallas_call | solution.py:423
  193.4 3.3 %collective-permute-start.39 = (bf16[128,1536]{1,0:T(8,128)(2,1)}, bf16[128,1536]{1,0:T(8,128)(2,1)}, u32[]{:S(2)}, u32[]{:S(2)}) collective-permute-start(bf16[128,1536]{1,0:T(8,128)(2,1)} %get-tuple-element.189), channel_id=1, source_target_pairs={{8,0},{10,2},{12,4},{14,6},{16,8},{18,10},{20,12},{22,14},{24,16},... | collective-permute-start | bytes 1179656 | tf_op jit(solution)/shard_map/ppermute | solution.py:347
  196.7 6.6 %all-to-all-done.1 = bf16[16,128,128]{2,1,0:T(8,128)(2,1)} async-done(((bf16[16,128,128]{2,1,0:T(8,128)(2,1)}), bf16[16,128,128]{2,1,0:T(8,128)(2,1)}, u32[]{:S(2)}, u32[]{:S(2)}) %all-to-all-start.1) | async-done | bytes 524320 | tf_op jit(solution)/shard_map/all_to_all | solution.py:611
  203.3 2.0 copy.9
  205.4 1.6 collective-permute-done.38.refs_3_
  207.0 5.5 %collective-permute-done.39.refs_4_ = bf16[128,1536]{1,0:T(8,128)(2,1)} collective-permute-done((bf16[128,1536]{1,0:T(8,128)(2,1)}, bf16[128,1536]{1,0:T(8,128)(2,1)}, u32[]{:S(2)}, u32[]{:S(2)}) %collective-permute-start.39) | collective-permute-done | bytes 393248 | tf_op jit(solution)/shard_map/ppermute | solution.py:347
  212.6 2.4 %assemble.17 = bf16[128,2048]{1,0:T(8,128)(2,1)} custom-call(bf16[128,2048]{1,0:T(8,128)(2,1)S(1)} %assemble.15.refs_0_, bf16[128,2048]{1,0:T(8,128)(2,1)S(1)} %collective-permute-done.36.refs_1_, bf16[128,2048]{1,0:T(8,128)(2,1)} %collective-permute-done.37.refs_2_, bf16[128,1536]{1,0:T(8,128)(2,1)} %collective-permute-done.38.refs_3_, ...), custom_call_target="tpu_custom_call" | custom-call | flops 524288 | bytes 2097152 | tf_op jit(solution)/shard_map/assemble/pallas_call | solution.py:423
  (133 shorter events, 31.8 us)
Async XLA Ops:
  2.7 24.8 %collective-permute-start = (bf16[128,2048]{1,0:T(8,128)(2,1)}, bf16[128,2048]{1,0:T(8,128)(2,1)S(1)}, u32[]{:S(2)}, u32[]{:S(2)}) collective-permute-start(bf16[128,2048]{1,0:T(8,128)(2,1)} %get-tuple-element.109.refs_0_), channel_id=1, source_target_pairs={{0,2},{2,0},{4,6},{6,4},{8,10},{10,8},{12,14},{14,12},{16,18},{18,... | collective-permute-start | bytes 1572872 | tf_op jit(solution)/shard_map/ppermute | solution.py:333
  5.7 21.8 %collective-permute-start.1 = (bf16[128,2048]{1,0:T(8,128)(2,1)}, bf16[128,2048]{1,0:T(8,128)(2,1)S(1)}, u32[]{:S(2)}, u32[]{:S(2)}) collective-permute-start(bf16[128,2048]{1,0:T(8,128)(2,1)} %get-tuple-element.109.refs_0_), channel_id=1, source_target_pairs={{0,4},{2,6},{4,0},{6,2},{8,12},{10,14},{12,8},{14,10},{16,20},{18,... | collective-permute-start | bytes 1572872 | tf_op jit(solution)/shard_map/ppermute | solution.py:337
  7.3 14.1 %collective-permute-start.2 = (bf16[96,2048]{1,0:T(8,128)(2,1)}, bf16[96,2048]{1,0:T(8,128)(2,1)S(1)}, u32[]{:S(2)}, u32[]{:S(2)}) collective-permute-start(bf16[96,2048]{1,0:T(8,128)(2,1)} %get-tuple-element.100), channel_id=1, source_target_pairs={{0,8},{2,10},{4,12},{6,14},{8,16},{10,18},{12,20},{14,22},{16,24},... | collective-permute-start | bytes 1179656 | tf_op jit(solution)/shard_map/ppermute | solution.py:342
  8.8 18.7 %collective-permute-start.3 = (bf16[96,2048]{1,0:T(8,128)(2,1)}, bf16[96,2048]{1,0:T(8,128)(2,1)S(1)}, u32[]{:S(2)}, u32[]{:S(2)}) collective-permute-start(bf16[96,2048]{1,0:T(8,128)(2,1)} %get-tuple-element.100), channel_id=1, source_target_pairs={{8,0},{10,2},{12,4},{14,6},{16,8},{18,10},{20,12},{22,14},{24,16},... | collective-permute-start | bytes 1179656 | tf_op jit(solution)/shard_map/ppermute | solution.py:347
  14.7 12.8 %copy-start.2 = (bf16[128,2048]{1,0:T(8,128)(2,1)S(1)}, bf16[128,2048]{1,0:T(8,128)(2,1)}, u32[]{:S(2)}) copy-start(bf16[128,2048]{1,0:T(8,128)(2,1)} %get-tuple-element.109.refs_0_) | copy-start | bytes 1572868
  14.8 56.5 %collective-permute-start.16 = (bf16[384,2048]{1,0:T(8,128)(2,1)}, bf16[384,2048]{1,0:T(8,128)(2,1)}, u32[]{:S(2)}, u32[]{:S(2)}) collective-permute-start(bf16[384,2048]{1,0:T(8,128)(2,1)} %get-tuple-element.141), channel_id=1, source_target_pairs={{0,1},{1,0},{2,3},{3,2},{4,5},{5,4},{6,7},{7,6},{8,9},{9,8},{10,11... | collective-permute-start | bytes 4718600 | tf_op jit(solution)/shard_map/ppermute | solution.py:329
  14.8 19.8 %copy-start.3 = (bf16[128,2048]{1,0:T(8,128)(2,1)S(1)}, bf16[128,2048]{1,0:T(8,128)(2,1)}, u32[]{:S(2)}) copy-start(bf16[128,2048]{1,0:T(8,128)(2,1)} %get-tuple-element.109.refs_0_) | copy-start | bytes 1572868
  21.4 8.3 %copy-start.7 = (bf16[96,2048]{1,0:T(8,128)(2,1)}, bf16[96,2048]{1,0:T(8,128)(2,1)S(1)}, u32[]{:S(2)}) copy-start(bf16[96,2048]{1,0:T(8,128)(2,1)S(1)} %collective-permute-done.2.refs_3_) | copy-start | bytes 1179652
  29.7 31.4 %collective-permute-start.4 = (bf16[256,2048]{1,0:T(8,128)(2,1)}, bf16[256,2048]{1,0:T(8,128)(2,1)S(1)}, u32[]{:S(2)}, u32[]{:S(2)}) collective-permute-start(bf16[256,2048]{1,0:T(8,128)(2,1)} %get-tuple-element.117), channel_id=1, source_target_pairs={{0,2},{2,0},{4,6},{6,4},{8,10},{10,8},{12,14},{14,12},{16,18},{18,... | collective-permute-start | bytes 3145736 | tf_op jit(solution)/shard_map/ppermute | solution.py:333
  30.3 30.8 %collective-permute-start.5 = (bf16[256,2048]{1,0:T(8,128)(2,1)}, bf16[256,2048]{1,0:T(8,128)(2,1)S(1)}, u32[]{:S(2)}, u32[]{:S(2)}) collective-permute-start(bf16[256,2048]{1,0:T(8,128)(2,1)} %get-tuple-element.118), channel_id=1, source_target_pairs={{0,4},{2,6},{4,0},{6,2},{8,12},{10,14},{12,8},{14,10},{16,20},{18,... | collective-permute-start | bytes 3145736 | tf_op jit(solution)/shard_map/ppermute | solution.py:337
  30.8 18.3 %collective-permute-start.6 = (bf16[144,2048]{1,0:T(8,128)(2,1)}, bf16[144,2048]{1,0:T(8,128)(2,1)S(1)}, u32[]{:S(2)}, u32[]{:S(2)}) collective-permute-start(bf16[144,2048]{1,0:T(8,128)(2,1)} %get-tuple-element.119), channel_id=1, source_target_pairs={{0,8},{2,10},{4,12},{6,14},{8,16},{10,18},{12,20},{14,22},{16,24},... | collective-permute-start | bytes 1769480 | tf_op jit(solution)/shard_map/ppermute | solution.py:342
  31.9 29.2 %collective-permute-start.7 = (bf16[144,2048]{1,0:T(8,128)(2,1)}, bf16[144,2048]{1,0:T(8,128)(2,1)S(1)}, u32[]{:S(2)}, u32[]{:S(2)}) collective-permute-start(bf16[144,2048]{1,0:T(8,128)(2,1)} %get-tuple-element.120), channel_id=1, source_target_pairs={{8,0},{10,2},{12,4},{14,6},{16,8},{18,10},{20,12},{22,14},{24,16},... | collective-permute-start | bytes 1769480 | tf_op jit(solution)/shard_map/ppermute | solution.py:347
  40.3 58.6 %all-to-all-start = ((bf16[128,16,128]{2,0,1:T(8,128)(2,1)}), bf16[128,16,128]{2,0,1:T(8,128)(2,1)}, u32[]{:S(2)}, u32[]{:S(2)}) async-start(bf16[128,16,128]{2,0,1:T(8,128)(2,1)} %copy.8), calls=%async_computation | async-start | bytes 1048576 | tf_op jit(solution)/shard_map/all_to_all | solution.py:470
  61.3 22.2 %collective-permute-start.8 = (bf16[192,2048]{1,0:T(8,128)(2,1)S(1)}, bf16[192,2048]{1,0:T(8,128)(2,1)S(1)}, u32[]{:S(2)}, u32[]{:S(2)}) collective-permute-start(bf16[192,2048]{1,0:T(8,128)(2,1)S(1)} %get-tuple-element.125), channel_id=1, source_target_pairs={{0,2},{2,0},{4,6},{6,4},{8,10},{10,8},{12,14},{14,12},{16,18},{18,... | collective-permute-start | bytes 2359304 | tf_op jit(solution)/shard_map/ppermute | solution.py:333
  62.8 20.7 %collective-permute-start.9 = (bf16[192,2048]{1,0:T(8,128)(2,1)S(1)}, bf16[192,2048]{1,0:T(8,128)(2,1)S(1)}, u32[]{:S(2)}, u32[]{:S(2)}) collective-permute-start(bf16[192,2048]{1,0:T(8,128)(2,1)S(1)} %get-tuple-element.126), channel_id=1, source_target_pairs={{0,4},{2,6},{4,0},{6,2},{8,12},{10,14},{12,8},{14,10},{16,20},{18,... | collective-permute-start | bytes 2359304 | tf_op jit(solution)/shard_map/ppermute | solution.py:337
  64.0 15.1 %collective-permute-start.10 = (bf16[80,2048]{1,0:T(8,128)(2,1)S(1)}, bf16[80,2048]{1,0:T(8,128)(2,1)S(1)}, u32[]{:S(2)}, u32[]{:S(2)}) collective-permute-start(bf16[80,2048]{1,0:T(8,128)(2,1)S(1)} %get-tuple-element.127), channel_id=1, source_target_pairs={{0,8},{2,10},{4,12},{6,14},{8,16},{10,18},{12,20},{14,22},{16,24},... | collective-permute-start | bytes 983048 | tf_op jit(solution)/shard_map/ppermute | solution.py:342
  64.5 17.2 %collective-permute-start.11 = (bf16[80,2048]{1,0:T(8,128)(2,1)S(1)}, bf16[80,2048]{1,0:T(8,128)(2,1)S(1)}, u32[]{:S(2)}, u32[]{:S(2)}) collective-permute-start(bf16[80,2048]{1,0:T(8,128)(2,1)S(1)} %get-tuple-element.128), channel_id=1, source_target_pairs={{8,0},{10,2},{12,4},{14,6},{16,8},{18,10},{20,12},{22,14},{24,16},... | collective-permute-start | bytes 983048 | tf_op jit(solution)/shard_map/ppermute | solution.py:347
  75.5 23.3 %collective-permute-start.18 = (bf16[800,384]{1,0:T(8,128)(2,1)}, bf16[800,384]{1,0:T(8,128)(2,1)S(1)}, u32[]{:S(2)}, u32[]{:S(2)}) collective-permute-start(bf16[800,384]{1,0:T(8,128)(2,1)} %convolution_convert_fusion.4), channel_id=1, source_target_pairs={{0,1},{1,0},{2,3},{3,2},{4,5},{5,4},{6,7},{7,6},{8,9},{9,8},{10,11... | collective-permute-start | bytes 1843208 | tf_op jit(solution)/shard_map/ppermute | solution.py:329
  83.6 12.3 %collective-permute-start.12 = (bf16[48,2048]{1,0:T(8,128)(2,1)S(1)}, bf16[48,2048]{1,0:T(8,128)(2,1)S(1)}, u32[]{:S(2)}, u32[]{:S(2)}) collective-permute-start(bf16[48,2048]{1,0:T(8,128)(2,1)S(1)} %get-tuple-element.133), channel_id=1, source_target_pairs={{0,2},{2,0},{4,6},{6,4},{8,10},{10,8},{12,14},{14,12},{16,18},{18,... | collective-permute-start | bytes 589832 | tf_op jit(solution)/shard_map/ppermute | solution.py:333
  84.8 11.2 %collective-permute-start.13 = (bf16[48,2048]{1,0:T(8,128)(2,1)S(1)}, bf16[48,2048]{1,0:T(8,128)(2,1)S(1)}, u32[]{:S(2)}, u32[]{:S(2)}) collective-permute-start(bf16[48,2048]{1,0:T(8,128)(2,1)S(1)} %get-tuple-element.134), channel_id=1, source_target_pairs={{0,4},{2,6},{4,0},{6,2},{8,12},{10,14},{12,8},{14,10},{16,20},{18,... | collective-permute-start | bytes 589832 | tf_op jit(solution)/shard_map/ppermute | solution.py:337
  85.7 9.7 %collective-permute-start.14 = (bf16[16,2048]{1,0:T(8,128)(2,1)S(1)}, bf16[16,2048]{1,0:T(8,128)(2,1)S(1)}, u32[]{:S(2)}, u32[]{:S(2)}) collective-permute-start(bf16[16,2048]{1,0:T(8,128)(2,1)S(1)} %get-tuple-element.135), channel_id=1, source_target_pairs={{0,8},{2,10},{4,12},{6,14},{8,16},{10,18},{12,20},{14,22},{16,24},... | collective-permute-start | bytes 196616 | tf_op jit(solution)/shard_map/ppermute | solution.py:342
  88.0 7.5 %collective-permute-start.15 = (bf16[16,2048]{1,0:T(8,128)(2,1)S(1)}, bf16[16,2048]{1,0:T(8,128)(2,1)S(1)}, u32[]{:S(2)}, u32[]{:S(2)}) collective-permute-start(bf16[16,2048]{1,0:T(8,128)(2,1)S(1)} %get-tuple-element.136), channel_id=1, source_target_pairs={{8,0},{10,2},{12,4},{14,6},{16,8},{18,10},{20,12},{22,14},{24,16},... | collective-permute-start | bytes 196616 | tf_op jit(solution)/shard_map/ppermute | solution.py:347
  95.4 3.5 %collective-permute-start.17 = (bf16[576,384]{1,0:T(8,128)(2,1)}, bf16[576,384]{1,0:T(8,128)(2,1)}, u32[]{:S(2)}, u32[]{:S(2)}) collective-permute-start(bf16[576,384]{1,0:T(8,128)(2,1)} %convolution_convert_fusion.5), channel_id=1, source_target_pairs={{0,1},{1,0},{2,3},{3,2},{4,5},{5,4},{6,7},{7,6},{8,9},{9,8},{10,11... | collective-permute-start | bytes 1327112 | tf_op jit(solution)/shard_map/ppermute | solution.py:329
  95.4 4.3 %collective-permute-start.19 = (bf16[544,384]{1,0:T(8,128)(2,1)}, bf16[544,384]{1,0:T(8,128)(2,1)}, u32[]{:S(2)}, u32[]{:S(2)}) collective-permute-start(bf16[544,384]{1,0:T(8,128)(2,1)} %convolution_convert_fusion.6), channel_id=1, source_target_pairs={{0,1},{1,0},{2,3},{3,2},{4,5},{5,4},{6,7},{7,6},{8,9},{9,8},{10,11... | collective-permute-start | bytes 1253384 | tf_op jit(solution)/shard_map/ppermute | solution.py:329
  98.1 1.6 collective-permute-start.20
  102.0 13.8 %copy-start.17 = (bf16[768,2048]{1,0:T(8,128)(2,1)S(1)}, bf16[768,2048]{1,0:T(8,128)(2,1)}, u32[]{:S(2)}) copy-start(bf16[768,2048]{1,0:T(8,128)(2,1)} %constant_dynamic-update-slice_fusion.18) | copy-start | bytes 9437188
  115.4 2.1 collective-permute-start.21
  117.3 32.8 %copy-start.18 = (bf16[768,2048]{1,0:T(8,128)(2,1)}, bf16[768,2048]{1,0:T(8,128)(2,1)S(1)}, u32[]{:S(2)}) copy-start(bf16[768,2048]{1,0:T(8,128)(2,1)S(1)} %constant_dynamic-update-slice_fusion.17) | copy-start | bytes 9437188
  117.3 9.4 %collective-permute-start.27 = (bf16[640,384]{1,0:T(8,128)(2,1)S(1)}, bf16[640,384]{1,0:T(8,128)(2,1)S(1)}, u32[]{:S(2)}, u32[]{:S(2)}) collective-permute-start(bf16[640,384]{1,0:T(8,128)(2,1)S(1)} %get-tuple-element.160), channel_id=1, source_target_pairs={{0,1},{1,0},{2,3},{3,2},{4,5},{5,4},{6,7},{7,6},{8,9},{9,8},{10,11... | collective-permute-start | bytes 1474568 | tf_op jit(solution)/shard_map/ppermute | solution.py:329
  118.1 8.5 %collective-permute-start.22 = (bf16[128,768]{1,0:T(8,128)(2,1)S(1)}, bf16[128,768]{1,0:T(8,128)(2,1)S(1)}, u32[]{:S(2)}, u32[]{:S(2)}) collective-permute-start(bf16[128,768]{1,0:T(8,128)(2,1)S(1)} %get-tuple-element.150), channel_id=1, source_target_pairs={{0,2},{2,0},{4,6},{6,4},{8,10},{10,8},{12,14},{14,12},{16,18},{18,... | collective-permute-start | bytes 589832 | tf_op jit(solution)/shard_map/ppermute | solution.py:333
  119.2 7.4 %collective-permute-start.23 = (bf16[128,768]{1,0:T(8,128)(2,1)S(1)}, bf16[128,768]{1,0:T(8,128)(2,1)S(1)}, u32[]{:S(2)}, u32[]{:S(2)}) collective-permute-start(bf16[128,768]{1,0:T(8,128)(2,1)S(1)} %get-tuple-element.151), channel_id=1, source_target_pairs={{0,4},{2,6},{4,0},{6,2},{8,12},{10,14},{12,8},{14,10},{16,20},{18,... | collective-permute-start | bytes 589832 | tf_op jit(solution)/shard_map/ppermute | solution.py:337
  120.2 6.4 %collective-permute-start.24 = (bf16[128,256]{1,0:T(8,128)(2,1)S(1)}, bf16[128,256]{1,0:T(8,128)(2,1)S(1)}, u32[]{:S(2)}, u32[]{:S(2)}) collective-permute-start(bf16[128,256]{1,0:T(8,128)(2,1)S(1)} %get-tuple-element.152), channel_id=1, source_target_pairs={{0,8},{2,10},{4,12},{6,14},{8,16},{10,18},{12,20},{14,22},{16,24},... | collective-permute-start | bytes 196616 | tf_op jit(solution)/shard_map/ppermute | solution.py:342
  120.2 6.4 %collective-permute-start.25 = (bf16[128,256]{1,0:T(8,128)(2,1)S(1)}, bf16[128,256]{1,0:T(8,128)(2,1)S(1)}, u32[]{:S(2)}, u32[]{:S(2)}) collective-permute-start(bf16[128,256]{1,0:T(8,128)(2,1)S(1)} %get-tuple-element.153), channel_id=1, source_target_pairs={{8,0},{10,2},{12,4},{14,6},{16,8},{18,10},{20,12},{22,14},{24,16},... | collective-permute-start | bytes 196616 | tf_op jit(solution)/shard_map/ppermute | solution.py:347
  126.6 23.4 %collective-permute-start.26 = (bf16[1280,384]{1,0:T(8,128)(2,1)S(1)}, bf16[1280,384]{1,0:T(8,128)(2,1)S(1)}, u32[]{:S(2)}, u32[]{:S(2)}) collective-permute-start(bf16[1280,384]{1,0:T(8,128)(2,1)S(1)} %get-tuple-element.159), channel_id=1, source_target_pairs={{0,1},{1,0},{2,3},{3,2},{4,5},{5,4},{6,7},{7,6},{8,9},{9,8},{10,11... | collective-permute-start | bytes 2949128 | tf_op jit(solution)/shard_map/ppermute | solution.py:329
  129.2 20.0 %collective-permute-start.28 = (bf16[128,3072]{1,0:T(8,128)(2,1)S(1)}, bf16[128,3072]{1,0:T(8,128)(2,1)S(1)}, u32[]{:S(2)}, u32[]{:S(2)}) collective-permute-start(bf16[128,3072]{1,0:T(8,128)(2,1)S(1)} %get-tuple-element.165), channel_id=1, source_target_pairs={{0,2},{2,0},{4,6},{6,4},{8,10},{10,8},{12,14},{14,12},{16,18},{18,... | collective-permute-start | bytes 2359304 | tf_op jit(solution)/shard_map/ppermute | solution.py:333
  130.3 19.7 %collective-permute-start.29 = (bf16[128,3072]{1,0:T(8,128)(2,1)S(1)}, bf16[128,3072]{1,0:T(8,128)(2,1)S(1)}, u32[]{:S(2)}, u32[]{:S(2)}) collective-permute-start(bf16[128,3072]{1,0:T(8,128)(2,1)S(1)} %get-tuple-element.166), channel_id=1, source_target_pairs={{0,4},{2,6},{4,0},{6,2},{8,12},{10,14},{12,8},{14,10},{16,20},{18,... | collective-permute-start | bytes 2359304 | tf_op jit(solution)/shard_map/ppermute | solution.py:337
  131.3 12.4 %collective-permute-start.30 = (bf16[128,1280]{1,0:T(8,128)(2,1)S(1)}, bf16[128,1280]{1,0:T(8,128)(2,1)S(1)}, u32[]{:S(2)}, u32[]{:S(2)}) collective-permute-start(bf16[128,1280]{1,0:T(8,128)(2,1)S(1)} %get-tuple-element.167), channel_id=1, source_target_pairs={{0,8},{2,10},{4,12},{6,14},{8,16},{10,18},{12,20},{14,22},{16,24},... | collective-permute-start | bytes 983048 | tf_op jit(solution)/shard_map/ppermute | solution.py:342
  131.3 16.6 %collective-permute-start.31 = (bf16[128,1280]{1,0:T(8,128)(2,1)S(1)}, bf16[128,1280]{1,0:T(8,128)(2,1)S(1)}, u32[]{:S(2)}, u32[]{:S(2)}) collective-permute-start(bf16[128,1280]{1,0:T(8,128)(2,1)S(1)} %get-tuple-element.168), channel_id=1, source_target_pairs={{8,0},{10,2},{12,4},{14,6},{16,8},{18,10},{20,12},{22,14},{24,16},... | collective-permute-start | bytes 983048 | tf_op jit(solution)/shard_map/ppermute | solution.py:347
  156.0 31.4 %collective-permute-start.32 = (bf16[128,4096]{1,0:T(8,128)(2,1)}, bf16[128,4096]{1,0:T(8,128)(2,1)}, u32[]{:S(2)}, u32[]{:S(2)}) collective-permute-start(bf16[128,4096]{1,0:T(8,128)(2,1)} %get-tuple-element.178), channel_id=1, source_target_pairs={{0,2},{2,0},{4,6},{6,4},{8,10},{10,8},{12,14},{14,12},{16,18},{18,... | collective-permute-start | bytes 3145736 | tf_op jit(solution)/shard_map/ppermute | solution.py:333
  157.0 30.5 %collective-permute-start.33 = (bf16[128,4096]{1,0:T(8,128)(2,1)}, bf16[128,4096]{1,0:T(8,128)(2,1)}, u32[]{:S(2)}, u32[]{:S(2)}) collective-permute-start(bf16[128,4096]{1,0:T(8,128)(2,1)} %get-tuple-element.179), channel_id=1, source_target_pairs={{0,4},{2,6},{4,0},{6,2},{8,12},{10,14},{12,8},{14,10},{16,20},{18,... | collective-permute-start | bytes 3145736 | tf_op jit(solution)/shard_map/ppermute | solution.py:337
  157.9 18.3 %collective-permute-start.34 = (bf16[128,2304]{1,0:T(8,128)(2,1)}, bf16[128,2304]{1,0:T(8,128)(2,1)S(1)}, u32[]{:S(2)}, u32[]{:S(2)}) collective-permute-start(bf16[128,2304]{1,0:T(8,128)(2,1)} %get-tuple-element.180), channel_id=1, source_target_pairs={{0,8},{2,10},{4,12},{6,14},{8,16},{10,18},{12,20},{14,22},{16,24},... | collective-permute-start | bytes 1769480 | tf_op jit(solution)/shard_map/ppermute | solution.py:342
  158.3 29.2 %collective-permute-start.35 = (bf16[128,2304]{1,0:T(8,128)(2,1)S(1)}, bf16[128,2304]{1,0:T(8,128)(2,1)S(1)}, u32[]{:S(2)}, u32[]{:S(2)}) collective-permute-start(bf16[128,2304]{1,0:T(8,128)(2,1)S(1)} %get-tuple-element.181), channel_id=1, source_target_pairs={{8,0},{10,2},{12,4},{14,6},{16,8},{18,10},{20,12},{22,14},{24,16},... | collective-permute-start | bytes 1769480 | tf_op jit(solution)/shard_map/ppermute | solution.py:347
  161.8 41.5 %all-to-all-start.1 = ((bf16[16,128,128]{2,1,0:T(8,128)(2,1)}), bf16[16,128,128]{2,1,0:T(8,128)(2,1)}, u32[]{:S(2)}, u32[]{:S(2)}) async-start(bf16[16,128,128]{2,1,0:T(8,128)(2,1)} %bitcast.13), calls=%async_computation.1 | async-start | bytes 1048576 | tf_op jit(solution)/shard_map/all_to_all | solution.py:611
  167.3 20.2 %copy-start.1 = (bf16[896,2048]{1,0:T(8,128)(2,1)S(1)}, bf16[896,2048]{1,0:T(8,128)(2,1)}, u32[]{:S(2)}) copy-start(bf16[896,2048]{1,0:T(8,128)(2,1)} %copy-done) | copy-start | bytes 11010052
  190.3 22.2 %collective-permute-start.36 = (bf16[128,2048]{1,0:T(8,128)(2,1)}, bf16[128,2048]{1,0:T(8,128)(2,1)S(1)}, u32[]{:S(2)}, u32[]{:S(2)}) collective-permute-start(bf16[128,2048]{1,0:T(8,128)(2,1)} %get-tuple-element.186), channel_id=1, source_target_pairs={{0,2},{2,0},{4,6},{6,4},{8,10},{10,8},{12,14},{14,12},{16,18},{18,... | collective-permute-start | bytes 1572872 | tf_op jit(solution)/shard_map/ppermute | solution.py:333
  191.4 21.2 %collective-permute-start.37 = (bf16[128,2048]{1,0:T(8,128)(2,1)}, bf16[128,2048]{1,0:T(8,128)(2,1)}, u32[]{:S(2)}, u32[]{:S(2)}) collective-permute-start(bf16[128,2048]{1,0:T(8,128)(2,1)} %get-tuple-element.187), channel_id=1, source_target_pairs={{0,4},{2,6},{4,0},{6,2},{8,12},{10,14},{12,8},{14,10},{16,20},{18,... | collective-permute-start | bytes 1572872 | tf_op jit(solution)/shard_map/ppermute | solution.py:337
  192.0 15.0 %collective-permute-start.38 = (bf16[128,1536]{1,0:T(8,128)(2,1)}, bf16[128,1536]{1,0:T(8,128)(2,1)}, u32[]{:S(2)}, u32[]{:S(2)}) collective-permute-start(bf16[128,1536]{1,0:T(8,128)(2,1)} %get-tuple-element.188), channel_id=1, source_target_pairs={{0,8},{2,10},{4,12},{6,14},{8,16},{10,18},{12,20},{14,22},{16,24},... | collective-permute-start | bytes 1179656 | tf_op jit(solution)/shard_map/ppermute | solution.py:342
  193.4 19.2 %collective-permute-start.39 = (bf16[128,1536]{1,0:T(8,128)(2,1)}, bf16[128,1536]{1,0:T(8,128)(2,1)}, u32[]{:S(2)}, u32[]{:S(2)}) collective-permute-start(bf16[128,1536]{1,0:T(8,128)(2,1)} %get-tuple-element.189), channel_id=1, source_target_pairs={{8,0},{10,2},{12,4},{14,6},{16,8},{18,10},{20,12},{22,14},{24,16},... | collective-permute-start | bytes 1179656 | tf_op jit(solution)/shard_map/ppermute | solution.py:347
  (18 other events, 57.7 us)

commit v4 on v2

--- a/solution.py
+++ b/solution.py
@@ -147,6 +147,7 @@
 
 
 GROUP = 4
+ROWS = 8
 PLANE = 4
 VMEM = 56 * 2**20
 
@@ -224,57 +225,80 @@
 
         lax.fori_loop(0, members, before, 0)
 
-    def at(step):
-        return aligned(step * chunks, chunks)
-
-    zero = jnp.zeros((chunks, width), jnp.float32)
+    sides = range(chunks // ROWS)
     scale = 1.0 / math.sqrt(length)
+
+    def rows_at(step, side):
+        return pl.ds(pl.multiple_of(step * chunks + side * ROWS, ROWS), ROWS)
+
+    def zeros(count):
+        zero = jnp.zeros((ROWS, width), jnp.float32)
+        return tuple((zero,) * len(sides) for _ in range(count))
+
+    def moved_on(states, decays, inputs):
+        return tuple(
+            tuple(decay * state[side] + inputs[side] for side in sides)
+            for decay, state in zip(decays, states)
+        )
+
+    def entered(states, rates, back):
+        whole = [
+            earlier_sum(
+                jnp.concatenate(state, axis=0),
+                jnp.concatenate([rate] * len(sides), axis=0),
+                span,
+                back,
+            )
+            for state, rate in zip(states, rates)
+        ]
+        return tuple(
+            tuple(state[side * ROWS : (side + 1) * ROWS, :] for side in sides) for state in whole
+        )
+
     for first in range(0, modes, GROUP):
         count = min(GROUP, modes - first)
         rates = [
-            jnp.broadcast_to(rate_ref[m : m + 1, :], (chunks, width))
+            jnp.broadcast_to(rate_ref[m : m + 1, :], (ROWS, width))
             for m in range(first, first + count)
         ]
         decays = [jnp.exp(-rate) for rate in rates]
         norms = [jnp.sqrt(2.0 * rate) for rate in rates]
-        gains = [
-            residue_ref[first + n : first + n + 1, :] * norms[n] for n in range(count)
-        ]
+        gains = [residue_ref[first + n : first + n + 1, :] * norms[n] for n in range(count)]
 
         def sums(step, state):
             ahead, behind = state
-            gated = gated_s[at(step), :]
-            slope = slope_s[at(span - 1 - step), :]
-            return (
-                tuple(decays[n] * ahead[n] + gated for n in range(count)),
-                tuple(decays[n] * behind[n] + slope for n in range(count)),
-            )
-
-        ahead, behind = lax.fori_loop(0, span, sums, ((zero,) * count, (zero,) * count), unroll=16)
-        ahead = tuple(earlier_sum(ahead[n], rates[n], span, False) for n in range(count))
-        behind = tuple(earlier_sum(behind[n], rates[n], span, True) for n in range(count))
+            gated = [gated_s[rows_at(step, side), :] for side in sides]
+            slope = [slope_s[rows_at(span - 1 - step, side), :] for side in sides]
+            return moved_on(ahead, decays, gated), moved_on(behind, decays, slope)
+
+        ahead, behind = lax.fori_loop(0, span, sums, (zeros(count), zeros(count)), unroll=16)
+        ahead, behind = entered(ahead, rates, False), entered(behind, rates, True)
 
         def outs(step, state):
             ahead, behind, grads = state
             other = span - 1 - step
-            gated = gated_s[at(step), :]
-            slope = slope_s[at(step), :]
-            slope_back = slope_s[at(other), :]
-            ahead = tuple(decays[n] * ahead[n] + gated for n in range(count))
-            behind = tuple(decays[n] * behind[n] + slope_back for n in range(count))
-            grads = tuple(grads[n] + slope * ahead[n] for n in range(count))
-            conv = added_up(gains[n] * ahead[n] for n in range(count))
-            back = added_up(gains[n] * behind[n] for n in range(count))
-            if first:
-                conv = conv + conv_s[at(step), :]
-                back = back + back_s[at(other), :]
-            conv_s[at(step), :] = conv
-            back_s[at(other), :] = back
+            gated = [gated_s[rows_at(step, side), :] for side in sides]
+            slope = [slope_s[rows_at(step, side), :] for side in sides]
+            slope_back = [slope_s[rows_at(other, side), :] for side in sides]
+            ahead = moved_on(ahead, decays, gated)
+            behind = moved_on(behind, decays, slope_back)
+            grads = tuple(
+                tuple(grad[side] + slope[side] * state[side] for side in sides)
+                for grad, state in zip(grads, ahead)
+            )
+            for side in sides:
+                conv = added_up(gains[n] * ahead[n][side] for n in range(count))
+                back = added_up(gains[n] * behind[n][side] for n in range(count))
+                if first:
+                    conv = conv + conv_s[rows_at(step, side), :]
+                    back = back + back_s[rows_at(other, side), :]
+                conv_s[rows_at(step, side), :] = conv
+                back_s[rows_at(other, side), :] = back
             return ahead, behind, grads
 
-        _, _, grads = lax.fori_loop(0, span, outs, (ahead, behind, (zero,) * count), unroll=8)
+        _, _, grads = lax.fori_loop(0, span, outs, (ahead, behind, zeros(count)), unroll=8)
         for n in range(count):
-            total = jnp.sum(grads[n] * norms[n], axis=0, keepdims=True) * scale
+            total = jnp.sum(added_up(grads[n]) * norms[n], axis=0, keepdims=True) * scale
             grad_ref[first + n : first + n + 1, :] = total
 
     for proj_ref, pieces in zip(proj_refs, order):
@@ -409,6 +433,12 @@
 
 
 def assemble(arrays, *plans):
+    used = sorted({source[0] for plan in plans for piece in plan for source in piece[4]})
+    arrays = [arrays[index] for index in used]
+    plans = [
+        [(*piece[:4], [(used.index(source[0]), *source[1:]) for source in piece[4]]) for piece in plan]
+        for plan in plans
+    ]
     shapes = [
         (max(p[0] + p[2] for p in plan), max(p[1] + p[3] for p in plan)) for plan in plans
     ]
@@ -644,8 +674,8 @@
         start = (group - 1 + side) * wide
         return term(group, 0, side, (x, 0, start), (y, 0, start), *more)
 
-    *sent, base = put(
-            [early, later, own, *third],
+    sent = put(
+        [early, later, own, *third],
             [
                 term(0, 1, 0),
                 term(0, 1, 1, (y, 0, 4 * wide)),
@@ -660,8 +690,11 @@
             ],
             [own_sum(1, 0, (below, 0, 0)), own_sum(1, 1)],
             [own_sum(3, 0), own_sum(3, 1, (above, 0, 0))],
-            [term(0, 0, 0), term(0, 0, 1), low_own(0, 0), low_own(0, 1)],
-        )
+    )
+    (base,) = put(
+        [early, later, own, *third],
+        [term(0, 0, 0), term(0, 0, 1), low_own(0, 0), low_own(0, 1)],
+    )
     (grad_input,) = put(
         [base, *all_ways(*sent)],
         [
@@ -678,7 +711,8 @@
     rows = weights[0].swapaxes(0, 1).reshape(3 * channels, weights.shape[3])
     tokens_half = halves((tokens,), (0, span, True), (0, span * 3 // 4, True))
     kept, given = halves((rows,), (0, 3 * channels, True), (0, 3 * channels, False))
-    taken = swapped(given)
+    count, columns = given.shape
+    (taken,) = assemble([swapped(given)], [(0, 0, count, columns, [(0, 0, 0)])])
     parts, runs, (kept, taken), cot_cols = gather_groups(*tokens_half, (kept, taken), cotangent)
     own, other = zip(*parts)
     hyena, grads, (early, later) = scan_all(

time: 206 us -> 205 us (level)
  waiting for transfers between devices: 74.4 us -> 80.2 us
  matrix products: 29.2 us -> 24.4 us
  Pallas kernels: 27.5 us -> 30.8 us
  starting transfers between devices: 58.9 us -> 55.8 us
    dot_general x8, matrix products: 19.5 us -> 15.3 us  [project(): jnp.einsum('td,rd->tr', rows, matrix, preferred_element_type=jnp.float32)]
    ppermute x8, starting transfers between devices: 8.09 us -> 4.64 us  [up(): lax.ppermute(value, 'ctx', [(i, (i + PLANE) % count) for i in range(count)])]
    ppermute x8, starting transfers between devices: 22.5 us -> 25.9 us  [down(): lax.ppermute(value, 'ctx', [((i + PLANE) % count, i) for i in range(count)])]
    pallas_call x8 -> x10, Pallas kernels: 8.5 us -> 11.7 us  [assemble(): pl.pallas_call(functools.partial(assemble_kernel, len(arrays), plans), ou...]
    ppermute x8, starting transfers between devices: 10.4 us -> 7.84 us  [over_x(): lax.ppermute(value, 'ctx', [(i, i ^ 1) for i in range(lax.axis_size('ctx'...]
    unnamed x62 -> x53, local copies, waits for them, and re-layouts: 6.93 us -> 6.66 us
  transfers between devices with their start and end apart: 41 -> 41, of which waited for: 16 -> 19; matrix products, arithmetic and copies ran while one was open for 19% -> 16% of each run, Pallas kernels for 4% -> 6%
where the time goes in v4:
time: 205 us; the launch traced here: 204 us
  waiting for transfers between devices  80.2 us (39%)
  starting transfers between devices  55.8 us (27%)
  Pallas kernels  30.8 us (15%)
  matrix products  24.4 us (12%)
  local copies, waits for them, and re-layouts  12 us (6%)
    ppermute x8, waiting for transfers between devices, down(): lax.ppermute(value, 'ctx', [((i + PLANE) % count, i) for i in range(count)])  40.9 us
    ppermute x8, waiting for transfers between devices, up(): lax.ppermute(value, 'ctx', [(i, (i + PLANE) % count) for i in range(count)])  31.4 us
    ppermute x8, starting transfers between devices, down(): lax.ppermute(value, 'ctx', [((i + PLANE) % count, i) for i in range(count)])  25.9 us
    dot_general x8, matrix products, project(): jnp.einsum('td,rd->tr', rows, matrix, preferred_element_type=jnp.float32)  15.3 us
    pallas_call x1, Pallas kernels, scan_all(): pl.pallas_call(functools.partial(scan_kernel, PLANE, runs, order), out_sh...  13.4 us
    pallas_call x10, Pallas kernels, assemble(): pl.pallas_call(functools.partial(assemble_kernel, len(arrays), plans), ou...  11.7 us
    dot_general x3, matrix products, product(): return narrowed(jnp.dot(both, matrix, preferred_element_type=jnp.float32))  9.07 us
    ppermute x8, starting transfers between devices, over_x(): lax.ppermute(value, 'ctx', [(i, i ^ 1) for i in range(lax.axis_size('ctx'...  7.84 us
  transfers between devices with their start and end apart: 41, of which 19 were waited for; matrix products, arithmetic and copies ran while one was open for 16% of the time, Pallas kernels for 6%

profile of v4, /device:TPU:0, one launch (start us, length us, event | category | flops | bytes accessed | tf_op | source)
XLA Modules:
  0.0 204.3 jit_solution(8206070155254208028)
XLA Ops:
  0.6 2.2 %halves.2 = (bf16[128,2048]{1,0:T(8,128)(2,1)}, bf16[96,2048]{1,0:T(8,128)(2,1)}) custom-call(s32[1]{0:T(128)} %bitcast.5.core_ref, bf16[128,4096]{1,0:T(8,128)(2,1)} %refs_0_.1), custom_call_target="tpu_custom_call" | custom-call | bytes 1835008 | tf_op jit(solution)/shard_map/halves/pallas_call | solution.py:409
  2.8 3.0 %collective-permute-start.1 = (bf16[128,2048]{1,0:T(8,128)(2,1)}, bf16[128,2048]{1,0:T(8,128)(2,1)S(1)}, u32[]{:S(2)}, u32[]{:S(2)}) collective-permute-start(bf16[128,2048]{1,0:T(8,128)(2,1)} %get-tuple-element.103.refs_0_), channel_id=1, source_target_pairs={{0,4},{2,6},{4,0},{6,2},{8,12},{10,14},{12,8},{14,10},{16,20},{18,... | collective-permute-start | bytes 1572872 | tf_op jit(solution)/shard_map/ppermute | solution.py:361
  5.8 1.5 collective-permute-start
  7.3 3.6 %collective-permute-start.3 = (bf16[96,2048]{1,0:T(8,128)(2,1)}, bf16[96,2048]{1,0:T(8,128)(2,1)S(1)}, u32[]{:S(2)}, u32[]{:S(2)}) collective-permute-start(bf16[96,2048]{1,0:T(8,128)(2,1)} %get-tuple-element.94), channel_id=1, source_target_pairs={{8,0},{10,2},{12,4},{14,6},{16,8},{18,10},{20,12},{22,14},{24,16},... | collective-permute-start | bytes 1179656 | tf_op jit(solution)/shard_map/ppermute | solution.py:371
  10.9 3.5 %halves.3 = (bf16[384,2048]{1,0:T(8,128)(2,1)}, bf16[384,2048]{1,0:T(8,128)(2,1)}) custom-call(s32[1]{0:T(128)} %bitcast.5.core_ref, bf16[384,4096]{1,0:T(8,128)(2,1)} %bitcast.45), custom_call_target="tpu_custom_call" | custom-call | bytes 6291456 | tf_op jit(solution)/shard_map/halves/pallas_call | solution.py:409
  14.6 6.3 %collective-permute-done.3.refs_4_ = bf16[96,2048]{1,0:T(8,128)(2,1)S(1)} collective-permute-done((bf16[96,2048]{1,0:T(8,128)(2,1)}, bf16[96,2048]{1,0:T(8,128)(2,1)S(1)}, u32[]{:S(2)}, u32[]{:S(2)}) %collective-permute-start.3) | collective-permute-done | bytes 393248 | tf_op jit(solution)/shard_map/ppermute | solution.py:371
  20.8 7.4 %collective-permute-done.2.refs_3_ = bf16[96,2048]{1,0:T(8,128)(2,1)S(1)} collective-permute-done((bf16[96,2048]{1,0:T(8,128)(2,1)}, bf16[96,2048]{1,0:T(8,128)(2,1)S(1)}, u32[]{:S(2)}, u32[]{:S(2)}) %collective-permute-start.2) | collective-permute-done | bytes 393248 | tf_op jit(solution)/shard_map/ppermute | solution.py:366
  28.3 2.1 %assemble.10 = (bf16[256,2048]{1,0:T(8,128)(2,1)}, bf16[256,2048]{1,0:T(8,128)(2,1)}, bf16[144,2048]{1,0:T(8,128)(2,1)}, bf16[144,2048]{1,0:T(8,128)(2,1)}) custom-call(bf16[128,2048]{1,0:T(8,128)(2,1)S(1)} %copy-done.4, bf16[128,2048]{1,0:T(8,128)(2,1)S(1)} %collective-permute-done.refs_1_, bf16[128,2048]{1,0:T(8,128)(2,1)S(1)} %collective-permute-done.1.refs_2_, ...), custom_call_target="tpu_custom_call" | custom-call | flops 3276800 | bytes 13107200 | tf_op jit(solution)/shard_map/assemble/pallas_call | solution.py:447
  30.4 1.6 collective-permute-start.6
  32.0 2.2 %collective-permute-start.7 = (bf16[144,2048]{1,0:T(8,128)(2,1)}, bf16[144,2048]{1,0:T(8,128)(2,1)S(1)}, u32[]{:S(2)}, u32[]{:S(2)}) collective-permute-start(bf16[144,2048]{1,0:T(8,128)(2,1)} %get-tuple-element.114), channel_id=1, source_target_pairs={{8,0},{10,2},{12,4},{14,6},{16,8},{18,10},{20,12},{22,14},{24,16},... | collective-permute-start | bytes 1769480 | tf_op jit(solution)/shard_map/ppermute | solution.py:371
  37.7 2.3 %fusion.12.refs_1_ = f32[576,384]{1,0:T(8,128)} fusion(bf16[576,2048]{1,0:T(8,128)(2,1)S(1)} %constant_dynamic-update-slice_fusion, bf16[384,2048]{1,0:T(8,128)(2,1)S(1)} %copy-done.15), kind=kOutput, calls=%fused_computation.37 | convolution fusion | flops 905969664 | bytes 4816896 | tf_op jit(solution)/shard_map/td,rd->tr/dot_general | solution.py:487
  40.0 2.0 copy.8
  42.1 4.3 %all-to-all-start = ((bf16[128,16,128]{2,0,1:T(8,128)(2,1)}), bf16[128,16,128]{2,0,1:T(8,128)(2,1)}, u32[]{:S(2)}, u32[]{:S(2)}) async-start(bf16[128,16,128]{2,0,1:T(8,128)(2,1)} %copy.8), calls=%async_computation | async-start | bytes 1048576 | tf_op jit(solution)/shard_map/all_to_all | solution.py:494
  46.3 2.4 %collective-permute-done.6.refs_2_ = bf16[144,2048]{1,0:T(8,128)(2,1)S(1)} collective-permute-done((bf16[144,2048]{1,0:T(8,128)(2,1)}, bf16[144,2048]{1,0:T(8,128)(2,1)S(1)}, u32[]{:S(2)}, u32[]{:S(2)}) %collective-permute-start.6) | collective-permute-done | bytes 589856 | tf_op jit(solution)/shard_map/ppermute | solution.py:366
  48.7 11.5 %collective-permute-done.7.refs_3_ = bf16[144,2048]{1,0:T(8,128)(2,1)S(1)} collective-permute-done((bf16[144,2048]{1,0:T(8,128)(2,1)}, bf16[144,2048]{1,0:T(8,128)(2,1)S(1)}, u32[]{:S(2)}, u32[]{:S(2)}) %collective-permute-start.7) | collective-permute-done | bytes 589856 | tf_op jit(solution)/shard_map/ppermute | solution.py:371
  60.9 3.3 %collective-permute-start.11 = (bf16[80,2048]{1,0:T(8,128)(2,1)S(1)}, bf16[80,2048]{1,0:T(8,128)(2,1)S(1)}, u32[]{:S(2)}, u32[]{:S(2)}) collective-permute-start(bf16[80,2048]{1,0:T(8,128)(2,1)S(1)} %get-tuple-element.122), channel_id=1, source_target_pairs={{8,0},{10,2},{12,4},{14,6},{16,8},{18,10},{20,12},{22,14},{24,16},... | collective-permute-start | bytes 983048 | tf_op jit(solution)/shard_map/ppermute | solution.py:371
  66.9 1.9 fusion.13.refs_2_
  68.8 1.7 assemble.13
  70.9 2.2 %convolution_convert_fusion.4 = bf16[576,384]{1,0:T(8,128)(2,1)} fusion(bf16[576,2048]{1,0:T(8,128)(2,1)S(1)} %copy-done.19, bf16[384,2048]{1,0:T(8,128)(2,1)S(1)} %assemble.13), kind=kOutput, calls=%fused_computation.8 | convolution fusion | flops 906190848 | bytes 4374528 | tf_op jit(solution)/shard_map/td,rd->tr/dot_general | solution.py:487
  73.1 2.7 %convolution_convert_fusion.3 = bf16[800,384]{1,0:T(8,128)(2,1)} fusion(bf16[800,2048]{1,0:T(8,128)(2,1)S(1)} %constant_dynamic-update-slice_fusion.5, bf16[384,2048]{1,0:T(8,128)(2,1)S(1)} %assemble.13), kind=kOutput, calls=%fused_computation.7 | convolution fusion | flops 1258598400 | bytes 5464064 | tf_op jit(solution)/shard_map/td,rd->tr/dot_general | solution.py:487
  76.8 3.8 %collective-permute-done.11.refs_3_ = bf16[80,2048]{1,0:T(8,128)(2,1)S(1)} collective-permute-done((bf16[80,2048]{1,0:T(8,128)(2,1)S(1)}, bf16[80,2048]{1,0:T(8,128)(2,1)S(1)}, u32[]{:S(2)}, u32[]{:S(2)}) %collective-permute-start.11) | collective-permute-done | bytes 327712 | tf_op jit(solution)/shard_map/ppermute | solution.py:371
  80.6 3.1 %collective-permute-done.8.refs_0_ = bf16[192,2048]{1,0:T(8,128)(2,1)S(1)} collective-permute-done((bf16[192,2048]{1,0:T(8,128)(2,1)S(1)}, bf16[192,2048]{1,0:T(8,128)(2,1)S(1)}, u32[]{:S(2)}, u32[]{:S(2)}) %collective-permute-start.8) | collective-permute-done | bytes 786464 | tf_op jit(solution)/shard_map/ppermute | solution.py:357
  84.0 3.8 %collective-permute-start.15 = (bf16[16,2048]{1,0:T(8,128)(2,1)S(1)}, bf16[16,2048]{1,0:T(8,128)(2,1)S(1)}, u32[]{:S(2)}, u32[]{:S(2)}) collective-permute-start(bf16[16,2048]{1,0:T(8,128)(2,1)S(1)} %get-tuple-element.130), channel_id=1, source_target_pairs={{8,0},{10,2},{12,4},{14,6},{16,8},{18,10},{20,12},{22,14},{24,16},... | collective-permute-start | bytes 196616 | tf_op jit(solution)/shard_map/ppermute | solution.py:371
  89.0 2.1 %convolution_convert_fusion.5 = bf16[544,384]{1,0:T(8,128)(2,1)} fusion(bf16[544,2048]{1,0:T(8,128)(2,1)S(1)} %constant_dynamic-update-slice_fusion.9, bf16[384,2048]{1,0:T(8,128)(2,1)S(1)} %assemble.13), kind=kOutput, calls=%fused_computation.9 | convolution fusion | flops 855846912 | bytes 4218880 | tf_op jit(solution)/shard_map/td,rd->tr/dot_general | solution.py:487
  91.1 2.3 %fusion.14.refs_3_ = f32[544,384]{1,0:T(8,128)} fusion(bf16[544,2048]{1,0:T(8,128)(2,1)S(1)} %constant_dynamic-update-slice_fusion.9, bf16[384,2048]{1,0:T(8,128)(2,1)S(1)} %copy-done.16), kind=kOutput, calls=%fused_computation.39 | convolution fusion | flops 855638016 | bytes 4636672 | tf_op jit(solution)/shard_map/td,rd->tr/dot_general | solution.py:487
  99.5 13.4 %modal_scan.1 = (bf16[2048,128]{1,0:T(8,128)(2,1)}, f32[16,128]{1,0:T(8,128)}, bf16[768,384]{1,0:T(8,128)(2,1)S(1)}, bf16[1280,384]{1,0:T(8,128)(2,1)S(1)}) custom-call(s32[1]{0:T(128)} %bitcast.me_ref, f32[16,128]{1,0:T(8,128)S(1)} %bitcast.43, f32[16,128]{1,0:T(8,128)S(1)} %bitcast.44, bf16[2048,128]{1,0:T(8,128)(2,1)} %bitcast.12.refs_0_, ...), custom_call_target="tpu_custom_call" | custom-call | tf_op jit(solution)/shard_map/modal_scan/pallas_call | solution.py:332
  113.4 1.5 collective-permute-done.21
  114.9 2.8 %convolution_convert_fusion.1.refs_0_ = bf16[768,2048]{1,0:T(8,128)(2,1)S(1)} fusion(bf16[768,384]{1,0:T(8,128)(2,1)S(1)} %collective-permute-done.21, bf16[768,384]{1,0:T(8,128)(2,1)S(1)} %get-tuple-element.138, bf16[384,2048]{1,0:T(8,128)(2,1)S(1)} %assemble.13, bf16[384,2048]{1,0:T(8,128)(2,1)S(1)} %copy-done.17), kind=kOutput, calls=%fused_computation.1 | convolution fusion | flops 2426142720 | bytes 7471104 | tf_op jit(solution)/shard_map/dot_general | solution.py:597
  119.0 1.4 collective-permute-start.23
  120.4 3.8 %collective-permute-start.25 = (bf16[128,256]{1,0:T(8,128)(2,1)S(1)}, bf16[128,256]{1,0:T(8,128)(2,1)S(1)}, u32[]{:S(2)}, u32[]{:S(2)}) collective-permute-start(bf16[128,256]{1,0:T(8,128)(2,1)S(1)} %get-tuple-element.142), channel_id=1, source_target_pairs={{8,0},{10,2},{12,4},{14,6},{16,8},{18,10},{20,12},{22,14},{24,16},... | collective-permute-start | bytes 196616 | tf_op jit(solution)/shard_map/ppermute | solution.py:371
  124.2 2.3 %collective-permute-done.24.refs_3_ = bf16[128,256]{1,0:T(8,128)(2,1)S(1)} collective-permute-done((bf16[128,256]{1,0:T(8,128)(2,1)S(1)}, bf16[128,256]{1,0:T(8,128)(2,1)S(1)}, u32[]{:S(2)}, u32[]{:S(2)}) %collective-permute-start.24) | collective-permute-done | bytes 65568 | tf_op jit(solution)/shard_map/ppermute | solution.py:366
  128.5 3.8 %collective-permute-start.30 = (bf16[128,1280]{1,0:T(8,128)(2,1)S(1)}, bf16[128,1280]{1,0:T(8,128)(2,1)S(1)}, u32[]{:S(2)}, u32[]{:S(2)}) collective-permute-start(bf16[128,1280]{1,0:T(8,128)(2,1)S(1)} %get-tuple-element.156), channel_id=1, source_target_pairs={{8,0},{10,2},{12,4},{14,6},{16,8},{18,10},{20,12},{22,14},{24,16},... | collective-permute-start | bytes 983048 | tf_op jit(solution)/shard_map/ppermute | solution.py:371
  132.4 3.2 %convolution_convert_fusion.refs_1_.refs_0_ = bf16[896,2048]{1,0:T(8,128)(2,1)S(1)} fusion(bf16[896,384]{1,0:T(8,128)(2,1)S(1)} %slice.17, bf16[896,384]{1,0:T(8,128)(2,1)S(1)} %slice.14, bf16[384,2048]{1,0:T(8,128)(2,1)S(1)} %assemble.13, bf16[384,2048]{1,0:T(8,128)(2,1)S(1)} %copy-done.17), kind=kOutput, calls=%fused_computation | convolution fusion | flops 2829451264 | bytes 8192000 | tf_op jit(solution)/shard_map/dot_general | solution.py:597
  135.6 5.3 %collective-permute-done.29.refs_4_ = bf16[128,1280]{1,0:T(8,128)(2,1)S(1)} collective-permute-done((bf16[128,1280]{1,0:T(8,128)(2,1)S(1)}, bf16[128,1280]{1,0:T(8,128)(2,1)S(1)}, u32[]{:S(2)}, u32[]{:S(2)}) %collective-permute-start.29) | collective-permute-done | bytes 327712 | tf_op jit(solution)/shard_map/ppermute | solution.py:366
  140.9 2.7 %collective-permute-done.30.refs_5_ = bf16[128,1280]{1,0:T(8,128)(2,1)S(1)} collective-permute-done((bf16[128,1280]{1,0:T(8,128)(2,1)S(1)}, bf16[128,1280]{1,0:T(8,128)(2,1)S(1)}, u32[]{:S(2)}, u32[]{:S(2)}) %collective-permute-start.30) | collective-permute-done | bytes 327712 | tf_op jit(solution)/shard_map/ppermute | solution.py:371
  145.4 1.8 assemble.16
  149.8 3.4 %collective-permute-start.34 = (bf16[128,2304]{1,0:T(8,128)(2,1)}, bf16[128,2304]{1,0:T(8,128)(2,1)}, u32[]{:S(2)}, u32[]{:S(2)}) collective-permute-start(bf16[128,2304]{1,0:T(8,128)(2,1)} %get-tuple-element.169), channel_id=1, source_target_pairs={{8,0},{10,2},{12,4},{14,6},{16,8},{18,10},{20,12},{22,14},{24,16},... | collective-permute-start | bytes 1769480 | tf_op jit(solution)/shard_map/ppermute | solution.py:371
  153.2 4.2 %all-to-all-start.1 = ((bf16[16,128,128]{2,1,0:T(8,128)(2,1)}), bf16[16,128,128]{2,1,0:T(8,128)(2,1)}, u32[]{:S(2)}, u32[]{:S(2)}) async-start(bf16[16,128,128]{2,1,0:T(8,128)(2,1)} %bitcast.13), calls=%async_computation.1 | async-start | bytes 1048576 | tf_op jit(solution)/shard_map/all_to_all | solution.py:629
  158.5 3.0 %convolution_convert_fusion.2.refs_0_.refs_1_ = bf16[384,2048]{1,0:T(8,128)(2,1)S(1)} fusion(bf16[384,2048]{1,0:T(8,128)(2,1)S(1)} %assemble.13, bf16[384,2048]{1,0:T(8,128)(2,1)} %get-tuple-element.108, bf16[384,384]{1,0:T(8,128)(2,1)S(1)} %slice.16, bf16[384,384]{1,0:T(8,128)(2,1)S(1)} %slice.12), kind=kOutput, calls=%fused_computation.3 | convolution fusion | flops 1216217088 | bytes 5308416 | tf_op jit(solution)/shard_map/dot_general | solution.py:597
  161.5 6.3 %collective-permute-done.33.refs_1_.refs_4_ = bf16[128,2304]{1,0:T(8,128)(2,1)} collective-permute-done((bf16[128,2304]{1,0:T(8,128)(2,1)}, bf16[128,2304]{1,0:T(8,128)(2,1)}, u32[]{:S(2)}, u32[]{:S(2)}) %collective-permute-start.33) | collective-permute-done | bytes 589856 | tf_op jit(solution)/shard_map/ppermute | solution.py:366
  167.8 10.0 %collective-permute-done.34.refs_2_.refs_5_ = bf16[128,2304]{1,0:T(8,128)(2,1)} collective-permute-done((bf16[128,2304]{1,0:T(8,128)(2,1)}, bf16[128,2304]{1,0:T(8,128)(2,1)}, u32[]{:S(2)}, u32[]{:S(2)}) %collective-permute-start.34) | collective-permute-done | bytes 589856 | tf_op jit(solution)/shard_map/ppermute | solution.py:371
  177.8 3.2 %assemble.18 = (bf16[128,2048]{1,0:T(8,128)(2,1)}, bf16[128,2048]{1,0:T(8,128)(2,1)}, bf16[128,1536]{1,0:T(8,128)(2,1)}, bf16[128,1536]{1,0:T(8,128)(2,1)}) custom-call(bf16[896,2048]{1,0:T(8,128)(2,1)S(1)} %copy-done.1, bf16[384,2048]{1,0:T(8,128)(2,1)S(1)} %convolution_convert_fusion.2.refs_0_.refs_1_, bf16[128,4096]{1,0:T(8,128)(2,1)} %collective-permute-done.31.refs_2_, ...), custom_call_target="tpu_custom_call" | custom-call | flops 1835008 | bytes 7340032 | tf_op jit(solution)/shard_map/assemble/pallas_call | solution.py:447
  182.5 1.9 collective-permute-start.37
  184.4 1.9 collective-permute-start.38
  186.3 2.0 copy.9
  188.4 1.3 assemble.17.refs_0_
  189.7 6.9 %collective-permute-done.37.refs_3_ = bf16[128,1536]{1,0:T(8,128)(2,1)S(1)} collective-permute-done((bf16[128,1536]{1,0:T(8,128)(2,1)}, bf16[128,1536]{1,0:T(8,128)(2,1)S(1)}, u32[]{:S(2)}, u32[]{:S(2)}) %collective-permute-start.37) | collective-permute-done | bytes 393248 | tf_op jit(solution)/shard_map/ppermute | solution.py:366
  196.6 6.7 %collective-permute-done.38.refs_4_ = bf16[128,1536]{1,0:T(8,128)(2,1)S(1)} collective-permute-done((bf16[128,1536]{1,0:T(8,128)(2,1)}, bf16[128,1536]{1,0:T(8,128)(2,1)S(1)}, u32[]{:S(2)}, u32[]{:S(2)}) %collective-permute-start.38) | collective-permute-done | bytes 393248 | tf_op jit(solution)/shard_map/ppermute | solution.py:371
  (121 shorter events, 27.4 us)
Async XLA Ops:
  2.8 25.4 %copy-start.4 = (bf16[128,2048]{1,0:T(8,128)(2,1)S(1)}, bf16[128,2048]{1,0:T(8,128)(2,1)}, u32[]{:S(2)}) copy-start(bf16[128,2048]{1,0:T(8,128)(2,1)} %get-tuple-element.103.refs_0_) | copy-start | bytes 1572868
  2.8 25.4 %collective-permute-start.1 = (bf16[128,2048]{1,0:T(8,128)(2,1)}, bf16[128,2048]{1,0:T(8,128)(2,1)S(1)}, u32[]{:S(2)}, u32[]{:S(2)}) collective-permute-start(bf16[128,2048]{1,0:T(8,128)(2,1)} %get-tuple-element.103.refs_0_), channel_id=1, source_target_pairs={{0,4},{2,6},{4,0},{6,2},{8,12},{10,14},{12,8},{14,10},{16,20},{18,... | collective-permute-start | bytes 1572872 | tf_op jit(solution)/shard_map/ppermute | solution.py:361
  5.8 22.4 %collective-permute-start = (bf16[128,2048]{1,0:T(8,128)(2,1)}, bf16[128,2048]{1,0:T(8,128)(2,1)S(1)}, u32[]{:S(2)}, u32[]{:S(2)}) collective-permute-start(bf16[128,2048]{1,0:T(8,128)(2,1)} %get-tuple-element.103.refs_0_), channel_id=1, source_target_pairs={{0,2},{2,0},{4,6},{6,4},{8,10},{10,8},{12,14},{14,12},{16,18},{18,... | collective-permute-start | bytes 1572872 | tf_op jit(solution)/shard_map/ppermute | solution.py:357
  7.3 13.5 %collective-permute-start.3 = (bf16[96,2048]{1,0:T(8,128)(2,1)}, bf16[96,2048]{1,0:T(8,128)(2,1)S(1)}, u32[]{:S(2)}, u32[]{:S(2)}) collective-permute-start(bf16[96,2048]{1,0:T(8,128)(2,1)} %get-tuple-element.94), channel_id=1, source_target_pairs={{8,0},{10,2},{12,4},{14,6},{16,8},{18,10},{20,12},{22,14},{24,16},... | collective-permute-start | bytes 1179656 | tf_op jit(solution)/shard_map/ppermute | solution.py:371
  10.9 17.3 %collective-permute-start.2 = (bf16[96,2048]{1,0:T(8,128)(2,1)}, bf16[96,2048]{1,0:T(8,128)(2,1)S(1)}, u32[]{:S(2)}, u32[]{:S(2)}) collective-permute-start(bf16[96,2048]{1,0:T(8,128)(2,1)} %get-tuple-element.94), channel_id=1, source_target_pairs={{0,8},{2,10},{4,12},{6,14},{8,16},{10,18},{12,20},{14,22},{16,24},... | collective-permute-start | bytes 1179656 | tf_op jit(solution)/shard_map/ppermute | solution.py:366
  14.5 54.3 %collective-permute-start.16 = (bf16[384,2048]{1,0:T(8,128)(2,1)}, bf16[384,2048]{1,0:T(8,128)(2,1)}, u32[]{:S(2)}, u32[]{:S(2)}) collective-permute-start(bf16[384,2048]{1,0:T(8,128)(2,1)} %get-tuple-element.135), channel_id=1, source_target_pairs={{0,1},{1,0},{2,3},{3,2},{4,5},{5,4},{6,7},{7,6},{8,9},{9,8},{10,11... | collective-permute-start | bytes 4718600 | tf_op jit(solution)/shard_map/ppermute | solution.py:353
  20.8 13.4 %copy-start.6 = (bf16[96,2048]{1,0:T(8,128)(2,1)}, bf16[96,2048]{1,0:T(8,128)(2,1)S(1)}, u32[]{:S(2)}) copy-start(bf16[96,2048]{1,0:T(8,128)(2,1)S(1)} %collective-permute-done.3.refs_4_) | copy-start | bytes 1179652
  30.4 7.2 %copy-start.9 = (bf16[96,2048]{1,0:T(8,128)(2,1)S(1)}, bf16[96,2048]{1,0:T(8,128)(2,1)}, u32[]{:S(2)}) copy-start(bf16[96,2048]{1,0:T(8,128)(2,1)} %copy-done.8) | copy-start | bytes 1179652
  30.4 18.3 %collective-permute-start.6 = (bf16[144,2048]{1,0:T(8,128)(2,1)}, bf16[144,2048]{1,0:T(8,128)(2,1)S(1)}, u32[]{:S(2)}, u32[]{:S(2)}) collective-permute-start(bf16[144,2048]{1,0:T(8,128)(2,1)} %get-tuple-element.113), channel_id=1, source_target_pairs={{0,8},{2,10},{4,12},{6,14},{8,16},{10,18},{12,20},{14,22},{16,24},... | collective-permute-start | bytes 1769480 | tf_op jit(solution)/shard_map/ppermute | solution.py:366
  32.0 28.2 %collective-permute-start.7 = (bf16[144,2048]{1,0:T(8,128)(2,1)}, bf16[144,2048]{1,0:T(8,128)(2,1)S(1)}, u32[]{:S(2)}, u32[]{:S(2)}) collective-permute-start(bf16[144,2048]{1,0:T(8,128)(2,1)} %get-tuple-element.114), channel_id=1, source_target_pairs={{8,0},{10,2},{12,4},{14,6},{16,8},{18,10},{20,12},{22,14},{24,16},... | collective-permute-start | bytes 1769480 | tf_op jit(solution)/shard_map/ppermute | solution.py:371
  34.3 26.0 %collective-permute-start.4 = (bf16[256,2048]{1,0:T(8,128)(2,1)}, bf16[256,2048]{1,0:T(8,128)(2,1)S(1)}, u32[]{:S(2)}, u32[]{:S(2)}) collective-permute-start(bf16[256,2048]{1,0:T(8,128)(2,1)} %get-tuple-element.111), channel_id=1, source_target_pairs={{0,2},{2,0},{4,6},{6,4},{8,10},{10,8},{12,14},{14,12},{16,18},{18,... | collective-permute-start | bytes 3145736 | tf_op jit(solution)/shard_map/ppermute | solution.py:357
  34.9 25.4 %collective-permute-start.5 = (bf16[256,2048]{1,0:T(8,128)(2,1)}, bf16[256,2048]{1,0:T(8,128)(2,1)S(1)}, u32[]{:S(2)}, u32[]{:S(2)}) collective-permute-start(bf16[256,2048]{1,0:T(8,128)(2,1)} %get-tuple-element.112), channel_id=1, source_target_pairs={{0,4},{2,6},{4,0},{6,2},{8,12},{10,14},{12,8},{14,10},{16,20},{18,... | collective-permute-start | bytes 3145736 | tf_op jit(solution)/shard_map/ppermute | solution.py:361
  42.1 54.2 %all-to-all-start = ((bf16[128,16,128]{2,0,1:T(8,128)(2,1)}), bf16[128,16,128]{2,0,1:T(8,128)(2,1)}, u32[]{:S(2)}, u32[]{:S(2)}) async-start(bf16[128,16,128]{2,0,1:T(8,128)(2,1)} %copy.8), calls=%async_computation | async-start | bytes 1048576 | tf_op jit(solution)/shard_map/all_to_all | solution.py:494
  60.4 16.4 %collective-permute-start.10 = (bf16[80,2048]{1,0:T(8,128)(2,1)S(1)}, bf16[80,2048]{1,0:T(8,128)(2,1)S(1)}, u32[]{:S(2)}, u32[]{:S(2)}) collective-permute-start(bf16[80,2048]{1,0:T(8,128)(2,1)S(1)} %get-tuple-element.121), channel_id=1, source_target_pairs={{0,8},{2,10},{4,12},{6,14},{8,16},{10,18},{12,20},{14,22},{16,24},... | collective-permute-start | bytes 983048 | tf_op jit(solution)/shard_map/ppermute | solution.py:366
  60.9 19.7 %collective-permute-start.11 = (bf16[80,2048]{1,0:T(8,128)(2,1)S(1)}, bf16[80,2048]{1,0:T(8,128)(2,1)S(1)}, u32[]{:S(2)}, u32[]{:S(2)}) collective-permute-start(bf16[80,2048]{1,0:T(8,128)(2,1)S(1)} %get-tuple-element.122), channel_id=1, source_target_pairs={{8,0},{10,2},{12,4},{14,6},{16,8},{18,10},{20,12},{22,14},{24,16},... | collective-permute-start | bytes 983048 | tf_op jit(solution)/shard_map/ppermute | solution.py:371
  64.3 19.5 %collective-permute-start.8 = (bf16[192,2048]{1,0:T(8,128)(2,1)S(1)}, bf16[192,2048]{1,0:T(8,128)(2,1)S(1)}, u32[]{:S(2)}, u32[]{:S(2)}) collective-permute-start(bf16[192,2048]{1,0:T(8,128)(2,1)S(1)} %get-tuple-element.119), channel_id=1, source_target_pairs={{0,2},{2,0},{4,6},{6,4},{8,10},{10,8},{12,14},{14,12},{16,18},{18,... | collective-permute-start | bytes 2359304 | tf_op jit(solution)/shard_map/ppermute | solution.py:357
  64.9 18.8 %collective-permute-start.9 = (bf16[192,2048]{1,0:T(8,128)(2,1)S(1)}, bf16[192,2048]{1,0:T(8,128)(2,1)S(1)}, u32[]{:S(2)}, u32[]{:S(2)}) collective-permute-start(bf16[192,2048]{1,0:T(8,128)(2,1)S(1)} %get-tuple-element.120), channel_id=1, source_target_pairs={{0,4},{2,6},{4,0},{6,2},{8,12},{10,14},{12,8},{14,10},{16,20},{18,... | collective-permute-start | bytes 2359304 | tf_op jit(solution)/shard_map/ppermute | solution.py:361
  73.1 23.2 %collective-permute-start.17 = (bf16[576,384]{1,0:T(8,128)(2,1)}, bf16[576,384]{1,0:T(8,128)(2,1)S(1)}, u32[]{:S(2)}, u32[]{:S(2)}) collective-permute-start(bf16[576,384]{1,0:T(8,128)(2,1)} %convolution_convert_fusion.4), channel_id=1, source_target_pairs={{0,1},{1,0},{2,3},{3,2},{4,5},{5,4},{6,7},{7,6},{8,9},{9,8},{10,11... | collective-permute-start | bytes 1327112 | tf_op jit(solution)/shard_map/ppermute | solution.py:353
  83.9 9.5 %collective-permute-start.14 = (bf16[16,2048]{1,0:T(8,128)(2,1)S(1)}, bf16[16,2048]{1,0:T(8,128)(2,1)S(1)}, u32[]{:S(2)}, u32[]{:S(2)}) collective-permute-start(bf16[16,2048]{1,0:T(8,128)(2,1)S(1)} %get-tuple-element.129), channel_id=1, source_target_pairs={{0,8},{2,10},{4,12},{6,14},{8,16},{10,18},{12,20},{14,22},{16,24},... | collective-permute-start | bytes 196616 | tf_op jit(solution)/shard_map/ppermute | solution.py:366
  84.0 9.4 %collective-permute-start.15 = (bf16[16,2048]{1,0:T(8,128)(2,1)S(1)}, bf16[16,2048]{1,0:T(8,128)(2,1)S(1)}, u32[]{:S(2)}, u32[]{:S(2)}) collective-permute-start(bf16[16,2048]{1,0:T(8,128)(2,1)S(1)} %get-tuple-element.130), channel_id=1, source_target_pairs={{8,0},{10,2},{12,4},{14,6},{16,8},{18,10},{20,12},{22,14},{24,16},... | collective-permute-start | bytes 196616 | tf_op jit(solution)/shard_map/ppermute | solution.py:371
  87.7 6.1 %collective-permute-start.12 = (bf16[48,2048]{1,0:T(8,128)(2,1)S(1)}, bf16[48,2048]{1,0:T(8,128)(2,1)S(1)}, u32[]{:S(2)}, u32[]{:S(2)}) collective-permute-start(bf16[48,2048]{1,0:T(8,128)(2,1)S(1)} %get-tuple-element.127), channel_id=1, source_target_pairs={{0,2},{2,0},{4,6},{6,4},{8,10},{10,8},{12,14},{14,12},{16,18},{18,... | collective-permute-start | bytes 589832 | tf_op jit(solution)/shard_map/ppermute | solution.py:357
  88.7 5.7 %collective-permute-start.13 = (bf16[48,2048]{1,0:T(8,128)(2,1)S(1)}, bf16[48,2048]{1,0:T(8,128)(2,1)S(1)}, u32[]{:S(2)}, u32[]{:S(2)}) collective-permute-start(bf16[48,2048]{1,0:T(8,128)(2,1)S(1)} %get-tuple-element.128), channel_id=1, source_target_pairs={{0,4},{2,6},{4,0},{6,2},{8,12},{10,14},{12,8},{14,10},{16,20},{18,... | collective-permute-start | bytes 589832 | tf_op jit(solution)/shard_map/ppermute | solution.py:361
  93.3 3.0 %collective-permute-start.18 = (bf16[800,384]{1,0:T(8,128)(2,1)}, bf16[800,384]{1,0:T(8,128)(2,1)}, u32[]{:S(2)}, u32[]{:S(2)}) collective-permute-start(bf16[800,384]{1,0:T(8,128)(2,1)} %convolution_convert_fusion.3), channel_id=1, source_target_pairs={{0,1},{1,0},{2,3},{3,2},{4,5},{5,4},{6,7},{7,6},{8,9},{9,8},{10,11... | collective-permute-start | bytes 1843208 | tf_op jit(solution)/shard_map/ppermute | solution.py:353
  93.4 3.8 %collective-permute-start.19 = (bf16[544,384]{1,0:T(8,128)(2,1)}, bf16[544,384]{1,0:T(8,128)(2,1)}, u32[]{:S(2)}, u32[]{:S(2)}) collective-permute-start(bf16[544,384]{1,0:T(8,128)(2,1)} %convolution_convert_fusion.5), channel_id=1, source_target_pairs={{0,1},{1,0},{2,3},{3,2},{4,5},{5,4},{6,7},{7,6},{8,9},{9,8},{10,11... | collective-permute-start | bytes 1253384 | tf_op jit(solution)/shard_map/ppermute | solution.py:353
  95.7 1.5 collective-permute-start.20
  99.5 15.4 %copy-start.17 = (bf16[384,2048]{1,0:T(8,128)(2,1)S(1)}, bf16[384,2048]{1,0:T(8,128)(2,1)}, u32[]{:S(2)}) copy-start(bf16[384,2048]{1,0:T(8,128)(2,1)} %get-tuple-element.108) | copy-start | bytes 4718596
  112.9 15.4 %copy-start.10 = (bf16[1280,384]{1,0:T(8,128)(2,1)}, bf16[1280,384]{1,0:T(8,128)(2,1)S(1)}, u32[]{:S(2)}) copy-start(bf16[1280,384]{1,0:T(8,128)(2,1)S(1)} %get-tuple-element.148) | copy-start | bytes 2949124
  112.9 2.0 collective-permute-start.21
  113.0 19.3 %collective-permute-start.26 = (bf16[1280,384]{1,0:T(8,128)(2,1)S(1)}, bf16[1280,384]{1,0:T(8,128)(2,1)S(1)}, u32[]{:S(2)}, u32[]{:S(2)}) collective-permute-start(bf16[1280,384]{1,0:T(8,128)(2,1)S(1)} %get-tuple-element.148), channel_id=1, source_target_pairs={{0,1},{1,0},{2,3},{3,2},{4,5},{5,4},{6,7},{7,6},{8,9},{9,8},{10,11... | collective-permute-start | bytes 2949128 | tf_op jit(solution)/shard_map/ppermute | solution.py:353
  117.8 8.7 %collective-permute-start.22 = (bf16[128,768]{1,0:T(8,128)(2,1)S(1)}, bf16[128,768]{1,0:T(8,128)(2,1)S(1)}, u32[]{:S(2)}, u32[]{:S(2)}) collective-permute-start(bf16[128,768]{1,0:T(8,128)(2,1)S(1)} %get-tuple-element.139), channel_id=1, source_target_pairs={{0,2},{2,0},{4,6},{6,4},{8,10},{10,8},{12,14},{14,12},{16,18},{18,... | collective-permute-start | bytes 589832 | tf_op jit(solution)/shard_map/ppermute | solution.py:357
  119.0 7.5 %collective-permute-start.23 = (bf16[128,768]{1,0:T(8,128)(2,1)S(1)}, bf16[128,768]{1,0:T(8,128)(2,1)S(1)}, u32[]{:S(2)}, u32[]{:S(2)}) collective-permute-start(bf16[128,768]{1,0:T(8,128)(2,1)S(1)} %get-tuple-element.140), channel_id=1, source_target_pairs={{0,4},{2,6},{4,0},{6,2},{8,12},{10,14},{12,8},{14,10},{16,20},{18,... | collective-permute-start | bytes 589832 | tf_op jit(solution)/shard_map/ppermute | solution.py:361
  120.4 6.1 %collective-permute-start.24 = (bf16[128,256]{1,0:T(8,128)(2,1)S(1)}, bf16[128,256]{1,0:T(8,128)(2,1)S(1)}, u32[]{:S(2)}, u32[]{:S(2)}) collective-permute-start(bf16[128,256]{1,0:T(8,128)(2,1)S(1)} %get-tuple-element.141), channel_id=1, source_target_pairs={{0,8},{2,10},{4,12},{6,14},{8,16},{10,18},{12,20},{14,22},{16,24},... | collective-permute-start | bytes 196616 | tf_op jit(solution)/shard_map/ppermute | solution.py:366
  120.4 6.1 %collective-permute-start.25 = (bf16[128,256]{1,0:T(8,128)(2,1)S(1)}, bf16[128,256]{1,0:T(8,128)(2,1)S(1)}, u32[]{:S(2)}, u32[]{:S(2)}) collective-permute-start(bf16[128,256]{1,0:T(8,128)(2,1)S(1)} %get-tuple-element.142), channel_id=1, source_target_pairs={{8,0},{10,2},{12,4},{14,6},{16,8},{18,10},{20,12},{22,14},{24,16},... | collective-permute-start | bytes 196616 | tf_op jit(solution)/shard_map/ppermute | solution.py:371
  126.7 18.0 %collective-permute-start.27 = (bf16[128,3072]{1,0:T(8,128)(2,1)S(1)}, bf16[128,3072]{1,0:T(8,128)(2,1)S(1)}, u32[]{:S(2)}, u32[]{:S(2)}) collective-permute-start(bf16[128,3072]{1,0:T(8,128)(2,1)S(1)} %get-tuple-element.153), channel_id=1, source_target_pairs={{0,2},{2,0},{4,6},{6,4},{8,10},{10,8},{12,14},{14,12},{16,18},{18,... | collective-permute-start | bytes 2359304 | tf_op jit(solution)/shard_map/ppermute | solution.py:357
  127.7 17.7 %collective-permute-start.28 = (bf16[128,3072]{1,0:T(8,128)(2,1)S(1)}, bf16[128,3072]{1,0:T(8,128)(2,1)S(1)}, u32[]{:S(2)}, u32[]{:S(2)}) collective-permute-start(bf16[128,3072]{1,0:T(8,128)(2,1)S(1)} %get-tuple-element.154), channel_id=1, source_target_pairs={{0,4},{2,6},{4,0},{6,2},{8,12},{10,14},{12,8},{14,10},{16,20},{18,... | collective-permute-start | bytes 2359304 | tf_op jit(solution)/shard_map/ppermute | solution.py:361
  128.4 12.5 %collective-permute-start.29 = (bf16[128,1280]{1,0:T(8,128)(2,1)S(1)}, bf16[128,1280]{1,0:T(8,128)(2,1)S(1)}, u32[]{:S(2)}, u32[]{:S(2)}) collective-permute-start(bf16[128,1280]{1,0:T(8,128)(2,1)S(1)} %get-tuple-element.155), channel_id=1, source_target_pairs={{0,8},{2,10},{4,12},{6,14},{8,16},{10,18},{12,20},{14,22},{16,24},... | collective-permute-start | bytes 983048 | tf_op jit(solution)/shard_map/ppermute | solution.py:366
  128.5 15.1 %collective-permute-start.30 = (bf16[128,1280]{1,0:T(8,128)(2,1)S(1)}, bf16[128,1280]{1,0:T(8,128)(2,1)S(1)}, u32[]{:S(2)}, u32[]{:S(2)}) collective-permute-start(bf16[128,1280]{1,0:T(8,128)(2,1)S(1)} %get-tuple-element.156), channel_id=1, source_target_pairs={{8,0},{10,2},{12,4},{14,6},{16,8},{18,10},{20,12},{22,14},{24,16},... | collective-permute-start | bytes 983048 | tf_op jit(solution)/shard_map/ppermute | solution.py:371
  135.6 11.6 %copy-start = (bf16[896,2048]{1,0:T(8,128)(2,1)}, bf16[896,2048]{1,0:T(8,128)(2,1)S(1)}, u32[]{:S(2)}) copy-start(bf16[896,2048]{1,0:T(8,128)(2,1)S(1)} %convolution_convert_fusion.refs_1_.refs_0_) | copy-start | bytes 11010052
  147.2 30.6 %collective-permute-start.31 = (bf16[128,4096]{1,0:T(8,128)(2,1)}, bf16[128,4096]{1,0:T(8,128)(2,1)}, u32[]{:S(2)}, u32[]{:S(2)}) collective-permute-start(bf16[128,4096]{1,0:T(8,128)(2,1)} %get-tuple-element.166), channel_id=1, source_target_pairs={{0,2},{2,0},{4,6},{6,4},{8,10},{10,8},{12,14},{14,12},{16,18},{18,... | collective-permute-start | bytes 3145736 | tf_op jit(solution)/shard_map/ppermute | solution.py:357
  148.3 29.5 %collective-permute-start.32 = (bf16[128,4096]{1,0:T(8,128)(2,1)}, bf16[128,4096]{1,0:T(8,128)(2,1)}, u32[]{:S(2)}, u32[]{:S(2)}) collective-permute-start(bf16[128,4096]{1,0:T(8,128)(2,1)} %get-tuple-element.167), channel_id=1, source_target_pairs={{0,4},{2,6},{4,0},{6,2},{8,12},{10,14},{12,8},{14,10},{16,20},{18,... | collective-permute-start | bytes 3145736 | tf_op jit(solution)/shard_map/ppermute | solution.py:361
  149.4 18.4 %collective-permute-start.33 = (bf16[128,2304]{1,0:T(8,128)(2,1)}, bf16[128,2304]{1,0:T(8,128)(2,1)}, u32[]{:S(2)}, u32[]{:S(2)}) collective-permute-start(bf16[128,2304]{1,0:T(8,128)(2,1)} %get-tuple-element.168), channel_id=1, source_target_pairs={{0,8},{2,10},{4,12},{6,14},{8,16},{10,18},{12,20},{14,22},{16,24},... | collective-permute-start | bytes 1769480 | tf_op jit(solution)/shard_map/ppermute | solution.py:366
  149.8 28.0 %collective-permute-start.34 = (bf16[128,2304]{1,0:T(8,128)(2,1)}, bf16[128,2304]{1,0:T(8,128)(2,1)}, u32[]{:S(2)}, u32[]{:S(2)}) collective-permute-start(bf16[128,2304]{1,0:T(8,128)(2,1)} %get-tuple-element.169), channel_id=1, source_target_pairs={{8,0},{10,2},{12,4},{14,6},{16,8},{18,10},{20,12},{22,14},{24,16},... | collective-permute-start | bytes 1769480 | tf_op jit(solution)/shard_map/ppermute | solution.py:371
  153.2 33.1 %all-to-all-start.1 = ((bf16[16,128,128]{2,1,0:T(8,128)(2,1)}), bf16[16,128,128]{2,1,0:T(8,128)(2,1)}, u32[]{:S(2)}, u32[]{:S(2)}) async-start(bf16[16,128,128]{2,1,0:T(8,128)(2,1)} %bitcast.13), calls=%async_computation.1 | async-start | bytes 1048576 | tf_op jit(solution)/shard_map/all_to_all | solution.py:629
  158.5 19.3 %copy-start.1 = (bf16[896,2048]{1,0:T(8,128)(2,1)S(1)}, bf16[896,2048]{1,0:T(8,128)(2,1)}, u32[]{:S(2)}) copy-start(bf16[896,2048]{1,0:T(8,128)(2,1)} %copy-done) | copy-start | bytes 11010052
  181.0 22.2 %collective-permute-start.35 = (bf16[128,2048]{1,0:T(8,128)(2,1)}, bf16[128,2048]{1,0:T(8,128)(2,1)S(1)}, u32[]{:S(2)}, u32[]{:S(2)}) collective-permute-start(bf16[128,2048]{1,0:T(8,128)(2,1)} %get-tuple-element.174), channel_id=1, source_target_pairs={{0,2},{2,0},{4,6},{6,4},{8,10},{10,8},{12,14},{14,12},{16,18},{18,... | collective-permute-start | bytes 1572872 | tf_op jit(solution)/shard_map/ppermute | solution.py:357
  182.0 21.2 %collective-permute-start.36 = (bf16[128,2048]{1,0:T(8,128)(2,1)}, bf16[128,2048]{1,0:T(8,128)(2,1)S(1)}, u32[]{:S(2)}, u32[]{:S(2)}) collective-permute-start(bf16[128,2048]{1,0:T(8,128)(2,1)} %get-tuple-element.175), channel_id=1, source_target_pairs={{0,4},{2,6},{4,0},{6,2},{8,12},{10,14},{12,8},{14,10},{16,20},{18,... | collective-permute-start | bytes 1572872 | tf_op jit(solution)/shard_map/ppermute | solution.py:361
  182.5 14.1 %collective-permute-start.37 = (bf16[128,1536]{1,0:T(8,128)(2,1)}, bf16[128,1536]{1,0:T(8,128)(2,1)S(1)}, u32[]{:S(2)}, u32[]{:S(2)}) collective-permute-start(bf16[128,1536]{1,0:T(8,128)(2,1)} %get-tuple-element.176), channel_id=1, source_target_pairs={{0,8},{2,10},{4,12},{6,14},{8,16},{10,18},{12,20},{14,22},{16,24},... | collective-permute-start | bytes 1179656 | tf_op jit(solution)/shard_map/ppermute | solution.py:366
  184.4 18.8 %collective-permute-start.38 = (bf16[128,1536]{1,0:T(8,128)(2,1)}, bf16[128,1536]{1,0:T(8,128)(2,1)S(1)}, u32[]{:S(2)}, u32[]{:S(2)}) collective-permute-start(bf16[128,1536]{1,0:T(8,128)(2,1)} %get-tuple-element.177), channel_id=1, source_target_pairs={{8,0},{10,2},{12,4},{14,6},{16,8},{18,10},{20,12},{22,14},{24,16},... | collective-permute-start | bytes 1179656 | tf_op jit(solution)/shard_map/ppermute | solution.py:371
  (13 other events, 35.3 us)

commit v5 on v4

--- a/solution.py
+++ b/solution.py
@@ -505,7 +505,7 @@
 
     own_x, own_y, wide_3, wide_1 = all_ways(tokens, tokens, wide, wide)
     first = (tokens, own_x, own_y, wide_3, wide_1)
-    members = ((0, n, m), (1, n, m), (2, n, m))
+    members = ((0, n, m), (1, n, m))
     sent = put(
         first,
         ((2, 0, nh), (2, n, mh), (3, 0, n), (4, 0, n)),
@@ -520,15 +520,15 @@
     across = ((0, nh, mh), (1, nh, mh))
     third = all_ways(
         *put(
-            second,
+            (*second, own_y),
             ((1, start, nh), (1, start + n, nh), *wide_2),
             ((0, start + nh, nh), (0, start + n + nh, nh), *wide_2),
-            (*across, (2, nh, nh)),
-            (*across, (3, 2 * nh, nh)),
+            (*across, (4, n, m), (2, nh, m)),
+            (*across, (4, n, m), (3, nh + m, m)),
         )
     )
     fourth = all_ways(
-        *put(third, ((1, n, nh),), ((0, n + nh, nh),), ((2, 0, mh),), ((3, mh, mh),))
+        *put(third, ((1, n, nh),), ((0, n + nh, nh),), ((2, 0, m),), ((3, m, m),))
     )
     runs = [
         (0, 0, 0, 0, 3, span, 0),
@@ -547,9 +547,9 @@
     for side in range(2):
         runs += [
             (1, offset, 2, 0, 1, nh, side * nh),
-            (1, offset + nh, 3 - 2 * side, 0, 3, m, n),
+            (1, offset + nh, 3 - 2 * side, 0, 2, m, n),
         ]
-        offset += nh + 3 * m
+        offset += nh + 2 * m
     offset = 0
     for side in range(2):
         runs += [
@@ -560,15 +560,15 @@
         offset += 2 * n
     runs += [
         (2, offset, 3, 3, 1, m, n),
-        (2, offset + m, 2, 0, 1, m, n),
-        (2, offset + 2 * m, 2, 1, 1, mh, n),
-        (2, offset + 2 * m + mh, 1, 3, 1, m, n),
-        (2, offset + 3 * m + mh, 2, 1, 1, mh, n + mh),
-        (2, offset + 3 * m + 2 * mh, 2, 2, 1, m, n),
+        (2, offset + m, 3, 2, 1, m, n),
+        (2, offset + 2 * m, 2, 0, 1, m, n),
+        (2, offset + 3 * m, 1, 3, 1, m, n),
+        (2, offset + 4 * m, 1, 2, 1, m, n),
+        (2, offset + 5 * m, 2, 1, 1, m, n),
         (3, 0, 2, 3, 1, nh, 0),
         (3, nh, 2, 3, 1, nh, nh),
-        (3, n, 2, 3, 1, mh, n),
-        (3, n + mh, 2, 3, 1, mh, n + mh),
+        (3, n, 2, 3, 1, m, n),
+        (3, n + m, 2, 2, 1, m, n),
     ]
     parts = [project(part, *matrices) for part in (first, second, third, fourth)]
     later, first = lax.optimization_barrier((later, parts[0][0]))
@@ -577,11 +577,11 @@
     return parts, tuple(runs), matrices, later
 
 
-ORDER = (((2, 0, 4), (1, 3, 1), (3, 3, 1)), ((1, 0, 3), (3, 0, 3), (0, 3, 1), (0, 0, 3)))
+ORDER = (((2, 0, 4), (1, 2, 2), (3, 2, 2)), ((1, 0, 2), (3, 0, 2), (0, 3, 1), (0, 0, 3)))
 
 
 def scatter_sum(early, later, matrix, hyena):
-    span = early.shape[0] // 6
+    span = early.shape[0] // 8
     columns = matrix.shape[1]
     wide, narrow = columns * 3 // 8, columns // 8
     places = {}
@@ -610,7 +610,13 @@
     early = product(early, swapped(early))
     other = swapped(later)
     first = all_ways(
-        *put([early], [term(2, 3, 0)], [term(2, 3, 1)], [low(2, 3, 0)], [low(2, 3, 1)])
+        *put(
+            [early],
+            [term(2, 3, 0)],
+            [term(2, 3, 1)],
+            [low(2, 3, 0), low(2, 2, 0)],
+            [low(2, 3, 1), low(2, 2, 1)],
+        )
     )
     later, hyena, first = lax.optimization_barrier((later, hyena, first))
     x, y, below, above = range(1, 5)
@@ -619,12 +625,26 @@
             [early, *first],
             [term(2, 1, 0), term(2, 1, 1, (y, 0, 0)), term(1, 3, 0), term(3, 3, 0)],
             [term(2, 2, 0, (x, 0, 0)), term(2, 2, 1), term(1, 3, 1), term(3, 3, 1)],
-            [low(1, 3, 0, (below, 0, 0)), low(1, 3, 1), *[low(2, k, 0) for k in range(3)]],
-            [low(3, 3, 0), low(3, 3, 1, (above, 0, 0)), *[low(2, k, 1) for k in range(3)]],
+            [
+                low(1, 3, 0, (below, 0, 0)),
+                low(1, 3, 1),
+                low(1, 2, 0, (below, 0, narrow)),
+                low(1, 2, 1),
+                low(2, 0, 0),
+                low(2, 1, 0),
+            ],
+            [
+                low(3, 3, 0),
+                low(3, 3, 1, (above, 0, 0)),
+                low(3, 2, 0),
+                low(3, 2, 1, (above, 0, narrow)),
+                low(2, 0, 1),
+                low(2, 1, 1),
+            ],
         )
     )
-    own = product(later[7 * span :], other[7 * span :])
-    later = product(later[: 7 * span], other[: 7 * span])
+    own = product(later[5 * span :], other[5 * span :])
+    later = product(later[: 5 * span], other[: 5 * span])
     later, second = lax.optimization_barrier((later, second))
     hyena_out = lax.all_to_all(hyena, "ctx", split_axis=0, concat_axis=1, tiled=True).T
     x, y, below, above = range(2, 6)
@@ -636,8 +656,8 @@
         return term(2, 0, side, (x, 0, side * wide), (y, 0, side * wide))
 
     for_above, for_below = [], []
-    for k in range(3):
-        start = (2 + k) * narrow
+    for k in range(2):
+        start = (4 + k) * narrow
         for_above += [low(1, k, 0, (below, 0, start)), low(1, k, 1)]
         for_below += [low(3, k, 0), low(3, k, 1, (above, 0, start))]
     third = all_ways(
@@ -664,9 +684,18 @@
         )
     )
 
+    (low_2,) = put(
+        [early, later, own, *second],
+        [
+            low(0, 2, side, *[(way, 0, (2 + side) * narrow) for way in (5, 6)])
+            for side in (0, 1)
+        ],
+    )
     x, y, below, above = range(3, 7)
 
     def low_own(k, side, *more):
+        if k == 2:
+            return (narrow, [(7, 0, side * narrow), *more])
         start = wide + (2 * k + side) * narrow
         return low(0, k, side, (below, 0, start), (above, 0, start), *more)
 
@@ -675,7 +704,7 @@
         return term(group, 0, side, (x, 0, start), (y, 0, start), *more)
 
     sent = put(
-        [early, later, own, *third],
+        [early, later, own, *third, low_2],
             [
                 term(0, 1, 0),
                 term(0, 1, 1, (y, 0, 4 * wide)),

time: 205 us -> 205 us (level)
  waiting for transfers between devices: 80.2 us -> 72.8 us
  starting transfers between devices: 55.8 us -> 59.1 us
  local copies, waits for them, and re-layouts: 12 us -> 14.4 us
    ppermute x8, starting transfers between devices: 4.64 us -> 10 us  [up(): lax.ppermute(value, 'ctx', [(i, (i + PLANE) % count) for i in range(count)])]
    ppermute x8, starting transfers between devices: 25.9 us -> 20.5 us  [down(): lax.ppermute(value, 'ctx', [((i + PLANE) % count, i) for i in range(count)])]
    ppermute x8, starting transfers between devices: 7.84 us -> 12.9 us  [over_x(): lax.ppermute(value, 'ctx', [(i, i ^ 1) for i in range(lax.axis_size('ctx'...]
    ppermute x8, waiting for transfers between devices: 4.31 us -> 0.3 us  [over_x(): lax.ppermute(value, 'ctx', [(i, i ^ 1) for i in range(lax.axis_size('ctx'...]
    ppermute x8, waiting for transfers between devices: 40.9 us -> 38 us  [down(): lax.ppermute(value, 'ctx', [((i + PLANE) % count, i) for i in range(count)])]
    unnamed x53 -> x57, local copies, waits for them, and re-layouts: 6.66 us -> 9.07 us
    pallas_call x10 -> x11, Pallas kernels: 11.7 us -> 13.9 us  [assemble(): pl.pallas_call(functools.partial(assemble_kernel, len(arrays), plans), ou...]
  transfers between devices with their start and end apart: 41 -> 41, of which waited for: 19 -> 17; matrix products, arithmetic and copies ran while one was open for 16% -> 16% of each run, Pallas kernels for 6% -> 6%
where the time goes in v5:
time: 205 us
  waiting for transfers between devices  72.8 us (36%)
  starting transfers between devices  59.1 us (29%)
  Pallas kernels  32.7 us (16%)
  matrix products  24.5 us (12%)
  local copies, waits for them, and re-layouts  14.4 us (7%)
    ppermute x8, waiting for transfers between devices, down(): lax.ppermute(value, 'ctx', [((i + PLANE) % count, i) for i in range(count)])  38 us
    ppermute x8, waiting for transfers between devices, up(): lax.ppermute(value, 'ctx', [(i, (i + PLANE) % count) for i in range(count)])  30.9 us
    ppermute x8, starting transfers between devices, down(): lax.ppermute(value, 'ctx', [((i + PLANE) % count, i) for i in range(count)])  20.5 us
    dot_general x8, matrix products, project(): jnp.einsum('td,rd->tr', rows, matrix, preferred_element_type=jnp.float32)  15.7 us
    pallas_call x11, Pallas kernels, assemble(): pl.pallas_call(functools.partial(assemble_kernel, len(arrays), plans), ou...  13.9 us
    pallas_call x1, Pallas kernels, scan_all(): pl.pallas_call(functools.partial(scan_kernel, PLANE, runs, order), out_sh...  13.1 us
    ppermute x8, starting transfers between devices, over_x(): lax.ppermute(value, 'ctx', [(i, i ^ 1) for i in range(lax.axis_size('ctx'...  12.9 us
    ppermute x8, starting transfers between devices, up(): lax.ppermute(value, 'ctx', [(i, (i + PLANE) % count) for i in range(count)])  10 us
  transfers between devices with their start and end apart: 41, of which 17 were waited for; matrix products, arithmetic and copies ran while one was open for 16% of the time, Pallas kernels for 6%

profile of v5, /device:TPU:0, one launch (start us, length us, event | category | flops | bytes accessed | tf_op | source)
XLA Modules:
  0.0 204.6 jit_solution(18021826254968162908)
XLA Ops:
  0.6 2.2 %halves.2 = (bf16[128,2048]{1,0:T(8,128)(2,1)}, bf16[96,2048]{1,0:T(8,128)(2,1)}) custom-call(s32[1]{0:T(128)} %bitcast.5.core_ref, bf16[128,4096]{1,0:T(8,128)(2,1)} %refs_0_.1), custom_call_target="tpu_custom_call" | custom-call | bytes 1835008 | tf_op jit(solution)/shard_map/halves/pallas_call | solution.py:409
  2.8 3.0 %collective-permute-start = (bf16[128,2048]{1,0:T(8,128)(2,1)}, bf16[128,2048]{1,0:T(8,128)(2,1)S(1)}, u32[]{:S(2)}, u32[]{:S(2)}) collective-permute-start(bf16[128,2048]{1,0:T(8,128)(2,1)} %get-tuple-element.103.refs_0_), channel_id=1, source_target_pairs={{0,2},{2,0},{4,6},{6,4},{8,10},{10,8},{12,14},{14,12},{16,18},{18,... | collective-permute-start | bytes 1572872 | tf_op jit(solution)/shard_map/ppermute | solution.py:357
  7.3 1.6 collective-permute-start.2
  8.9 2.2 %collective-permute-start.3 = (bf16[96,2048]{1,0:T(8,128)(2,1)}, bf16[96,2048]{1,0:T(8,128)(2,1)S(1)}, u32[]{:S(2)}, u32[]{:S(2)}) collective-permute-start(bf16[96,2048]{1,0:T(8,128)(2,1)} %get-tuple-element.94), channel_id=1, source_target_pairs={{8,0},{10,2},{12,4},{14,6},{16,8},{18,10},{20,12},{22,14},{24,16},... | collective-permute-start | bytes 1179656 | tf_op jit(solution)/shard_map/ppermute | solution.py:371
  11.2 3.5 %halves.3 = (bf16[384,2048]{1,0:T(8,128)(2,1)}, bf16[384,2048]{1,0:T(8,128)(2,1)}) custom-call(s32[1]{0:T(128)} %bitcast.5.core_ref, bf16[384,4096]{1,0:T(8,128)(2,1)} %bitcast.46), custom_call_target="tpu_custom_call" | custom-call | bytes 6291456 | tf_op jit(solution)/shard_map/halves/pallas_call | solution.py:409
  14.8 6.6 %collective-permute-done.2.refs_3_ = bf16[96,2048]{1,0:T(8,128)(2,1)S(1)} collective-permute-done((bf16[96,2048]{1,0:T(8,128)(2,1)}, bf16[96,2048]{1,0:T(8,128)(2,1)S(1)}, u32[]{:S(2)}, u32[]{:S(2)}) %collective-permute-start.2) | collective-permute-done | bytes 393248 | tf_op jit(solution)/shard_map/ppermute | solution.py:366
  21.5 6.0 %collective-permute-done.3.refs_4_ = bf16[96,2048]{1,0:T(8,128)(2,1)S(1)} collective-permute-done((bf16[96,2048]{1,0:T(8,128)(2,1)}, bf16[96,2048]{1,0:T(8,128)(2,1)S(1)}, u32[]{:S(2)}, u32[]{:S(2)}) %collective-permute-start.3) | collective-permute-done | bytes 393248 | tf_op jit(solution)/shard_map/ppermute | solution.py:371
  27.5 1.9 assemble.11
  31.7 2.7 %collective-permute-start.7 = (bf16[112,2048]{1,0:T(8,128)(2,1)}, bf16[112,2048]{1,0:T(8,128)(2,1)}, u32[]{:S(2)}, u32[]{:S(2)}) collective-permute-start(bf16[112,2048]{1,0:T(8,128)(2,1)} %get-tuple-element.114), channel_id=1, source_target_pairs={{8,0},{10,2},{12,4},{14,6},{16,8},{18,10},{20,12},{22,14},{24,16},... | collective-permute-start | bytes 1376264 | tf_op jit(solution)/shard_map/ppermute | solution.py:371
  35.6 2.4 %fusion.12.refs_1_ = f32[576,384]{1,0:T(8,128)} fusion(bf16[576,2048]{1,0:T(8,128)(2,1)S(1)} %constant_dynamic-update-slice_fusion, bf16[384,2048]{1,0:T(8,128)(2,1)S(1)} %copy-done.15), kind=kOutput, calls=%fused_computation.37 | convolution fusion | flops 905969664 | bytes 4816896 | tf_op jit(solution)/shard_map/td,rd->tr/dot_general | solution.py:487
  39.0 3.8 %all-to-all-start = ((bf16[128,16,128]{2,0,1:T(8,128)(2,1)}), bf16[128,16,128]{2,0,1:T(8,128)(2,1)S(1)}, u32[]{:S(2)}, u32[]{:S(2)}) async-start(bf16[128,16,128]{2,0,1:T(8,128)(2,1)} %copy.8), calls=%async_computation | async-start | bytes 1048576 | tf_op jit(solution)/shard_map/all_to_all | solution.py:494
  42.8 3.3 %collective-permute-done.6.refs_2_ = bf16[112,2048]{1,0:T(8,128)(2,1)} collective-permute-done((bf16[112,2048]{1,0:T(8,128)(2,1)}, bf16[112,2048]{1,0:T(8,128)(2,1)}, u32[]{:S(2)}, u32[]{:S(2)}) %collective-permute-start.6) | collective-permute-done | bytes 458784 | tf_op jit(solution)/shard_map/ppermute | solution.py:366
  46.1 9.2 %collective-permute-done.7.refs_3_ = bf16[112,2048]{1,0:T(8,128)(2,1)} collective-permute-done((bf16[112,2048]{1,0:T(8,128)(2,1)}, bf16[112,2048]{1,0:T(8,128)(2,1)}, u32[]{:S(2)}, u32[]{:S(2)}) %collective-permute-start.7) | collective-permute-done | bytes 458784 | tf_op jit(solution)/shard_map/ppermute | solution.py:371
  57.7 2.1 %collective-permute-start.8 = (bf16[192,2048]{1,0:T(8,128)(2,1)S(1)}, bf16[192,2048]{1,0:T(8,128)(2,1)S(1)}, u32[]{:S(2)}, u32[]{:S(2)}) collective-permute-start(bf16[192,2048]{1,0:T(8,128)(2,1)S(1)} %get-tuple-element.119), channel_id=1, source_target_pairs={{0,2},{2,0},{4,6},{6,4},{8,10},{10,8},{12,14},{14,12},{16,18},{18,... | collective-permute-start | bytes 2359304 | tf_op jit(solution)/shard_map/ppermute | solution.py:357
  59.8 2.2 %collective-permute-start.10 = (bf16[96,2048]{1,0:T(8,128)(2,1)S(1)}, bf16[96,2048]{1,0:T(8,128)(2,1)S(1)}, u32[]{:S(2)}, u32[]{:S(2)}) collective-permute-start(bf16[96,2048]{1,0:T(8,128)(2,1)S(1)} %get-tuple-element.121), channel_id=1, source_target_pairs={{0,8},{2,10},{4,12},{6,14},{8,16},{10,18},{12,20},{14,22},{16,24},... | collective-permute-start | bytes 1179656 | tf_op jit(solution)/shard_map/ppermute | solution.py:366
  62.0 1.6 collective-permute-start.11
  66.1 2.7 %fusion.13.refs_2_ = f32[736,384]{1,0:T(8,128)} fusion(bf16[736,2048]{1,0:T(8,128)(2,1)S(1)} %constant_dynamic-update-slice_fusion.5, bf16[384,2048]{1,0:T(8,128)(2,1)S(1)} %copy-done.16), kind=kOutput, calls=%fused_computation.38 | convolution fusion | flops 1157627904 | bytes 5718016 | tf_op jit(solution)/shard_map/td,rd->tr/dot_general | solution.py:487
  70.3 2.6 %convolution_convert_fusion.3 = bf16[736,384]{1,0:T(8,128)(2,1)} fusion(bf16[736,2048]{1,0:T(8,128)(2,1)S(1)} %constant_dynamic-update-slice_fusion.5, bf16[384,2048]{1,0:T(8,128)(2,1)S(1)} %assemble.14), kind=kOutput, calls=%fused_computation.7 | convolution fusion | flops 1157910528 | bytes 5152768 | tf_op jit(solution)/shard_map/td,rd->tr/dot_general | solution.py:487
  72.9 2.2 %convolution_convert_fusion.5 = bf16[576,384]{1,0:T(8,128)(2,1)} fusion(bf16[576,2048]{1,0:T(8,128)(2,1)S(1)} %copy-done.21, bf16[384,2048]{1,0:T(8,128)(2,1)S(1)} %assemble.14), kind=kOutput, calls=%fused_computation.9 | convolution fusion | flops 906190848 | bytes 4374528 | tf_op jit(solution)/shard_map/td,rd->tr/dot_general | solution.py:487
  75.1 3.6 %collective-permute-done.11.refs_3_ = bf16[96,2048]{1,0:T(8,128)(2,1)S(1)} collective-permute-done((bf16[96,2048]{1,0:T(8,128)(2,1)S(1)}, bf16[96,2048]{1,0:T(8,128)(2,1)S(1)}, u32[]{:S(2)}, u32[]{:S(2)}) %collective-permute-start.11) | collective-permute-done | bytes 393248 | tf_op jit(solution)/shard_map/ppermute | solution.py:371
  80.3 1.6 collective-permute-start.13
  81.9 3.0 %collective-permute-start.14 = (bf16[32,2048]{1,0:T(8,128)(2,1)S(1)}, bf16[32,2048]{1,0:T(8,128)(2,1)S(1)}, u32[]{:S(2)}, u32[]{:S(2)}) collective-permute-start(bf16[32,2048]{1,0:T(8,128)(2,1)S(1)} %get-tuple-element.129), channel_id=1, source_target_pairs={{0,8},{2,10},{4,12},{6,14},{8,16},{10,18},{12,20},{14,22},{16,24},... | collective-permute-start | bytes 393224 | tf_op jit(solution)/shard_map/ppermute | solution.py:366
  85.8 2.2 %convolution_convert_fusion.4 = bf16[576,384]{1,0:T(8,128)(2,1)} fusion(bf16[576,2048]{1,0:T(8,128)(2,1)S(1)} %constant_dynamic-update-slice_fusion.9, bf16[384,2048]{1,0:T(8,128)(2,1)S(1)} %assemble.14), kind=kOutput, calls=%fused_computation.8 | convolution fusion | flops 906190848 | bytes 4374528 | tf_op jit(solution)/shard_map/td,rd->tr/dot_general | solution.py:487
  88.0 2.4 %fusion.14.refs_3_ = f32[576,384]{1,0:T(8,128)} fusion(bf16[576,2048]{1,0:T(8,128)(2,1)S(1)} %constant_dynamic-update-slice_fusion.9, bf16[384,2048]{1,0:T(8,128)(2,1)S(1)} %copy-done.16), kind=kOutput, calls=%fused_computation.39 | convolution fusion | flops 905969664 | bytes 4816896 | tf_op jit(solution)/shard_map/td,rd->tr/dot_general | solution.py:487
  98.0 13.1 %modal_scan.1 = (bf16[2048,128]{1,0:T(8,128)(2,1)}, f32[16,128]{1,0:T(8,128)}, bf16[1024,384]{1,0:T(8,128)(2,1)S(1)}, bf16[1024,384]{1,0:T(8,128)(2,1)S(1)}) custom-call(s32[1]{0:T(128)} %bitcast.me_ref, f32[16,128]{1,0:T(8,128)S(1)} %bitcast.44, f32[16,128]{1,0:T(8,128)S(1)} %bitcast.45, bf16[2048,128]{1,0:T(8,128)(2,1)S(1)} %bitcast.43, ...), custom_call_target="tpu_custom_call" | custom-call | tf_op jit(solution)/shard_map/modal_scan/pallas_call | solution.py:332
  111.7 1.8 collective-permute-done.21
  113.5 3.6 %convolution_convert_fusion.refs_0_ = bf16[1024,2048]{1,0:T(8,128)(2,1)S(1)} fusion(bf16[1024,384]{1,0:T(8,128)(2,1)S(1)} %collective-permute-done.21, bf16[1024,384]{1,0:T(8,128)(2,1)S(1)} %get-tuple-element.138, bf16[384,2048]{1,0:T(8,128)(2,1)S(1)} %assemble.14, bf16[384,2048]{1,0:T(8,128)(2,1)S(1)} %copy-done.17), kind=kOutput, calls=%fused_computation | convolution fusion | flops 3232759808 | bytes 8912896 | tf_op jit(solution)/shard_map/dot_general | solution.py:597
  119.5 3.1 %collective-permute-start.25 = (bf16[128,512]{1,0:T(8,128)(2,1)S(1)}, bf16[128,512]{1,0:T(8,128)(2,1)S(1)}, u32[]{:S(2)}, u32[]{:S(2)}) collective-permute-start(bf16[128,512]{1,0:T(8,128)(2,1)S(1)} %get-tuple-element.142), channel_id=1, source_target_pairs={{8,0},{10,2},{12,4},{14,6},{16,8},{18,10},{20,12},{22,14},{24,16},... | collective-permute-start | bytes 393224 | tf_op jit(solution)/shard_map/ppermute | solution.py:371
  122.7 4.4 %collective-permute-done.24.refs_3_ = bf16[128,512]{1,0:T(8,128)(2,1)S(1)} collective-permute-done((bf16[128,512]{1,0:T(8,128)(2,1)S(1)}, bf16[128,512]{1,0:T(8,128)(2,1)S(1)}, u32[]{:S(2)}, u32[]{:S(2)}) %collective-permute-start.24) | collective-permute-done | bytes 131104 | tf_op jit(solution)/shard_map/ppermute | solution.py:366
  127.5 1.6 collective-permute-start.27
  129.1 1.5 collective-permute-start.28
  131.7 2.7 %collective-permute-start.30 = (bf16[128,1536]{1,0:T(8,128)(2,1)S(1)}, bf16[128,1536]{1,0:T(8,128)(2,1)S(1)}, u32[]{:S(2)}, u32[]{:S(2)}) collective-permute-start(bf16[128,1536]{1,0:T(8,128)(2,1)S(1)} %get-tuple-element.156), channel_id=1, source_target_pairs={{8,0},{10,2},{12,4},{14,6},{16,8},{18,10},{20,12},{22,14},{24,16},... | collective-permute-start | bytes 1179656 | tf_op jit(solution)/shard_map/ppermute | solution.py:371
  135.4 2.2 %convolution_convert_fusion.1.refs_1_.refs_0_ = bf16[640,2048]{1,0:T(8,128)(2,1)S(1)} fusion(bf16[640,384]{1,0:T(8,128)(2,1)S(1)} %slice.17, bf16[640,384]{1,0:T(8,128)(2,1)S(1)} %slice.14, bf16[384,2048]{1,0:T(8,128)(2,1)S(1)} %assemble.14, bf16[384,2048]{1,0:T(8,128)(2,1)S(1)} %copy-done.17), kind=kOutput, calls=%fused_computation.1 | convolution fusion | flops 2022834176 | bytes 6750208 | tf_op jit(solution)/shard_map/dot_general | solution.py:597
  137.6 6.9 %collective-permute-done.29.refs_4_.refs_1_ = bf16[128,1536]{1,0:T(8,128)(2,1)S(1)} collective-permute-done((bf16[128,1536]{1,0:T(8,128)(2,1)S(1)}, bf16[128,1536]{1,0:T(8,128)(2,1)S(1)}, u32[]{:S(2)}, u32[]{:S(2)}) %collective-permute-start.29) | collective-permute-done | bytes 393248 | tf_op jit(solution)/shard_map/ppermute | solution.py:366
  144.4 5.5 %collective-permute-done.30.refs_5_.refs_2_ = bf16[128,1536]{1,0:T(8,128)(2,1)S(1)} collective-permute-done((bf16[128,1536]{1,0:T(8,128)(2,1)S(1)}, bf16[128,1536]{1,0:T(8,128)(2,1)S(1)}, u32[]{:S(2)}, u32[]{:S(2)}) %collective-permute-start.30) | collective-permute-done | bytes 393248 | tf_op jit(solution)/shard_map/ppermute | solution.py:371
  150.0 2.0 assemble.17
  153.4 3.5 %collective-permute-start.34 = (bf16[128,1792]{1,0:T(8,128)(2,1)}, bf16[128,1792]{1,0:T(8,128)(2,1)}, u32[]{:S(2)}, u32[]{:S(2)}) collective-permute-start(bf16[128,1792]{1,0:T(8,128)(2,1)} %get-tuple-element.169), channel_id=1, source_target_pairs={{8,0},{10,2},{12,4},{14,6},{16,8},{18,10},{20,12},{22,14},{24,16},... | collective-permute-start | bytes 1376264 | tf_op jit(solution)/shard_map/ppermute | solution.py:371
  156.8 4.5 %all-to-all-start.1 = ((bf16[16,128,128]{2,1,0:T(8,128)(2,1)}), bf16[16,128,128]{2,1,0:T(8,128)(2,1)}, u32[]{:S(2)}, u32[]{:S(2)}) async-start(bf16[16,128,128]{2,1,0:T(8,128)(2,1)} %bitcast.13), calls=%async_computation.1 | async-start | bytes 1048576 | tf_op jit(solution)/shard_map/all_to_all | solution.py:649
  162.4 3.0 %convolution_convert_fusion.2.refs_0_.refs_1_ = bf16[384,2048]{1,0:T(8,128)(2,1)S(1)} fusion(bf16[384,2048]{1,0:T(8,128)(2,1)S(1)} %assemble.14, bf16[384,2048]{1,0:T(8,128)(2,1)} %get-tuple-element.108, bf16[384,384]{1,0:T(8,128)(2,1)S(1)} %slice.16, bf16[384,384]{1,0:T(8,128)(2,1)S(1)} %slice.12), kind=kOutput, calls=%fused_computation.3 | convolution fusion | flops 1216217088 | bytes 5308416 | tf_op jit(solution)/shard_map/dot_general | solution.py:597
  165.4 3.1 %collective-permute-done.33.refs_1_.refs_4_ = bf16[128,1792]{1,0:T(8,128)(2,1)} collective-permute-done((bf16[128,1792]{1,0:T(8,128)(2,1)}, bf16[128,1792]{1,0:T(8,128)(2,1)}, u32[]{:S(2)}, u32[]{:S(2)}) %collective-permute-start.33) | collective-permute-done | bytes 458784 | tf_op jit(solution)/shard_map/ppermute | solution.py:366
  168.6 10.6 %collective-permute-done.34.refs_2_.refs_5_ = bf16[128,1792]{1,0:T(8,128)(2,1)} collective-permute-done((bf16[128,1792]{1,0:T(8,128)(2,1)}, bf16[128,1792]{1,0:T(8,128)(2,1)}, u32[]{:S(2)}, u32[]{:S(2)}) %collective-permute-start.34) | collective-permute-done | bytes 458784 | tf_op jit(solution)/shard_map/ppermute | solution.py:371
  180.2 3.1 %assemble.20 = (bf16[128,2048]{1,0:T(8,128)(2,1)}, bf16[128,2048]{1,0:T(8,128)(2,1)}, bf16[128,1536]{1,0:T(8,128)(2,1)}, bf16[128,1536]{1,0:T(8,128)(2,1)}) custom-call(bf16[640,2048]{1,0:T(8,128)(2,1)S(1)} %copy-done.1, bf16[384,2048]{1,0:T(8,128)(2,1)S(1)} %convolution_convert_fusion.2.refs_0_.refs_1_, bf16[128,4096]{1,0:T(8,128)(2,1)} %collective-permute-done.31.refs_2_, ...), custom_call_target="tpu_custom_call" | custom-call | flops 1835008 | bytes 7340032 | tf_op jit(solution)/shard_map/assemble/pallas_call | solution.py:447
  183.3 2.4 %collective-permute-start.35 = (bf16[128,2048]{1,0:T(8,128)(2,1)}, bf16[128,2048]{1,0:T(8,128)(2,1)}, u32[]{:S(2)}, u32[]{:S(2)}) collective-permute-start(bf16[128,2048]{1,0:T(8,128)(2,1)} %get-tuple-element.174), channel_id=1, source_target_pairs={{0,2},{2,0},{4,6},{6,4},{8,10},{10,8},{12,14},{14,12},{16,18},{18,... | collective-permute-start | bytes 1572872 | tf_op jit(solution)/shard_map/ppermute | solution.py:357
  185.7 3.8 %collective-permute-start.38 = (bf16[128,1536]{1,0:T(8,128)(2,1)}, bf16[128,1536]{1,0:T(8,128)(2,1)}, u32[]{:S(2)}, u32[]{:S(2)}) collective-permute-start(bf16[128,1536]{1,0:T(8,128)(2,1)} %get-tuple-element.177), channel_id=1, source_target_pairs={{8,0},{10,2},{12,4},{14,6},{16,8},{18,10},{20,12},{22,14},{24,16},... | collective-permute-start | bytes 1179656 | tf_op jit(solution)/shard_map/ppermute | solution.py:371
  189.5 2.0 copy.9
  192.8 6.6 %collective-permute-done.37.refs_3_ = bf16[128,1536]{1,0:T(8,128)(2,1)S(1)} collective-permute-done((bf16[128,1536]{1,0:T(8,128)(2,1)}, bf16[128,1536]{1,0:T(8,128)(2,1)S(1)}, u32[]{:S(2)}, u32[]{:S(2)}) %collective-permute-start.37) | collective-permute-done | bytes 393248 | tf_op jit(solution)/shard_map/ppermute | solution.py:366
  199.4 2.8 %collective-permute-done.38.refs_4_ = bf16[128,1536]{1,0:T(8,128)(2,1)} collective-permute-done((bf16[128,1536]{1,0:T(8,128)(2,1)}, bf16[128,1536]{1,0:T(8,128)(2,1)}, u32[]{:S(2)}, u32[]{:S(2)}) %collective-permute-start.38) | collective-permute-done | bytes 393248 | tf_op jit(solution)/shard_map/ppermute | solution.py:371
  202.2 2.4 %assemble.21 = bf16[128,2048]{1,0:T(8,128)(2,1)} custom-call(bf16[128,2048]{1,0:T(8,128)(2,1)S(1)} %assemble.18.refs_0_, bf16[128,2048]{1,0:T(8,128)(2,1)} %collective-permute-done.35.refs_1_, bf16[128,2048]{1,0:T(8,128)(2,1)} %collective-permute-done.36.refs_2_, bf16[128,1536]{1,0:T(8,128)(2,1)S(1)} %collective-permute-done.37.refs_3_, ...), custom_call_target="tpu_custom_call" | custom-call | flops 524288 | bytes 2097152 | tf_op jit(solution)/shard_map/assemble/pallas_call | solution.py:447
  (126 shorter events, 32.5 us)
Async XLA Ops:
  2.8 24.7 %copy-start.2 = (bf16[128,2048]{1,0:T(8,128)(2,1)S(1)}, bf16[128,2048]{1,0:T(8,128)(2,1)}, u32[]{:S(2)}) copy-start(bf16[128,2048]{1,0:T(8,128)(2,1)} %get-tuple-element.103.refs_0_) | copy-start | bytes 1572868
  2.8 24.7 %collective-permute-start = (bf16[128,2048]{1,0:T(8,128)(2,1)}, bf16[128,2048]{1,0:T(8,128)(2,1)S(1)}, u32[]{:S(2)}, u32[]{:S(2)}) collective-permute-start(bf16[128,2048]{1,0:T(8,128)(2,1)} %get-tuple-element.103.refs_0_), channel_id=1, source_target_pairs={{0,2},{2,0},{4,6},{6,4},{8,10},{10,8},{12,14},{14,12},{16,18},{18,... | collective-permute-start | bytes 1572872 | tf_op jit(solution)/shard_map/ppermute | solution.py:357
  5.8 21.7 %collective-permute-start.1 = (bf16[128,2048]{1,0:T(8,128)(2,1)}, bf16[128,2048]{1,0:T(8,128)(2,1)S(1)}, u32[]{:S(2)}, u32[]{:S(2)}) collective-permute-start(bf16[128,2048]{1,0:T(8,128)(2,1)} %get-tuple-element.103.refs_0_), channel_id=1, source_target_pairs={{0,4},{2,6},{4,0},{6,2},{8,12},{10,14},{12,8},{14,10},{16,20},{18,... | collective-permute-start | bytes 1572872 | tf_op jit(solution)/shard_map/ppermute | solution.py:361
  7.3 14.1 %collective-permute-start.2 = (bf16[96,2048]{1,0:T(8,128)(2,1)}, bf16[96,2048]{1,0:T(8,128)(2,1)S(1)}, u32[]{:S(2)}, u32[]{:S(2)}) collective-permute-start(bf16[96,2048]{1,0:T(8,128)(2,1)} %get-tuple-element.94), channel_id=1, source_target_pairs={{0,8},{2,10},{4,12},{6,14},{8,16},{10,18},{12,20},{14,22},{16,24},... | collective-permute-start | bytes 1179656 | tf_op jit(solution)/shard_map/ppermute | solution.py:366
  8.9 18.6 %collective-permute-start.3 = (bf16[96,2048]{1,0:T(8,128)(2,1)}, bf16[96,2048]{1,0:T(8,128)(2,1)S(1)}, u32[]{:S(2)}, u32[]{:S(2)}) collective-permute-start(bf16[96,2048]{1,0:T(8,128)(2,1)} %get-tuple-element.94), channel_id=1, source_target_pairs={{8,0},{10,2},{12,4},{14,6},{16,8},{18,10},{20,12},{22,14},{24,16},... | collective-permute-start | bytes 1179656 | tf_op jit(solution)/shard_map/ppermute | solution.py:371
  14.7 54.1 %collective-permute-start.16 = (bf16[384,2048]{1,0:T(8,128)(2,1)}, bf16[384,2048]{1,0:T(8,128)(2,1)}, u32[]{:S(2)}, u32[]{:S(2)}) collective-permute-start(bf16[384,2048]{1,0:T(8,128)(2,1)} %get-tuple-element.135), channel_id=1, source_target_pairs={{0,1},{1,0},{2,3},{3,2},{4,5},{5,4},{6,7},{7,6},{8,9},{9,8},{10,11... | collective-permute-start | bytes 4718600 | tf_op jit(solution)/shard_map/ppermute | solution.py:353
  29.4 6.2 %copy-start.15 = (bf16[384,2048]{1,0:T(8,128)(2,1)S(1)}, bf16[384,2048]{1,0:T(8,128)(2,1)}, u32[]{:S(2)}) copy-start(bf16[384,2048]{1,0:T(8,128)(2,1)} %get-tuple-element.108) | copy-start | bytes 4718596
  29.4 25.9 %collective-permute-start.4 = (bf16[256,2048]{1,0:T(8,128)(2,1)}, bf16[256,2048]{1,0:T(8,128)(2,1)S(1)}, u32[]{:S(2)}, u32[]{:S(2)}) collective-permute-start(bf16[256,2048]{1,0:T(8,128)(2,1)} %get-tuple-element.111), channel_id=1, source_target_pairs={{0,2},{2,0},{4,6},{6,4},{8,10},{10,8},{12,14},{14,12},{16,18},{18,... | collective-permute-start | bytes 3145736 | tf_op jit(solution)/shard_map/ppermute | solution.py:357
  30.0 5.5 %copy-start.7 = (bf16[96,2048]{1,0:T(8,128)(2,1)S(1)}, bf16[96,2048]{1,0:T(8,128)(2,1)}, u32[]{:S(2)}) copy-start(bf16[96,2048]{1,0:T(8,128)(2,1)} %copy-done.6) | copy-start | bytes 1179652
  30.0 26.4 %collective-permute-start.5 = (bf16[256,2048]{1,0:T(8,128)(2,1)}, bf16[256,2048]{1,0:T(8,128)(2,1)S(1)}, u32[]{:S(2)}, u32[]{:S(2)}) collective-permute-start(bf16[256,2048]{1,0:T(8,128)(2,1)} %get-tuple-element.112), channel_id=1, source_target_pairs={{0,4},{2,6},{4,0},{6,2},{8,12},{10,14},{12,8},{14,10},{16,20},{18,... | collective-permute-start | bytes 3145736 | tf_op jit(solution)/shard_map/ppermute | solution.py:361
  30.5 15.6 %collective-permute-start.6 = (bf16[112,2048]{1,0:T(8,128)(2,1)}, bf16[112,2048]{1,0:T(8,128)(2,1)}, u32[]{:S(2)}, u32[]{:S(2)}) collective-permute-start(bf16[112,2048]{1,0:T(8,128)(2,1)} %get-tuple-element.113), channel_id=1, source_target_pairs={{0,8},{2,10},{4,12},{6,14},{8,16},{10,18},{12,20},{14,22},{16,24},... | collective-permute-start | bytes 1376264 | tf_op jit(solution)/shard_map/ppermute | solution.py:366
  31.7 23.7 %collective-permute-start.7 = (bf16[112,2048]{1,0:T(8,128)(2,1)}, bf16[112,2048]{1,0:T(8,128)(2,1)}, u32[]{:S(2)}, u32[]{:S(2)}) collective-permute-start(bf16[112,2048]{1,0:T(8,128)(2,1)} %get-tuple-element.114), channel_id=1, source_target_pairs={{8,0},{10,2},{12,4},{14,6},{16,8},{18,10},{20,12},{22,14},{24,16},... | collective-permute-start | bytes 1376264 | tf_op jit(solution)/shard_map/ppermute | solution.py:371
  39.0 53.5 %all-to-all-start = ((bf16[128,16,128]{2,0,1:T(8,128)(2,1)}), bf16[128,16,128]{2,0,1:T(8,128)(2,1)S(1)}, u32[]{:S(2)}, u32[]{:S(2)}) async-start(bf16[128,16,128]{2,0,1:T(8,128)(2,1)} %copy.8), calls=%async_computation | async-start | bytes 1048576 | tf_op jit(solution)/shard_map/all_to_all | solution.py:494
  57.7 21.0 %collective-permute-start.8 = (bf16[192,2048]{1,0:T(8,128)(2,1)S(1)}, bf16[192,2048]{1,0:T(8,128)(2,1)S(1)}, u32[]{:S(2)}, u32[]{:S(2)}) collective-permute-start(bf16[192,2048]{1,0:T(8,128)(2,1)S(1)} %get-tuple-element.119), channel_id=1, source_target_pairs={{0,2},{2,0},{4,6},{6,4},{8,10},{10,8},{12,14},{14,12},{16,18},{18,... | collective-permute-start | bytes 2359304 | tf_op jit(solution)/shard_map/ppermute | solution.py:357
  59.8 18.8 %collective-permute-start.9 = (bf16[192,2048]{1,0:T(8,128)(2,1)S(1)}, bf16[192,2048]{1,0:T(8,128)(2,1)S(1)}, u32[]{:S(2)}, u32[]{:S(2)}) collective-permute-start(bf16[192,2048]{1,0:T(8,128)(2,1)S(1)} %get-tuple-element.120), channel_id=1, source_target_pairs={{0,4},{2,6},{4,0},{6,2},{8,12},{10,14},{12,8},{14,10},{16,20},{18,... | collective-permute-start | bytes 2359304 | tf_op jit(solution)/shard_map/ppermute | solution.py:361
  59.8 15.2 %collective-permute-start.10 = (bf16[96,2048]{1,0:T(8,128)(2,1)S(1)}, bf16[96,2048]{1,0:T(8,128)(2,1)S(1)}, u32[]{:S(2)}, u32[]{:S(2)}) collective-permute-start(bf16[96,2048]{1,0:T(8,128)(2,1)S(1)} %get-tuple-element.121), channel_id=1, source_target_pairs={{0,8},{2,10},{4,12},{6,14},{8,16},{10,18},{12,20},{14,22},{16,24},... | collective-permute-start | bytes 1179656 | tf_op jit(solution)/shard_map/ppermute | solution.py:366
  62.0 16.7 %collective-permute-start.11 = (bf16[96,2048]{1,0:T(8,128)(2,1)S(1)}, bf16[96,2048]{1,0:T(8,128)(2,1)S(1)}, u32[]{:S(2)}, u32[]{:S(2)}) collective-permute-start(bf16[96,2048]{1,0:T(8,128)(2,1)S(1)} %get-tuple-element.122), channel_id=1, source_target_pairs={{8,0},{10,2},{12,4},{14,6},{16,8},{18,10},{20,12},{22,14},{24,16},... | collective-permute-start | bytes 1179656 | tf_op jit(solution)/shard_map/ppermute | solution.py:371
  72.9 19.7 %collective-permute-start.18 = (bf16[736,384]{1,0:T(8,128)(2,1)}, bf16[736,384]{1,0:T(8,128)(2,1)S(1)}, u32[]{:S(2)}, u32[]{:S(2)}) collective-permute-start(bf16[736,384]{1,0:T(8,128)(2,1)} %convolution_convert_fusion.3), channel_id=1, source_target_pairs={{0,1},{1,0},{2,3},{3,2},{4,5},{5,4},{6,7},{7,6},{8,9},{9,8},{10,11... | collective-permute-start | bytes 1695752 | tf_op jit(solution)/shard_map/ppermute | solution.py:353
  78.8 12.1 %collective-permute-start.12 = (bf16[48,2048]{1,0:T(8,128)(2,1)S(1)}, bf16[48,2048]{1,0:T(8,128)(2,1)S(1)}, u32[]{:S(2)}, u32[]{:S(2)}) collective-permute-start(bf16[48,2048]{1,0:T(8,128)(2,1)S(1)} %get-tuple-element.127), channel_id=1, source_target_pairs={{0,2},{2,0},{4,6},{6,4},{8,10},{10,8},{12,14},{14,12},{16,18},{18,... | collective-permute-start | bytes 589832 | tf_op jit(solution)/shard_map/ppermute | solution.py:357
  80.3 10.7 %collective-permute-start.13 = (bf16[48,2048]{1,0:T(8,128)(2,1)S(1)}, bf16[48,2048]{1,0:T(8,128)(2,1)S(1)}, u32[]{:S(2)}, u32[]{:S(2)}) collective-permute-start(bf16[48,2048]{1,0:T(8,128)(2,1)S(1)} %get-tuple-element.128), channel_id=1, source_target_pairs={{0,4},{2,6},{4,0},{6,2},{8,12},{10,14},{12,8},{14,10},{16,20},{18,... | collective-permute-start | bytes 589832 | tf_op jit(solution)/shard_map/ppermute | solution.py:361
  81.9 8.5 %collective-permute-start.14 = (bf16[32,2048]{1,0:T(8,128)(2,1)S(1)}, bf16[32,2048]{1,0:T(8,128)(2,1)S(1)}, u32[]{:S(2)}, u32[]{:S(2)}) collective-permute-start(bf16[32,2048]{1,0:T(8,128)(2,1)S(1)} %get-tuple-element.129), channel_id=1, source_target_pairs={{0,8},{2,10},{4,12},{6,14},{8,16},{10,18},{12,20},{14,22},{16,24},... | collective-permute-start | bytes 393224 | tf_op jit(solution)/shard_map/ppermute | solution.py:366
  84.9 5.5 %collective-permute-start.15 = (bf16[32,2048]{1,0:T(8,128)(2,1)S(1)}, bf16[32,2048]{1,0:T(8,128)(2,1)S(1)}, u32[]{:S(2)}, u32[]{:S(2)}) collective-permute-start(bf16[32,2048]{1,0:T(8,128)(2,1)S(1)} %get-tuple-element.130), channel_id=1, source_target_pairs={{8,0},{10,2},{12,4},{14,6},{16,8},{18,10},{20,12},{22,14},{24,16},... | collective-permute-start | bytes 393224 | tf_op jit(solution)/shard_map/ppermute | solution.py:371
  90.4 2.1 %collective-permute-start.17 = (bf16[576,384]{1,0:T(8,128)(2,1)}, bf16[576,384]{1,0:T(8,128)(2,1)}, u32[]{:S(2)}, u32[]{:S(2)}) collective-permute-start(bf16[576,384]{1,0:T(8,128)(2,1)} %convolution_convert_fusion.5), channel_id=1, source_target_pairs={{0,1},{1,0},{2,3},{3,2},{4,5},{5,4},{6,7},{7,6},{8,9},{9,8},{10,11... | collective-permute-start | bytes 1327112 | tf_op jit(solution)/shard_map/ppermute | solution.py:353
  90.4 3.0 %collective-permute-start.19 = (bf16[576,384]{1,0:T(8,128)(2,1)}, bf16[576,384]{1,0:T(8,128)(2,1)}, u32[]{:S(2)}, u32[]{:S(2)}) collective-permute-start(bf16[576,384]{1,0:T(8,128)(2,1)} %convolution_convert_fusion.4), channel_id=1, source_target_pairs={{0,1},{1,0},{2,3},{3,2},{4,5},{5,4},{6,7},{7,6},{8,9},{9,8},{10,11... | collective-permute-start | bytes 1327112 | tf_op jit(solution)/shard_map/ppermute | solution.py:353
  91.7 1.7 collective-permute-start.20
  98.0 15.5 %copy-start.17 = (bf16[384,2048]{1,0:T(8,128)(2,1)S(1)}, bf16[384,2048]{1,0:T(8,128)(2,1)}, u32[]{:S(2)}) copy-start(bf16[384,2048]{1,0:T(8,128)(2,1)} %get-tuple-element.108) | copy-start | bytes 4718596
  111.2 2.3 %collective-permute-start.21 = (bf16[1024,384]{1,0:T(8,128)(2,1)S(1)}, bf16[1024,384]{1,0:T(8,128)(2,1)S(1)}, u32[]{:S(2)}, u32[]{:S(2)}) collective-permute-start(bf16[1024,384]{1,0:T(8,128)(2,1)S(1)} %get-tuple-element.138), channel_id=1, source_target_pairs={{0,1},{1,0},{2,3},{3,2},{4,5},{5,4},{6,7},{7,6},{8,9},{9,8},{10,11... | collective-permute-start | bytes 2359304 | tf_op jit(solution)/shard_map/ppermute | solution.py:353
  111.6 22.8 %collective-permute-start.26 = (bf16[1024,384]{1,0:T(8,128)(2,1)S(1)}, bf16[1024,384]{1,0:T(8,128)(2,1)S(1)}, u32[]{:S(2)}, u32[]{:S(2)}) collective-permute-start(bf16[1024,384]{1,0:T(8,128)(2,1)S(1)} %get-tuple-element.148), channel_id=1, source_target_pairs={{0,1},{1,0},{2,3},{3,2},{4,5},{5,4},{6,7},{7,6},{8,9},{9,8},{10,11... | collective-permute-start | bytes 2359304 | tf_op jit(solution)/shard_map/ppermute | solution.py:353
  117.2 10.1 %collective-permute-start.22 = (bf16[128,768]{1,0:T(8,128)(2,1)S(1)}, bf16[128,768]{1,0:T(8,128)(2,1)S(1)}, u32[]{:S(2)}, u32[]{:S(2)}) collective-permute-start(bf16[128,768]{1,0:T(8,128)(2,1)S(1)} %get-tuple-element.139), channel_id=1, source_target_pairs={{0,2},{2,0},{4,6},{6,4},{8,10},{10,8},{12,14},{14,12},{16,18},{18,... | collective-permute-start | bytes 589832 | tf_op jit(solution)/shard_map/ppermute | solution.py:357
  118.6 8.7 %collective-permute-start.23 = (bf16[128,768]{1,0:T(8,128)(2,1)S(1)}, bf16[128,768]{1,0:T(8,128)(2,1)S(1)}, u32[]{:S(2)}, u32[]{:S(2)}) collective-permute-start(bf16[128,768]{1,0:T(8,128)(2,1)S(1)} %get-tuple-element.140), channel_id=1, source_target_pairs={{0,4},{2,6},{4,0},{6,2},{8,12},{10,14},{12,8},{14,10},{16,20},{18,... | collective-permute-start | bytes 589832 | tf_op jit(solution)/shard_map/ppermute | solution.py:361
  118.9 8.2 %collective-permute-start.24 = (bf16[128,512]{1,0:T(8,128)(2,1)S(1)}, bf16[128,512]{1,0:T(8,128)(2,1)S(1)}, u32[]{:S(2)}, u32[]{:S(2)}) collective-permute-start(bf16[128,512]{1,0:T(8,128)(2,1)S(1)} %get-tuple-element.141), channel_id=1, source_target_pairs={{0,8},{2,10},{4,12},{6,14},{8,16},{10,18},{12,20},{14,22},{16,24},... | collective-permute-start | bytes 393224 | tf_op jit(solution)/shard_map/ppermute | solution.py:366
  119.5 7.7 %collective-permute-start.25 = (bf16[128,512]{1,0:T(8,128)(2,1)S(1)}, bf16[128,512]{1,0:T(8,128)(2,1)S(1)}, u32[]{:S(2)}, u32[]{:S(2)}) collective-permute-start(bf16[128,512]{1,0:T(8,128)(2,1)S(1)} %get-tuple-element.142), channel_id=1, source_target_pairs={{8,0},{10,2},{12,4},{14,6},{16,8},{18,10},{20,12},{22,14},{24,16},... | collective-permute-start | bytes 393224 | tf_op jit(solution)/shard_map/ppermute | solution.py:371
  127.5 22.4 %collective-permute-start.27 = (bf16[128,3072]{1,0:T(8,128)(2,1)S(1)}, bf16[128,3072]{1,0:T(8,128)(2,1)S(1)}, u32[]{:S(2)}, u32[]{:S(2)}) collective-permute-start(bf16[128,3072]{1,0:T(8,128)(2,1)S(1)} %get-tuple-element.153), channel_id=1, source_target_pairs={{0,2},{2,0},{4,6},{6,4},{8,10},{10,8},{12,14},{14,12},{16,18},{18,... | collective-permute-start | bytes 2359304 | tf_op jit(solution)/shard_map/ppermute | solution.py:357
  129.1 20.9 %collective-permute-start.28 = (bf16[128,3072]{1,0:T(8,128)(2,1)S(1)}, bf16[128,3072]{1,0:T(8,128)(2,1)S(1)}, u32[]{:S(2)}, u32[]{:S(2)}) collective-permute-start(bf16[128,3072]{1,0:T(8,128)(2,1)S(1)} %get-tuple-element.154), channel_id=1, source_target_pairs={{0,4},{2,6},{4,0},{6,2},{8,12},{10,14},{12,8},{14,10},{16,20},{18,... | collective-permute-start | bytes 2359304 | tf_op jit(solution)/shard_map/ppermute | solution.py:361
  130.6 13.9 %collective-permute-start.29 = (bf16[128,1536]{1,0:T(8,128)(2,1)S(1)}, bf16[128,1536]{1,0:T(8,128)(2,1)S(1)}, u32[]{:S(2)}, u32[]{:S(2)}) collective-permute-start(bf16[128,1536]{1,0:T(8,128)(2,1)S(1)} %get-tuple-element.155), channel_id=1, source_target_pairs={{0,8},{2,10},{4,12},{6,14},{8,16},{10,18},{12,20},{14,22},{16,24},... | collective-permute-start | bytes 1179656 | tf_op jit(solution)/shard_map/ppermute | solution.py:366
  131.7 18.2 %collective-permute-start.30 = (bf16[128,1536]{1,0:T(8,128)(2,1)S(1)}, bf16[128,1536]{1,0:T(8,128)(2,1)S(1)}, u32[]{:S(2)}, u32[]{:S(2)}) collective-permute-start(bf16[128,1536]{1,0:T(8,128)(2,1)S(1)} %get-tuple-element.156), channel_id=1, source_target_pairs={{8,0},{10,2},{12,4},{14,6},{16,8},{18,10},{20,12},{22,14},{24,16},... | collective-permute-start | bytes 1179656 | tf_op jit(solution)/shard_map/ppermute | solution.py:371
  137.6 14.4 %copy-start = (bf16[640,2048]{1,0:T(8,128)(2,1)}, bf16[640,2048]{1,0:T(8,128)(2,1)S(1)}, u32[]{:S(2)}) copy-start(bf16[640,2048]{1,0:T(8,128)(2,1)S(1)} %convolution_convert_fusion.1.refs_1_.refs_0_) | copy-start | bytes 7864324
  152.0 27.4 %collective-permute-start.31 = (bf16[128,4096]{1,0:T(8,128)(2,1)}, bf16[128,4096]{1,0:T(8,128)(2,1)}, u32[]{:S(2)}, u32[]{:S(2)}) collective-permute-start(bf16[128,4096]{1,0:T(8,128)(2,1)} %get-tuple-element.166), channel_id=1, source_target_pairs={{0,2},{2,0},{4,6},{6,4},{8,10},{10,8},{12,14},{14,12},{16,18},{18,... | collective-permute-start | bytes 3145736 | tf_op jit(solution)/shard_map/ppermute | solution.py:357
  152.4 27.8 %collective-permute-start.32 = (bf16[128,4096]{1,0:T(8,128)(2,1)}, bf16[128,4096]{1,0:T(8,128)(2,1)}, u32[]{:S(2)}, u32[]{:S(2)}) collective-permute-start(bf16[128,4096]{1,0:T(8,128)(2,1)} %get-tuple-element.167), channel_id=1, source_target_pairs={{0,4},{2,6},{4,0},{6,2},{8,12},{10,14},{12,8},{14,10},{16,20},{18,... | collective-permute-start | bytes 3145736 | tf_op jit(solution)/shard_map/ppermute | solution.py:361
  153.0 15.6 %collective-permute-start.33 = (bf16[128,1792]{1,0:T(8,128)(2,1)}, bf16[128,1792]{1,0:T(8,128)(2,1)}, u32[]{:S(2)}, u32[]{:S(2)}) collective-permute-start(bf16[128,1792]{1,0:T(8,128)(2,1)} %get-tuple-element.168), channel_id=1, source_target_pairs={{0,8},{2,10},{4,12},{6,14},{8,16},{10,18},{12,20},{14,22},{16,24},... | collective-permute-start | bytes 1376264 | tf_op jit(solution)/shard_map/ppermute | solution.py:366
  153.4 25.8 %collective-permute-start.34 = (bf16[128,1792]{1,0:T(8,128)(2,1)}, bf16[128,1792]{1,0:T(8,128)(2,1)}, u32[]{:S(2)}, u32[]{:S(2)}) collective-permute-start(bf16[128,1792]{1,0:T(8,128)(2,1)} %get-tuple-element.169), channel_id=1, source_target_pairs={{8,0},{10,2},{12,4},{14,6},{16,8},{18,10},{20,12},{22,14},{24,16},... | collective-permute-start | bytes 1376264 | tf_op jit(solution)/shard_map/ppermute | solution.py:371
  156.8 32.7 %all-to-all-start.1 = ((bf16[16,128,128]{2,1,0:T(8,128)(2,1)}), bf16[16,128,128]{2,1,0:T(8,128)(2,1)}, u32[]{:S(2)}, u32[]{:S(2)}) async-start(bf16[16,128,128]{2,1,0:T(8,128)(2,1)} %bitcast.13), calls=%async_computation.1 | async-start | bytes 1048576 | tf_op jit(solution)/shard_map/all_to_all | solution.py:649
  162.3 3.0 %copy-start.5 = (bf16[128,1536]{1,0:T(8,128)(2,1)S(1)}, bf16[128,1536]{1,0:T(8,128)(2,1)}, u32[]{:S(2)}) copy-start(bf16[128,1536]{1,0:T(8,128)(2,1)} %copy-done.4) | copy-start | bytes 1179652
  162.4 17.8 %copy-start.1 = (bf16[640,2048]{1,0:T(8,128)(2,1)S(1)}, bf16[640,2048]{1,0:T(8,128)(2,1)}, u32[]{:S(2)}) copy-start(bf16[640,2048]{1,0:T(8,128)(2,1)} %copy-done) | copy-start | bytes 7864324
  183.3 18.9 %collective-permute-start.35 = (bf16[128,2048]{1,0:T(8,128)(2,1)}, bf16[128,2048]{1,0:T(8,128)(2,1)}, u32[]{:S(2)}, u32[]{:S(2)}) collective-permute-start(bf16[128,2048]{1,0:T(8,128)(2,1)} %get-tuple-element.174), channel_id=1, source_target_pairs={{0,2},{2,0},{4,6},{6,4},{8,10},{10,8},{12,14},{14,12},{16,18},{18,... | collective-permute-start | bytes 1572872 | tf_op jit(solution)/shard_map/ppermute | solution.py:357
  185.7 16.5 %collective-permute-start.36 = (bf16[128,2048]{1,0:T(8,128)(2,1)}, bf16[128,2048]{1,0:T(8,128)(2,1)}, u32[]{:S(2)}, u32[]{:S(2)}) collective-permute-start(bf16[128,2048]{1,0:T(8,128)(2,1)} %get-tuple-element.175), channel_id=1, source_target_pairs={{0,4},{2,6},{4,0},{6,2},{8,12},{10,14},{12,8},{14,10},{16,20},{18,... | collective-permute-start | bytes 1572872 | tf_op jit(solution)/shard_map/ppermute | solution.py:361
  185.7 13.7 %collective-permute-start.37 = (bf16[128,1536]{1,0:T(8,128)(2,1)}, bf16[128,1536]{1,0:T(8,128)(2,1)S(1)}, u32[]{:S(2)}, u32[]{:S(2)}) collective-permute-start(bf16[128,1536]{1,0:T(8,128)(2,1)} %get-tuple-element.176), channel_id=1, source_target_pairs={{0,8},{2,10},{4,12},{6,14},{8,16},{10,18},{12,20},{14,22},{16,24},... | collective-permute-start | bytes 1179656 | tf_op jit(solution)/shard_map/ppermute | solution.py:366
  185.7 16.5 %collective-permute-start.38 = (bf16[128,1536]{1,0:T(8,128)(2,1)}, bf16[128,1536]{1,0:T(8,128)(2,1)}, u32[]{:S(2)}, u32[]{:S(2)}) collective-permute-start(bf16[128,1536]{1,0:T(8,128)(2,1)} %get-tuple-element.177), channel_id=1, source_target_pairs={{8,0},{10,2},{12,4},{14,6},{16,8},{18,10},{20,12},{22,14},{24,16},... | collective-permute-start | bytes 1179656 | tf_op jit(solution)/shard_map/ppermute | solution.py:371
  (15 other events, 26.6 us)

commit v6 on v4

--- a/solution.py
+++ b/solution.py
@@ -212,7 +212,7 @@
             member = base + step
             index = place(group, member)
             rows = pl.ds(pl.multiple_of(offset + step * count, 16), count)
-            feats = own[source][rows, :] + other[source][rows, :].astype(jnp.float32)
+            feats = widened(own[source][rows, :]) + widened(other[source][rows, :])
             feats = rounded(feats)
             slot = (group * PLANE + member) * span + first
             feats_s[pl.ds(pl.multiple_of(slot, 16), count), :] = feats
@@ -487,7 +487,7 @@
         jnp.einsum("td,rd->tr", rows, matrix, preferred_element_type=jnp.float32)
         for matrix in (kept, taken)
     )
-    return own, swapped(narrowed(given))
+    return narrowed(own), swapped(narrowed(given))
 
 
 def columns_held(rows):
@@ -505,7 +505,7 @@
 
     own_x, own_y, wide_3, wide_1 = all_ways(tokens, tokens, wide, wide)
     first = (tokens, own_x, own_y, wide_3, wide_1)
-    members = ((0, n, m), (1, n, m), (2, n, m))
+    members = ((0, n, m), (1, n, m))
     sent = put(
         first,
         ((2, 0, nh), (2, n, mh), (3, 0, n), (4, 0, n)),
@@ -520,15 +520,15 @@
     across = ((0, nh, mh), (1, nh, mh))
     third = all_ways(
         *put(
-            second,
+            (*second, own_y),
             ((1, start, nh), (1, start + n, nh), *wide_2),
             ((0, start + nh, nh), (0, start + n + nh, nh), *wide_2),
-            (*across, (2, nh, nh)),
-            (*across, (3, 2 * nh, nh)),
+            (*across, (4, n, m), (2, nh, m)),
+            (*across, (4, n, m), (3, nh + m, m)),
         )
     )
     fourth = all_ways(
-        *put(third, ((1, n, nh),), ((0, n + nh, nh),), ((2, 0, mh),), ((3, mh, mh),))
+        *put(third, ((1, n, nh),), ((0, n + nh, nh),), ((2, 0, m),), ((3, m, m),))
     )
     runs = [
         (0, 0, 0, 0, 3, span, 0),
@@ -547,9 +547,9 @@
     for side in range(2):
         runs += [
             (1, offset, 2, 0, 1, nh, side * nh),
-            (1, offset + nh, 3 - 2 * side, 0, 3, m, n),
+            (1, offset + nh, 3 - 2 * side, 0, 2, m, n),
         ]
-        offset += nh + 3 * m
+        offset += nh + 2 * m
     offset = 0
     for side in range(2):
         runs += [
@@ -560,15 +560,15 @@
         offset += 2 * n
     runs += [
         (2, offset, 3, 3, 1, m, n),
-        (2, offset + m, 2, 0, 1, m, n),
-        (2, offset + 2 * m, 2, 1, 1, mh, n),
-        (2, offset + 2 * m + mh, 1, 3, 1, m, n),
-        (2, offset + 3 * m + mh, 2, 1, 1, mh, n + mh),
-        (2, offset + 3 * m + 2 * mh, 2, 2, 1, m, n),
+        (2, offset + m, 3, 2, 1, m, n),
+        (2, offset + 2 * m, 2, 0, 1, m, n),
+        (2, offset + 3 * m, 1, 3, 1, m, n),
+        (2, offset + 4 * m, 1, 2, 1, m, n),
+        (2, offset + 5 * m, 2, 1, 1, m, n),
         (3, 0, 2, 3, 1, nh, 0),
         (3, nh, 2, 3, 1, nh, nh),
-        (3, n, 2, 3, 1, mh, n),
-        (3, n + mh, 2, 3, 1, mh, n + mh),
+        (3, n, 2, 3, 1, m, n),
+        (3, n + m, 2, 2, 1, m, n),
     ]
     parts = [project(part, *matrices) for part in (first, second, third, fourth)]
     later, first = lax.optimization_barrier((later, parts[0][0]))

time: 205 us -> 208 us (1.015)
  waiting for transfers between devices: 80.2 us -> 76.9 us
  local copies, waits for them, and re-layouts: 12 us -> 15.2 us
    ppermute x8, waiting for transfers between devices: 40.9 us -> 34.8 us  [down(): lax.ppermute(value, 'ctx', [((i + PLANE) % count, i) for i in range(count)])]
    unnamed x53 -> x57, local copies, waits for them, and re-layouts: 6.66 us -> 10.9 us
    ppermute x8, waiting for transfers between devices: 4.31 us -> 7.76 us  [over_x(): lax.ppermute(value, 'ctx', [(i, i ^ 1) for i in range(lax.axis_size('ctx'...]
    pallas_call x10, Pallas kernels: 11.7 us -> 13.9 us  [assemble(): pl.pallas_call(functools.partial(assemble_kernel, len(arrays), plans), ou...]
  transfers between devices with their start and end apart: 41 -> 41, of which waited for: 19 -> 19; matrix products, arithmetic and copies ran while one was open for 16% -> 15% of each run, Pallas kernels for 6% -> 6%
where the time goes in v6:
time: 208 us; the launch traced here: 207 us
  waiting for transfers between devices  76.9 us (37%)
  starting transfers between devices  56.9 us (27%)
  Pallas kernels  32.8 us (16%)
  matrix products  24.1 us (12%)
  local copies, waits for them, and re-layouts  15.2 us (7%)
    ppermute x8, waiting for transfers between devices, down(): lax.ppermute(value, 'ctx', [((i + PLANE) % count, i) for i in range(count)])  34.8 us
    ppermute x8, waiting for transfers between devices, up(): lax.ppermute(value, 'ctx', [(i, (i + PLANE) % count) for i in range(count)])  30.3 us
    ppermute x8, starting transfers between devices, down(): lax.ppermute(value, 'ctx', [((i + PLANE) % count, i) for i in range(count)])  26.7 us
    dot_general x8, matrix products, project(): jnp.einsum('td,rd->tr', rows, matrix, preferred_element_type=jnp.float32)  15.1 us
    pallas_call x10, Pallas kernels, assemble(): pl.pallas_call(functools.partial(assemble_kernel, len(arrays), plans), ou...  13.9 us
    pallas_call x1, Pallas kernels, scan_all(): pl.pallas_call(functools.partial(scan_kernel, PLANE, runs, order), out_sh...  13.2 us
    unnamed x57, local copies, waits for them, and re-layouts  10.9 us
    dot_general x3, matrix products, product(): return narrowed(jnp.dot(both, matrix, preferred_element_type=jnp.float32))  9.01 us
  transfers between devices with their start and end apart: 41, of which 19 were waited for; matrix products, arithmetic and copies ran while one was open for 15% of the time, Pallas kernels for 6%

profile of v6, /device:TPU:0, one launch (start us, length us, event | category | flops | bytes accessed | tf_op | source)
XLA Modules:
  0.0 207.1 jit_solution(14872506202435805296)
XLA Ops:
  0.6 2.2 %halves.2 = (bf16[128,2048]{1,0:T(8,128)(2,1)}, bf16[96,2048]{1,0:T(8,128)(2,1)}) custom-call(s32[1]{0:T(128)} %bitcast.5.core_ref, bf16[128,4096]{1,0:T(8,128)(2,1)} %refs_0_.1), custom_call_target="tpu_custom_call" | custom-call | bytes 1835008 | tf_op jit(solution)/shard_map/halves/pallas_call | solution.py:409
  2.8 3.0 %collective-permute-start.1 = (bf16[128,2048]{1,0:T(8,128)(2,1)}, bf16[128,2048]{1,0:T(8,128)(2,1)S(1)}, u32[]{:S(2)}, u32[]{:S(2)}) collective-permute-start(bf16[128,2048]{1,0:T(8,128)(2,1)} %get-tuple-element.103.refs_0_), channel_id=1, source_target_pairs={{0,4},{2,6},{4,0},{6,2},{8,12},{10,14},{12,8},{14,10},{16,20},{18,... | collective-permute-start | bytes 1572872 | tf_op jit(solution)/shard_map/ppermute | solution.py:361
  5.8 1.5 collective-permute-start
  7.3 3.6 %collective-permute-start.3 = (bf16[96,2048]{1,0:T(8,128)(2,1)}, bf16[96,2048]{1,0:T(8,128)(2,1)S(1)}, u32[]{:S(2)}, u32[]{:S(2)}) collective-permute-start(bf16[96,2048]{1,0:T(8,128)(2,1)} %get-tuple-element.94), channel_id=1, source_target_pairs={{8,0},{10,2},{12,4},{14,6},{16,8},{18,10},{20,12},{22,14},{24,16},... | collective-permute-start | bytes 1179656 | tf_op jit(solution)/shard_map/ppermute | solution.py:371
  10.9 3.5 %halves.3 = (bf16[384,2048]{1,0:T(8,128)(2,1)}, bf16[384,2048]{1,0:T(8,128)(2,1)}) custom-call(s32[1]{0:T(128)} %bitcast.5.core_ref, bf16[384,4096]{1,0:T(8,128)(2,1)} %bitcast.46), custom_call_target="tpu_custom_call" | custom-call | bytes 6291456 | tf_op jit(solution)/shard_map/halves/pallas_call | solution.py:409
  14.6 6.3 %collective-permute-done.3.refs_4_ = bf16[96,2048]{1,0:T(8,128)(2,1)S(1)} collective-permute-done((bf16[96,2048]{1,0:T(8,128)(2,1)}, bf16[96,2048]{1,0:T(8,128)(2,1)S(1)}, u32[]{:S(2)}, u32[]{:S(2)}) %collective-permute-start.3) | collective-permute-done | bytes 393248 | tf_op jit(solution)/shard_map/ppermute | solution.py:371
  20.8 7.4 %collective-permute-done.2.refs_3_ = bf16[96,2048]{1,0:T(8,128)(2,1)S(1)} collective-permute-done((bf16[96,2048]{1,0:T(8,128)(2,1)}, bf16[96,2048]{1,0:T(8,128)(2,1)S(1)}, u32[]{:S(2)}, u32[]{:S(2)}) %collective-permute-start.2) | collective-permute-done | bytes 393248 | tf_op jit(solution)/shard_map/ppermute | solution.py:366
  28.3 1.9 assemble.10
  30.2 1.6 collective-permute-start.6
  31.8 2.2 %collective-permute-start.7 = (bf16[112,2048]{1,0:T(8,128)(2,1)}, bf16[112,2048]{1,0:T(8,128)(2,1)}, u32[]{:S(2)}, u32[]{:S(2)}) collective-permute-start(bf16[112,2048]{1,0:T(8,128)(2,1)} %get-tuple-element.114), channel_id=1, source_target_pairs={{8,0},{10,2},{12,4},{14,6},{16,8},{18,10},{20,12},{22,14},{24,16},... | collective-permute-start | bytes 1376264 | tf_op jit(solution)/shard_map/ppermute | solution.py:371
  36.3 2.2 %convolution_convert_fusion.8.refs_1_ = bf16[576,384]{1,0:T(8,128)(2,1)} fusion(bf16[576,2048]{1,0:T(8,128)(2,1)S(1)} %constant_dynamic-update-slice_fusion, bf16[384,2048]{1,0:T(8,128)(2,1)S(1)} %copy-done.15), kind=kOutput, calls=%fused_computation.12 | convolution fusion | flops 906190848 | bytes 4374528 | tf_op jit(solution)/shard_map/td,rd->tr/dot_general | solution.py:487
  39.5 3.8 %all-to-all-start = ((bf16[128,16,128]{2,0,1:T(8,128)(2,1)}), bf16[128,16,128]{2,0,1:T(8,128)(2,1)S(1)}, u32[]{:S(2)}, u32[]{:S(2)}) async-start(bf16[128,16,128]{2,0,1:T(8,128)(2,1)} %copy.8), calls=%async_computation | async-start | bytes 1048576 | tf_op jit(solution)/shard_map/all_to_all | solution.py:494
  43.3 2.4 %collective-permute-done.6.refs_2_ = bf16[112,2048]{1,0:T(8,128)(2,1)} collective-permute-done((bf16[112,2048]{1,0:T(8,128)(2,1)}, bf16[112,2048]{1,0:T(8,128)(2,1)}, u32[]{:S(2)}, u32[]{:S(2)}) %collective-permute-start.6) | collective-permute-done | bytes 458784 | tf_op jit(solution)/shard_map/ppermute | solution.py:366
  45.7 8.7 %collective-permute-done.7.refs_3_ = bf16[112,2048]{1,0:T(8,128)(2,1)} collective-permute-done((bf16[112,2048]{1,0:T(8,128)(2,1)}, bf16[112,2048]{1,0:T(8,128)(2,1)}, u32[]{:S(2)}, u32[]{:S(2)}) %collective-permute-start.7) | collective-permute-done | bytes 458784 | tf_op jit(solution)/shard_map/ppermute | solution.py:371
  54.5 6.7 %collective-permute-done.4.refs_0_ = bf16[256,2048]{1,0:T(8,128)(2,1)S(1)} collective-permute-done((bf16[256,2048]{1,0:T(8,128)(2,1)}, bf16[256,2048]{1,0:T(8,128)(2,1)S(1)}, u32[]{:S(2)}, u32[]{:S(2)}) %collective-permute-start.4) | collective-permute-done | bytes 1048608 | tf_op jit(solution)/shard_map/ppermute | solution.py:357
  63.8 3.8 %collective-permute-start.11 = (bf16[96,2048]{1,0:T(8,128)(2,1)S(1)}, bf16[96,2048]{1,0:T(8,128)(2,1)S(1)}, u32[]{:S(2)}, u32[]{:S(2)}) collective-permute-start(bf16[96,2048]{1,0:T(8,128)(2,1)S(1)} %get-tuple-element.122), channel_id=1, source_target_pairs={{8,0},{10,2},{12,4},{14,6},{16,8},{18,10},{20,12},{22,14},{24,16},... | collective-permute-start | bytes 1179656 | tf_op jit(solution)/shard_map/ppermute | solution.py:371
  71.8 2.6 %convolution_convert_fusion.4.refs_2_ = bf16[736,384]{1,0:T(8,128)(2,1)} fusion(bf16[736,2048]{1,0:T(8,128)(2,1)S(1)} %constant_dynamic-update-slice_fusion.5, bf16[384,2048]{1,0:T(8,128)(2,1)S(1)} %copy-done.16), kind=kOutput, calls=%fused_computation.8 | convolution fusion | flops 1157910528 | bytes 5152768 | tf_op jit(solution)/shard_map/td,rd->tr/dot_general | solution.py:487
  74.3 1.7 assemble.13
  76.5 2.2 %convolution_convert_fusion.6 = bf16[576,384]{1,0:T(8,128)(2,1)} fusion(bf16[576,2048]{1,0:T(8,128)(2,1)S(1)} %copy-done.21, bf16[384,2048]{1,0:T(8,128)(2,1)S(1)} %assemble.13), kind=kOutput, calls=%fused_computation.10 | convolution fusion | flops 906190848 | bytes 4374528 | tf_op jit(solution)/shard_map/td,rd->tr/dot_general | solution.py:487
  78.6 2.5 %convolution_convert_fusion.3 = bf16[736,384]{1,0:T(8,128)(2,1)} fusion(bf16[736,2048]{1,0:T(8,128)(2,1)S(1)} %constant_dynamic-update-slice_fusion.5, bf16[384,2048]{1,0:T(8,128)(2,1)S(1)} %assemble.13), kind=kOutput, calls=%fused_computation.7 | convolution fusion | flops 1157910528 | bytes 5152768 | tf_op jit(solution)/shard_map/td,rd->tr/dot_general | solution.py:487
  81.7 3.8 %collective-permute-start.15 = (bf16[32,2048]{1,0:T(8,128)(2,1)S(1)}, bf16[32,2048]{1,0:T(8,128)(2,1)S(1)}, u32[]{:S(2)}, u32[]{:S(2)}) collective-permute-start(bf16[32,2048]{1,0:T(8,128)(2,1)S(1)} %get-tuple-element.130), channel_id=1, source_target_pairs={{8,0},{10,2},{12,4},{14,6},{16,8},{18,10},{20,12},{22,14},{24,16},... | collective-permute-start | bytes 393224 | tf_op jit(solution)/shard_map/ppermute | solution.py:371
  87.7 2.2 %convolution_convert_fusion.7.refs_3_ = bf16[576,384]{1,0:T(8,128)(2,1)} fusion(bf16[576,2048]{1,0:T(8,128)(2,1)S(1)} %constant_dynamic-update-slice_fusion.9, bf16[384,2048]{1,0:T(8,128)(2,1)S(1)} %copy-done.16), kind=kOutput, calls=%fused_computation.11 | convolution fusion | flops 906190848 | bytes 4374528 | tf_op jit(solution)/shard_map/td,rd->tr/dot_general | solution.py:487
  89.9 2.2 %convolution_convert_fusion.5 = bf16[576,384]{1,0:T(8,128)(2,1)} fusion(bf16[576,2048]{1,0:T(8,128)(2,1)S(1)} %constant_dynamic-update-slice_fusion.9, bf16[384,2048]{1,0:T(8,128)(2,1)S(1)} %assemble.13), kind=kOutput, calls=%fused_computation.9 | convolution fusion | flops 906190848 | bytes 4374528 | tf_op jit(solution)/shard_map/td,rd->tr/dot_general | solution.py:487
  99.3 13.2 %modal_scan.1 = (bf16[2048,128]{1,0:T(8,128)(2,1)}, f32[16,128]{1,0:T(8,128)}, bf16[768,384]{1,0:T(8,128)(2,1)S(1)}, bf16[1280,384]{1,0:T(8,128)(2,1)S(1)}) custom-call(s32[1]{0:T(128)} %bitcast.me_ref, f32[16,128]{1,0:T(8,128)S(1)} %bitcast.44, f32[16,128]{1,0:T(8,128)S(1)} %bitcast.45, bf16[2048,128]{1,0:T(8,128)(2,1)S(1)} %bitcast.43, ...), custom_call_target="tpu_custom_call" | custom-call | tf_op jit(solution)/shard_map/modal_scan/pallas_call | solution.py:332
  113.0 1.5 collective-permute-done.21
  114.5 2.8 %convolution_convert_fusion.1.refs_0_ = bf16[768,2048]{1,0:T(8,128)(2,1)S(1)} fusion(bf16[768,384]{1,0:T(8,128)(2,1)S(1)} %collective-permute-done.21, bf16[768,384]{1,0:T(8,128)(2,1)S(1)} %get-tuple-element.138, bf16[384,2048]{1,0:T(8,128)(2,1)S(1)} %assemble.13, bf16[384,2048]{1,0:T(8,128)(2,1)S(1)} %copy-done.17), kind=kOutput, calls=%fused_computation.1 | convolution fusion | flops 2426142720 | bytes 7471104 | tf_op jit(solution)/shard_map/dot_general | solution.py:597
  118.6 1.4 collective-permute-start.23
  120.0 3.8 %collective-permute-start.25 = (bf16[128,256]{1,0:T(8,128)(2,1)S(1)}, bf16[128,256]{1,0:T(8,128)(2,1)S(1)}, u32[]{:S(2)}, u32[]{:S(2)}) collective-permute-start(bf16[128,256]{1,0:T(8,128)(2,1)S(1)} %get-tuple-element.142), channel_id=1, source_target_pairs={{8,0},{10,2},{12,4},{14,6},{16,8},{18,10},{20,12},{22,14},{24,16},... | collective-permute-start | bytes 196616 | tf_op jit(solution)/shard_map/ppermute | solution.py:371
  123.9 2.5 %collective-permute-done.24.refs_3_ = bf16[128,256]{1,0:T(8,128)(2,1)S(1)} collective-permute-done((bf16[128,256]{1,0:T(8,128)(2,1)S(1)}, bf16[128,256]{1,0:T(8,128)(2,1)S(1)}, u32[]{:S(2)}, u32[]{:S(2)}) %collective-permute-start.24) | collective-permute-done | bytes 65568 | tf_op jit(solution)/shard_map/ppermute | solution.py:366
  128.2 3.8 %collective-permute-start.30 = (bf16[128,1280]{1,0:T(8,128)(2,1)S(1)}, bf16[128,1280]{1,0:T(8,128)(2,1)S(1)}, u32[]{:S(2)}, u32[]{:S(2)}) collective-permute-start(bf16[128,1280]{1,0:T(8,128)(2,1)S(1)} %get-tuple-element.156), channel_id=1, source_target_pairs={{8,0},{10,2},{12,4},{14,6},{16,8},{18,10},{20,12},{22,14},{24,16},... | collective-permute-start | bytes 983048 | tf_op jit(solution)/shard_map/ppermute | solution.py:371
  133.0 3.2 %convolution_convert_fusion.refs_1_.refs_0_ = bf16[896,2048]{1,0:T(8,128)(2,1)S(1)} fusion(bf16[896,384]{1,0:T(8,128)(2,1)S(1)} %slice.17, bf16[896,384]{1,0:T(8,128)(2,1)S(1)} %slice.14, bf16[384,2048]{1,0:T(8,128)(2,1)S(1)} %assemble.13, bf16[384,2048]{1,0:T(8,128)(2,1)S(1)} %copy-done.17), kind=kOutput, calls=%fused_computation | convolution fusion | flops 2829451264 | bytes 8192000 | tf_op jit(solution)/shard_map/dot_general | solution.py:597
  136.3 4.3 %collective-permute-done.29.refs_4_ = bf16[128,1280]{1,0:T(8,128)(2,1)S(1)} collective-permute-done((bf16[128,1280]{1,0:T(8,128)(2,1)S(1)}, bf16[128,1280]{1,0:T(8,128)(2,1)S(1)}, u32[]{:S(2)}, u32[]{:S(2)}) %collective-permute-start.29) | collective-permute-done | bytes 327712 | tf_op jit(solution)/shard_map/ppermute | solution.py:366
  140.6 2.9 %collective-permute-done.30.refs_5_ = bf16[128,1280]{1,0:T(8,128)(2,1)S(1)} collective-permute-done((bf16[128,1280]{1,0:T(8,128)(2,1)S(1)}, bf16[128,1280]{1,0:T(8,128)(2,1)S(1)}, u32[]{:S(2)}, u32[]{:S(2)}) %collective-permute-start.30) | collective-permute-done | bytes 327712 | tf_op jit(solution)/shard_map/ppermute | solution.py:371
  145.1 1.9 assemble.16
  148.2 1.3 collective-permute-start.32
  149.6 3.7 %collective-permute-start.34 = (bf16[128,2304]{1,0:T(8,128)(2,1)}, bf16[128,2304]{1,0:T(8,128)(2,1)}, u32[]{:S(2)}, u32[]{:S(2)}) collective-permute-start(bf16[128,2304]{1,0:T(8,128)(2,1)} %get-tuple-element.169), channel_id=1, source_target_pairs={{8,0},{10,2},{12,4},{14,6},{16,8},{18,10},{20,12},{22,14},{24,16},... | collective-permute-start | bytes 1769480 | tf_op jit(solution)/shard_map/ppermute | solution.py:371
  153.3 4.5 %all-to-all-start.1 = ((bf16[16,128,128]{2,1,0:T(8,128)(2,1)}), bf16[16,128,128]{2,1,0:T(8,128)(2,1)}, u32[]{:S(2)}, u32[]{:S(2)}) async-start(bf16[16,128,128]{2,1,0:T(8,128)(2,1)} %bitcast.13), calls=%async_computation.1 | async-start | bytes 1048576 | tf_op jit(solution)/shard_map/all_to_all | solution.py:629
  157.8 3.0 %convolution_convert_fusion.2.refs_0_.refs_1_ = bf16[384,2048]{1,0:T(8,128)(2,1)S(1)} fusion(bf16[384,2048]{1,0:T(8,128)(2,1)S(1)} %assemble.13, bf16[384,2048]{1,0:T(8,128)(2,1)} %get-tuple-element.108, bf16[384,384]{1,0:T(8,128)(2,1)S(1)} %slice-done, bf16[384,384]{1,0:T(8,128)(2,1)S(1)} %slice.12), kind=kOutput, calls=%fused_computation.3 | convolution fusion | flops 1216217088 | bytes 5308416 | tf_op jit(solution)/shard_map/dot_general | solution.py:597
  160.8 7.0 %collective-permute-done.33.refs_1_.refs_4_ = bf16[128,2304]{1,0:T(8,128)(2,1)} collective-permute-done((bf16[128,2304]{1,0:T(8,128)(2,1)}, bf16[128,2304]{1,0:T(8,128)(2,1)}, u32[]{:S(2)}, u32[]{:S(2)}) %collective-permute-start.33) | collective-permute-done | bytes 589856 | tf_op jit(solution)/shard_map/ppermute | solution.py:366
  167.9 10.5 %collective-permute-done.34.refs_2_.refs_5_ = bf16[128,2304]{1,0:T(8,128)(2,1)} collective-permute-done((bf16[128,2304]{1,0:T(8,128)(2,1)}, bf16[128,2304]{1,0:T(8,128)(2,1)}, u32[]{:S(2)}, u32[]{:S(2)}) %collective-permute-start.34) | collective-permute-done | bytes 589856 | tf_op jit(solution)/shard_map/ppermute | solution.py:371
  178.3 3.3 %assemble.18 = (bf16[128,2048]{1,0:T(8,128)(2,1)}, bf16[128,2048]{1,0:T(8,128)(2,1)}, bf16[128,1536]{1,0:T(8,128)(2,1)}, bf16[128,1536]{1,0:T(8,128)(2,1)}) custom-call(bf16[896,2048]{1,0:T(8,128)(2,1)S(1)} %copy-done.1, bf16[384,2048]{1,0:T(8,128)(2,1)S(1)} %convolution_convert_fusion.2.refs_0_.refs_1_, bf16[128,4096]{1,0:T(8,128)(2,1)} %collective-permute-done.31.refs_2_, ...), custom_call_target="tpu_custom_call" | custom-call | flops 1835008 | bytes 7340032 | tf_op jit(solution)/shard_map/assemble/pallas_call | solution.py:447
  182.6 1.9 collective-permute-start.37
  184.6 1.9 collective-permute-start.38
  186.6 2.0 copy.9
  188.7 1.3 assemble.17.refs_0_
  190.0 6.7 %collective-permute-done.37.refs_3_ = bf16[128,1536]{1,0:T(8,128)(2,1)S(1)} collective-permute-done((bf16[128,1536]{1,0:T(8,128)(2,1)}, bf16[128,1536]{1,0:T(8,128)(2,1)S(1)}, u32[]{:S(2)}, u32[]{:S(2)}) %collective-permute-start.37) | collective-permute-done | bytes 393248 | tf_op jit(solution)/shard_map/ppermute | solution.py:366
  196.7 6.4 %collective-permute-done.38.refs_4_ = bf16[128,1536]{1,0:T(8,128)(2,1)S(1)} collective-permute-done((bf16[128,1536]{1,0:T(8,128)(2,1)}, bf16[128,1536]{1,0:T(8,128)(2,1)S(1)}, u32[]{:S(2)}, u32[]{:S(2)}) %collective-permute-start.38) | collective-permute-done | bytes 393248 | tf_op jit(solution)/shard_map/ppermute | solution.py:371
  204.8 2.3 %assemble.19 = bf16[128,2048]{1,0:T(8,128)(2,1)} custom-call(bf16[128,2048]{1,0:T(8,128)(2,1)S(1)} %assemble.17.refs_0_, bf16[128,2048]{1,0:T(8,128)(2,1)} %collective-permute-done.35.refs_1_, bf16[128,2048]{1,0:T(8,128)(2,1)} %collective-permute-done.36.refs_2_, bf16[128,1536]{1,0:T(8,128)(2,1)S(1)} %collective-permute-done.37.refs_3_, ...), custom_call_target="tpu_custom_call" | custom-call | flops 524288 | bytes 2097152 | tf_op jit(solution)/shard_map/assemble/pallas_call | solution.py:447
  (126 shorter events, 30.9 us)
Async XLA Ops:
  2.8 25.4 %copy-start.2 = (bf16[128,2048]{1,0:T(8,128)(2,1)S(1)}, bf16[128,2048]{1,0:T(8,128)(2,1)}, u32[]{:S(2)}) copy-start(bf16[128,2048]{1,0:T(8,128)(2,1)} %get-tuple-element.103.refs_0_) | copy-start | bytes 1572868
  2.8 25.4 %collective-permute-start.1 = (bf16[128,2048]{1,0:T(8,128)(2,1)}, bf16[128,2048]{1,0:T(8,128)(2,1)S(1)}, u32[]{:S(2)}, u32[]{:S(2)}) collective-permute-start(bf16[128,2048]{1,0:T(8,128)(2,1)} %get-tuple-element.103.refs_0_), channel_id=1, source_target_pairs={{0,4},{2,6},{4,0},{6,2},{8,12},{10,14},{12,8},{14,10},{16,20},{18,... | collective-permute-start | bytes 1572872 | tf_op jit(solution)/shard_map/ppermute | solution.py:361
  5.8 22.4 %collective-permute-start = (bf16[128,2048]{1,0:T(8,128)(2,1)}, bf16[128,2048]{1,0:T(8,128)(2,1)S(1)}, u32[]{:S(2)}, u32[]{:S(2)}) collective-permute-start(bf16[128,2048]{1,0:T(8,128)(2,1)} %get-tuple-element.103.refs_0_), channel_id=1, source_target_pairs={{0,2},{2,0},{4,6},{6,4},{8,10},{10,8},{12,14},{14,12},{16,18},{18,... | collective-permute-start | bytes 1572872 | tf_op jit(solution)/shard_map/ppermute | solution.py:357
  7.3 13.5 %collective-permute-start.3 = (bf16[96,2048]{1,0:T(8,128)(2,1)}, bf16[96,2048]{1,0:T(8,128)(2,1)S(1)}, u32[]{:S(2)}, u32[]{:S(2)}) collective-permute-start(bf16[96,2048]{1,0:T(8,128)(2,1)} %get-tuple-element.94), channel_id=1, source_target_pairs={{8,0},{10,2},{12,4},{14,6},{16,8},{18,10},{20,12},{22,14},{24,16},... | collective-permute-start | bytes 1179656 | tf_op jit(solution)/shard_map/ppermute | solution.py:371
  10.9 17.3 %collective-permute-start.2 = (bf16[96,2048]{1,0:T(8,128)(2,1)}, bf16[96,2048]{1,0:T(8,128)(2,1)S(1)}, u32[]{:S(2)}, u32[]{:S(2)}) collective-permute-start(bf16[96,2048]{1,0:T(8,128)(2,1)} %get-tuple-element.94), channel_id=1, source_target_pairs={{0,8},{2,10},{4,12},{6,14},{8,16},{10,18},{12,20},{14,22},{16,24},... | collective-permute-start | bytes 1179656 | tf_op jit(solution)/shard_map/ppermute | solution.py:366
  14.5 59.8 %collective-permute-start.16 = (bf16[384,2048]{1,0:T(8,128)(2,1)}, bf16[384,2048]{1,0:T(8,128)(2,1)}, u32[]{:S(2)}, u32[]{:S(2)}) collective-permute-start(bf16[384,2048]{1,0:T(8,128)(2,1)} %get-tuple-element.135), channel_id=1, source_target_pairs={{0,1},{1,0},{2,3},{3,2},{4,5},{5,4},{6,7},{7,6},{8,9},{9,8},{10,11... | collective-permute-start | bytes 4718600 | tf_op jit(solution)/shard_map/ppermute | solution.py:353
  28.2 5.8 %copy-start.4 = (bf16[96,2048]{1,0:T(8,128)(2,1)}, bf16[96,2048]{1,0:T(8,128)(2,1)S(1)}, u32[]{:S(2)}) copy-start(bf16[96,2048]{1,0:T(8,128)(2,1)S(1)} %collective-permute-done.2.refs_3_) | copy-start | bytes 1179652
  30.2 6.1 %copy-start.15 = (bf16[384,2048]{1,0:T(8,128)(2,1)S(1)}, bf16[384,2048]{1,0:T(8,128)(2,1)}, u32[]{:S(2)}) copy-start(bf16[384,2048]{1,0:T(8,128)(2,1)} %get-tuple-element.108) | copy-start | bytes 4718596
  30.2 15.6 %collective-permute-start.6 = (bf16[112,2048]{1,0:T(8,128)(2,1)}, bf16[112,2048]{1,0:T(8,128)(2,1)}, u32[]{:S(2)}, u32[]{:S(2)}) collective-permute-start(bf16[112,2048]{1,0:T(8,128)(2,1)} %get-tuple-element.113), channel_id=1, source_target_pairs={{0,8},{2,10},{4,12},{6,14},{8,16},{10,18},{12,20},{14,22},{16,24},... | collective-permute-start | bytes 1376264 | tf_op jit(solution)/shard_map/ppermute | solution.py:366
  31.8 22.7 %collective-permute-start.7 = (bf16[112,2048]{1,0:T(8,128)(2,1)}, bf16[112,2048]{1,0:T(8,128)(2,1)}, u32[]{:S(2)}, u32[]{:S(2)}) collective-permute-start(bf16[112,2048]{1,0:T(8,128)(2,1)} %get-tuple-element.114), channel_id=1, source_target_pairs={{8,0},{10,2},{12,4},{14,6},{16,8},{18,10},{20,12},{22,14},{24,16},... | collective-permute-start | bytes 1376264 | tf_op jit(solution)/shard_map/ppermute | solution.py:371
  34.0 27.2 %collective-permute-start.4 = (bf16[256,2048]{1,0:T(8,128)(2,1)}, bf16[256,2048]{1,0:T(8,128)(2,1)S(1)}, u32[]{:S(2)}, u32[]{:S(2)}) collective-permute-start(bf16[256,2048]{1,0:T(8,128)(2,1)} %get-tuple-element.111), channel_id=1, source_target_pairs={{0,2},{2,0},{4,6},{6,4},{8,10},{10,8},{12,14},{14,12},{16,18},{18,... | collective-permute-start | bytes 3145736 | tf_op jit(solution)/shard_map/ppermute | solution.py:357
  34.5 27.9 %collective-permute-start.5 = (bf16[256,2048]{1,0:T(8,128)(2,1)}, bf16[256,2048]{1,0:T(8,128)(2,1)S(1)}, u32[]{:S(2)}, u32[]{:S(2)}) collective-permute-start(bf16[256,2048]{1,0:T(8,128)(2,1)} %get-tuple-element.112), channel_id=1, source_target_pairs={{0,4},{2,6},{4,0},{6,2},{8,12},{10,14},{12,8},{14,10},{16,20},{18,... | collective-permute-start | bytes 3145736 | tf_op jit(solution)/shard_map/ppermute | solution.py:361
  39.5 54.7 %all-to-all-start = ((bf16[128,16,128]{2,0,1:T(8,128)(2,1)}), bf16[128,16,128]{2,0,1:T(8,128)(2,1)S(1)}, u32[]{:S(2)}, u32[]{:S(2)}) async-start(bf16[128,16,128]{2,0,1:T(8,128)(2,1)} %copy.8), calls=%async_computation | async-start | bytes 1048576 | tf_op jit(solution)/shard_map/all_to_all | solution.py:494
  63.8 17.4 %collective-permute-start.10 = (bf16[96,2048]{1,0:T(8,128)(2,1)S(1)}, bf16[96,2048]{1,0:T(8,128)(2,1)S(1)}, u32[]{:S(2)}, u32[]{:S(2)}) collective-permute-start(bf16[96,2048]{1,0:T(8,128)(2,1)S(1)} %get-tuple-element.121), channel_id=1, source_target_pairs={{0,8},{2,10},{4,12},{6,14},{8,16},{10,18},{12,20},{14,22},{16,24},... | collective-permute-start | bytes 1179656 | tf_op jit(solution)/shard_map/ppermute | solution.py:366
  63.8 17.3 %collective-permute-start.11 = (bf16[96,2048]{1,0:T(8,128)(2,1)S(1)}, bf16[96,2048]{1,0:T(8,128)(2,1)S(1)}, u32[]{:S(2)}, u32[]{:S(2)}) collective-permute-start(bf16[96,2048]{1,0:T(8,128)(2,1)S(1)} %get-tuple-element.122), channel_id=1, source_target_pairs={{8,0},{10,2},{12,4},{14,6},{16,8},{18,10},{20,12},{22,14},{24,16},... | collective-permute-start | bytes 1179656 | tf_op jit(solution)/shard_map/ppermute | solution.py:371
  67.7 13.5 %collective-permute-start.8 = (bf16[192,2048]{1,0:T(8,128)(2,1)S(1)}, bf16[192,2048]{1,0:T(8,128)(2,1)S(1)}, u32[]{:S(2)}, u32[]{:S(2)}) collective-permute-start(bf16[192,2048]{1,0:T(8,128)(2,1)S(1)} %get-tuple-element.119), channel_id=1, source_target_pairs={{0,2},{2,0},{4,6},{6,4},{8,10},{10,8},{12,14},{14,12},{16,18},{18,... | collective-permute-start | bytes 2359304 | tf_op jit(solution)/shard_map/ppermute | solution.py:357
  68.8 12.7 %collective-permute-start.9 = (bf16[192,2048]{1,0:T(8,128)(2,1)S(1)}, bf16[192,2048]{1,0:T(8,128)(2,1)S(1)}, u32[]{:S(2)}, u32[]{:S(2)}) collective-permute-start(bf16[192,2048]{1,0:T(8,128)(2,1)S(1)} %get-tuple-element.120), channel_id=1, source_target_pairs={{0,4},{2,6},{4,0},{6,2},{8,12},{10,14},{12,8},{14,10},{16,20},{18,... | collective-permute-start | bytes 2359304 | tf_op jit(solution)/shard_map/ppermute | solution.py:361
  78.6 15.6 %collective-permute-start.17 = (bf16[576,384]{1,0:T(8,128)(2,1)}, bf16[576,384]{1,0:T(8,128)(2,1)}, u32[]{:S(2)}, u32[]{:S(2)}) collective-permute-start(bf16[576,384]{1,0:T(8,128)(2,1)} %convolution_convert_fusion.6), channel_id=1, source_target_pairs={{0,1},{1,0},{2,3},{3,2},{4,5},{5,4},{6,7},{7,6},{8,9},{9,8},{10,11... | collective-permute-start | bytes 1327112 | tf_op jit(solution)/shard_map/ppermute | solution.py:353
  81.7 10.4 %collective-permute-start.14 = (bf16[32,2048]{1,0:T(8,128)(2,1)S(1)}, bf16[32,2048]{1,0:T(8,128)(2,1)S(1)}, u32[]{:S(2)}, u32[]{:S(2)}) collective-permute-start(bf16[32,2048]{1,0:T(8,128)(2,1)S(1)} %get-tuple-element.129), channel_id=1, source_target_pairs={{0,8},{2,10},{4,12},{6,14},{8,16},{10,18},{12,20},{14,22},{16,24},... | collective-permute-start | bytes 393224 | tf_op jit(solution)/shard_map/ppermute | solution.py:366
  81.7 10.4 %collective-permute-start.15 = (bf16[32,2048]{1,0:T(8,128)(2,1)S(1)}, bf16[32,2048]{1,0:T(8,128)(2,1)S(1)}, u32[]{:S(2)}, u32[]{:S(2)}) collective-permute-start(bf16[32,2048]{1,0:T(8,128)(2,1)S(1)} %get-tuple-element.130), channel_id=1, source_target_pairs={{8,0},{10,2},{12,4},{14,6},{16,8},{18,10},{20,12},{22,14},{24,16},... | collective-permute-start | bytes 393224 | tf_op jit(solution)/shard_map/ppermute | solution.py:371
  85.5 7.1 %collective-permute-start.12 = (bf16[48,2048]{1,0:T(8,128)(2,1)S(1)}, bf16[48,2048]{1,0:T(8,128)(2,1)S(1)}, u32[]{:S(2)}, u32[]{:S(2)}) collective-permute-start(bf16[48,2048]{1,0:T(8,128)(2,1)S(1)} %get-tuple-element.127), channel_id=1, source_target_pairs={{0,2},{2,0},{4,6},{6,4},{8,10},{10,8},{12,14},{14,12},{16,18},{18,... | collective-permute-start | bytes 589832 | tf_op jit(solution)/shard_map/ppermute | solution.py:357
  86.4 6.2 %collective-permute-start.13 = (bf16[48,2048]{1,0:T(8,128)(2,1)S(1)}, bf16[48,2048]{1,0:T(8,128)(2,1)S(1)}, u32[]{:S(2)}, u32[]{:S(2)}) collective-permute-start(bf16[48,2048]{1,0:T(8,128)(2,1)S(1)} %get-tuple-element.128), channel_id=1, source_target_pairs={{0,4},{2,6},{4,0},{6,2},{8,12},{10,14},{12,8},{14,10},{16,20},{18,... | collective-permute-start | bytes 589832 | tf_op jit(solution)/shard_map/ppermute | solution.py:361
  92.1 2.3 %collective-permute-start.18 = (bf16[736,384]{1,0:T(8,128)(2,1)}, bf16[736,384]{1,0:T(8,128)(2,1)S(1)}, u32[]{:S(2)}, u32[]{:S(2)}) collective-permute-start(bf16[736,384]{1,0:T(8,128)(2,1)} %convolution_convert_fusion.3), channel_id=1, source_target_pairs={{0,1},{1,0},{2,3},{3,2},{4,5},{5,4},{6,7},{7,6},{8,9},{9,8},{10,11... | collective-permute-start | bytes 1695752 | tf_op jit(solution)/shard_map/ppermute | solution.py:353
  92.1 3.1 %collective-permute-start.19 = (bf16[576,384]{1,0:T(8,128)(2,1)}, bf16[576,384]{1,0:T(8,128)(2,1)}, u32[]{:S(2)}, u32[]{:S(2)}) collective-permute-start(bf16[576,384]{1,0:T(8,128)(2,1)} %convolution_convert_fusion.5), channel_id=1, source_target_pairs={{0,1},{1,0},{2,3},{3,2},{4,5},{5,4},{6,7},{7,6},{8,9},{9,8},{10,11... | collective-permute-start | bytes 1327112 | tf_op jit(solution)/shard_map/ppermute | solution.py:353
  93.4 1.8 collective-permute-start.20
  99.3 15.2 %copy-start.17 = (bf16[384,2048]{1,0:T(8,128)(2,1)S(1)}, bf16[384,2048]{1,0:T(8,128)(2,1)}, u32[]{:S(2)}) copy-start(bf16[384,2048]{1,0:T(8,128)(2,1)} %get-tuple-element.108) | copy-start | bytes 4718596
  112.5 2.0 collective-permute-start.21
  112.8 19.2 %collective-permute-start.26 = (bf16[1280,384]{1,0:T(8,128)(2,1)S(1)}, bf16[1280,384]{1,0:T(8,128)(2,1)S(1)}, u32[]{:S(2)}, u32[]{:S(2)}) collective-permute-start(bf16[1280,384]{1,0:T(8,128)(2,1)S(1)} %get-tuple-element.148), channel_id=1, source_target_pairs={{0,1},{1,0},{2,3},{3,2},{4,5},{5,4},{6,7},{7,6},{8,9},{9,8},{10,11... | collective-permute-start | bytes 2949128 | tf_op jit(solution)/shard_map/ppermute | solution.py:353
  117.4 8.9 %collective-permute-start.22 = (bf16[128,768]{1,0:T(8,128)(2,1)S(1)}, bf16[128,768]{1,0:T(8,128)(2,1)S(1)}, u32[]{:S(2)}, u32[]{:S(2)}) collective-permute-start(bf16[128,768]{1,0:T(8,128)(2,1)S(1)} %get-tuple-element.139), channel_id=1, source_target_pairs={{0,2},{2,0},{4,6},{6,4},{8,10},{10,8},{12,14},{14,12},{16,18},{18,... | collective-permute-start | bytes 589832 | tf_op jit(solution)/shard_map/ppermute | solution.py:357
  118.6 7.7 %collective-permute-start.23 = (bf16[128,768]{1,0:T(8,128)(2,1)S(1)}, bf16[128,768]{1,0:T(8,128)(2,1)S(1)}, u32[]{:S(2)}, u32[]{:S(2)}) collective-permute-start(bf16[128,768]{1,0:T(8,128)(2,1)S(1)} %get-tuple-element.140), channel_id=1, source_target_pairs={{0,4},{2,6},{4,0},{6,2},{8,12},{10,14},{12,8},{14,10},{16,20},{18,... | collective-permute-start | bytes 589832 | tf_op jit(solution)/shard_map/ppermute | solution.py:361
  120.0 6.3 %collective-permute-start.24 = (bf16[128,256]{1,0:T(8,128)(2,1)S(1)}, bf16[128,256]{1,0:T(8,128)(2,1)S(1)}, u32[]{:S(2)}, u32[]{:S(2)}) collective-permute-start(bf16[128,256]{1,0:T(8,128)(2,1)S(1)} %get-tuple-element.141), channel_id=1, source_target_pairs={{0,8},{2,10},{4,12},{6,14},{8,16},{10,18},{12,20},{14,22},{16,24},... | collective-permute-start | bytes 196616 | tf_op jit(solution)/shard_map/ppermute | solution.py:366
  120.0 6.3 %collective-permute-start.25 = (bf16[128,256]{1,0:T(8,128)(2,1)S(1)}, bf16[128,256]{1,0:T(8,128)(2,1)S(1)}, u32[]{:S(2)}, u32[]{:S(2)}) collective-permute-start(bf16[128,256]{1,0:T(8,128)(2,1)S(1)} %get-tuple-element.142), channel_id=1, source_target_pairs={{8,0},{10,2},{12,4},{14,6},{16,8},{18,10},{20,12},{22,14},{24,16},... | collective-permute-start | bytes 196616 | tf_op jit(solution)/shard_map/ppermute | solution.py:371
  126.5 18.0 %collective-permute-start.27 = (bf16[128,3072]{1,0:T(8,128)(2,1)S(1)}, bf16[128,3072]{1,0:T(8,128)(2,1)S(1)}, u32[]{:S(2)}, u32[]{:S(2)}) collective-permute-start(bf16[128,3072]{1,0:T(8,128)(2,1)S(1)} %get-tuple-element.153), channel_id=1, source_target_pairs={{0,2},{2,0},{4,6},{6,4},{8,10},{10,8},{12,14},{14,12},{16,18},{18,... | collective-permute-start | bytes 2359304 | tf_op jit(solution)/shard_map/ppermute | solution.py:357
  127.5 17.7 %collective-permute-start.28 = (bf16[128,3072]{1,0:T(8,128)(2,1)S(1)}, bf16[128,3072]{1,0:T(8,128)(2,1)S(1)}, u32[]{:S(2)}, u32[]{:S(2)}) collective-permute-start(bf16[128,3072]{1,0:T(8,128)(2,1)S(1)} %get-tuple-element.154), channel_id=1, source_target_pairs={{0,4},{2,6},{4,0},{6,2},{8,12},{10,14},{12,8},{14,10},{16,20},{18,... | collective-permute-start | bytes 2359304 | tf_op jit(solution)/shard_map/ppermute | solution.py:361
  128.1 12.5 %collective-permute-start.29 = (bf16[128,1280]{1,0:T(8,128)(2,1)S(1)}, bf16[128,1280]{1,0:T(8,128)(2,1)S(1)}, u32[]{:S(2)}, u32[]{:S(2)}) collective-permute-start(bf16[128,1280]{1,0:T(8,128)(2,1)S(1)} %get-tuple-element.155), channel_id=1, source_target_pairs={{0,8},{2,10},{4,12},{6,14},{8,16},{10,18},{12,20},{14,22},{16,24},... | collective-permute-start | bytes 983048 | tf_op jit(solution)/shard_map/ppermute | solution.py:366
  128.2 15.4 %collective-permute-start.30 = (bf16[128,1280]{1,0:T(8,128)(2,1)S(1)}, bf16[128,1280]{1,0:T(8,128)(2,1)S(1)}, u32[]{:S(2)}, u32[]{:S(2)}) collective-permute-start(bf16[128,1280]{1,0:T(8,128)(2,1)S(1)} %get-tuple-element.156), channel_id=1, source_target_pairs={{8,0},{10,2},{12,4},{14,6},{16,8},{18,10},{20,12},{22,14},{24,16},... | collective-permute-start | bytes 983048 | tf_op jit(solution)/shard_map/ppermute | solution.py:371
  136.3 10.8 %copy-start = (bf16[896,2048]{1,0:T(8,128)(2,1)}, bf16[896,2048]{1,0:T(8,128)(2,1)S(1)}, u32[]{:S(2)}) copy-start(bf16[896,2048]{1,0:T(8,128)(2,1)S(1)} %convolution_convert_fusion.refs_1_.refs_0_) | copy-start | bytes 11010052
  136.3 21.5 %slice-start = ((bf16[1280,384]{1,0:T(8,128)(2,1)}), bf16[384,384]{1,0:T(8,128)(2,1)S(1)}, s32[]{:S(2)}) async-start(bf16[1280,384]{1,0:T(8,128)(2,1)} %copy-done.18), calls=%async_computation.2 | async-start | bytes 589824 | tf_op jit(solution)/shard_map/slice | solution.py:626
  147.0 31.3 %collective-permute-start.31 = (bf16[128,4096]{1,0:T(8,128)(2,1)}, bf16[128,4096]{1,0:T(8,128)(2,1)}, u32[]{:S(2)}, u32[]{:S(2)}) collective-permute-start(bf16[128,4096]{1,0:T(8,128)(2,1)} %get-tuple-element.166), channel_id=1, source_target_pairs={{0,2},{2,0},{4,6},{6,4},{8,10},{10,8},{12,14},{14,12},{16,18},{18,... | collective-permute-start | bytes 3145736 | tf_op jit(solution)/shard_map/ppermute | solution.py:357
  148.2 30.2 %collective-permute-start.32 = (bf16[128,4096]{1,0:T(8,128)(2,1)}, bf16[128,4096]{1,0:T(8,128)(2,1)}, u32[]{:S(2)}, u32[]{:S(2)}) collective-permute-start(bf16[128,4096]{1,0:T(8,128)(2,1)} %get-tuple-element.167), channel_id=1, source_target_pairs={{0,4},{2,6},{4,0},{6,2},{8,12},{10,14},{12,8},{14,10},{16,20},{18,... | collective-permute-start | bytes 3145736 | tf_op jit(solution)/shard_map/ppermute | solution.py:361
  149.5 18.4 %collective-permute-start.33 = (bf16[128,2304]{1,0:T(8,128)(2,1)}, bf16[128,2304]{1,0:T(8,128)(2,1)}, u32[]{:S(2)}, u32[]{:S(2)}) collective-permute-start(bf16[128,2304]{1,0:T(8,128)(2,1)} %get-tuple-element.168), channel_id=1, source_target_pairs={{0,8},{2,10},{4,12},{6,14},{8,16},{10,18},{12,20},{14,22},{16,24},... | collective-permute-start | bytes 1769480 | tf_op jit(solution)/shard_map/ppermute | solution.py:366
  149.6 28.7 %collective-permute-start.34 = (bf16[128,2304]{1,0:T(8,128)(2,1)}, bf16[128,2304]{1,0:T(8,128)(2,1)}, u32[]{:S(2)}, u32[]{:S(2)}) collective-permute-start(bf16[128,2304]{1,0:T(8,128)(2,1)} %get-tuple-element.169), channel_id=1, source_target_pairs={{8,0},{10,2},{12,4},{14,6},{16,8},{18,10},{20,12},{22,14},{24,16},... | collective-permute-start | bytes 1769480 | tf_op jit(solution)/shard_map/ppermute | solution.py:371
  153.3 33.3 %all-to-all-start.1 = ((bf16[16,128,128]{2,1,0:T(8,128)(2,1)}), bf16[16,128,128]{2,1,0:T(8,128)(2,1)}, u32[]{:S(2)}, u32[]{:S(2)}) async-start(bf16[16,128,128]{2,1,0:T(8,128)(2,1)} %bitcast.13), calls=%async_computation.1 | async-start | bytes 1048576 | tf_op jit(solution)/shard_map/all_to_all | solution.py:629
  157.8 20.5 %copy-start.1 = (bf16[896,2048]{1,0:T(8,128)(2,1)S(1)}, bf16[896,2048]{1,0:T(8,128)(2,1)}, u32[]{:S(2)}) copy-start(bf16[896,2048]{1,0:T(8,128)(2,1)} %copy-done) | copy-start | bytes 11010052
  181.6 22.2 %collective-permute-start.35 = (bf16[128,2048]{1,0:T(8,128)(2,1)}, bf16[128,2048]{1,0:T(8,128)(2,1)}, u32[]{:S(2)}, u32[]{:S(2)}) collective-permute-start(bf16[128,2048]{1,0:T(8,128)(2,1)} %get-tuple-element.174), channel_id=1, source_target_pairs={{0,2},{2,0},{4,6},{6,4},{8,10},{10,8},{12,14},{14,12},{16,18},{18,... | collective-permute-start | bytes 1572872 | tf_op jit(solution)/shard_map/ppermute | solution.py:357
  182.2 21.6 %collective-permute-start.36 = (bf16[128,2048]{1,0:T(8,128)(2,1)}, bf16[128,2048]{1,0:T(8,128)(2,1)}, u32[]{:S(2)}, u32[]{:S(2)}) collective-permute-start(bf16[128,2048]{1,0:T(8,128)(2,1)} %get-tuple-element.175), channel_id=1, source_target_pairs={{0,4},{2,6},{4,0},{6,2},{8,12},{10,14},{12,8},{14,10},{16,20},{18,... | collective-permute-start | bytes 1572872 | tf_op jit(solution)/shard_map/ppermute | solution.py:361
  182.6 14.1 %collective-permute-start.37 = (bf16[128,1536]{1,0:T(8,128)(2,1)}, bf16[128,1536]{1,0:T(8,128)(2,1)S(1)}, u32[]{:S(2)}, u32[]{:S(2)}) collective-permute-start(bf16[128,1536]{1,0:T(8,128)(2,1)} %get-tuple-element.176), channel_id=1, source_target_pairs={{0,8},{2,10},{4,12},{6,14},{8,16},{10,18},{12,20},{14,22},{16,24},... | collective-permute-start | bytes 1179656 | tf_op jit(solution)/shard_map/ppermute | solution.py:366
  184.6 18.5 %collective-permute-start.38 = (bf16[128,1536]{1,0:T(8,128)(2,1)}, bf16[128,1536]{1,0:T(8,128)(2,1)S(1)}, u32[]{:S(2)}, u32[]{:S(2)}) collective-permute-start(bf16[128,1536]{1,0:T(8,128)(2,1)} %get-tuple-element.177), channel_id=1, source_target_pairs={{8,0},{10,2},{12,4},{14,6},{16,8},{18,10},{20,12},{22,14},{24,16},... | collective-permute-start | bytes 1179656 | tf_op jit(solution)/shard_map/ppermute | solution.py:371
  (16 other events, 28.8 us)

commit v7 on v6

--- a/solution.py
+++ b/solution.py
@@ -212,7 +212,7 @@
             member = base + step
             index = place(group, member)
             rows = pl.ds(pl.multiple_of(offset + step * count, 16), count)
-            feats = widened(own[source][rows, :]) + widened(other[source][rows, :])
+            feats = own[source][rows, :] + other[source][rows, :].astype(jnp.float32)
             feats = rounded(feats)
             slot = (group * PLANE + member) * span + first
             feats_s[pl.ds(pl.multiple_of(slot, 16), count), :] = feats
@@ -343,7 +343,7 @@
         out_specs=(vmem,) * (2 + len(order)),
         scratch_shapes=[pltpu.VMEM((length, width), jnp.float32)] * 4
         + [pltpu.VMEM((length, 3 * width), jnp.float32)],
-        compiler_params=pltpu.CompilerParams(vmem_limit_bytes=40 * 2**20),
+        compiler_params=pltpu.CompilerParams(vmem_limit_bytes=24 * 2**20),
         name="modal_scan",
     )(me, residue_rows, rate_rows, *arrays)
     return outs[0], outs[1], outs[2:]
@@ -487,7 +487,7 @@
         jnp.einsum("td,rd->tr", rows, matrix, preferred_element_type=jnp.float32)
         for matrix in (kept, taken)
     )
-    return narrowed(own), swapped(narrowed(given))
+    return own, swapped(narrowed(given))
 
 
 def columns_held(rows):

time: 208 us -> 211 us (1.014)
  local copies, waits for them, and re-layouts: 15.2 us -> 17.5 us
    unnamed x57 -> x61, local copies, waits for them, and re-layouts: 10.9 us -> 13.2 us
  transfers between devices with their start and end apart: 41 -> 41, of which waited for: 19 -> 18; matrix products, arithmetic and copies ran while one was open for 15% -> 15% of each run, Pallas kernels for 6% -> 6%
where the time goes in v7:
time: 211 us; the launch traced here: 210 us
  waiting for transfers between devices  76.4 us (36%)
  starting transfers between devices  57.3 us (27%)
  Pallas kernels  32.5 us (15%)
  matrix products  25.3 us (12%)
  local copies, waits for them, and re-layouts  17.5 us (8%)
    ppermute x8, waiting for transfers between devices, down(): lax.ppermute(value, 'ctx', [((i + PLANE) % count, i) for i in range(count)])  34.6 us
    ppermute x8, waiting for transfers between devices, up(): lax.ppermute(value, 'ctx', [(i, (i + PLANE) % count) for i in range(count)])  30.2 us
    ppermute x8, starting transfers between devices, down(): lax.ppermute(value, 'ctx', [((i + PLANE) % count, i) for i in range(count)])  26.6 us
    dot_general x8, matrix products, project(): jnp.einsum('td,rd->tr', rows, matrix, preferred_element_type=jnp.float32)  16.3 us
    pallas_call x10, Pallas kernels, assemble(): pl.pallas_call(functools.partial(assemble_kernel, len(arrays), plans), ou...  13.8 us
    unnamed x61, local copies, waits for them, and re-layouts  13.2 us
    pallas_call x1, Pallas kernels, scan_all(): pl.pallas_call(functools.partial(scan_kernel, PLANE, runs, order), out_sh...  13 us
    ppermute x8, starting transfers between devices, over_y(): lax.ppermute(value, 'ctx', [(i, i ^ 2) for i in range(lax.axis_size('ctx'...  9.09 us
  transfers between devices with their start and end apart: 41, of which 18 were waited for; matrix products, arithmetic and copies ran while one was open for 15% of the time, Pallas kernels for 6%

profile of v7, /device:TPU:0, one launch (start us, length us, event | category | flops | bytes accessed | tf_op | source)
XLA Modules:
  0.0 210.2 jit_solution(4077400910188569239)
XLA Ops:
  0.6 2.2 %halves.2 = (bf16[128,2048]{1,0:T(8,128)(2,1)}, bf16[96,2048]{1,0:T(8,128)(2,1)}) custom-call(s32[1]{0:T(128)} %bitcast.5.core_ref, bf16[128,4096]{1,0:T(8,128)(2,1)} %refs_0_.1), custom_call_target="tpu_custom_call" | custom-call | bytes 1835008 | tf_op jit(solution)/shard_map/halves/pallas_call | solution.py:409
  2.8 3.0 %collective-permute-start.1 = (bf16[128,2048]{1,0:T(8,128)(2,1)}, bf16[128,2048]{1,0:T(8,128)(2,1)S(1)}, u32[]{:S(2)}, u32[]{:S(2)}) collective-permute-start(bf16[128,2048]{1,0:T(8,128)(2,1)} %get-tuple-element.103.refs_0_), channel_id=1, source_target_pairs={{0,4},{2,6},{4,0},{6,2},{8,12},{10,14},{12,8},{14,10},{16,20},{18,... | collective-permute-start | bytes 1572872 | tf_op jit(solution)/shard_map/ppermute | solution.py:361
  5.8 1.5 collective-permute-start
  7.3 3.6 %collective-permute-start.3 = (bf16[96,2048]{1,0:T(8,128)(2,1)}, bf16[96,2048]{1,0:T(8,128)(2,1)S(1)}, u32[]{:S(2)}, u32[]{:S(2)}) collective-permute-start(bf16[96,2048]{1,0:T(8,128)(2,1)} %get-tuple-element.94), channel_id=1, source_target_pairs={{8,0},{10,2},{12,4},{14,6},{16,8},{18,10},{20,12},{22,14},{24,16},... | collective-permute-start | bytes 1179656 | tf_op jit(solution)/shard_map/ppermute | solution.py:371
  10.9 3.5 %halves.3 = (bf16[384,2048]{1,0:T(8,128)(2,1)}, bf16[384,2048]{1,0:T(8,128)(2,1)}) custom-call(s32[1]{0:T(128)} %bitcast.5.core_ref, bf16[384,4096]{1,0:T(8,128)(2,1)} %bitcast.46), custom_call_target="tpu_custom_call" | custom-call | bytes 6291456 | tf_op jit(solution)/shard_map/halves/pallas_call | solution.py:409
  14.6 6.3 %collective-permute-done.3.refs_4_ = bf16[96,2048]{1,0:T(8,128)(2,1)S(1)} collective-permute-done((bf16[96,2048]{1,0:T(8,128)(2,1)}, bf16[96,2048]{1,0:T(8,128)(2,1)S(1)}, u32[]{:S(2)}, u32[]{:S(2)}) %collective-permute-start.3) | collective-permute-done | bytes 393248 | tf_op jit(solution)/shard_map/ppermute | solution.py:371
  20.8 7.4 %collective-permute-done.2.refs_3_ = bf16[96,2048]{1,0:T(8,128)(2,1)S(1)} collective-permute-done((bf16[96,2048]{1,0:T(8,128)(2,1)}, bf16[96,2048]{1,0:T(8,128)(2,1)S(1)}, u32[]{:S(2)}, u32[]{:S(2)}) %collective-permute-start.2) | collective-permute-done | bytes 393248 | tf_op jit(solution)/shard_map/ppermute | solution.py:366
  28.3 1.9 assemble.10
  30.1 1.6 collective-permute-start.6
  31.8 2.2 %collective-permute-start.7 = (bf16[112,2048]{1,0:T(8,128)(2,1)}, bf16[112,2048]{1,0:T(8,128)(2,1)}, u32[]{:S(2)}, u32[]{:S(2)}) collective-permute-start(bf16[112,2048]{1,0:T(8,128)(2,1)} %get-tuple-element.114), channel_id=1, source_target_pairs={{8,0},{10,2},{12,4},{14,6},{16,8},{18,10},{20,12},{22,14},{24,16},... | collective-permute-start | bytes 1376264 | tf_op jit(solution)/shard_map/ppermute | solution.py:371
  36.3 2.3 %fusion.12.refs_1_ = f32[576,384]{1,0:T(8,128)} fusion(bf16[576,2048]{1,0:T(8,128)(2,1)S(1)} %constant_dynamic-update-slice_fusion, bf16[384,2048]{1,0:T(8,128)(2,1)S(1)} %copy-done.17), kind=kOutput, calls=%fused_computation.37 | convolution fusion | flops 905969664 | bytes 4816896 | tf_op jit(solution)/shard_map/td,rd->tr/dot_general | solution.py:487
  39.6 3.8 %all-to-all-start = ((bf16[128,16,128]{2,0,1:T(8,128)(2,1)}), bf16[128,16,128]{2,0,1:T(8,128)(2,1)S(1)}, u32[]{:S(2)}, u32[]{:S(2)}) async-start(bf16[128,16,128]{2,0,1:T(8,128)(2,1)} %copy.8), calls=%async_computation | async-start | bytes 1048576 | tf_op jit(solution)/shard_map/all_to_all | solution.py:494
  43.5 2.2 %collective-permute-done.6.refs_2_ = bf16[112,2048]{1,0:T(8,128)(2,1)} collective-permute-done((bf16[112,2048]{1,0:T(8,128)(2,1)}, bf16[112,2048]{1,0:T(8,128)(2,1)}, u32[]{:S(2)}, u32[]{:S(2)}) %collective-permute-start.6) | collective-permute-done | bytes 458784 | tf_op jit(solution)/shard_map/ppermute | solution.py:366
  45.7 8.7 %collective-permute-done.7.refs_3_ = bf16[112,2048]{1,0:T(8,128)(2,1)} collective-permute-done((bf16[112,2048]{1,0:T(8,128)(2,1)}, bf16[112,2048]{1,0:T(8,128)(2,1)}, u32[]{:S(2)}, u32[]{:S(2)}) %collective-permute-start.7) | collective-permute-done | bytes 458784 | tf_op jit(solution)/shard_map/ppermute | solution.py:371
  54.4 6.7 %collective-permute-done.4.refs_0_ = bf16[256,2048]{1,0:T(8,128)(2,1)S(1)} collective-permute-done((bf16[256,2048]{1,0:T(8,128)(2,1)}, bf16[256,2048]{1,0:T(8,128)(2,1)S(1)}, u32[]{:S(2)}, u32[]{:S(2)}) %collective-permute-start.4) | collective-permute-done | bytes 1048608 | tf_op jit(solution)/shard_map/ppermute | solution.py:357
  62.4 1.3 assemble.11
  63.8 3.8 %collective-permute-start.11 = (bf16[96,2048]{1,0:T(8,128)(2,1)S(1)}, bf16[96,2048]{1,0:T(8,128)(2,1)S(1)}, u32[]{:S(2)}, u32[]{:S(2)}) collective-permute-start(bf16[96,2048]{1,0:T(8,128)(2,1)S(1)} %get-tuple-element.122), channel_id=1, source_target_pairs={{8,0},{10,2},{12,4},{14,6},{16,8},{18,10},{20,12},{22,14},{24,16},... | collective-permute-start | bytes 1179656 | tf_op jit(solution)/shard_map/ppermute | solution.py:371
  71.7 2.7 %fusion.13.refs_2_ = f32[736,384]{1,0:T(8,128)} fusion(bf16[736,2048]{1,0:T(8,128)(2,1)S(1)} %constant_dynamic-update-slice_fusion.5, bf16[384,2048]{1,0:T(8,128)(2,1)S(1)} %copy-done.18), kind=kOutput, calls=%fused_computation.38 | convolution fusion | flops 1157627904 | bytes 5718016 | tf_op jit(solution)/shard_map/td,rd->tr/dot_general | solution.py:487
  74.5 1.7 assemble.13
  76.6 2.2 %convolution_convert_fusion.5 = bf16[576,384]{1,0:T(8,128)(2,1)} fusion(bf16[576,2048]{1,0:T(8,128)(2,1)S(1)} %copy-done.23, bf16[384,2048]{1,0:T(8,128)(2,1)S(1)} %assemble.13), kind=kOutput, calls=%fused_computation.9 | convolution fusion | flops 906190848 | bytes 4374528 | tf_op jit(solution)/shard_map/td,rd->tr/dot_general | solution.py:487
  78.8 2.6 %convolution_convert_fusion.3 = bf16[736,384]{1,0:T(8,128)(2,1)} fusion(bf16[736,2048]{1,0:T(8,128)(2,1)S(1)} %constant_dynamic-update-slice_fusion.5, bf16[384,2048]{1,0:T(8,128)(2,1)S(1)} %assemble.13), kind=kOutput, calls=%fused_computation.7 | convolution fusion | flops 1157910528 | bytes 5152768 | tf_op jit(solution)/shard_map/td,rd->tr/dot_general | solution.py:487
  81.7 3.8 %collective-permute-start.15 = (bf16[32,2048]{1,0:T(8,128)(2,1)S(1)}, bf16[32,2048]{1,0:T(8,128)(2,1)S(1)}, u32[]{:S(2)}, u32[]{:S(2)}) collective-permute-start(bf16[32,2048]{1,0:T(8,128)(2,1)S(1)} %get-tuple-element.130), channel_id=1, source_target_pairs={{8,0},{10,2},{12,4},{14,6},{16,8},{18,10},{20,12},{22,14},{24,16},... | collective-permute-start | bytes 393224 | tf_op jit(solution)/shard_map/ppermute | solution.py:371
  86.4 1.4 collective-permute-start.13
  87.9 2.3 %fusion.14.refs_3_ = f32[576,384]{1,0:T(8,128)} fusion(bf16[576,2048]{1,0:T(8,128)(2,1)S(1)} %constant_dynamic-update-slice_fusion.9, bf16[384,2048]{1,0:T(8,128)(2,1)S(1)} %copy-done.18), kind=kOutput, calls=%fused_computation.39 | convolution fusion | flops 905969664 | bytes 4816896 | tf_op jit(solution)/shard_map/td,rd->tr/dot_general | solution.py:487
  90.2 2.2 %convolution_convert_fusion.4 = bf16[576,384]{1,0:T(8,128)(2,1)} fusion(bf16[576,2048]{1,0:T(8,128)(2,1)S(1)} %constant_dynamic-update-slice_fusion.9, bf16[384,2048]{1,0:T(8,128)(2,1)S(1)} %assemble.13), kind=kOutput, calls=%fused_computation.8 | convolution fusion | flops 906190848 | bytes 4374528 | tf_op jit(solution)/shard_map/td,rd->tr/dot_general | solution.py:487
  102.4 13.0 %modal_scan.1 = (bf16[2048,128]{1,0:T(8,128)(2,1)}, f32[16,128]{1,0:T(8,128)}, bf16[768,384]{1,0:T(8,128)(2,1)S(1)}, bf16[1280,384]{1,0:T(8,128)(2,1)S(1)}) custom-call(s32[1]{0:T(128)} %bitcast.me_ref, f32[16,128]{1,0:T(8,128)S(1)} %bitcast.44, f32[16,128]{1,0:T(8,128)S(1)} %bitcast.45, bf16[2048,128]{1,0:T(8,128)(2,1)S(1)} %bitcast.43, ...), custom_call_target="tpu_custom_call" | custom-call | tf_op jit(solution)/shard_map/modal_scan/pallas_call | solution.py:332
  115.9 1.6 collective-permute-done.21
  117.5 2.8 %convolution_convert_fusion.1.refs_0_ = bf16[768,2048]{1,0:T(8,128)(2,1)S(1)} fusion(bf16[768,384]{1,0:T(8,128)(2,1)S(1)} %collective-permute-done.21, bf16[768,384]{1,0:T(8,128)(2,1)S(1)} %get-tuple-element.138, bf16[384,2048]{1,0:T(8,128)(2,1)S(1)} %assemble.13, bf16[384,2048]{1,0:T(8,128)(2,1)S(1)} %copy-done.19), kind=kOutput, calls=%fused_computation.1 | convolution fusion | flops 2426142720 | bytes 7471104 | tf_op jit(solution)/shard_map/dot_general | solution.py:597
  122.9 3.8 %collective-permute-start.25 = (bf16[128,256]{1,0:T(8,128)(2,1)S(1)}, bf16[128,256]{1,0:T(8,128)(2,1)S(1)}, u32[]{:S(2)}, u32[]{:S(2)}) collective-permute-start(bf16[128,256]{1,0:T(8,128)(2,1)S(1)} %get-tuple-element.142), channel_id=1, source_target_pairs={{8,0},{10,2},{12,4},{14,6},{16,8},{18,10},{20,12},{22,14},{24,16},... | collective-permute-start | bytes 196616 | tf_op jit(solution)/shard_map/ppermute | solution.py:371
  126.7 2.5 %collective-permute-done.24.refs_3_ = bf16[128,256]{1,0:T(8,128)(2,1)S(1)} collective-permute-done((bf16[128,256]{1,0:T(8,128)(2,1)S(1)}, bf16[128,256]{1,0:T(8,128)(2,1)S(1)}, u32[]{:S(2)}, u32[]{:S(2)}) %collective-permute-start.24) | collective-permute-done | bytes 65568 | tf_op jit(solution)/shard_map/ppermute | solution.py:366
  131.2 3.8 %collective-permute-start.30 = (bf16[128,1280]{1,0:T(8,128)(2,1)S(1)}, bf16[128,1280]{1,0:T(8,128)(2,1)S(1)}, u32[]{:S(2)}, u32[]{:S(2)}) collective-permute-start(bf16[128,1280]{1,0:T(8,128)(2,1)S(1)} %get-tuple-element.156), channel_id=1, source_target_pairs={{8,0},{10,2},{12,4},{14,6},{16,8},{18,10},{20,12},{22,14},{24,16},... | collective-permute-start | bytes 983048 | tf_op jit(solution)/shard_map/ppermute | solution.py:371
  136.1 3.2 %convolution_convert_fusion.refs_1_.refs_0_ = bf16[896,2048]{1,0:T(8,128)(2,1)S(1)} fusion(bf16[896,384]{1,0:T(8,128)(2,1)S(1)} %slice.17, bf16[896,384]{1,0:T(8,128)(2,1)S(1)} %slice.14, bf16[384,2048]{1,0:T(8,128)(2,1)S(1)} %assemble.13, bf16[384,2048]{1,0:T(8,128)(2,1)S(1)} %copy-done.19), kind=kOutput, calls=%fused_computation | convolution fusion | flops 2829451264 | bytes 8192000 | tf_op jit(solution)/shard_map/dot_general | solution.py:597
  139.3 4.3 %collective-permute-done.29.refs_4_ = bf16[128,1280]{1,0:T(8,128)(2,1)S(1)} collective-permute-done((bf16[128,1280]{1,0:T(8,128)(2,1)S(1)}, bf16[128,1280]{1,0:T(8,128)(2,1)S(1)}, u32[]{:S(2)}, u32[]{:S(2)}) %collective-permute-start.29) | collective-permute-done | bytes 327712 | tf_op jit(solution)/shard_map/ppermute | solution.py:366
  143.6 2.8 %collective-permute-done.30.refs_5_ = bf16[128,1280]{1,0:T(8,128)(2,1)S(1)} collective-permute-done((bf16[128,1280]{1,0:T(8,128)(2,1)S(1)}, bf16[128,1280]{1,0:T(8,128)(2,1)S(1)}, u32[]{:S(2)}, u32[]{:S(2)}) %collective-permute-start.30) | collective-permute-done | bytes 327712 | tf_op jit(solution)/shard_map/ppermute | solution.py:371
  148.0 1.8 assemble.16
  152.5 3.7 %collective-permute-start.34 = (bf16[128,2304]{1,0:T(8,128)(2,1)}, bf16[128,2304]{1,0:T(8,128)(2,1)}, u32[]{:S(2)}, u32[]{:S(2)}) collective-permute-start(bf16[128,2304]{1,0:T(8,128)(2,1)} %get-tuple-element.169), channel_id=1, source_target_pairs={{8,0},{10,2},{12,4},{14,6},{16,8},{18,10},{20,12},{22,14},{24,16},... | collective-permute-start | bytes 1769480 | tf_op jit(solution)/shard_map/ppermute | solution.py:371
  156.1 4.5 %all-to-all-start.1 = ((bf16[16,128,128]{2,1,0:T(8,128)(2,1)}), bf16[16,128,128]{2,1,0:T(8,128)(2,1)}, u32[]{:S(2)}, u32[]{:S(2)}) async-start(bf16[16,128,128]{2,1,0:T(8,128)(2,1)} %bitcast.13), calls=%async_computation.1 | async-start | bytes 1048576 | tf_op jit(solution)/shard_map/all_to_all | solution.py:629
  160.7 3.0 %convolution_convert_fusion.2.refs_0_.refs_1_ = bf16[384,2048]{1,0:T(8,128)(2,1)S(1)} fusion(bf16[384,2048]{1,0:T(8,128)(2,1)S(1)} %assemble.13, bf16[384,2048]{1,0:T(8,128)(2,1)} %get-tuple-element.108, bf16[384,384]{1,0:T(8,128)(2,1)S(1)} %slice-done, bf16[384,384]{1,0:T(8,128)(2,1)S(1)} %slice.12), kind=kOutput, calls=%fused_computation.3 | convolution fusion | flops 1216217088 | bytes 5308416 | tf_op jit(solution)/shard_map/dot_general | solution.py:597
  163.7 7.0 %collective-permute-done.33.refs_1_.refs_4_ = bf16[128,2304]{1,0:T(8,128)(2,1)} collective-permute-done((bf16[128,2304]{1,0:T(8,128)(2,1)}, bf16[128,2304]{1,0:T(8,128)(2,1)}, u32[]{:S(2)}, u32[]{:S(2)}) %collective-permute-start.33) | collective-permute-done | bytes 589856 | tf_op jit(solution)/shard_map/ppermute | solution.py:366
  170.7 10.0 %collective-permute-done.34.refs_2_.refs_5_ = bf16[128,2304]{1,0:T(8,128)(2,1)} collective-permute-done((bf16[128,2304]{1,0:T(8,128)(2,1)}, bf16[128,2304]{1,0:T(8,128)(2,1)}, u32[]{:S(2)}, u32[]{:S(2)}) %collective-permute-start.34) | collective-permute-done | bytes 589856 | tf_op jit(solution)/shard_map/ppermute | solution.py:371
  180.7 3.3 %assemble.18 = (bf16[128,2048]{1,0:T(8,128)(2,1)}, bf16[128,2048]{1,0:T(8,128)(2,1)}, bf16[128,1536]{1,0:T(8,128)(2,1)}, bf16[128,1536]{1,0:T(8,128)(2,1)}) custom-call(bf16[896,2048]{1,0:T(8,128)(2,1)S(1)} %copy-done.1, bf16[384,2048]{1,0:T(8,128)(2,1)S(1)} %convolution_convert_fusion.2.refs_0_.refs_1_, bf16[128,4096]{1,0:T(8,128)(2,1)} %collective-permute-done.31.refs_2_, ...), custom_call_target="tpu_custom_call" | custom-call | flops 1835008 | bytes 7340032 | tf_op jit(solution)/shard_map/assemble/pallas_call | solution.py:447
  185.2 1.9 collective-permute-start.37
  187.1 1.9 collective-permute-start.38
  189.3 2.0 copy.9
  191.3 1.3 assemble.17.refs_0_
  192.6 6.7 %collective-permute-done.37.refs_3_ = bf16[128,1536]{1,0:T(8,128)(2,1)S(1)} collective-permute-done((bf16[128,1536]{1,0:T(8,128)(2,1)}, bf16[128,1536]{1,0:T(8,128)(2,1)S(1)}, u32[]{:S(2)}, u32[]{:S(2)}) %collective-permute-start.37) | collective-permute-done | bytes 393248 | tf_op jit(solution)/shard_map/ppermute | solution.py:366
  199.3 6.8 %collective-permute-done.38.refs_4_ = bf16[128,1536]{1,0:T(8,128)(2,1)S(1)} collective-permute-done((bf16[128,1536]{1,0:T(8,128)(2,1)}, bf16[128,1536]{1,0:T(8,128)(2,1)S(1)}, u32[]{:S(2)}, u32[]{:S(2)}) %collective-permute-start.38) | collective-permute-done | bytes 393248 | tf_op jit(solution)/shard_map/ppermute | solution.py:371
  207.9 2.3 %assemble.19 = bf16[128,2048]{1,0:T(8,128)(2,1)} custom-call(bf16[128,2048]{1,0:T(8,128)(2,1)S(1)} %assemble.17.refs_0_, bf16[128,2048]{1,0:T(8,128)(2,1)} %collective-permute-done.35.refs_1_, bf16[128,2048]{1,0:T(8,128)(2,1)} %collective-permute-done.36.refs_2_, bf16[128,1536]{1,0:T(8,128)(2,1)S(1)} %collective-permute-done.37.refs_3_, ...), custom_call_target="tpu_custom_call" | custom-call | flops 524288 | bytes 2097152 | tf_op jit(solution)/shard_map/assemble/pallas_call | solution.py:447
  (130 shorter events, 33.9 us)
Async XLA Ops:
  2.8 25.4 %copy-start.2 = (bf16[128,2048]{1,0:T(8,128)(2,1)S(1)}, bf16[128,2048]{1,0:T(8,128)(2,1)}, u32[]{:S(2)}) copy-start(bf16[128,2048]{1,0:T(8,128)(2,1)} %get-tuple-element.103.refs_0_) | copy-start | bytes 1572868
  2.8 25.4 %collective-permute-start.1 = (bf16[128,2048]{1,0:T(8,128)(2,1)}, bf16[128,2048]{1,0:T(8,128)(2,1)S(1)}, u32[]{:S(2)}, u32[]{:S(2)}) collective-permute-start(bf16[128,2048]{1,0:T(8,128)(2,1)} %get-tuple-element.103.refs_0_), channel_id=1, source_target_pairs={{0,4},{2,6},{4,0},{6,2},{8,12},{10,14},{12,8},{14,10},{16,20},{18,... | collective-permute-start | bytes 1572872 | tf_op jit(solution)/shard_map/ppermute | solution.py:361
  5.8 22.4 %collective-permute-start = (bf16[128,2048]{1,0:T(8,128)(2,1)}, bf16[128,2048]{1,0:T(8,128)(2,1)S(1)}, u32[]{:S(2)}, u32[]{:S(2)}) collective-permute-start(bf16[128,2048]{1,0:T(8,128)(2,1)} %get-tuple-element.103.refs_0_), channel_id=1, source_target_pairs={{0,2},{2,0},{4,6},{6,4},{8,10},{10,8},{12,14},{14,12},{16,18},{18,... | collective-permute-start | bytes 1572872 | tf_op jit(solution)/shard_map/ppermute | solution.py:357
  7.3 13.5 %collective-permute-start.3 = (bf16[96,2048]{1,0:T(8,128)(2,1)}, bf16[96,2048]{1,0:T(8,128)(2,1)S(1)}, u32[]{:S(2)}, u32[]{:S(2)}) collective-permute-start(bf16[96,2048]{1,0:T(8,128)(2,1)} %get-tuple-element.94), channel_id=1, source_target_pairs={{8,0},{10,2},{12,4},{14,6},{16,8},{18,10},{20,12},{22,14},{24,16},... | collective-permute-start | bytes 1179656 | tf_op jit(solution)/shard_map/ppermute | solution.py:371
  10.9 17.3 %collective-permute-start.2 = (bf16[96,2048]{1,0:T(8,128)(2,1)}, bf16[96,2048]{1,0:T(8,128)(2,1)S(1)}, u32[]{:S(2)}, u32[]{:S(2)}) collective-permute-start(bf16[96,2048]{1,0:T(8,128)(2,1)} %get-tuple-element.94), channel_id=1, source_target_pairs={{0,8},{2,10},{4,12},{6,14},{8,16},{10,18},{12,20},{14,22},{16,24},... | collective-permute-start | bytes 1179656 | tf_op jit(solution)/shard_map/ppermute | solution.py:366
  14.5 60.0 %collective-permute-start.16 = (bf16[384,2048]{1,0:T(8,128)(2,1)}, bf16[384,2048]{1,0:T(8,128)(2,1)}, u32[]{:S(2)}, u32[]{:S(2)}) collective-permute-start(bf16[384,2048]{1,0:T(8,128)(2,1)} %get-tuple-element.135), channel_id=1, source_target_pairs={{0,1},{1,0},{2,3},{3,2},{4,5},{5,4},{6,7},{7,6},{8,9},{9,8},{10,11... | collective-permute-start | bytes 4718600 | tf_op jit(solution)/shard_map/ppermute | solution.py:353
  28.2 5.7 %copy-start.4 = (bf16[96,2048]{1,0:T(8,128)(2,1)}, bf16[96,2048]{1,0:T(8,128)(2,1)S(1)}, u32[]{:S(2)}) copy-start(bf16[96,2048]{1,0:T(8,128)(2,1)S(1)} %collective-permute-done.2.refs_3_) | copy-start | bytes 1179652
  30.1 6.1 %copy-start.17 = (bf16[384,2048]{1,0:T(8,128)(2,1)S(1)}, bf16[384,2048]{1,0:T(8,128)(2,1)}, u32[]{:S(2)}) copy-start(bf16[384,2048]{1,0:T(8,128)(2,1)} %get-tuple-element.108) | copy-start | bytes 4718596
  30.1 15.6 %collective-permute-start.6 = (bf16[112,2048]{1,0:T(8,128)(2,1)}, bf16[112,2048]{1,0:T(8,128)(2,1)}, u32[]{:S(2)}, u32[]{:S(2)}) collective-permute-start(bf16[112,2048]{1,0:T(8,128)(2,1)} %get-tuple-element.113), channel_id=1, source_target_pairs={{0,8},{2,10},{4,12},{6,14},{8,16},{10,18},{12,20},{14,22},{16,24},... | collective-permute-start | bytes 1376264 | tf_op jit(solution)/shard_map/ppermute | solution.py:366
  31.8 22.7 %collective-permute-start.7 = (bf16[112,2048]{1,0:T(8,128)(2,1)}, bf16[112,2048]{1,0:T(8,128)(2,1)}, u32[]{:S(2)}, u32[]{:S(2)}) collective-permute-start(bf16[112,2048]{1,0:T(8,128)(2,1)} %get-tuple-element.114), channel_id=1, source_target_pairs={{8,0},{10,2},{12,4},{14,6},{16,8},{18,10},{20,12},{22,14},{24,16},... | collective-permute-start | bytes 1376264 | tf_op jit(solution)/shard_map/ppermute | solution.py:371
  34.0 27.2 %collective-permute-start.4 = (bf16[256,2048]{1,0:T(8,128)(2,1)}, bf16[256,2048]{1,0:T(8,128)(2,1)S(1)}, u32[]{:S(2)}, u32[]{:S(2)}) collective-permute-start(bf16[256,2048]{1,0:T(8,128)(2,1)} %get-tuple-element.111), channel_id=1, source_target_pairs={{0,2},{2,0},{4,6},{6,4},{8,10},{10,8},{12,14},{14,12},{16,18},{18,... | collective-permute-start | bytes 3145736 | tf_op jit(solution)/shard_map/ppermute | solution.py:357
  34.5 27.9 %collective-permute-start.5 = (bf16[256,2048]{1,0:T(8,128)(2,1)}, bf16[256,2048]{1,0:T(8,128)(2,1)S(1)}, u32[]{:S(2)}, u32[]{:S(2)}) collective-permute-start(bf16[256,2048]{1,0:T(8,128)(2,1)} %get-tuple-element.112), channel_id=1, source_target_pairs={{0,4},{2,6},{4,0},{6,2},{8,12},{10,14},{12,8},{14,10},{16,20},{18,... | collective-permute-start | bytes 3145736 | tf_op jit(solution)/shard_map/ppermute | solution.py:361
  39.6 55.4 %all-to-all-start = ((bf16[128,16,128]{2,0,1:T(8,128)(2,1)}), bf16[128,16,128]{2,0,1:T(8,128)(2,1)S(1)}, u32[]{:S(2)}, u32[]{:S(2)}) async-start(bf16[128,16,128]{2,0,1:T(8,128)(2,1)} %copy.8), calls=%async_computation | async-start | bytes 1048576 | tf_op jit(solution)/shard_map/all_to_all | solution.py:494
  63.8 17.6 %collective-permute-start.10 = (bf16[96,2048]{1,0:T(8,128)(2,1)S(1)}, bf16[96,2048]{1,0:T(8,128)(2,1)S(1)}, u32[]{:S(2)}, u32[]{:S(2)}) collective-permute-start(bf16[96,2048]{1,0:T(8,128)(2,1)S(1)} %get-tuple-element.121), channel_id=1, source_target_pairs={{0,8},{2,10},{4,12},{6,14},{8,16},{10,18},{12,20},{14,22},{16,24},... | collective-permute-start | bytes 1179656 | tf_op jit(solution)/shard_map/ppermute | solution.py:366
  63.8 17.5 %collective-permute-start.11 = (bf16[96,2048]{1,0:T(8,128)(2,1)S(1)}, bf16[96,2048]{1,0:T(8,128)(2,1)S(1)}, u32[]{:S(2)}, u32[]{:S(2)}) collective-permute-start(bf16[96,2048]{1,0:T(8,128)(2,1)S(1)} %get-tuple-element.122), channel_id=1, source_target_pairs={{8,0},{10,2},{12,4},{14,6},{16,8},{18,10},{20,12},{22,14},{24,16},... | collective-permute-start | bytes 1179656 | tf_op jit(solution)/shard_map/ppermute | solution.py:371
  67.6 13.7 %collective-permute-start.8 = (bf16[192,2048]{1,0:T(8,128)(2,1)S(1)}, bf16[192,2048]{1,0:T(8,128)(2,1)S(1)}, u32[]{:S(2)}, u32[]{:S(2)}) collective-permute-start(bf16[192,2048]{1,0:T(8,128)(2,1)S(1)} %get-tuple-element.119), channel_id=1, source_target_pairs={{0,2},{2,0},{4,6},{6,4},{8,10},{10,8},{12,14},{14,12},{16,18},{18,... | collective-permute-start | bytes 2359304 | tf_op jit(solution)/shard_map/ppermute | solution.py:357
  68.8 12.7 %collective-permute-start.9 = (bf16[192,2048]{1,0:T(8,128)(2,1)S(1)}, bf16[192,2048]{1,0:T(8,128)(2,1)S(1)}, u32[]{:S(2)}, u32[]{:S(2)}) collective-permute-start(bf16[192,2048]{1,0:T(8,128)(2,1)S(1)} %get-tuple-element.120), channel_id=1, source_target_pairs={{0,4},{2,6},{4,0},{6,2},{8,12},{10,14},{12,8},{14,10},{16,20},{18,... | collective-permute-start | bytes 2359304 | tf_op jit(solution)/shard_map/ppermute | solution.py:361
  78.8 16.3 %collective-permute-start.17 = (bf16[576,384]{1,0:T(8,128)(2,1)}, bf16[576,384]{1,0:T(8,128)(2,1)S(1)}, u32[]{:S(2)}, u32[]{:S(2)}) collective-permute-start(bf16[576,384]{1,0:T(8,128)(2,1)} %convolution_convert_fusion.5), channel_id=1, source_target_pairs={{0,1},{1,0},{2,3},{3,2},{4,5},{5,4},{6,7},{7,6},{8,9},{9,8},{10,11... | collective-permute-start | bytes 1327112 | tf_op jit(solution)/shard_map/ppermute | solution.py:353
  81.6 10.8 %collective-permute-start.14 = (bf16[32,2048]{1,0:T(8,128)(2,1)S(1)}, bf16[32,2048]{1,0:T(8,128)(2,1)S(1)}, u32[]{:S(2)}, u32[]{:S(2)}) collective-permute-start(bf16[32,2048]{1,0:T(8,128)(2,1)S(1)} %get-tuple-element.129), channel_id=1, source_target_pairs={{0,8},{2,10},{4,12},{6,14},{8,16},{10,18},{12,20},{14,22},{16,24},... | collective-permute-start | bytes 393224 | tf_op jit(solution)/shard_map/ppermute | solution.py:366
  81.7 10.7 %collective-permute-start.15 = (bf16[32,2048]{1,0:T(8,128)(2,1)S(1)}, bf16[32,2048]{1,0:T(8,128)(2,1)S(1)}, u32[]{:S(2)}, u32[]{:S(2)}) collective-permute-start(bf16[32,2048]{1,0:T(8,128)(2,1)S(1)} %get-tuple-element.130), channel_id=1, source_target_pairs={{8,0},{10,2},{12,4},{14,6},{16,8},{18,10},{20,12},{22,14},{24,16},... | collective-permute-start | bytes 393224 | tf_op jit(solution)/shard_map/ppermute | solution.py:371
  85.5 7.4 %collective-permute-start.12 = (bf16[48,2048]{1,0:T(8,128)(2,1)S(1)}, bf16[48,2048]{1,0:T(8,128)(2,1)S(1)}, u32[]{:S(2)}, u32[]{:S(2)}) collective-permute-start(bf16[48,2048]{1,0:T(8,128)(2,1)S(1)} %get-tuple-element.127), channel_id=1, source_target_pairs={{0,2},{2,0},{4,6},{6,4},{8,10},{10,8},{12,14},{14,12},{16,18},{18,... | collective-permute-start | bytes 589832 | tf_op jit(solution)/shard_map/ppermute | solution.py:357
  86.4 6.6 %collective-permute-start.13 = (bf16[48,2048]{1,0:T(8,128)(2,1)S(1)}, bf16[48,2048]{1,0:T(8,128)(2,1)S(1)}, u32[]{:S(2)}, u32[]{:S(2)}) collective-permute-start(bf16[48,2048]{1,0:T(8,128)(2,1)S(1)} %get-tuple-element.128), channel_id=1, source_target_pairs={{0,4},{2,6},{4,0},{6,2},{8,12},{10,14},{12,8},{14,10},{16,20},{18,... | collective-permute-start | bytes 589832 | tf_op jit(solution)/shard_map/ppermute | solution.py:361
  92.4 3.5 %collective-permute-start.18 = (bf16[736,384]{1,0:T(8,128)(2,1)}, bf16[736,384]{1,0:T(8,128)(2,1)S(1)}, u32[]{:S(2)}, u32[]{:S(2)}) collective-permute-start(bf16[736,384]{1,0:T(8,128)(2,1)} %convolution_convert_fusion.3), channel_id=1, source_target_pairs={{0,1},{1,0},{2,3},{3,2},{4,5},{5,4},{6,7},{7,6},{8,9},{9,8},{10,11... | collective-permute-start | bytes 1695752 | tf_op jit(solution)/shard_map/ppermute | solution.py:353
  92.4 4.3 %collective-permute-start.19 = (bf16[576,384]{1,0:T(8,128)(2,1)}, bf16[576,384]{1,0:T(8,128)(2,1)}, u32[]{:S(2)}, u32[]{:S(2)}) collective-permute-start(bf16[576,384]{1,0:T(8,128)(2,1)} %convolution_convert_fusion.4), channel_id=1, source_target_pairs={{0,1},{1,0},{2,3},{3,2},{4,5},{5,4},{6,7},{7,6},{8,9},{9,8},{10,11... | collective-permute-start | bytes 1327112 | tf_op jit(solution)/shard_map/ppermute | solution.py:353
  94.3 2.3 %collective-permute-start.20 = (bf16[160,384]{1,0:T(8,128)(2,1)}, bf16[160,384]{1,0:T(8,128)(2,1)S(1)}, u32[]{:S(2)}, u32[]{:S(2)}) collective-permute-start(bf16[160,384]{1,0:T(8,128)(2,1)} %convolution_convert_fusion.6), channel_id=1, source_target_pairs={{0,1},{1,0},{2,3},{3,2},{4,5},{5,4},{6,7},{7,6},{8,9},{9,8},{10,11... | collective-permute-start | bytes 368648 | tf_op jit(solution)/shard_map/ppermute | solution.py:353
  102.4 15.1 %copy-start.19 = (bf16[384,2048]{1,0:T(8,128)(2,1)S(1)}, bf16[384,2048]{1,0:T(8,128)(2,1)}, u32[]{:S(2)}) copy-start(bf16[384,2048]{1,0:T(8,128)(2,1)} %get-tuple-element.108) | copy-start | bytes 4718596
  115.4 2.1 collective-permute-start.21
  115.8 19.2 %collective-permute-start.26 = (bf16[1280,384]{1,0:T(8,128)(2,1)S(1)}, bf16[1280,384]{1,0:T(8,128)(2,1)S(1)}, u32[]{:S(2)}, u32[]{:S(2)}) collective-permute-start(bf16[1280,384]{1,0:T(8,128)(2,1)S(1)} %get-tuple-element.148), channel_id=1, source_target_pairs={{0,1},{1,0},{2,3},{3,2},{4,5},{5,4},{6,7},{7,6},{8,9},{9,8},{10,11... | collective-permute-start | bytes 2949128 | tf_op jit(solution)/shard_map/ppermute | solution.py:353
  120.3 8.9 %collective-permute-start.22 = (bf16[128,768]{1,0:T(8,128)(2,1)S(1)}, bf16[128,768]{1,0:T(8,128)(2,1)S(1)}, u32[]{:S(2)}, u32[]{:S(2)}) collective-permute-start(bf16[128,768]{1,0:T(8,128)(2,1)S(1)} %get-tuple-element.139), channel_id=1, source_target_pairs={{0,2},{2,0},{4,6},{6,4},{8,10},{10,8},{12,14},{14,12},{16,18},{18,... | collective-permute-start | bytes 589832 | tf_op jit(solution)/shard_map/ppermute | solution.py:357
  121.6 7.6 %collective-permute-start.23 = (bf16[128,768]{1,0:T(8,128)(2,1)S(1)}, bf16[128,768]{1,0:T(8,128)(2,1)S(1)}, u32[]{:S(2)}, u32[]{:S(2)}) collective-permute-start(bf16[128,768]{1,0:T(8,128)(2,1)S(1)} %get-tuple-element.140), channel_id=1, source_target_pairs={{0,4},{2,6},{4,0},{6,2},{8,12},{10,14},{12,8},{14,10},{16,20},{18,... | collective-permute-start | bytes 589832 | tf_op jit(solution)/shard_map/ppermute | solution.py:361
  122.9 6.3 %collective-permute-start.24 = (bf16[128,256]{1,0:T(8,128)(2,1)S(1)}, bf16[128,256]{1,0:T(8,128)(2,1)S(1)}, u32[]{:S(2)}, u32[]{:S(2)}) collective-permute-start(bf16[128,256]{1,0:T(8,128)(2,1)S(1)} %get-tuple-element.141), channel_id=1, source_target_pairs={{0,8},{2,10},{4,12},{6,14},{8,16},{10,18},{12,20},{14,22},{16,24},... | collective-permute-start | bytes 196616 | tf_op jit(solution)/shard_map/ppermute | solution.py:366
  122.9 6.3 %collective-permute-start.25 = (bf16[128,256]{1,0:T(8,128)(2,1)S(1)}, bf16[128,256]{1,0:T(8,128)(2,1)S(1)}, u32[]{:S(2)}, u32[]{:S(2)}) collective-permute-start(bf16[128,256]{1,0:T(8,128)(2,1)S(1)} %get-tuple-element.142), channel_id=1, source_target_pairs={{8,0},{10,2},{12,4},{14,6},{16,8},{18,10},{20,12},{22,14},{24,16},... | collective-permute-start | bytes 196616 | tf_op jit(solution)/shard_map/ppermute | solution.py:371
  129.4 18.0 %collective-permute-start.27 = (bf16[128,3072]{1,0:T(8,128)(2,1)S(1)}, bf16[128,3072]{1,0:T(8,128)(2,1)S(1)}, u32[]{:S(2)}, u32[]{:S(2)}) collective-permute-start(bf16[128,3072]{1,0:T(8,128)(2,1)S(1)} %get-tuple-element.153), channel_id=1, source_target_pairs={{0,2},{2,0},{4,6},{6,4},{8,10},{10,8},{12,14},{14,12},{16,18},{18,... | collective-permute-start | bytes 2359304 | tf_op jit(solution)/shard_map/ppermute | solution.py:357
  130.3 17.7 %collective-permute-start.28 = (bf16[128,3072]{1,0:T(8,128)(2,1)S(1)}, bf16[128,3072]{1,0:T(8,128)(2,1)S(1)}, u32[]{:S(2)}, u32[]{:S(2)}) collective-permute-start(bf16[128,3072]{1,0:T(8,128)(2,1)S(1)} %get-tuple-element.154), channel_id=1, source_target_pairs={{0,4},{2,6},{4,0},{6,2},{8,12},{10,14},{12,8},{14,10},{16,20},{18,... | collective-permute-start | bytes 2359304 | tf_op jit(solution)/shard_map/ppermute | solution.py:361
  131.1 12.5 %collective-permute-start.29 = (bf16[128,1280]{1,0:T(8,128)(2,1)S(1)}, bf16[128,1280]{1,0:T(8,128)(2,1)S(1)}, u32[]{:S(2)}, u32[]{:S(2)}) collective-permute-start(bf16[128,1280]{1,0:T(8,128)(2,1)S(1)} %get-tuple-element.155), channel_id=1, source_target_pairs={{0,8},{2,10},{4,12},{6,14},{8,16},{10,18},{12,20},{14,22},{16,24},... | collective-permute-start | bytes 983048 | tf_op jit(solution)/shard_map/ppermute | solution.py:366
  131.2 15.2 %collective-permute-start.30 = (bf16[128,1280]{1,0:T(8,128)(2,1)S(1)}, bf16[128,1280]{1,0:T(8,128)(2,1)S(1)}, u32[]{:S(2)}, u32[]{:S(2)}) collective-permute-start(bf16[128,1280]{1,0:T(8,128)(2,1)S(1)} %get-tuple-element.156), channel_id=1, source_target_pairs={{8,0},{10,2},{12,4},{14,6},{16,8},{18,10},{20,12},{22,14},{24,16},... | collective-permute-start | bytes 983048 | tf_op jit(solution)/shard_map/ppermute | solution.py:371
  139.3 10.6 %copy-start = (bf16[896,2048]{1,0:T(8,128)(2,1)}, bf16[896,2048]{1,0:T(8,128)(2,1)S(1)}, u32[]{:S(2)}) copy-start(bf16[896,2048]{1,0:T(8,128)(2,1)S(1)} %convolution_convert_fusion.refs_1_.refs_0_) | copy-start | bytes 11010052
  139.3 21.4 %slice-start = ((bf16[1280,384]{1,0:T(8,128)(2,1)}), bf16[384,384]{1,0:T(8,128)(2,1)S(1)}, s32[]{:S(2)}) async-start(bf16[1280,384]{1,0:T(8,128)(2,1)} %copy-done.20), calls=%async_computation.2 | async-start | bytes 589824 | tf_op jit(solution)/shard_map/slice | solution.py:626
  149.9 30.9 %collective-permute-start.31 = (bf16[128,4096]{1,0:T(8,128)(2,1)}, bf16[128,4096]{1,0:T(8,128)(2,1)}, u32[]{:S(2)}, u32[]{:S(2)}) collective-permute-start(bf16[128,4096]{1,0:T(8,128)(2,1)} %get-tuple-element.166), channel_id=1, source_target_pairs={{0,2},{2,0},{4,6},{6,4},{8,10},{10,8},{12,14},{14,12},{16,18},{18,... | collective-permute-start | bytes 3145736 | tf_op jit(solution)/shard_map/ppermute | solution.py:357
  151.0 29.7 %collective-permute-start.32 = (bf16[128,4096]{1,0:T(8,128)(2,1)}, bf16[128,4096]{1,0:T(8,128)(2,1)}, u32[]{:S(2)}, u32[]{:S(2)}) collective-permute-start(bf16[128,4096]{1,0:T(8,128)(2,1)} %get-tuple-element.167), channel_id=1, source_target_pairs={{0,4},{2,6},{4,0},{6,2},{8,12},{10,14},{12,8},{14,10},{16,20},{18,... | collective-permute-start | bytes 3145736 | tf_op jit(solution)/shard_map/ppermute | solution.py:361
  152.3 18.4 %collective-permute-start.33 = (bf16[128,2304]{1,0:T(8,128)(2,1)}, bf16[128,2304]{1,0:T(8,128)(2,1)}, u32[]{:S(2)}, u32[]{:S(2)}) collective-permute-start(bf16[128,2304]{1,0:T(8,128)(2,1)} %get-tuple-element.168), channel_id=1, source_target_pairs={{0,8},{2,10},{4,12},{6,14},{8,16},{10,18},{12,20},{14,22},{16,24},... | collective-permute-start | bytes 1769480 | tf_op jit(solution)/shard_map/ppermute | solution.py:366
  152.5 28.3 %collective-permute-start.34 = (bf16[128,2304]{1,0:T(8,128)(2,1)}, bf16[128,2304]{1,0:T(8,128)(2,1)}, u32[]{:S(2)}, u32[]{:S(2)}) collective-permute-start(bf16[128,2304]{1,0:T(8,128)(2,1)} %get-tuple-element.169), channel_id=1, source_target_pairs={{8,0},{10,2},{12,4},{14,6},{16,8},{18,10},{20,12},{22,14},{24,16},... | collective-permute-start | bytes 1769480 | tf_op jit(solution)/shard_map/ppermute | solution.py:371
  156.1 33.1 %all-to-all-start.1 = ((bf16[16,128,128]{2,1,0:T(8,128)(2,1)}), bf16[16,128,128]{2,1,0:T(8,128)(2,1)}, u32[]{:S(2)}, u32[]{:S(2)}) async-start(bf16[16,128,128]{2,1,0:T(8,128)(2,1)} %bitcast.13), calls=%async_computation.1 | async-start | bytes 1048576 | tf_op jit(solution)/shard_map/all_to_all | solution.py:629
  160.7 20.1 %copy-start.1 = (bf16[896,2048]{1,0:T(8,128)(2,1)S(1)}, bf16[896,2048]{1,0:T(8,128)(2,1)}, u32[]{:S(2)}) copy-start(bf16[896,2048]{1,0:T(8,128)(2,1)} %copy-done) | copy-start | bytes 11010052
  184.0 22.9 %collective-permute-start.35 = (bf16[128,2048]{1,0:T(8,128)(2,1)}, bf16[128,2048]{1,0:T(8,128)(2,1)}, u32[]{:S(2)}, u32[]{:S(2)}) collective-permute-start(bf16[128,2048]{1,0:T(8,128)(2,1)} %get-tuple-element.174), channel_id=1, source_target_pairs={{0,2},{2,0},{4,6},{6,4},{8,10},{10,8},{12,14},{14,12},{16,18},{18,... | collective-permute-start | bytes 1572872 | tf_op jit(solution)/shard_map/ppermute | solution.py:357
  184.9 22.0 %collective-permute-start.36 = (bf16[128,2048]{1,0:T(8,128)(2,1)}, bf16[128,2048]{1,0:T(8,128)(2,1)}, u32[]{:S(2)}, u32[]{:S(2)}) collective-permute-start(bf16[128,2048]{1,0:T(8,128)(2,1)} %get-tuple-element.175), channel_id=1, source_target_pairs={{0,4},{2,6},{4,0},{6,2},{8,12},{10,14},{12,8},{14,10},{16,20},{18,... | collective-permute-start | bytes 1572872 | tf_op jit(solution)/shard_map/ppermute | solution.py:361
  185.2 14.1 %collective-permute-start.37 = (bf16[128,1536]{1,0:T(8,128)(2,1)}, bf16[128,1536]{1,0:T(8,128)(2,1)S(1)}, u32[]{:S(2)}, u32[]{:S(2)}) collective-permute-start(bf16[128,1536]{1,0:T(8,128)(2,1)} %get-tuple-element.176), channel_id=1, source_target_pairs={{0,8},{2,10},{4,12},{6,14},{8,16},{10,18},{12,20},{14,22},{16,24},... | collective-permute-start | bytes 1179656 | tf_op jit(solution)/shard_map/ppermute | solution.py:366
  187.1 19.0 %collective-permute-start.38 = (bf16[128,1536]{1,0:T(8,128)(2,1)}, bf16[128,1536]{1,0:T(8,128)(2,1)S(1)}, u32[]{:S(2)}, u32[]{:S(2)}) collective-permute-start(bf16[128,1536]{1,0:T(8,128)(2,1)} %get-tuple-element.177), channel_id=1, source_target_pairs={{8,0},{10,2},{12,4},{14,6},{16,8},{18,10},{20,12},{22,14},{24,16},... | collective-permute-start | bytes 1179656 | tf_op jit(solution)/shard_map/ppermute | solution.py:371
  (18 other events, 33.9 us)

commit v8 on v4

--- a/solution.py
+++ b/solution.py
@@ -476,8 +476,8 @@
 
 
 def all_ways(for_x, for_y, for_above, for_below):
+    got_x, got_y = over_x(for_x), over_y(for_y)
     from_below, from_above = up(for_above), down(for_below)
-    got_x, got_y = over_x(for_x), over_y(for_y)
     return lax.optimization_barrier((got_x, got_y, from_below, from_above))
 
 

time: 205 us -> 205 us (level)
  no operation moved by 1% of the time
where the time goes in v8:
time: 205 us; the launch traced here: 204 us
  waiting for transfers between devices  80.2 us (39%)
  starting transfers between devices  55.8 us (27%)
  Pallas kernels  30.8 us (15%)
  matrix products  24.4 us (12%)
  local copies, waits for them, and re-layouts  12 us (6%)
    ppermute x8, waiting for transfers between devices, down(): lax.ppermute(value, 'ctx', [((i + PLANE) % count, i) for i in range(count)])  40.9 us
    ppermute x8, waiting for transfers between devices, up(): lax.ppermute(value, 'ctx', [(i, (i + PLANE) % count) for i in range(count)])  31.4 us
    ppermute x8, starting transfers between devices, down(): lax.ppermute(value, 'ctx', [((i + PLANE) % count, i) for i in range(count)])  25.9 us
    dot_general x8, matrix products, project(): jnp.einsum('td,rd->tr', rows, matrix, preferred_element_type=jnp.float32)  15.3 us
    pallas_call x1, Pallas kernels, scan_all(): pl.pallas_call(functools.partial(scan_kernel, PLANE, runs, order), out_sh...  13.4 us
    pallas_call x10, Pallas kernels, assemble(): pl.pallas_call(functools.partial(assemble_kernel, len(arrays), plans), ou...  11.7 us
    dot_general x3, matrix products, product(): return narrowed(jnp.dot(both, matrix, preferred_element_type=jnp.float32))  9.07 us
    ppermute x8, starting transfers between devices, over_x(): lax.ppermute(value, 'ctx', [(i, i ^ 1) for i in range(lax.axis_size('ctx'...  7.84 us
  transfers between devices with their start and end apart: 41, of which 19 were waited for; matrix products, arithmetic and copies ran while one was open for 16% of the time, Pallas kernels for 6%

profile of v8, /device:TPU:0, one launch (start us, length us, event | category | flops | bytes accessed | tf_op | source)
XLA Modules:
  0.0 204.3 jit_solution(8206070155254208028)
XLA Ops:
  0.6 2.2 %halves.2 = (bf16[128,2048]{1,0:T(8,128)(2,1)}, bf16[96,2048]{1,0:T(8,128)(2,1)}) custom-call(s32[1]{0:T(128)} %bitcast.5.core_ref, bf16[128,4096]{1,0:T(8,128)(2,1)} %refs_0_.1), custom_call_target="tpu_custom_call" | custom-call | bytes 1835008 | tf_op jit(solution)/shard_map/halves/pallas_call | solution.py:409
  2.8 3.0 %collective-permute-start.1 = (bf16[128,2048]{1,0:T(8,128)(2,1)}, bf16[128,2048]{1,0:T(8,128)(2,1)S(1)}, u32[]{:S(2)}, u32[]{:S(2)}) collective-permute-start(bf16[128,2048]{1,0:T(8,128)(2,1)} %get-tuple-element.103.refs_0_), channel_id=1, source_target_pairs={{0,4},{2,6},{4,0},{6,2},{8,12},{10,14},{12,8},{14,10},{16,20},{18,... | collective-permute-start | bytes 1572872 | tf_op jit(solution)/shard_map/ppermute | solution.py:361
  5.8 1.5 collective-permute-start
  7.3 3.6 %collective-permute-start.3 = (bf16[96,2048]{1,0:T(8,128)(2,1)}, bf16[96,2048]{1,0:T(8,128)(2,1)S(1)}, u32[]{:S(2)}, u32[]{:S(2)}) collective-permute-start(bf16[96,2048]{1,0:T(8,128)(2,1)} %get-tuple-element.94), channel_id=1, source_target_pairs={{8,0},{10,2},{12,4},{14,6},{16,8},{18,10},{20,12},{22,14},{24,16},... | collective-permute-start | bytes 1179656 | tf_op jit(solution)/shard_map/ppermute | solution.py:371
  10.9 3.5 %halves.3 = (bf16[384,2048]{1,0:T(8,128)(2,1)}, bf16[384,2048]{1,0:T(8,128)(2,1)}) custom-call(s32[1]{0:T(128)} %bitcast.5.core_ref, bf16[384,4096]{1,0:T(8,128)(2,1)} %bitcast.45), custom_call_target="tpu_custom_call" | custom-call | bytes 6291456 | tf_op jit(solution)/shard_map/halves/pallas_call | solution.py:409
  14.6 6.3 %collective-permute-done.3.refs_4_ = bf16[96,2048]{1,0:T(8,128)(2,1)S(1)} collective-permute-done((bf16[96,2048]{1,0:T(8,128)(2,1)}, bf16[96,2048]{1,0:T(8,128)(2,1)S(1)}, u32[]{:S(2)}, u32[]{:S(2)}) %collective-permute-start.3) | collective-permute-done | bytes 393248 | tf_op jit(solution)/shard_map/ppermute | solution.py:371
  20.8 7.4 %collective-permute-done.2.refs_3_ = bf16[96,2048]{1,0:T(8,128)(2,1)S(1)} collective-permute-done((bf16[96,2048]{1,0:T(8,128)(2,1)}, bf16[96,2048]{1,0:T(8,128)(2,1)S(1)}, u32[]{:S(2)}, u32[]{:S(2)}) %collective-permute-start.2) | collective-permute-done | bytes 393248 | tf_op jit(solution)/shard_map/ppermute | solution.py:366
  28.3 2.1 %assemble.10 = (bf16[256,2048]{1,0:T(8,128)(2,1)}, bf16[256,2048]{1,0:T(8,128)(2,1)}, bf16[144,2048]{1,0:T(8,128)(2,1)}, bf16[144,2048]{1,0:T(8,128)(2,1)}) custom-call(bf16[128,2048]{1,0:T(8,128)(2,1)S(1)} %copy-done.4, bf16[128,2048]{1,0:T(8,128)(2,1)S(1)} %collective-permute-done.refs_1_, bf16[128,2048]{1,0:T(8,128)(2,1)S(1)} %collective-permute-done.1.refs_2_, ...), custom_call_target="tpu_custom_call" | custom-call | flops 3276800 | bytes 13107200 | tf_op jit(solution)/shard_map/assemble/pallas_call | solution.py:447
  30.4 1.6 collective-permute-start.6
  32.0 2.2 %collective-permute-start.7 = (bf16[144,2048]{1,0:T(8,128)(2,1)}, bf16[144,2048]{1,0:T(8,128)(2,1)S(1)}, u32[]{:S(2)}, u32[]{:S(2)}) collective-permute-start(bf16[144,2048]{1,0:T(8,128)(2,1)} %get-tuple-element.114), channel_id=1, source_target_pairs={{8,0},{10,2},{12,4},{14,6},{16,8},{18,10},{20,12},{22,14},{24,16},... | collective-permute-start | bytes 1769480 | tf_op jit(solution)/shard_map/ppermute | solution.py:371
  37.7 2.3 %fusion.12.refs_1_ = f32[576,384]{1,0:T(8,128)} fusion(bf16[576,2048]{1,0:T(8,128)(2,1)S(1)} %constant_dynamic-update-slice_fusion, bf16[384,2048]{1,0:T(8,128)(2,1)S(1)} %copy-done.15), kind=kOutput, calls=%fused_computation.37 | convolution fusion | flops 905969664 | bytes 4816896 | tf_op jit(solution)/shard_map/td,rd->tr/dot_general | solution.py:487
  40.0 2.0 copy.8
  42.1 4.3 %all-to-all-start = ((bf16[128,16,128]{2,0,1:T(8,128)(2,1)}), bf16[128,16,128]{2,0,1:T(8,128)(2,1)}, u32[]{:S(2)}, u32[]{:S(2)}) async-start(bf16[128,16,128]{2,0,1:T(8,128)(2,1)} %copy.8), calls=%async_computation | async-start | bytes 1048576 | tf_op jit(solution)/shard_map/all_to_all | solution.py:494
  46.3 2.4 %collective-permute-done.6.refs_2_ = bf16[144,2048]{1,0:T(8,128)(2,1)S(1)} collective-permute-done((bf16[144,2048]{1,0:T(8,128)(2,1)}, bf16[144,2048]{1,0:T(8,128)(2,1)S(1)}, u32[]{:S(2)}, u32[]{:S(2)}) %collective-permute-start.6) | collective-permute-done | bytes 589856 | tf_op jit(solution)/shard_map/ppermute | solution.py:366
  48.7 11.5 %collective-permute-done.7.refs_3_ = bf16[144,2048]{1,0:T(8,128)(2,1)S(1)} collective-permute-done((bf16[144,2048]{1,0:T(8,128)(2,1)}, bf16[144,2048]{1,0:T(8,128)(2,1)S(1)}, u32[]{:S(2)}, u32[]{:S(2)}) %collective-permute-start.7) | collective-permute-done | bytes 589856 | tf_op jit(solution)/shard_map/ppermute | solution.py:371
  60.9 3.3 %collective-permute-start.11 = (bf16[80,2048]{1,0:T(8,128)(2,1)S(1)}, bf16[80,2048]{1,0:T(8,128)(2,1)S(1)}, u32[]{:S(2)}, u32[]{:S(2)}) collective-permute-start(bf16[80,2048]{1,0:T(8,128)(2,1)S(1)} %get-tuple-element.122), channel_id=1, source_target_pairs={{8,0},{10,2},{12,4},{14,6},{16,8},{18,10},{20,12},{22,14},{24,16},... | collective-permute-start | bytes 983048 | tf_op jit(solution)/shard_map/ppermute | solution.py:371
  66.9 1.9 fusion.13.refs_2_
  68.8 1.7 assemble.13
  70.9 2.2 %convolution_convert_fusion.4 = bf16[576,384]{1,0:T(8,128)(2,1)} fusion(bf16[576,2048]{1,0:T(8,128)(2,1)S(1)} %copy-done.19, bf16[384,2048]{1,0:T(8,128)(2,1)S(1)} %assemble.13), kind=kOutput, calls=%fused_computation.8 | convolution fusion | flops 906190848 | bytes 4374528 | tf_op jit(solution)/shard_map/td,rd->tr/dot_general | solution.py:487
  73.1 2.7 %convolution_convert_fusion.3 = bf16[800,384]{1,0:T(8,128)(2,1)} fusion(bf16[800,2048]{1,0:T(8,128)(2,1)S(1)} %constant_dynamic-update-slice_fusion.5, bf16[384,2048]{1,0:T(8,128)(2,1)S(1)} %assemble.13), kind=kOutput, calls=%fused_computation.7 | convolution fusion | flops 1258598400 | bytes 5464064 | tf_op jit(solution)/shard_map/td,rd->tr/dot_general | solution.py:487
  76.8 3.8 %collective-permute-done.11.refs_3_ = bf16[80,2048]{1,0:T(8,128)(2,1)S(1)} collective-permute-done((bf16[80,2048]{1,0:T(8,128)(2,1)S(1)}, bf16[80,2048]{1,0:T(8,128)(2,1)S(1)}, u32[]{:S(2)}, u32[]{:S(2)}) %collective-permute-start.11) | collective-permute-done | bytes 327712 | tf_op jit(solution)/shard_map/ppermute | solution.py:371
  80.6 3.1 %collective-permute-done.8.refs_0_ = bf16[192,2048]{1,0:T(8,128)(2,1)S(1)} collective-permute-done((bf16[192,2048]{1,0:T(8,128)(2,1)S(1)}, bf16[192,2048]{1,0:T(8,128)(2,1)S(1)}, u32[]{:S(2)}, u32[]{:S(2)}) %collective-permute-start.8) | collective-permute-done | bytes 786464 | tf_op jit(solution)/shard_map/ppermute | solution.py:357
  84.0 3.8 %collective-permute-start.15 = (bf16[16,2048]{1,0:T(8,128)(2,1)S(1)}, bf16[16,2048]{1,0:T(8,128)(2,1)S(1)}, u32[]{:S(2)}, u32[]{:S(2)}) collective-permute-start(bf16[16,2048]{1,0:T(8,128)(2,1)S(1)} %get-tuple-element.130), channel_id=1, source_target_pairs={{8,0},{10,2},{12,4},{14,6},{16,8},{18,10},{20,12},{22,14},{24,16},... | collective-permute-start | bytes 196616 | tf_op jit(solution)/shard_map/ppermute | solution.py:371
  89.0 2.1 %convolution_convert_fusion.5 = bf16[544,384]{1,0:T(8,128)(2,1)} fusion(bf16[544,2048]{1,0:T(8,128)(2,1)S(1)} %constant_dynamic-update-slice_fusion.9, bf16[384,2048]{1,0:T(8,128)(2,1)S(1)} %assemble.13), kind=kOutput, calls=%fused_computation.9 | convolution fusion | flops 855846912 | bytes 4218880 | tf_op jit(solution)/shard_map/td,rd->tr/dot_general | solution.py:487
  91.1 2.3 %fusion.14.refs_3_ = f32[544,384]{1,0:T(8,128)} fusion(bf16[544,2048]{1,0:T(8,128)(2,1)S(1)} %constant_dynamic-update-slice_fusion.9, bf16[384,2048]{1,0:T(8,128)(2,1)S(1)} %copy-done.16), kind=kOutput, calls=%fused_computation.39 | convolution fusion | flops 855638016 | bytes 4636672 | tf_op jit(solution)/shard_map/td,rd->tr/dot_general | solution.py:487
  99.5 13.4 %modal_scan.1 = (bf16[2048,128]{1,0:T(8,128)(2,1)}, f32[16,128]{1,0:T(8,128)}, bf16[768,384]{1,0:T(8,128)(2,1)S(1)}, bf16[1280,384]{1,0:T(8,128)(2,1)S(1)}) custom-call(s32[1]{0:T(128)} %bitcast.me_ref, f32[16,128]{1,0:T(8,128)S(1)} %bitcast.43, f32[16,128]{1,0:T(8,128)S(1)} %bitcast.44, bf16[2048,128]{1,0:T(8,128)(2,1)} %bitcast.12.refs_0_, ...), custom_call_target="tpu_custom_call" | custom-call | tf_op jit(solution)/shard_map/modal_scan/pallas_call | solution.py:332
  113.4 1.5 collective-permute-done.21
  114.9 2.8 %convolution_convert_fusion.1.refs_0_ = bf16[768,2048]{1,0:T(8,128)(2,1)S(1)} fusion(bf16[768,384]{1,0:T(8,128)(2,1)S(1)} %collective-permute-done.21, bf16[768,384]{1,0:T(8,128)(2,1)S(1)} %get-tuple-element.138, bf16[384,2048]{1,0:T(8,128)(2,1)S(1)} %assemble.13, bf16[384,2048]{1,0:T(8,128)(2,1)S(1)} %copy-done.17), kind=kOutput, calls=%fused_computation.1 | convolution fusion | flops 2426142720 | bytes 7471104 | tf_op jit(solution)/shard_map/dot_general | solution.py:597
  119.0 1.4 collective-permute-start.23
  120.4 3.8 %collective-permute-start.25 = (bf16[128,256]{1,0:T(8,128)(2,1)S(1)}, bf16[128,256]{1,0:T(8,128)(2,1)S(1)}, u32[]{:S(2)}, u32[]{:S(2)}) collective-permute-start(bf16[128,256]{1,0:T(8,128)(2,1)S(1)} %get-tuple-element.142), channel_id=1, source_target_pairs={{8,0},{10,2},{12,4},{14,6},{16,8},{18,10},{20,12},{22,14},{24,16},... | collective-permute-start | bytes 196616 | tf_op jit(solution)/shard_map/ppermute | solution.py:371
  124.2 2.3 %collective-permute-done.24.refs_3_ = bf16[128,256]{1,0:T(8,128)(2,1)S(1)} collective-permute-done((bf16[128,256]{1,0:T(8,128)(2,1)S(1)}, bf16[128,256]{1,0:T(8,128)(2,1)S(1)}, u32[]{:S(2)}, u32[]{:S(2)}) %collective-permute-start.24) | collective-permute-done | bytes 65568 | tf_op jit(solution)/shard_map/ppermute | solution.py:366
  128.5 3.8 %collective-permute-start.30 = (bf16[128,1280]{1,0:T(8,128)(2,1)S(1)}, bf16[128,1280]{1,0:T(8,128)(2,1)S(1)}, u32[]{:S(2)}, u32[]{:S(2)}) collective-permute-start(bf16[128,1280]{1,0:T(8,128)(2,1)S(1)} %get-tuple-element.156), channel_id=1, source_target_pairs={{8,0},{10,2},{12,4},{14,6},{16,8},{18,10},{20,12},{22,14},{24,16},... | collective-permute-start | bytes 983048 | tf_op jit(solution)/shard_map/ppermute | solution.py:371
  132.4 3.2 %convolution_convert_fusion.refs_1_.refs_0_ = bf16[896,2048]{1,0:T(8,128)(2,1)S(1)} fusion(bf16[896,384]{1,0:T(8,128)(2,1)S(1)} %slice.17, bf16[896,384]{1,0:T(8,128)(2,1)S(1)} %slice.14, bf16[384,2048]{1,0:T(8,128)(2,1)S(1)} %assemble.13, bf16[384,2048]{1,0:T(8,128)(2,1)S(1)} %copy-done.17), kind=kOutput, calls=%fused_computation | convolution fusion | flops 2829451264 | bytes 8192000 | tf_op jit(solution)/shard_map/dot_general | solution.py:597
  135.6 5.3 %collective-permute-done.29.refs_4_ = bf16[128,1280]{1,0:T(8,128)(2,1)S(1)} collective-permute-done((bf16[128,1280]{1,0:T(8,128)(2,1)S(1)}, bf16[128,1280]{1,0:T(8,128)(2,1)S(1)}, u32[]{:S(2)}, u32[]{:S(2)}) %collective-permute-start.29) | collective-permute-done | bytes 327712 | tf_op jit(solution)/shard_map/ppermute | solution.py:366
  140.9 2.7 %collective-permute-done.30.refs_5_ = bf16[128,1280]{1,0:T(8,128)(2,1)S(1)} collective-permute-done((bf16[128,1280]{1,0:T(8,128)(2,1)S(1)}, bf16[128,1280]{1,0:T(8,128)(2,1)S(1)}, u32[]{:S(2)}, u32[]{:S(2)}) %collective-permute-start.30) | collective-permute-done | bytes 327712 | tf_op jit(solution)/shard_map/ppermute | solution.py:371
  145.4 1.8 assemble.16
  149.8 3.4 %collective-permute-start.34 = (bf16[128,2304]{1,0:T(8,128)(2,1)}, bf16[128,2304]{1,0:T(8,128)(2,1)}, u32[]{:S(2)}, u32[]{:S(2)}) collective-permute-start(bf16[128,2304]{1,0:T(8,128)(2,1)} %get-tuple-element.169), channel_id=1, source_target_pairs={{8,0},{10,2},{12,4},{14,6},{16,8},{18,10},{20,12},{22,14},{24,16},... | collective-permute-start | bytes 1769480 | tf_op jit(solution)/shard_map/ppermute | solution.py:371
  153.2 4.2 %all-to-all-start.1 = ((bf16[16,128,128]{2,1,0:T(8,128)(2,1)}), bf16[16,128,128]{2,1,0:T(8,128)(2,1)}, u32[]{:S(2)}, u32[]{:S(2)}) async-start(bf16[16,128,128]{2,1,0:T(8,128)(2,1)} %bitcast.13), calls=%async_computation.1 | async-start | bytes 1048576 | tf_op jit(solution)/shard_map/all_to_all | solution.py:629
  158.5 3.0 %convolution_convert_fusion.2.refs_0_.refs_1_ = bf16[384,2048]{1,0:T(8,128)(2,1)S(1)} fusion(bf16[384,2048]{1,0:T(8,128)(2,1)S(1)} %assemble.13, bf16[384,2048]{1,0:T(8,128)(2,1)} %get-tuple-element.108, bf16[384,384]{1,0:T(8,128)(2,1)S(1)} %slice.16, bf16[384,384]{1,0:T(8,128)(2,1)S(1)} %slice.12), kind=kOutput, calls=%fused_computation.3 | convolution fusion | flops 1216217088 | bytes 5308416 | tf_op jit(solution)/shard_map/dot_general | solution.py:597
  161.5 6.3 %collective-permute-done.33.refs_1_.refs_4_ = bf16[128,2304]{1,0:T(8,128)(2,1)} collective-permute-done((bf16[128,2304]{1,0:T(8,128)(2,1)}, bf16[128,2304]{1,0:T(8,128)(2,1)}, u32[]{:S(2)}, u32[]{:S(2)}) %collective-permute-start.33) | collective-permute-done | bytes 589856 | tf_op jit(solution)/shard_map/ppermute | solution.py:366
  167.8 10.0 %collective-permute-done.34.refs_2_.refs_5_ = bf16[128,2304]{1,0:T(8,128)(2,1)} collective-permute-done((bf16[128,2304]{1,0:T(8,128)(2,1)}, bf16[128,2304]{1,0:T(8,128)(2,1)}, u32[]{:S(2)}, u32[]{:S(2)}) %collective-permute-start.34) | collective-permute-done | bytes 589856 | tf_op jit(solution)/shard_map/ppermute | solution.py:371
  177.8 3.2 %assemble.18 = (bf16[128,2048]{1,0:T(8,128)(2,1)}, bf16[128,2048]{1,0:T(8,128)(2,1)}, bf16[128,1536]{1,0:T(8,128)(2,1)}, bf16[128,1536]{1,0:T(8,128)(2,1)}) custom-call(bf16[896,2048]{1,0:T(8,128)(2,1)S(1)} %copy-done.1, bf16[384,2048]{1,0:T(8,128)(2,1)S(1)} %convolution_convert_fusion.2.refs_0_.refs_1_, bf16[128,4096]{1,0:T(8,128)(2,1)} %collective-permute-done.31.refs_2_, ...), custom_call_target="tpu_custom_call" | custom-call | flops 1835008 | bytes 7340032 | tf_op jit(solution)/shard_map/assemble/pallas_call | solution.py:447
  182.5 1.9 collective-permute-start.37
  184.4 1.9 collective-permute-start.38
  186.3 2.0 copy.9
  188.4 1.3 assemble.17.refs_0_
  189.7 6.9 %collective-permute-done.37.refs_3_ = bf16[128,1536]{1,0:T(8,128)(2,1)S(1)} collective-permute-done((bf16[128,1536]{1,0:T(8,128)(2,1)}, bf16[128,1536]{1,0:T(8,128)(2,1)S(1)}, u32[]{:S(2)}, u32[]{:S(2)}) %collective-permute-start.37) | collective-permute-done | bytes 393248 | tf_op jit(solution)/shard_map/ppermute | solution.py:366
  196.6 6.7 %collective-permute-done.38.refs_4_ = bf16[128,1536]{1,0:T(8,128)(2,1)S(1)} collective-permute-done((bf16[128,1536]{1,0:T(8,128)(2,1)}, bf16[128,1536]{1,0:T(8,128)(2,1)S(1)}, u32[]{:S(2)}, u32[]{:S(2)}) %collective-permute-start.38) | collective-permute-done | bytes 393248 | tf_op jit(solution)/shard_map/ppermute | solution.py:371
  (121 shorter events, 27.4 us)
Async XLA Ops:
  2.8 25.4 %copy-start.4 = (bf16[128,2048]{1,0:T(8,128)(2,1)S(1)}, bf16[128,2048]{1,0:T(8,128)(2,1)}, u32[]{:S(2)}) copy-start(bf16[128,2048]{1,0:T(8,128)(2,1)} %get-tuple-element.103.refs_0_) | copy-start | bytes 1572868
  2.8 25.4 %collective-permute-start.1 = (bf16[128,2048]{1,0:T(8,128)(2,1)}, bf16[128,2048]{1,0:T(8,128)(2,1)S(1)}, u32[]{:S(2)}, u32[]{:S(2)}) collective-permute-start(bf16[128,2048]{1,0:T(8,128)(2,1)} %get-tuple-element.103.refs_0_), channel_id=1, source_target_pairs={{0,4},{2,6},{4,0},{6,2},{8,12},{10,14},{12,8},{14,10},{16,20},{18,... | collective-permute-start | bytes 1572872 | tf_op jit(solution)/shard_map/ppermute | solution.py:361
  5.8 22.4 %collective-permute-start = (bf16[128,2048]{1,0:T(8,128)(2,1)}, bf16[128,2048]{1,0:T(8,128)(2,1)S(1)}, u32[]{:S(2)}, u32[]{:S(2)}) collective-permute-start(bf16[128,2048]{1,0:T(8,128)(2,1)} %get-tuple-element.103.refs_0_), channel_id=1, source_target_pairs={{0,2},{2,0},{4,6},{6,4},{8,10},{10,8},{12,14},{14,12},{16,18},{18,... | collective-permute-start | bytes 1572872 | tf_op jit(solution)/shard_map/ppermute | solution.py:357
  7.3 13.5 %collective-permute-start.3 = (bf16[96,2048]{1,0:T(8,128)(2,1)}, bf16[96,2048]{1,0:T(8,128)(2,1)S(1)}, u32[]{:S(2)}, u32[]{:S(2)}) collective-permute-start(bf16[96,2048]{1,0:T(8,128)(2,1)} %get-tuple-element.94), channel_id=1, source_target_pairs={{8,0},{10,2},{12,4},{14,6},{16,8},{18,10},{20,12},{22,14},{24,16},... | collective-permute-start | bytes 1179656 | tf_op jit(solution)/shard_map/ppermute | solution.py:371
  10.9 17.3 %collective-permute-start.2 = (bf16[96,2048]{1,0:T(8,128)(2,1)}, bf16[96,2048]{1,0:T(8,128)(2,1)S(1)}, u32[]{:S(2)}, u32[]{:S(2)}) collective-permute-start(bf16[96,2048]{1,0:T(8,128)(2,1)} %get-tuple-element.94), channel_id=1, source_target_pairs={{0,8},{2,10},{4,12},{6,14},{8,16},{10,18},{12,20},{14,22},{16,24},... | collective-permute-start | bytes 1179656 | tf_op jit(solution)/shard_map/ppermute | solution.py:366
  14.5 54.3 %collective-permute-start.16 = (bf16[384,2048]{1,0:T(8,128)(2,1)}, bf16[384,2048]{1,0:T(8,128)(2,1)}, u32[]{:S(2)}, u32[]{:S(2)}) collective-permute-start(bf16[384,2048]{1,0:T(8,128)(2,1)} %get-tuple-element.135), channel_id=1, source_target_pairs={{0,1},{1,0},{2,3},{3,2},{4,5},{5,4},{6,7},{7,6},{8,9},{9,8},{10,11... | collective-permute-start | bytes 4718600 | tf_op jit(solution)/shard_map/ppermute | solution.py:353
  20.8 13.4 %copy-start.6 = (bf16[96,2048]{1,0:T(8,128)(2,1)}, bf16[96,2048]{1,0:T(8,128)(2,1)S(1)}, u32[]{:S(2)}) copy-start(bf16[96,2048]{1,0:T(8,128)(2,1)S(1)} %collective-permute-done.3.refs_4_) | copy-start | bytes 1179652
  30.4 7.2 %copy-start.9 = (bf16[96,2048]{1,0:T(8,128)(2,1)S(1)}, bf16[96,2048]{1,0:T(8,128)(2,1)}, u32[]{:S(2)}) copy-start(bf16[96,2048]{1,0:T(8,128)(2,1)} %copy-done.8) | copy-start | bytes 1179652
  30.4 18.3 %collective-permute-start.6 = (bf16[144,2048]{1,0:T(8,128)(2,1)}, bf16[144,2048]{1,0:T(8,128)(2,1)S(1)}, u32[]{:S(2)}, u32[]{:S(2)}) collective-permute-start(bf16[144,2048]{1,0:T(8,128)(2,1)} %get-tuple-element.113), channel_id=1, source_target_pairs={{0,8},{2,10},{4,12},{6,14},{8,16},{10,18},{12,20},{14,22},{16,24},... | collective-permute-start | bytes 1769480 | tf_op jit(solution)/shard_map/ppermute | solution.py:366
  32.0 28.2 %collective-permute-start.7 = (bf16[144,2048]{1,0:T(8,128)(2,1)}, bf16[144,2048]{1,0:T(8,128)(2,1)S(1)}, u32[]{:S(2)}, u32[]{:S(2)}) collective-permute-start(bf16[144,2048]{1,0:T(8,128)(2,1)} %get-tuple-element.114), channel_id=1, source_target_pairs={{8,0},{10,2},{12,4},{14,6},{16,8},{18,10},{20,12},{22,14},{24,16},... | collective-permute-start | bytes 1769480 | tf_op jit(solution)/shard_map/ppermute | solution.py:371
  34.3 26.0 %collective-permute-start.4 = (bf16[256,2048]{1,0:T(8,128)(2,1)}, bf16[256,2048]{1,0:T(8,128)(2,1)S(1)}, u32[]{:S(2)}, u32[]{:S(2)}) collective-permute-start(bf16[256,2048]{1,0:T(8,128)(2,1)} %get-tuple-element.111), channel_id=1, source_target_pairs={{0,2},{2,0},{4,6},{6,4},{8,10},{10,8},{12,14},{14,12},{16,18},{18,... | collective-permute-start | bytes 3145736 | tf_op jit(solution)/shard_map/ppermute | solution.py:357
  34.9 25.4 %collective-permute-start.5 = (bf16[256,2048]{1,0:T(8,128)(2,1)}, bf16[256,2048]{1,0:T(8,128)(2,1)S(1)}, u32[]{:S(2)}, u32[]{:S(2)}) collective-permute-start(bf16[256,2048]{1,0:T(8,128)(2,1)} %get-tuple-element.112), channel_id=1, source_target_pairs={{0,4},{2,6},{4,0},{6,2},{8,12},{10,14},{12,8},{14,10},{16,20},{18,... | collective-permute-start | bytes 3145736 | tf_op jit(solution)/shard_map/ppermute | solution.py:361
  42.1 54.2 %all-to-all-start = ((bf16[128,16,128]{2,0,1:T(8,128)(2,1)}), bf16[128,16,128]{2,0,1:T(8,128)(2,1)}, u32[]{:S(2)}, u32[]{:S(2)}) async-start(bf16[128,16,128]{2,0,1:T(8,128)(2,1)} %copy.8), calls=%async_computation | async-start | bytes 1048576 | tf_op jit(solution)/shard_map/all_to_all | solution.py:494
  60.4 16.4 %collective-permute-start.10 = (bf16[80,2048]{1,0:T(8,128)(2,1)S(1)}, bf16[80,2048]{1,0:T(8,128)(2,1)S(1)}, u32[]{:S(2)}, u32[]{:S(2)}) collective-permute-start(bf16[80,2048]{1,0:T(8,128)(2,1)S(1)} %get-tuple-element.121), channel_id=1, source_target_pairs={{0,8},{2,10},{4,12},{6,14},{8,16},{10,18},{12,20},{14,22},{16,24},... | collective-permute-start | bytes 983048 | tf_op jit(solution)/shard_map/ppermute | solution.py:366
  60.9 19.7 %collective-permute-start.11 = (bf16[80,2048]{1,0:T(8,128)(2,1)S(1)}, bf16[80,2048]{1,0:T(8,128)(2,1)S(1)}, u32[]{:S(2)}, u32[]{:S(2)}) collective-permute-start(bf16[80,2048]{1,0:T(8,128)(2,1)S(1)} %get-tuple-element.122), channel_id=1, source_target_pairs={{8,0},{10,2},{12,4},{14,6},{16,8},{18,10},{20,12},{22,14},{24,16},... | collective-permute-start | bytes 983048 | tf_op jit(solution)/shard_map/ppermute | solution.py:371
  64.3 19.5 %collective-permute-start.8 = (bf16[192,2048]{1,0:T(8,128)(2,1)S(1)}, bf16[192,2048]{1,0:T(8,128)(2,1)S(1)}, u32[]{:S(2)}, u32[]{:S(2)}) collective-permute-start(bf16[192,2048]{1,0:T(8,128)(2,1)S(1)} %get-tuple-element.119), channel_id=1, source_target_pairs={{0,2},{2,0},{4,6},{6,4},{8,10},{10,8},{12,14},{14,12},{16,18},{18,... | collective-permute-start | bytes 2359304 | tf_op jit(solution)/shard_map/ppermute | solution.py:357
  64.9 18.8 %collective-permute-start.9 = (bf16[192,2048]{1,0:T(8,128)(2,1)S(1)}, bf16[192,2048]{1,0:T(8,128)(2,1)S(1)}, u32[]{:S(2)}, u32[]{:S(2)}) collective-permute-start(bf16[192,2048]{1,0:T(8,128)(2,1)S(1)} %get-tuple-element.120), channel_id=1, source_target_pairs={{0,4},{2,6},{4,0},{6,2},{8,12},{10,14},{12,8},{14,10},{16,20},{18,... | collective-permute-start | bytes 2359304 | tf_op jit(solution)/shard_map/ppermute | solution.py:361
  73.1 23.2 %collective-permute-start.17 = (bf16[576,384]{1,0:T(8,128)(2,1)}, bf16[576,384]{1,0:T(8,128)(2,1)S(1)}, u32[]{:S(2)}, u32[]{:S(2)}) collective-permute-start(bf16[576,384]{1,0:T(8,128)(2,1)} %convolution_convert_fusion.4), channel_id=1, source_target_pairs={{0,1},{1,0},{2,3},{3,2},{4,5},{5,4},{6,7},{7,6},{8,9},{9,8},{10,11... | collective-permute-start | bytes 1327112 | tf_op jit(solution)/shard_map/ppermute | solution.py:353
  83.9 9.5 %collective-permute-start.14 = (bf16[16,2048]{1,0:T(8,128)(2,1)S(1)}, bf16[16,2048]{1,0:T(8,128)(2,1)S(1)}, u32[]{:S(2)}, u32[]{:S(2)}) collective-permute-start(bf16[16,2048]{1,0:T(8,128)(2,1)S(1)} %get-tuple-element.129), channel_id=1, source_target_pairs={{0,8},{2,10},{4,12},{6,14},{8,16},{10,18},{12,20},{14,22},{16,24},... | collective-permute-start | bytes 196616 | tf_op jit(solution)/shard_map/ppermute | solution.py:366
  84.0 9.4 %collective-permute-start.15 = (bf16[16,2048]{1,0:T(8,128)(2,1)S(1)}, bf16[16,2048]{1,0:T(8,128)(2,1)S(1)}, u32[]{:S(2)}, u32[]{:S(2)}) collective-permute-start(bf16[16,2048]{1,0:T(8,128)(2,1)S(1)} %get-tuple-element.130), channel_id=1, source_target_pairs={{8,0},{10,2},{12,4},{14,6},{16,8},{18,10},{20,12},{22,14},{24,16},... | collective-permute-start | bytes 196616 | tf_op jit(solution)/shard_map/ppermute | solution.py:371
  87.7 6.1 %collective-permute-start.12 = (bf16[48,2048]{1,0:T(8,128)(2,1)S(1)}, bf16[48,2048]{1,0:T(8,128)(2,1)S(1)}, u32[]{:S(2)}, u32[]{:S(2)}) collective-permute-start(bf16[48,2048]{1,0:T(8,128)(2,1)S(1)} %get-tuple-element.127), channel_id=1, source_target_pairs={{0,2},{2,0},{4,6},{6,4},{8,10},{10,8},{12,14},{14,12},{16,18},{18,... | collective-permute-start | bytes 589832 | tf_op jit(solution)/shard_map/ppermute | solution.py:357
  88.7 5.7 %collective-permute-start.13 = (bf16[48,2048]{1,0:T(8,128)(2,1)S(1)}, bf16[48,2048]{1,0:T(8,128)(2,1)S(1)}, u32[]{:S(2)}, u32[]{:S(2)}) collective-permute-start(bf16[48,2048]{1,0:T(8,128)(2,1)S(1)} %get-tuple-element.128), channel_id=1, source_target_pairs={{0,4},{2,6},{4,0},{6,2},{8,12},{10,14},{12,8},{14,10},{16,20},{18,... | collective-permute-start | bytes 589832 | tf_op jit(solution)/shard_map/ppermute | solution.py:361
  93.3 3.0 %collective-permute-start.18 = (bf16[800,384]{1,0:T(8,128)(2,1)}, bf16[800,384]{1,0:T(8,128)(2,1)}, u32[]{:S(2)}, u32[]{:S(2)}) collective-permute-start(bf16[800,384]{1,0:T(8,128)(2,1)} %convolution_convert_fusion.3), channel_id=1, source_target_pairs={{0,1},{1,0},{2,3},{3,2},{4,5},{5,4},{6,7},{7,6},{8,9},{9,8},{10,11... | collective-permute-start | bytes 1843208 | tf_op jit(solution)/shard_map/ppermute | solution.py:353
  93.4 3.8 %collective-permute-start.19 = (bf16[544,384]{1,0:T(8,128)(2,1)}, bf16[544,384]{1,0:T(8,128)(2,1)}, u32[]{:S(2)}, u32[]{:S(2)}) collective-permute-start(bf16[544,384]{1,0:T(8,128)(2,1)} %convolution_convert_fusion.5), channel_id=1, source_target_pairs={{0,1},{1,0},{2,3},{3,2},{4,5},{5,4},{6,7},{7,6},{8,9},{9,8},{10,11... | collective-permute-start | bytes 1253384 | tf_op jit(solution)/shard_map/ppermute | solution.py:353
  95.7 1.5 collective-permute-start.20
  99.5 15.4 %copy-start.17 = (bf16[384,2048]{1,0:T(8,128)(2,1)S(1)}, bf16[384,2048]{1,0:T(8,128)(2,1)}, u32[]{:S(2)}) copy-start(bf16[384,2048]{1,0:T(8,128)(2,1)} %get-tuple-element.108) | copy-start | bytes 4718596
  112.9 15.4 %copy-start.10 = (bf16[1280,384]{1,0:T(8,128)(2,1)}, bf16[1280,384]{1,0:T(8,128)(2,1)S(1)}, u32[]{:S(2)}) copy-start(bf16[1280,384]{1,0:T(8,128)(2,1)S(1)} %get-tuple-element.148) | copy-start | bytes 2949124
  112.9 2.0 collective-permute-start.21
  113.0 19.3 %collective-permute-start.26 = (bf16[1280,384]{1,0:T(8,128)(2,1)S(1)}, bf16[1280,384]{1,0:T(8,128)(2,1)S(1)}, u32[]{:S(2)}, u32[]{:S(2)}) collective-permute-start(bf16[1280,384]{1,0:T(8,128)(2,1)S(1)} %get-tuple-element.148), channel_id=1, source_target_pairs={{0,1},{1,0},{2,3},{3,2},{4,5},{5,4},{6,7},{7,6},{8,9},{9,8},{10,11... | collective-permute-start | bytes 2949128 | tf_op jit(solution)/shard_map/ppermute | solution.py:353
  117.8 8.7 %collective-permute-start.22 = (bf16[128,768]{1,0:T(8,128)(2,1)S(1)}, bf16[128,768]{1,0:T(8,128)(2,1)S(1)}, u32[]{:S(2)}, u32[]{:S(2)}) collective-permute-start(bf16[128,768]{1,0:T(8,128)(2,1)S(1)} %get-tuple-element.139), channel_id=1, source_target_pairs={{0,2},{2,0},{4,6},{6,4},{8,10},{10,8},{12,14},{14,12},{16,18},{18,... | collective-permute-start | bytes 589832 | tf_op jit(solution)/shard_map/ppermute | solution.py:357
  119.0 7.5 %collective-permute-start.23 = (bf16[128,768]{1,0:T(8,128)(2,1)S(1)}, bf16[128,768]{1,0:T(8,128)(2,1)S(1)}, u32[]{:S(2)}, u32[]{:S(2)}) collective-permute-start(bf16[128,768]{1,0:T(8,128)(2,1)S(1)} %get-tuple-element.140), channel_id=1, source_target_pairs={{0,4},{2,6},{4,0},{6,2},{8,12},{10,14},{12,8},{14,10},{16,20},{18,... | collective-permute-start | bytes 589832 | tf_op jit(solution)/shard_map/ppermute | solution.py:361
  120.4 6.1 %collective-permute-start.24 = (bf16[128,256]{1,0:T(8,128)(2,1)S(1)}, bf16[128,256]{1,0:T(8,128)(2,1)S(1)}, u32[]{:S(2)}, u32[]{:S(2)}) collective-permute-start(bf16[128,256]{1,0:T(8,128)(2,1)S(1)} %get-tuple-element.141), channel_id=1, source_target_pairs={{0,8},{2,10},{4,12},{6,14},{8,16},{10,18},{12,20},{14,22},{16,24},... | collective-permute-start | bytes 196616 | tf_op jit(solution)/shard_map/ppermute | solution.py:366
  120.4 6.1 %collective-permute-start.25 = (bf16[128,256]{1,0:T(8,128)(2,1)S(1)}, bf16[128,256]{1,0:T(8,128)(2,1)S(1)}, u32[]{:S(2)}, u32[]{:S(2)}) collective-permute-start(bf16[128,256]{1,0:T(8,128)(2,1)S(1)} %get-tuple-element.142), channel_id=1, source_target_pairs={{8,0},{10,2},{12,4},{14,6},{16,8},{18,10},{20,12},{22,14},{24,16},... | collective-permute-start | bytes 196616 | tf_op jit(solution)/shard_map/ppermute | solution.py:371
  126.7 18.0 %collective-permute-start.27 = (bf16[128,3072]{1,0:T(8,128)(2,1)S(1)}, bf16[128,3072]{1,0:T(8,128)(2,1)S(1)}, u32[]{:S(2)}, u32[]{:S(2)}) collective-permute-start(bf16[128,3072]{1,0:T(8,128)(2,1)S(1)} %get-tuple-element.153), channel_id=1, source_target_pairs={{0,2},{2,0},{4,6},{6,4},{8,10},{10,8},{12,14},{14,12},{16,18},{18,... | collective-permute-start | bytes 2359304 | tf_op jit(solution)/shard_map/ppermute | solution.py:357
  127.7 17.7 %collective-permute-start.28 = (bf16[128,3072]{1,0:T(8,128)(2,1)S(1)}, bf16[128,3072]{1,0:T(8,128)(2,1)S(1)}, u32[]{:S(2)}, u32[]{:S(2)}) collective-permute-start(bf16[128,3072]{1,0:T(8,128)(2,1)S(1)} %get-tuple-element.154), channel_id=1, source_target_pairs={{0,4},{2,6},{4,0},{6,2},{8,12},{10,14},{12,8},{14,10},{16,20},{18,... | collective-permute-start | bytes 2359304 | tf_op jit(solution)/shard_map/ppermute | solution.py:361
  128.4 12.5 %collective-permute-start.29 = (bf16[128,1280]{1,0:T(8,128)(2,1)S(1)}, bf16[128,1280]{1,0:T(8,128)(2,1)S(1)}, u32[]{:S(2)}, u32[]{:S(2)}) collective-permute-start(bf16[128,1280]{1,0:T(8,128)(2,1)S(1)} %get-tuple-element.155), channel_id=1, source_target_pairs={{0,8},{2,10},{4,12},{6,14},{8,16},{10,18},{12,20},{14,22},{16,24},... | collective-permute-start | bytes 983048 | tf_op jit(solution)/shard_map/ppermute | solution.py:366
  128.5 15.1 %collective-permute-start.30 = (bf16[128,1280]{1,0:T(8,128)(2,1)S(1)}, bf16[128,1280]{1,0:T(8,128)(2,1)S(1)}, u32[]{:S(2)}, u32[]{:S(2)}) collective-permute-start(bf16[128,1280]{1,0:T(8,128)(2,1)S(1)} %get-tuple-element.156), channel_id=1, source_target_pairs={{8,0},{10,2},{12,4},{14,6},{16,8},{18,10},{20,12},{22,14},{24,16},... | collective-permute-start | bytes 983048 | tf_op jit(solution)/shard_map/ppermute | solution.py:371
  135.6 11.6 %copy-start = (bf16[896,2048]{1,0:T(8,128)(2,1)}, bf16[896,2048]{1,0:T(8,128)(2,1)S(1)}, u32[]{:S(2)}) copy-start(bf16[896,2048]{1,0:T(8,128)(2,1)S(1)} %convolution_convert_fusion.refs_1_.refs_0_) | copy-start | bytes 11010052
  147.2 30.6 %collective-permute-start.31 = (bf16[128,4096]{1,0:T(8,128)(2,1)}, bf16[128,4096]{1,0:T(8,128)(2,1)}, u32[]{:S(2)}, u32[]{:S(2)}) collective-permute-start(bf16[128,4096]{1,0:T(8,128)(2,1)} %get-tuple-element.166), channel_id=1, source_target_pairs={{0,2},{2,0},{4,6},{6,4},{8,10},{10,8},{12,14},{14,12},{16,18},{18,... | collective-permute-start | bytes 3145736 | tf_op jit(solution)/shard_map/ppermute | solution.py:357
  148.3 29.5 %collective-permute-start.32 = (bf16[128,4096]{1,0:T(8,128)(2,1)}, bf16[128,4096]{1,0:T(8,128)(2,1)}, u32[]{:S(2)}, u32[]{:S(2)}) collective-permute-start(bf16[128,4096]{1,0:T(8,128)(2,1)} %get-tuple-element.167), channel_id=1, source_target_pairs={{0,4},{2,6},{4,0},{6,2},{8,12},{10,14},{12,8},{14,10},{16,20},{18,... | collective-permute-start | bytes 3145736 | tf_op jit(solution)/shard_map/ppermute | solution.py:361
  149.4 18.4 %collective-permute-start.33 = (bf16[128,2304]{1,0:T(8,128)(2,1)}, bf16[128,2304]{1,0:T(8,128)(2,1)}, u32[]{:S(2)}, u32[]{:S(2)}) collective-permute-start(bf16[128,2304]{1,0:T(8,128)(2,1)} %get-tuple-element.168), channel_id=1, source_target_pairs={{0,8},{2,10},{4,12},{6,14},{8,16},{10,18},{12,20},{14,22},{16,24},... | collective-permute-start | bytes 1769480 | tf_op jit(solution)/shard_map/ppermute | solution.py:366
  149.8 28.0 %collective-permute-start.34 = (bf16[128,2304]{1,0:T(8,128)(2,1)}, bf16[128,2304]{1,0:T(8,128)(2,1)}, u32[]{:S(2)}, u32[]{:S(2)}) collective-permute-start(bf16[128,2304]{1,0:T(8,128)(2,1)} %get-tuple-element.169), channel_id=1, source_target_pairs={{8,0},{10,2},{12,4},{14,6},{16,8},{18,10},{20,12},{22,14},{24,16},... | collective-permute-start | bytes 1769480 | tf_op jit(solution)/shard_map/ppermute | solution.py:371
  153.2 33.1 %all-to-all-start.1 = ((bf16[16,128,128]{2,1,0:T(8,128)(2,1)}), bf16[16,128,128]{2,1,0:T(8,128)(2,1)}, u32[]{:S(2)}, u32[]{:S(2)}) async-start(bf16[16,128,128]{2,1,0:T(8,128)(2,1)} %bitcast.13), calls=%async_computation.1 | async-start | bytes 1048576 | tf_op jit(solution)/shard_map/all_to_all | solution.py:629
  158.5 19.3 %copy-start.1 = (bf16[896,2048]{1,0:T(8,128)(2,1)S(1)}, bf16[896,2048]{1,0:T(8,128)(2,1)}, u32[]{:S(2)}) copy-start(bf16[896,2048]{1,0:T(8,128)(2,1)} %copy-done) | copy-start | bytes 11010052
  181.0 22.2 %collective-permute-start.35 = (bf16[128,2048]{1,0:T(8,128)(2,1)}, bf16[128,2048]{1,0:T(8,128)(2,1)S(1)}, u32[]{:S(2)}, u32[]{:S(2)}) collective-permute-start(bf16[128,2048]{1,0:T(8,128)(2,1)} %get-tuple-element.174), channel_id=1, source_target_pairs={{0,2},{2,0},{4,6},{6,4},{8,10},{10,8},{12,14},{14,12},{16,18},{18,... | collective-permute-start | bytes 1572872 | tf_op jit(solution)/shard_map/ppermute | solution.py:357
  182.0 21.2 %collective-permute-start.36 = (bf16[128,2048]{1,0:T(8,128)(2,1)}, bf16[128,2048]{1,0:T(8,128)(2,1)S(1)}, u32[]{:S(2)}, u32[]{:S(2)}) collective-permute-start(bf16[128,2048]{1,0:T(8,128)(2,1)} %get-tuple-element.175), channel_id=1, source_target_pairs={{0,4},{2,6},{4,0},{6,2},{8,12},{10,14},{12,8},{14,10},{16,20},{18,... | collective-permute-start | bytes 1572872 | tf_op jit(solution)/shard_map/ppermute | solution.py:361
  182.5 14.1 %collective-permute-start.37 = (bf16[128,1536]{1,0:T(8,128)(2,1)}, bf16[128,1536]{1,0:T(8,128)(2,1)S(1)}, u32[]{:S(2)}, u32[]{:S(2)}) collective-permute-start(bf16[128,1536]{1,0:T(8,128)(2,1)} %get-tuple-element.176), channel_id=1, source_target_pairs={{0,8},{2,10},{4,12},{6,14},{8,16},{10,18},{12,20},{14,22},{16,24},... | collective-permute-start | bytes 1179656 | tf_op jit(solution)/shard_map/ppermute | solution.py:366
  184.4 18.8 %collective-permute-start.38 = (bf16[128,1536]{1,0:T(8,128)(2,1)}, bf16[128,1536]{1,0:T(8,128)(2,1)S(1)}, u32[]{:S(2)}, u32[]{:S(2)}) collective-permute-start(bf16[128,1536]{1,0:T(8,128)(2,1)} %get-tuple-element.177), channel_id=1, source_target_pairs={{8,0},{10,2},{12,4},{14,6},{16,8},{18,10},{20,12},{22,14},{24,16},... | collective-permute-start | bytes 1179656 | tf_op jit(solution)/shard_map/ppermute | solution.py:371
  (13 other events, 35.3 us)
